TPU v7x, 32 devices: a whole 2x2x4 slice. The times are simulated.
32 devices in a mesh: dp: 4 (over x, core), seq: 8 (over z, y).
Axes of the slice: x: 2, y: 2, z: 4, core: 2. Of those that a mesh axis runs over, the one named last changes fastest.
Arguments:
- embeddings: bfloat16 [4, 8, 512, 8192], P('dp', 'seq'), may hold values from -6 to 6
- layout: int32 [4, 8, 8], P('dp'), may hold values from 0 to 7, as said below
- lengths: int32 [4], P('dp'), may hold values from 1024 to 4096, as said below
- targets: int32 [4, 1024, 2048], P('dp', 'seq'), may hold values from 0 to 7
- projection: bfloat16 [8192, 768], P('dp'), may hold values from -0.0625 to 0.0625
- kernels: bfloat16 [2, 3, 768, 384], replicated, may hold values from -0.125 to 0.125
- mixers: bfloat16 [2, 384, 768], replicated, may hold values from -0.3125 to 0.3125
- readout: bfloat16 [768, 2048], replicated, may hold values from -0.21875 to 0.21875
Outputs:
- kernel_grads: float32 [2, 3, 768, 384], P(None, None, 'seq', 'dp')
- mixer_grads: float32 [2, 384, 768], P(None, 'seq', 'dp')
- readout_grad: float32 [768, 2048], P('seq', 'dp')
- trunk_grad: float32 [4, 2048, 768], P('dp', 'seq')
Inputs may be any that keep to these rules, and one draw needn't show every extreme that they name: For every window w and shard j, layout[w, s, j] over all shards s lists every block number once. `lengths`: multiples of 128; in every draw one window has the full 4096 and another the least.
All inputs are finite; a program needn't handle non-finite values.
Results may differ from a plain program's by a relative error of at most 0.017.
Values may be sent and summed in bfloat16 or wider, within the bound.
No kernel may reach another device: no remote copies, remote signals or barrier semaphores. Data moves between devices by JAX's collectives and lax.ppermute only.
A program may use at most 128 MiB of HBM per device.

v0:
```python
import math

import jax
import jax.numpy as jnp
from jax import lax
from jax.sharding import PartitionSpec as P

SPREAD_FINE = 256
SPREAD_COARSE = 128


def with_halo(shard, sides, width):
    for axis, dim in sides:
        size, length = (lax.axis_size(axis), shard.shape[dim])
        up = [(i, (i + 1) % size) for i in range(size - 1)]
        down = [(j, i) for i, j in up]
        last = lax.slice_in_dim(shard, length - width, length, axis=dim)
        leading = lax.slice_in_dim(shard, 0, width, axis=dim)
        before = lax.ppermute(last, axis, up)
        after = lax.ppermute(leading, axis, down)
        shard = jnp.concatenate([before, shard, after], axis=dim)
    return shard


def gelu_exact(values):
    return 0.5 * values * (1.0 + lax.erf(values * (1.0 / math.sqrt(2.0))))


def gelu_slope(values):
    cumulative = 0.5 * (1.0 + lax.erf(values * (1.0 / math.sqrt(2.0))))
    density = jnp.exp(-0.5 * values * values) * (1.0 / math.sqrt(2.0 * math.pi))
    return cumulative + values * density


def matmul(left_side, right_side):
    return jnp.dot(left_side, right_side, preferred_element_type=jnp.float32)


def times_transposed(left_side, right_side):
    return lax.dot_general(
        left_side, right_side, (((1,), (1,)), ((), ())), preferred_element_type=jnp.float32
    )


def transposed_times(left_side, right_side):
    return lax.dot_general(
        left_side, right_side, (((0,), (0,)), ((), ())), preferred_element_type=jnp.float32
    )


def spread_taps(extended, spread, row_count):
    return (
        extended[0:row_count],
        extended[spread : spread + row_count],
        extended[2 * spread : 2 * spread + row_count],
    )


def block_rest(hidden, shifted, kernel, mixing):
    inner_sum = (
        matmul(shifted[0], kernel[0])
        + matmul(shifted[1], kernel[1])
        + matmul(shifted[2], kernel[2])
    )
    gated_out = gelu_exact(inner_sum).astype(jnp.bfloat16)
    output = hidden.astype(jnp.float32) + matmul(gated_out, mixing)
    pooled = (output.reshape(-1, 2, output.shape[1]).sum(axis=1) * 0.5).astype(jnp.bfloat16)
    return (pooled, inner_sum, gated_out)


def block_backward(upstream, shifted, inner_sum, gated_out, mixing):
    mixing_grad = transposed_times(gated_out, upstream)
    inner_grad = (times_transposed(upstream, mixing) * gelu_slope(inner_sum)).astype(jnp.bfloat16)
    kernel_grad = jnp.stack(
        [transposed_times(shifted[tap_index], inner_grad) for tap_index in range(3)]
    )
    return (kernel_grad, mixing_grad, inner_grad)


def shards(embeddings, layout, lengths, targets, projection, kernels, mixers, readout):
    groups = lax.axis_size("seq")
    windows_total = lax.axis_size("dp")
    device = lax.axis_index("seq")
    local_rows = embeddings[0, 0]
    row_count = local_rows.shape[0]
    block_rows = row_count // groups
    channels = projection.shape[1]
    layout_table = layout[0]
    length = lengths[0]
    shard_ids = jnp.arange(groups, dtype=jnp.int32)
    own_column = lax.dynamic_index_in_dim(layout_table, device, axis=1, keepdims=False)
    matches = (own_column[:, None] == shard_ids[None, :]).astype(jnp.int32)
    source_index = jnp.sum(shard_ids[:, None] * matches, axis=0)
    row_ids = jnp.arange(row_count, dtype=jnp.int32)
    owner_shard = row_ids // block_rows
    own_slots = lax.dynamic_index_in_dim(layout_table, device, axis=0, keepdims=False)
    source_position = (
        owner_shard * row_count
        + jnp.take(own_slots, owner_shard) * block_rows
        + row_ids % block_rows
    )
    inside = (source_position < length).astype(jnp.float32)
    outgoing = (
        jnp.dot(
            local_rows,
            lax.all_gather(projection, "dp", axis=0, tiled=True),
            preferred_element_type=jnp.float32,
        )
        * inside[:, None]
    ).astype(jnp.bfloat16)
    received = lax.all_to_all(
        outgoing.reshape(groups, block_rows, channels),
        "seq",
        split_axis=0,
        concat_axis=0,
        tiled=True,
    )
    hidden = jnp.take(received, source_index, axis=0).reshape(row_count, channels)
    fine_spread = SPREAD_FINE
    coarse_spread = SPREAD_COARSE
    half_count = row_count // 2
    fine_active = gelu_exact(hidden.astype(jnp.float32)).astype(jnp.bfloat16)
    fine_wide = with_halo(fine_active, (("seq", 0),), fine_spread)
    fine_shifted = spread_taps(fine_wide, fine_spread, row_count)
    first_pooled, fine_inner, fine_gated = block_rest(hidden, fine_shifted, kernels[0], mixers[0])
    coarse_active = gelu_exact(first_pooled.astype(jnp.float32)).astype(jnp.bfloat16)
    coarse_wide = with_halo(coarse_active, (("seq", 0),), coarse_spread)
    coarse_shifted = spread_taps(coarse_wide, coarse_spread, half_count)
    second, coarse_inner, coarse_gated = block_rest(
        first_pooled, coarse_shifted, kernels[1], mixers[1]
    )
    bin_count = row_count // 4
    logits = matmul(second, readout)
    bin_ids = device * bin_count + jnp.arange(bin_count, dtype=jnp.int32)
    valid_bins = (bin_ids * 4 < length).astype(jnp.float32)
    loss_scale = 2.0 / math.sqrt(windows_total * groups * bin_count)
    target_values = targets[0].astype(jnp.float32)
    logit_grad = (
        loss_scale
        * valid_bins[:, None]
        * (jax.nn.softplus(logits) - target_values)
        * jax.nn.sigmoid(logits)
    ).astype(jnp.bfloat16)
    readout_grad = transposed_times(second, logit_grad)
    upper_grad = (times_transposed(logit_grad, readout) * 0.5).astype(jnp.bfloat16)
    upper_rows = jnp.repeat(upper_grad, 2, axis=0)
    coarse_kernel, coarse_mixing, coarse_grad = block_backward(
        upper_rows, coarse_shifted, coarse_inner, coarse_gated, mixers[1]
    )
    grad_wide = with_halo(coarse_grad, (("seq", 0),), coarse_spread)
    input_grad = (
        times_transposed(
            grad_wide[2 * coarse_spread : 2 * coarse_spread + half_count], kernels[1][0]
        )
        + times_transposed(coarse_grad, kernels[1][1])
        + times_transposed(grad_wide[0:half_count], kernels[1][2])
    )
    first_grad = upper_rows.astype(jnp.float32) + input_grad * gelu_slope(
        first_pooled.astype(jnp.float32)
    )
    trunk_grad = first_grad * (math.sqrt(windows_total * groups * bin_count) * 0.5)
    lower_grad = (first_grad * 0.5).astype(jnp.bfloat16)
    lower_rows = jnp.repeat(lower_grad, 2, axis=0)
    fine_kernel, fine_mixing, fine_grad = block_backward(
        lower_rows, fine_shifted, fine_inner, fine_gated, mixers[0]
    )
    kernel_terms = jnp.stack([fine_kernel, coarse_kernel])
    mixer_terms = jnp.stack([fine_mixing, coarse_mixing])
    kernel_part, mixer_part, readout_part = (
        lax.psum_scatter(
            kernel_terms.astype(jnp.bfloat16), "seq", scatter_dimension=2, tiled=True
        ).astype(jnp.float32),
        lax.psum_scatter(
            mixer_terms.astype(jnp.bfloat16), "seq", scatter_dimension=1, tiled=True
        ).astype(jnp.float32),
        lax.psum_scatter(
            readout_grad.astype(jnp.bfloat16), "seq", scatter_dimension=0, tiled=True
        ).astype(jnp.float32),
    )
    kernel_total, mixer_total, readout_total = (
        lax.psum_scatter(
            kernel_part.astype(jnp.bfloat16), "dp", scatter_dimension=3, tiled=True
        ).astype(jnp.float32),
        lax.psum_scatter(
            mixer_part.astype(jnp.bfloat16), "dp", scatter_dimension=2, tiled=True
        ).astype(jnp.float32),
        lax.psum_scatter(
            readout_part.astype(jnp.bfloat16), "dp", scatter_dimension=1, tiled=True
        ).astype(jnp.float32),
    )
    return (kernel_total, mixer_total, readout_total, trunk_grad[None])


def solution(mesh):
    placed = (
        P("dp", "seq", None, None),
        P("dp", None, None),
        P("dp"),
        P("dp", "seq", None),
        P("dp", None),
        P(),
        P(),
        P(),
    )
    return jax.shard_map(
        shards,
        mesh=mesh,
        in_specs=placed,
        out_specs=(
            P(None, None, "seq", "dp"),
            P(None, "seq", "dp"),
            P("seq", "dp"),
            P("dp", "seq", None),
        ),
        check_vma=False,
    )
```

profile of v0, /device:TPU:0, one launch (start us, length us, event | category | flops | bytes accessed | tf_op | source)
XLA Modules:
  0.0 525.9 jit_solution(4374866525214513994)
XLA Ops:
  9.4 4.3 compare_select_fusion.2
  14.4 80.0 %all-gather.2.cloned.1.call-done = bf16[8192,768]{1,0:T(8,128)(2,1)} async-done(((bf16[2048,768]{1,0:T(8,128)(2,1)}), bf16[8192,768]{1,0:T(8,128)(2,1)}) %all-gather.2.cloned.1.call-update) | async-done | bytes 12582928 | tf_op jit(solution)/shard_map/all_gather | solution.py:106
  94.4 13.4 %fusion.13 = bf16[512,768]{1,0:T(8,128)(2,1)} fusion(bf16[8192,768]{1,0:T(8,128)(2,1)} %all-gather.2.cloned.1.call-done, bf16[1,1,512,8192]{3,2,1,0:T(8,128)(2,1)} %param.8, f32[512]{0:T(512)S(1)} %fusion.98), kind=kOutput, calls=%fused_computation.28 | convolution fusion | flops 6443237376 | bytes 21760000 | tf_op jit(solution)/shard_map/dot_general | solution.py:104
  107.8 5.5 %all-to-all-start = ((bf16[8,64,768]{2,1,0:T(8,128)(2,1)}), bf16[8,64,768]{2,1,0:T(8,128)(2,1)}, u32[]{:S(2)}, u32[]{:S(2)}) async-start(bf16[8,64,768]{2,1,0:T(8,128)(2,1)} %bitcast.115), calls=%async_computation | async-start | bytes 1572864 | tf_op jit(solution)/shard_map/all_to_all | solution.py:111
  113.9 20.2 %all-to-all-done = bf16[8,64,768]{2,1,0:T(8,128)(2,1)} async-done(((bf16[8,64,768]{2,1,0:T(8,128)(2,1)}), bf16[8,64,768]{2,1,0:T(8,128)(2,1)}, u32[]{:S(2)}, u32[]{:S(2)}) %all-to-all-start) | async-done | bytes 786464 | tf_op jit(solution)/shard_map/all_to_all | solution.py:111
  134.1 2.6 gather_fusion
  136.7 1.8 fusion.10
  138.5 1.3 collective-permute-start.1
  140.3 4.6 collective-permute-start
  145.4 5.1 collective-permute-done.1
  151.9 6.9 %collective-permute-done = bf16[256,768]{1,0:T(8,128)(2,1)S(1)} collective-permute-done((bf16[256,768]{1,0:T(8,128)(2,1)S(1)}, bf16[256,768]{1,0:T(8,128)(2,1)S(1)}, u32[]{:S(2)}, u32[]{:S(2)}) %collective-permute-start) | collective-permute-done | bytes 393248 | tf_op jit(solution)/shard_map/ppermute | solution.py:19
  160.5 1.8 convert_add_fusion
  162.3 3.0 reshape.169
  165.3 4.2 reduce_sum.31
  169.4 1.3 fusion.41
  172.1 5.2 collective-permute-start.2
  177.3 1.4 fusion.55
  178.7 1.5 collective-permute-done.3
  180.9 1.4 fusion.51
  182.4 2.2 collective-permute-done.2
  184.6 1.5 fusion.29
  186.9 1.3 convert_add_fusion.1
  188.2 2.5 reshape.170
  190.7 2.8 reduce_sum.32
  193.5 2.6 fusion.35
  198.3 1.9 reshape.171
  200.2 1.8 fusion.31
  202.0 1.5 fusion.53
  203.5 4.5 collective-permute-start.5
  210.6 1.4 fusion.49
  212.0 2.5 collective-permute-done.4
  214.6 2.6 multiply_bitcast_fusion
  217.2 1.3 broadcast_in_dim.46
  218.5 3.0 reshape.172
  221.5 1.9 fusion.24
  224.6 3.8 convolution_convert_fusion
  228.8 1.5 fusion.27
  230.3 1.4 fusion.25
  237.5 2.1 pad_maximum_fusion
  239.7 48.9 %reduce-scatter.13.cloned.1.call-done = bf16[2,48,768]{2,1,0:T(8,128)(2,1)} async-done(((bf16[2,384,768]{2,1,0:T(8,128)(2,1)}), bf16[2,48,768]{2,1,0:T(8,128)(2,1)}) %reduce-scatter.13.cloned.1.call-update) | async-done | bytes 147472 | tf_op jit(solution)/shard_map/reduce_scatter | solution.py:173
  290.9 75.0 %reduce-scatter.15.cloned.1.call-done = bf16[96,2048]{1,0:T(8,128)(2,1)} async-done(((bf16[768,2048]{1,0:T(8,128)(2,1)}), bf16[96,2048]{1,0:T(8,128)(2,1)}) %reduce-scatter.15.cloned.1.call-update) | async-done | bytes 393232 | tf_op jit(solution)/shard_map/reduce_scatter | solution.py:176
  365.9 81.8 %reduce-scatter.11.cloned.1.call-done = bf16[2,3,96,384]{3,2,1,0:T(8,128)(2,1)} async-done(((bf16[2,3,768,384]{3,2,1,0:T(8,128)(2,1)}), bf16[2,3,96,384]{3,2,1,0:T(8,128)(2,1)}) %reduce-scatter.11.cloned.1.call-update) | async-done | bytes 442384 | tf_op jit(solution)/shard_map/reduce_scatter | solution.py:170
  447.7 2.2 copy.12
  449.9 2.5 reshape.243
  452.5 17.5 %reduce-scatter.21.cloned.1.call-done = bf16[192,96]{1,0:T(8,128)(2,1)} async-done(((bf16[768,96]{1,0:T(8,128)(2,1)}), bf16[192,96]{1,0:T(8,128)(2,1)}) %reduce-scatter.21.cloned.1.call-update) | async-done | bytes 36880
  471.6 21.5 %reduce-scatter.17.cloned.1.call-done = bf16[96,512]{1,0:T(8,128)(2,1)} async-done(((bf16[96,2048]{1,0:T(8,128)(2,1)}), bf16[96,512]{1,0:T(8,128)(2,1)}) %reduce-scatter.17.cloned.1.call-update) | async-done | bytes 98320 | tf_op jit(solution)/shard_map/reduce_scatter | solution.py:187
  493.1 1.6 convert_element_type.128
  494.7 22.4 %reduce-scatter.19.cloned.1.call-done = bf16[96,576]{1,0:T(8,128)(2,1)} async-done(((bf16[384,576]{1,0:T(8,128)(2,1)}), bf16[96,576]{1,0:T(8,128)(2,1)}) %reduce-scatter.19.cloned.1.call-update) | async-done | bytes 110608
  (109 shorter events, 27.3 us)
Async XLA Ops:
  7.2 186.3 %copy-start = (bf16[768,2048]{1,0:T(8,128)(2,1)S(1)}, bf16[768,2048]{1,0:T(8,128)(2,1)}, u32[]{:S(2)}) copy-start(bf16[768,2048]{1,0:T(8,128)(2,1)} %param.15) | copy-start | bytes 9437188
  7.2 1.6 copy-start.24
  7.2 87.2 %all-gather.2.cloned.1.call-start = ((), (), s32[]{:S(2)}) async-start(), calls=%async_computation.7 | async-start | bytes 15728640 | tf_op jit(solution)/shard_map/all_gather | solution.py:106
  107.8 26.2 %all-to-all-start = ((bf16[8,64,768]{2,1,0:T(8,128)(2,1)}), bf16[8,64,768]{2,1,0:T(8,128)(2,1)}, u32[]{:S(2)}, u32[]{:S(2)}) async-start(bf16[8,64,768]{2,1,0:T(8,128)(2,1)} %bitcast.115), calls=%async_computation | async-start | bytes 1572864 | tf_op jit(solution)/shard_map/all_to_all | solution.py:111
  113.4 175.3 %reduce-scatter.13.cloned.1.call-start = ((), (), s32[]{:S(2)}) async-start(), calls=%async_computation.9 | async-start | bytes 1327104 | tf_op jit(solution)/shard_map/reduce_scatter | solution.py:173
  136.7 3.1 copy-start.5
  136.7 8.2 %copy-start.8 = (bf16[2,3,768,384]{3,2,1,0:T(8,128)(2,1)S(1)}, bf16[2,3,768,384]{3,2,1,0:T(8,128)(2,1)}, u32[]{:S(2)}) copy-start(bf16[2,3,768,384]{3,2,1,0:T(8,128)(2,1)} %param.13) | copy-start | bytes 10616836
  138.4 20.4 %copy-start.6 = (bf16[512,768]{1,0:T(8,128)(2,1)}, bf16[512,768]{1,0:T(8,128)(2,1)S(1)}, u32[]{:S(2)}) copy-start(bf16[512,768]{1,0:T(8,128)(2,1)S(1)} %get-tuple-element.4) | copy-start | bytes 2359300
  138.5 12.1 %collective-permute-start.1 = (bf16[256,768]{1,0:T(8,128)(2,1)S(1)}, bf16[256,768]{1,0:T(8,128)(2,1)S(1)}, u32[]{:S(2)}, u32[]{:S(2)}) collective-permute-start(bf16[256,768]{1,0:T(8,128)(2,1)S(1)} %get-tuple-element.9), channel_id=1, source_target_pairs={{1,0},{2,1},{3,2},{4,3},{5,4},{6,5},{7,6},{9,8},{10,9},{11,10},{12... | collective-permute-start | bytes 1179656 | tf_op jit(solution)/shard_map/ppermute | solution.py:20
  140.3 18.6 %collective-permute-start = (bf16[256,768]{1,0:T(8,128)(2,1)S(1)}, bf16[256,768]{1,0:T(8,128)(2,1)S(1)}, u32[]{:S(2)}, u32[]{:S(2)}) collective-permute-start(bf16[256,768]{1,0:T(8,128)(2,1)S(1)} %get-tuple-element.8), channel_id=1, source_target_pairs={{0,1},{1,2},{2,3},{3,4},{4,5},{5,6},{6,7},{8,9},{9,10},{10,11},{11... | collective-permute-start | bytes 1179656 | tf_op jit(solution)/shard_map/ppermute | solution.py:19
  150.6 0.7 copy-start.25
  151.9 8.6 %copy-start.16 = (bf16[2,384,768]{2,1,0:T(8,128)(2,1)S(1)}, bf16[2,384,768]{2,1,0:T(8,128)(2,1)}, u32[]{:S(2)}) copy-start(bf16[2,384,768]{2,1,0:T(8,128)(2,1)} %param.14) | copy-start | bytes 3538948
  158.8 0.7 copy-start.21
  159.6 0.9 copy-start.12
  170.8 9.5 %collective-permute-start.3 = (bf16[128,768]{1,0:T(8,128)(2,1)S(1)}, bf16[128,768]{1,0:T(8,128)(2,1)S(1)}, u32[]{:S(2)}, u32[]{:S(2)}) collective-permute-start(bf16[128,768]{1,0:T(8,128)(2,1)S(1)} %get-tuple-element.11), channel_id=1, source_target_pairs={{1,0},{2,1},{3,2},{4,3},{5,4},{6,5},{7,6},{9,8},{10,9},{11,10},{12... | collective-permute-start | bytes 589832 | tf_op jit(solution)/shard_map/ppermute | solution.py:20
  172.1 12.5 %collective-permute-start.2 = (bf16[128,768]{1,0:T(8,128)(2,1)S(1)}, bf16[128,768]{1,0:T(8,128)(2,1)S(1)}, u32[]{:S(2)}, u32[]{:S(2)}) collective-permute-start(bf16[128,768]{1,0:T(8,128)(2,1)S(1)} %get-tuple-element.10), channel_id=1, source_target_pairs={{0,1},{1,2},{2,3},{3,4},{4,5},{5,6},{6,7},{8,9},{9,10},{10,11},{11... | collective-permute-start | bytes 589832 | tf_op jit(solution)/shard_map/ppermute | solution.py:19
  180.2 0.7 copy-start.23
  182.3 4.6 copy-start.1
  182.4 4.5 copy-start.17
  184.6 1.5 copy-start.20
  186.1 0.8 copy-start.9
  196.1 1.2 copy-start.15
  200.2 9.2 %copy-start.10 = (f32[256,384]{1,0:T(8,128)S(1)}, f32[256,384]{1,0:T(8,128)}, u32[]{:S(2)}) copy-start(f32[256,384]{1,0:T(8,128)} %copy-done.9) | copy-start | bytes 1179652
  200.2 9.2 %copy-start.11 = (bf16[256,768]{1,0:T(8,128)(2,1)S(1)}, bf16[256,768]{1,0:T(8,128)(2,1)}, u32[]{:S(2)}) copy-start(bf16[256,768]{1,0:T(8,128)(2,1)} %reshape.171) | copy-start | bytes 1179652
  202.0 12.6 %copy-start.3 = (bf16[256,384]{1,0:T(8,128)(2,1)}, bf16[256,384]{1,0:T(8,128)(2,1)S(1)}, u32[]{:S(2)}) copy-start(bf16[256,384]{1,0:T(8,128)(2,1)S(1)} %fusion.31) | copy-start | bytes 589828
  203.5 11.1 %copy-start.2 = (f32[256,768]{1,0:T(8,128)S(1)}, f32[256,768]{1,0:T(8,128)}, u32[]{:S(2)}) copy-start(f32[256,768]{1,0:T(8,128)} %reduce_sum.31) | copy-start | bytes 2359300
  203.5 7.0 %collective-permute-start.5 = (bf16[128,384]{1,0:T(8,128)(2,1)S(1)}, bf16[128,384]{1,0:T(8,128)(2,1)S(1)}, u32[]{:S(2)}, u32[]{:S(2)}) collective-permute-start(bf16[128,384]{1,0:T(8,128)(2,1)S(1)} %get-tuple-element.13), channel_id=1, source_target_pairs={{0,1},{1,2},{2,3},{3,4},{4,5},{5,6},{6,7},{8,9},{9,10},{10,11},{11... | collective-permute-start | bytes 294920 | tf_op jit(solution)/shard_map/ppermute | solution.py:19
  208.0 6.5 %collective-permute-start.4 = (bf16[128,384]{1,0:T(8,128)(2,1)S(1)}, bf16[128,384]{1,0:T(8,128)(2,1)S(1)}, u32[]{:S(2)}, u32[]{:S(2)}) collective-permute-start(bf16[128,384]{1,0:T(8,128)(2,1)S(1)} %get-tuple-element.12), channel_id=1, source_target_pairs={{1,0},{2,1},{3,2},{4,3},{5,4},{6,5},{7,6},{9,8},{10,9},{11,10},{12... | collective-permute-start | bytes 294920 | tf_op jit(solution)/shard_map/ppermute | solution.py:20
  221.5 2.0 copy-start.14
  224.6 141.2 %reduce-scatter.15.cloned.1.call-start = ((), (), s32[]{:S(2)}) async-start(), calls=%async_computation.10 | async-start | bytes 3538944 | tf_op jit(solution)/shard_map/reduce_scatter | solution.py:176
  228.5 219.2 %reduce-scatter.11.cloned.1.call-start = ((), (), s32[]{:S(2)}) async-start(), calls=%async_computation.8 | async-start | bytes 3981312 | tf_op jit(solution)/shard_map/reduce_scatter | solution.py:170
  228.8 2.9 copy-start.4
  232.1 1.1 copy-start.13
  232.1 1.5 copy-start.18
  232.1 1.7 copy-start.19
  233.8 1.1 copy-start.7
  233.8 1.2 copy-start.26
  235.1 1.0 copy-start.22
  239.7 230.3 %reduce-scatter.21.cloned.1.call-start = ((), (), s32[]{:S(2)}) async-start(), calls=%async_computation.13 | async-start | bytes 245760
  290.8 202.3 %reduce-scatter.17.cloned.1.call-start = ((), (), s32[]{:S(2)}) async-start(), calls=%async_computation.11 | async-start | bytes 491520 | tf_op jit(solution)/shard_map/reduce_scatter | solution.py:187
  365.9 151.2 %reduce-scatter.19.cloned.1.call-start = ((), (), s32[]{:S(2)}) async-start(), calls=%async_computation.12 | async-start | bytes 614400
Sparse Core Ops, SparseCore 0:
  9.6 84.7 all-gather.1
  224.7 63.9 reduce-scatter.12
  292.3 73.5 reduce-scatter.14
  369.3 78.3 reduce-scatter.10
  450.6 19.2 reduce-scatter.20
  472.3 20.7 reduce-scatter.16
  495.7 21.3 reduce-scatter.18
where the time goes:
time: 527 us; the launch traced here: 526 us
  waiting for transfers between devices  386 us (73%)
  matrix products  46.4 us (9%)
  local copies, waits for them, and re-layouts  31.2 us (6%)
  starting transfers between devices  24.2 us (5%)
  other arithmetic  22.3 us (4%)
  between operations  15.4 us (3%)
    reduce_scatter x1, waiting for transfers between devices, shards(): lax.psum_scatter(kernel_terms.astype(jnp.bfloat16), 'seq', scatter_dimens...  81.8 us
    all_gather x1, waiting for transfers between devices, shards(): lax.all_gather(projection, 'dp', axis=0, tiled=True)  80 us
    reduce_scatter x1, waiting for transfers between devices, shards(): lax.psum_scatter(readout_grad.astype(jnp.bfloat16), 'seq', scatter_dimens...  75 us
    reduce_scatter x1, waiting for transfers between devices, shards(): lax.psum_scatter(mixer_terms.astype(jnp.bfloat16), 'seq', scatter_dimensi...  48.9 us
    unnamed x9, waiting for transfers between devices  40.6 us
    reduce_scatter x1, waiting for transfers between devices, shards(): lax.psum_scatter(readout_part.astype(jnp.bfloat16), 'dp', scatter_dimensi...  21.5 us
    all_to_all x1, waiting for transfers between devices, shards(): lax.all_to_all(outgoing.reshape(groups, block_rows, channels), 'seq', spl...  20.2 us
    unnamed x62, local copies, waits for them, and re-layouts  14.8 us
  transfers between devices with their start and end apart: 14, of which 13 were waited for; matrix products, arithmetic and copies ran while one was open for 7% of the time, Pallas kernels for 0%

commit v1 on v0

v1 whole, which is shorter than its diff:
```python
import math

import jax
import jax.numpy as jnp
import ml_dtypes
import numpy as np
from jax import lax
from jax.experimental import pallas as pl
from jax.experimental.pallas import tpu as pltpu
from jax.sharding import PartitionSpec as P

SPREAD_FINE = 256
SPREAD_COARSE = 128
BF = jnp.bfloat16
F32 = jnp.float32
PIECES = 2

VMEM = pl.BlockSpec(memory_space=pltpu.VMEM)
SMEM = pl.BlockSpec(memory_space=pltpu.SMEM)


def params(mib):
    return pltpu.CompilerParams(vmem_limit_bytes=mib * 1024 * 1024)


def cost(flops, arrays):
    total = sum(int(np.prod(a.shape)) * a.dtype.itemsize for a in arrays)
    return pl.CostEstimate(flops=int(flops), bytes_accessed=int(total), transcendentals=0)


def gelu(v):
    return 0.5 * v * (1.0 + lax.erf(v * (1.0 / math.sqrt(2.0))))


def gelu_slope(v):
    cumulative = 0.5 * (1.0 + lax.erf(v * (1.0 / math.sqrt(2.0))))
    density = jnp.exp(-0.5 * v * v) * (1.0 / math.sqrt(2.0 * math.pi))
    return cumulative + v * density


def nn(a, b):
    return jnp.dot(a, b, preferred_element_type=F32)


def nt(a, b):
    return lax.dot_general(a, b, (((1,), (1,)), ((), ())), preferred_element_type=F32)


def tn(a, b):
    return lax.dot_general(a, b, (((0,), (0,)), ((), ())), preferred_element_type=F32)


def call(body, inputs, outs, flops, mib, smem=0, scratch=()):
    outs = [jax.ShapeDtypeStruct(s, d) for s, d in outs]
    return pl.pallas_call(
        body,
        out_shape=outs,
        in_specs=[SMEM] * smem + [VMEM] * (len(inputs) - smem),
        out_specs=[VMEM] * len(outs),
        scratch_shapes=list(scratch),
        compiler_params=params(mib),
        cost_estimate=cost(flops, list(inputs) + outs),
    )(*inputs)


def project(total, rows, weights, starts, final):
    count = len(weights)
    row_count = rows.shape[0]
    depth, channels = weights[0].shape
    block = min(512, depth)
    steps = depth // block

    def body(starts_ref, *refs):
        row_refs, weight_refs = refs[:count], refs[count : 2 * count]
        rest = refs[2 * count :]
        step = pl.program_id(0)
        part = nn(row_refs[0][...], weight_refs[0][...])
        for r, w in zip(row_refs[1:], weight_refs[1:]):
            part = part + nn(r[...], w[...])
        if total is None:
            out_ref = rest[0]

            @pl.when(step == 0)
            def _():
                out_ref[...] = part

            @pl.when(step > 0)
            def _():
                out_ref[...] += part
        else:
            old_ref, out_ref = rest
            if steps == 1:
                out_ref[...] = (old_ref[...] + part).astype(out_ref.dtype)
            else:

                @pl.when(step == 0)
                def _():
                    out_ref[...] = old_ref[...] + part

                @pl.when(step > 0)
                def _():
                    out_ref[...] += part

    def row_map(k):
        return lambda i, s: (0, s[k] + i)

    whole = pl.BlockSpec((row_count, channels), lambda i, s: (0, 0))
    in_specs = [pl.BlockSpec((row_count, block), row_map(k)) for k in range(count)]
    in_specs += [pl.BlockSpec((block, channels), lambda i, s: (i, 0)) for _ in range(count)]
    inputs = [rows] * count + list(weights)
    if total is not None:
        in_specs.append(whole)
        inputs.append(total)
    out = jax.ShapeDtypeStruct((row_count, channels), BF if final else F32)
    return pl.pallas_call(
        body,
        out_shape=out,
        grid_spec=pltpu.PrefetchScalarGridSpec(
            num_scalar_prefetch=1, grid=(steps,), in_specs=in_specs, out_specs=whole
        ),
        compiler_params=params(24),
        cost_estimate=cost(2 * row_count * depth * channels * count, list(weights) * 2 + [out]),
    )(jnp.stack(starts).astype(jnp.int32) // block, *inputs)


def place_body(target_ref, received_ref, hidden_ref, low_ref, high_ref):
    half = low_ref.shape[0]
    rows = received_ref[...]
    for h, out in enumerate((low_ref, high_ref)):
        order = lax.broadcasted_iota(jnp.int32, (half, rows.shape[0]), 0) + h * half
        pick = jnp.where(order == target_ref[...], 1.0, 0.0).astype(BF)
        placed = nn(pick, rows)
        hidden_ref[h * half : (h + 1) * half] = placed.astype(BF)
        out[...] = gelu(placed).astype(BF)


def fine_body(
    prev_ref, low_ref, high_ref, next_ref, hidden_ref, kernel_ref, mixer_ref,
    inner_ref, gated_ref, first_ref, alow_ref, ahigh_ref,
):
    half = low_ref.shape[0]
    slab = half // 4
    taps = (prev_ref, low_ref, high_ref, next_ref)
    for h, active in enumerate((alow_ref, ahigh_ref)):
        inner = (
            nn(taps[h + 1][...], kernel_ref[1])
            + nn(taps[h][...], kernel_ref[0])
            + nn(taps[h + 2][...], kernel_ref[2])
        )
        inner_ref[h * half : (h + 1) * half] = inner
        gated = gelu(inner).astype(BF)
        gated_ref[h * half : (h + 1) * half] = gated
        out = hidden_ref[h * half : (h + 1) * half].astype(F32) + nn(gated, mixer_ref[...])
        for s in range(2):
            a = out[2 * s * slab : (2 * s + 1) * slab]
            b = out[(2 * s + 1) * slab : (2 * s + 2) * slab]
            pooled = ((a + b) * 0.5).astype(BF)
            start = h * half // 2 + s * slab
            first_ref[start : start + slab] = pooled
            active[s * slab : (s + 1) * slab] = gelu(pooled.astype(F32)).astype(BF)


def coarse_body(
    scale, bins_per,
    ids_ref, prev_ref, low_ref, high_ref, next_ref, first_ref, kernel_ref, mixer_ref, readout_ref, targets_ref,
    gated_ref, second_ref, logit_ref, upper_ref, glow_ref, ghigh_ref,
):
    half = low_ref.shape[0]
    slab = half // 2
    taps = (prev_ref, low_ref, high_ref, next_ref)
    slopes = []
    for h in range(2):
        inner = (
            nn(taps[h + 1][...], kernel_ref[1])
            + nn(taps[h][...], kernel_ref[0])
            + nn(taps[h + 2][...], kernel_ref[2])
        )
        slopes.append(gelu_slope(inner))
        gated = gelu(inner).astype(BF)
        gated_ref[h * half : (h + 1) * half] = gated
        out = first_ref[h * half : (h + 1) * half].astype(F32) + nn(gated, mixer_ref[...])
        second_ref[h * slab : (h + 1) * slab] = ((out[:slab] + out[slab:]) * 0.5).astype(BF)
    bins = second_ref.shape[0]
    tracks = readout_ref.shape[1]
    width = min(512, tracks)
    bin_ids = ids_ref[0] * bins_per + lax.broadcasted_iota(jnp.int32, (bins, 1), 0)
    weight = jnp.where(bin_ids * 4 < ids_ref[1], scale, 0.0).astype(F32)
    second = second_ref[...]
    upper = jnp.zeros((bins, second.shape[1]), F32)
    for n in range(tracks // width):
        cols = slice(n * width, (n + 1) * width)
        readout = readout_ref[:, cols]
        logits = nn(second, readout)
        small = jnp.exp(-jnp.abs(logits))
        plus = jnp.maximum(logits, 0.0) + jnp.log1p(small)
        gate = jnp.where(logits >= 0.0, 1.0, small) / (1.0 + small)
        grad = (weight * (plus - targets_ref[:, cols].astype(F32)) * gate).astype(BF)
        logit_ref[:, cols] = grad
        upper = upper + nt(grad, readout)
    upper = (upper * 0.5).astype(BF)
    upper_ref[...] = upper
    back = nt(upper, mixer_ref[...])
    for h, out in enumerate((glow_ref, ghigh_ref)):
        piece = back[h * slab : (h + 1) * slab]
        for s in range(2):
            out[s * slab : (s + 1) * slab] = (piece * slopes[h][s * slab : (s + 1) * slab]).astype(BF)


def readout_body(ids_ref, second_ref, logit_ref, keep_ref, send_ref):
    width = keep_ref.shape[2]
    second = second_ref[...]
    for k in range(4):
        start = pl.multiple_of((ids_ref[0] ^ k) * width, width)
        out = send_ref if k & 1 else keep_ref
        out[k >> 1] = tn(second, logit_ref[:, pl.ds(start, width)]).astype(BF)


def store_blocks(ids_ref, pieces, keep_ref, send_ref):
    width = pieces[0].shape[1] // 4
    for d in range(4):
        block = jnp.concatenate([p[:, d * width : (d + 1) * width] for p in pieces], axis=1)
        far = (ids_ref[0] >> 1) ^ (d >> 1)

        @pl.when((ids_ref[0] & 1) == (d & 1))
        def _(block=block, far=far):
            keep_ref[far] = block

        @pl.when((ids_ref[0] & 1) != (d & 1))
        def _(block=block, far=far):
            send_ref[far] = block


def weight_pieces(taps, grads, gated, upstream, spread_ref, split_ref):
    pieces = []
    for t in range(3):
        pieces.append((tn(taps[t][...], grads[0]) + tn(taps[t + 1][...], grads[1])).astype(BF))
    mixed = 0.0
    for j in range(2):
        left = nn(gated, spread_ref[j]).astype(BF)
        right = nn(upstream, split_ref[j]).astype(BF)
        mixed = mixed + tn(left, right)
    pieces.append(mixed.astype(BF))
    return pieces


def coarse_grad_body(
    ids_ref, prev_ref, low_ref, high_ref, next_ref, glow_ref, ghigh_ref, gated_ref, upper_ref, spread_ref, split_ref,
    keep_ref, send_ref,
):
    slab = low_ref.shape[0] // 2
    upper = upper_ref[...]
    rows = jnp.concatenate([upper[:slab], upper[:slab], upper[slab:], upper[slab:]], axis=0)
    pieces = weight_pieces(
        (prev_ref, low_ref, high_ref, next_ref), (glow_ref[...], ghigh_ref[...]), gated_ref[...], rows,
        spread_ref, split_ref,
    )
    store_blocks(ids_ref, pieces, keep_ref, send_ref)


def fine_grad_body(
    scale,
    ids_ref, gprev_ref, glow_ref, ghigh_ref, gnext_ref, upper_ref, first_ref, kernel_ref, mixer_ref,
    prev_ref, low_ref, high_ref, next_ref, inner_ref, gated_ref, spread_ref, split_ref,
    trunk_ref, keep_ref, send_ref, lanes_ref,
):
    half = glow_ref.shape[0]
    slab = half // 2
    grads = (gprev_ref, glow_ref, ghigh_ref, gnext_ref)
    upper = upper_ref[...].astype(F32)
    inner_grads, rows = [], []
    for h in range(2):
        back = (
            nt(grads[h + 2][...], kernel_ref[0])
            + nt(grads[h + 1][...], kernel_ref[1])
            + nt(grads[h][...], kernel_ref[2])
        )
        slope = gelu_slope(first_ref[h * half : (h + 1) * half].astype(F32))
        base = upper[h * slab : (h + 1) * slab]
        total = jnp.concatenate([base, base], axis=0) + back * slope
        for t in range(lanes_ref.shape[0]):
            cols = slice(t * 128, (t + 1) * 128)
            for s in range(2):
                lanes_ref[t, pl.ds(s, slab, stride=2), :] = total[s * slab : (s + 1) * slab, cols] * scale
            trunk_ref[h * half : (h + 1) * half, cols] = lanes_ref[t]
        lower = (total * 0.5).astype(BF)
        inner = nt(lower, mixer_ref[...])
        spread_inner = jnp.concatenate([inner[:slab], inner[:slab], inner[slab:], inner[slab:]], axis=0)
        slope = gelu_slope(inner_ref[2 * h * half : 2 * (h + 1) * half])
        inner_grads.append((spread_inner * slope).astype(BF))
        rows += [lower[:slab], lower[:slab], lower[slab:], lower[slab:]]
    pieces = weight_pieces(
        (prev_ref, low_ref, high_ref, next_ref), inner_grads, gated_ref[...], jnp.concatenate(rows, axis=0),
        spread_ref, split_ref,
    )
    store_blocks(ids_ref, pieces, keep_ref, send_ref)


def swap(value, axis, bit):
    size = lax.axis_size(axis)
    return lax.ppermute(value, axis, [(i, i ^ bit) for i in range(size)])


def halo(low, high):
    size = lax.axis_size("seq")
    up = [(i, i + 1) for i in range(size - 1)]
    return (
        lax.ppermute(high, "seq", up),
        lax.ppermute(low, "seq", [(j, i) for i, j in up]),
    )


def scatter_sum(keep, send):
    came = swap(send, "dp", 1)
    away = (keep[1].astype(F32) + came[1].astype(F32)).astype(BF)
    here = keep[0].astype(F32) + came[0].astype(F32)
    total = (here + swap(away, "dp", 2).astype(F32)).astype(BF)
    groups = lax.axis_size("seq")
    rows, columns = total.shape
    parts = lax.all_to_all(
        total.reshape(groups, rows // groups, columns), "seq", split_axis=0, concat_axis=0, tiled=True
    )
    return parts.astype(F32).sum(axis=0)


def shards(embeddings, layout, lengths, targets, projection, kernels, mixers, readout):
    groups = lax.axis_size("seq")
    windows = lax.axis_size("dp")
    me = lax.axis_index("dp")
    device = lax.axis_index("seq")
    rows = embeddings[0, 0]
    row_count = rows.shape[0]
    depth, channels = projection.shape
    width = kernels.shape[3]
    tracks = readout.shape[1]
    half, quarter, eighth = row_count // 2, row_count // 4, row_count // 8
    length = lengths[0]

    side = device % 2
    share = depth // 2
    piece = share // PIECES
    from_core = swap(projection, "dp", 1)
    mine = lax.dynamic_slice_in_dim(projection, side * share, share, axis=0)
    far = [swap(lax.slice_in_dim(mine, i * piece, (i + 1) * piece), "dp", 2) for i in range(PIECES)]
    far_side = [swap(f, "seq", 1) for f in far]
    far_core = [swap(f, "dp", 1) for f in far]
    far_side_core = [swap(f, "dp", 1) for f in far_side]
    total = project(None, rows, [projection], [me * depth], False)
    total = project(total, rows, [from_core], [(me ^ 1) * depth], False)
    for i in range(PIECES):
        at = side * share + i * piece
        total = project(
            total, rows, [far[i], far_core[i]], [(me ^ 2) * depth + at, (me ^ 3) * depth + at], False
        )
    for i in range(PIECES):
        at = (1 - side) * share + i * piece
        total = project(
            total, rows, [far_side[i], far_side_core[i]],
            [(me ^ 2) * depth + at, (me ^ 3) * depth + at], i == PIECES - 1,
        )

    block = row_count // groups
    received = lax.all_to_all(
        total.reshape(groups, block, channels), "seq", split_axis=0, concat_axis=0, tiled=True
    ).reshape(row_count, channels)
    column = lax.dynamic_index_in_dim(layout[0], device, axis=1, keepdims=True)
    position = column * block + jnp.arange(block, dtype=jnp.int32)[None, :]
    slot = (position // half) * half + (position % 4) * eighth + (position % half) // 4
    target = jnp.where(device * row_count + position < length, slot, -1).reshape(1, row_count)

    hidden, low, high = call(
        place_body, (target, received),
        [((row_count, channels), BF), ((half, channels), BF), ((half, channels), BF)],
        2 * row_count * row_count * channels, 24,
    )
    prev, nxt = halo(low, high)
    inner, gated, first, alow, ahigh = call(
        fine_body, (prev, low, high, nxt, hidden, kernels[0], mixers[0]),
        [((row_count, width), F32), ((row_count, width), BF), ((half, channels), BF),
         ((quarter, channels), BF), ((quarter, channels), BF)],
        8 * row_count * width * channels, 24,
    )
    aprev, anext = halo(alow, ahigh)
    bins = quarter
    loss = 2.0 / math.sqrt(windows * groups * bins)
    ids = jnp.stack([device, length]).astype(jnp.int32)
    place = jnp.stack([me, device]).astype(jnp.int32)

    def coarse(*refs):
        coarse_body(loss, bins, *refs)

    cgated, second, logit_grad, upper, glow, ghigh = call(
        coarse, (ids, aprev, alow, ahigh, anext, first, kernels[1], mixers[1], readout, targets[0]),
        [((half, width), BF), ((bins, channels), BF), ((bins, tracks), BF), ((bins, channels), BF),
         ((quarter, width), BF), ((quarter, width), BF)],
        8 * half * width * channels + 4 * bins * tracks * channels, 32, smem=1,
    )
    gprev, gnext = halo(glow, ghigh)
    track_keep, track_send = call(
        readout_body, (place, second, logit_grad), [((2, channels, tracks // 4), BF)] * 2,
        2 * bins * tracks * channels, 24, smem=1,
    )
    readout_total = scatter_sum(track_keep, track_send)

    per = width // groups
    fold = np.zeros((2, width, channels), ml_dtypes.bfloat16)
    split = np.zeros((2, channels, width), ml_dtypes.bfloat16)
    for j in range(2):
        for a in range(width):
            fold[j, a, (a // per) * 2 * per + j * per + a % per] = 1
        piece_width = width // 4
        for b in range(width):
            split[j, (b // piece_width) * 2 * piece_width + j * piece_width + b % piece_width, b] = 1
    fold, split = jnp.asarray(fold), jnp.asarray(split)
    pair = [((2, channels, width), BF)] * 2
    coarse_keep, coarse_send = call(
        coarse_grad_body, (place, aprev, alow, ahigh, anext, glow, ghigh, cgated, upper, fold, split), pair,
        12 * half * width * channels, 32, smem=1,
    )
    coarse_total = scatter_sum(coarse_keep, coarse_send)

    def fine(*refs):
        fine_grad_body(math.sqrt(windows * groups * bins) * 0.5, *refs)

    trunk, fine_keep, fine_send = call(
        fine,
        (place, gprev, glow, ghigh, gnext, upper, first, kernels[1], mixers[0],
         prev, low, high, nxt, inner, gated, fold, split),
        [((half, channels), F32)] + pair,
        20 * row_count * width * channels, 40, smem=1,
        scratch=[pltpu.VMEM((channels // 128, quarter, 128), F32)],
    )
    fine_total = scatter_sum(fine_keep, fine_send)

    cut = width // windows
    kernel_rows, mixer_rows = [], []
    for value in (fine_total, coarse_total):
        kernel_rows.append(jnp.stack([value[:, t * cut : (t + 1) * cut] for t in range(3)]))
        tail = value[:, 3 * cut :]
        mixer_rows.append(jnp.concatenate([tail[:per], tail[per:]], axis=1))
    return (jnp.stack(kernel_rows), jnp.stack(mixer_rows), readout_total, trunk[None])


def solution(mesh):
    placed = (
        P("dp", "seq", None, None),
        P("dp", None, None),
        P("dp"),
        P("dp", "seq", None),
        P("dp", None),
        P(),
        P(),
        P(),
    )
    return jax.shard_map(
        shards,
        mesh=mesh,
        in_specs=placed,
        out_specs=(
            P(None, None, "seq", "dp"),
            P(None, "seq", "dp"),
            P("seq", "dp"),
            P("dp", "seq", None),
        ),
        check_vma=False,
    )
```

time: 527 us -> 259 us (0.49)
  waiting for transfers between devices: 386 us -> 146 us
  matrix products: 46.4 us -> 0 us
  Pallas kernels: 0 us -> 42.6 us
  local copies, waits for them, and re-layouts: 31.2 us -> 6.09 us
  starting transfers between devices: 24.2 us -> 48.6 us
  between operations: 15.4 us -> 1.62 us
  other arithmetic: 22.3 us -> 12.7 us
    reduce_scatter x4 -> x0, waiting for transfers between devices: 227 us -> none  [the longest x1 81.8 us: shards(): lax.psum_scatter(kernel_terms.astype(jnp.bfloat16), 'seq', scatter_dimens...]
    ppermute x6 -> x21, waiting for transfers between devices: 18.4 us -> 107 us  [the longest x15 84 us: swap(): return lax.ppermute(value, axis, [(i, i ^ bit) for i in range(size)])]
    all_gather x1 -> x0, waiting for transfers between devices: 80 us -> none  [shards(): lax.all_gather(projection, 'dp', axis=0, tiled=True)]
    dot_general x25 -> x0, matrix products: 46.4 us -> none  [the longest x1 13.4 us: shards(): jnp.dot(local_rows, lax.all_gather(projection, 'dp', axis=0, tiled=True),...]
    pallas_call x0 -> x12, Pallas kernels: none -> 42.6 us  [the longest x6 22.1 us: call(): pl.pallas_call(body, out_shape=outs, in_specs=[SMEM] * smem + [VMEM] * (l...]
    unnamed x9 -> x0, waiting for transfers between devices: 40.6 us -> none
    all_to_all x1 -> x4, waiting for transfers between devices: 20.2 us -> 39 us  [the longest x1 19.8 us: shards(): lax.all_to_all(total.reshape(groups, block, channels), 'seq', split_axis=...]
    all_to_all x1 -> x4, starting transfers between devices: 5.52 us -> 19.4 us  [the longest x3 13.4 us: scatter_sum(): lax.all_to_all(total.reshape(groups, rows // groups, columns), 'seq', spl...]
  transfers between devices with their start and end apart: 14 -> 25, of which waited for: 13 -> 14; matrix products, arithmetic and copies ran while one was open for 7% -> 6% of each run, Pallas kernels for 0% -> 11%
where the time goes in v1:
time: 259 us; the launch traced here: 258 us
  waiting for transfers between devices  146 us (56%)
  starting transfers between devices  48.6 us (19%)
  Pallas kernels  42.6 us (16%)
  other arithmetic  12.7 us (5%)
  local copies, waits for them, and re-layouts  6.09 us (2%)
    ppermute x15, waiting for transfers between devices, swap(): return lax.ppermute(value, axis, [(i, i ^ bit) for i in range(size)])  84 us
    pallas_call x6, Pallas kernels, call(): pl.pallas_call(body, out_shape=outs, in_specs=[SMEM] * smem + [VMEM] * (l...  22.1 us
    pallas_call x6, Pallas kernels, project(): pl.pallas_call(body, out_shape=out, grid_spec=pltpu.PrefetchScalarGridSpe...  20.5 us
    all_to_all x1, waiting for transfers between devices, shards(): lax.all_to_all(total.reshape(groups, block, channels), 'seq', split_axis=...  19.8 us
    all_to_all x3, waiting for transfers between devices, scatter_sum(): lax.all_to_all(total.reshape(groups, rows // groups, columns), 'seq', spl...  19.2 us
    ppermute x3, waiting for transfers between devices, halo(): lax.ppermute(high, 'seq', up)  15.2 us
    all_to_all x3, starting transfers between devices, scatter_sum(): lax.all_to_all(total.reshape(groups, rows // groups, columns), 'seq', spl...  13.4 us
    ppermute x3, starting transfers between devices, halo(): lax.ppermute(high, 'seq', up)  13.4 us
  transfers between devices with their start and end apart: 25, of which 14 were waited for; matrix products, arithmetic and copies ran while one was open for 6% of the time, Pallas kernels for 11%

profile of v1, /device:TPU:0, one launch (start us, length us, event | category | flops | bytes accessed | tf_op | source)
XLA Modules:
  0.0 258.1 jit_solution(18005039685856452685)
XLA Ops:
  1.2 1.6 constant_dynamic-slice_fusion
  2.8 2.6 %collective-permute-start.3 = (bf16[512,768]{1,0:T(8,128)(2,1)S(1)}, bf16[512,768]{1,0:T(8,128)(2,1)}, u32[]{:S(2)}, u32[]{:S(2)}) collective-permute-start(bf16[512,768]{1,0:T(8,128)(2,1)S(1)} %get-tuple-element.48), channel_id=1, source_target_pairs={{0,16},{8,24},{16,0},{24,8},{1,17},{9,25},{17,1},{25,9},{2,18},{10... | collective-permute-start | bytes 2359304 | tf_op jit(solution)/shard_map/ppermute | solution.py:300
  5.5 18.4 %collective-permute-done.3.refs_2_ = bf16[512,768]{1,0:T(8,128)(2,1)} collective-permute-done((bf16[512,768]{1,0:T(8,128)(2,1)S(1)}, bf16[512,768]{1,0:T(8,128)(2,1)}, u32[]{:S(2)}, u32[]{:S(2)}) %collective-permute-start.3) | collective-permute-done | bytes 786464 | tf_op jit(solution)/shard_map/ppermute | solution.py:300
  23.9 2.0 collective-permute-start.4
  25.9 14.7 %collective-permute-done.refs_2_ = bf16[512,768]{1,0:T(8,128)(2,1)} collective-permute-done((bf16[512,768]{1,0:T(8,128)(2,1)S(1)}, bf16[512,768]{1,0:T(8,128)(2,1)}, u32[]{:S(2)}, u32[]{:S(2)}) %collective-permute-start) | collective-permute-done | bytes 786464 | tf_op jit(solution)/shard_map/ppermute | solution.py:300
  40.5 1.8 collective-permute-start.1
  43.3 16.8 %collective-permute-done.1.refs_2_ = bf16[512,768]{1,0:T(8,128)(2,1)} collective-permute-done((bf16[512,768]{1,0:T(8,128)(2,1)}, bf16[512,768]{1,0:T(8,128)(2,1)}, u32[]{:S(2)}, u32[]{:S(2)}) %collective-permute-start.1) | collective-permute-done | bytes 786464 | tf_op jit(solution)/shard_map/ppermute | solution.py:300
  60.4 3.4 %copy-done = bf16[1,1,512,8192]{3,2,1,0:T(8,128)(2,1)S(1)} copy-done((bf16[1,1,512,8192]{3,2,1,0:T(8,128)(2,1)S(1)}, bf16[1,1,512,8192]{3,2,1,0:T(8,128)(2,1)}, u32[]{:S(2)}) %copy-start) | copy-done | bytes 8388632
  63.8 3.1 %shard_map.129.refs_2_ = f32[512,768]{1,0:T(8,128)S(1)} custom-call(s32[1]{0:T(128)S(6)} %select_n.106.starts_ref, bf16[512,8192]{1,0:T(8,128)(2,1)S(1)} %bitcast.68, bf16[2048,768]{1,0:T(8,128)(2,1)S(1)} %copy-done.2), custom_call_target="tpu_custom_call" | custom-call | flops 1610612736 | bytes 7864320 | tf_op jit(solution)/shard_map/pallas_call | solution.py:115
  67.2 4.7 %shard_map.130.refs_4_ = f32[512,768]{1,0:T(8,128)S(1)} custom-call(s32[1]{0:T(128)S(6)} %select_n.105.starts_ref, bf16[512,8192]{1,0:T(8,128)(2,1)S(1)} %bitcast.69, bf16[2048,768]{1,0:T(8,128)(2,1)} %collective-permute-done.8.refs_1_, f32[512,768]{1,0:T(8,128)S(1)} %shard_map.129.refs_2_), custom_call_target="tpu_custom_call" | custom-call | flops 1610612736 | bytes 7864320 | tf_op jit(solution)/shard_map/pallas_call | solution.py:115
  71.9 2.9 %shard_map.131.refs_4_ = f32[512,768]{1,0:T(8,128)S(1)} custom-call(s32[2]{0:T(128)S(1)} %and_select_fusion.4.starts_ref, bf16[512,8192]{1,0:T(8,128)(2,1)S(1)} %bitcast.70, bf16[512,8192]{1,0:T(8,128)(2,1)S(1)} %bitcast.71, bf16[512,768]{1,0:T(8,128)(2,1)} %collective-permute-done.3.refs_2_, bf16[512,768]{1,0:T(8,128)(2,1)} %collective-permute-done.7.refs_3_, ...), custom_call_target="tpu_custom_call" | custom-call | flops 805306368 | bytes 4718592 | tf_op jit(solution)/shard_map/pallas_call | solution.py:115
  74.9 2.9 %shard_map.132.refs_4_ = f32[512,768]{1,0:T(8,128)S(1)} custom-call(s32[2]{0:T(128)S(1)} %and_select_fusion.5.starts_ref, bf16[512,8192]{1,0:T(8,128)(2,1)S(1)} %bitcast.72, bf16[512,8192]{1,0:T(8,128)(2,1)S(1)} %bitcast.73, bf16[512,768]{1,0:T(8,128)(2,1)} %collective-permute-done.refs_2_, bf16[512,768]{1,0:T(8,128)(2,1)} %collective-permute-done.6.refs_3_, ...), custom_call_target="tpu_custom_call" | custom-call | flops 805306368 | bytes 4718592 | tf_op jit(solution)/shard_map/pallas_call | solution.py:115
  77.8 2.9 %shard_map.133.refs_4_ = f32[512,768]{1,0:T(8,128)S(1)} custom-call(s32[2]{0:T(128)S(1)} %and_select_fusion.6.starts_ref, bf16[512,8192]{1,0:T(8,128)(2,1)S(1)} %bitcast.74, bf16[512,8192]{1,0:T(8,128)(2,1)S(1)} %bitcast.75, bf16[512,768]{1,0:T(8,128)(2,1)} %collective-permute-done.4.refs_2_, bf16[512,768]{1,0:T(8,128)(2,1)} %collective-permute-done.5.refs_3_, ...), custom_call_target="tpu_custom_call" | custom-call | flops 805306368 | bytes 4718592 | tf_op jit(solution)/shard_map/pallas_call | solution.py:115
  80.8 3.8 %shard_map.134 = bf16[512,768]{1,0:T(8,128)(2,1)} custom-call(s32[2]{0:T(128)S(1)} %and_select_fusion.7.starts_ref, bf16[512,8192]{1,0:T(8,128)(2,1)S(1)} %bitcast.76, bf16[512,8192]{1,0:T(8,128)(2,1)S(1)} %bitcast.77, bf16[512,768]{1,0:T(8,128)(2,1)} %collective-permute-done.1.refs_2_, bf16[512,768]{1,0:T(8,128)(2,1)} %collective-permute-done.2.refs_3_, ...), custom_call_target="tpu_custom_call" | custom-call | flops 805306368 | bytes 3932160 | tf_op jit(solution)/shard_map/pallas_call | solution.py:115
  84.6 6.0 %all-to-all-start = ((bf16[8,64,768]{2,1,0:T(8,128)(2,1)}), bf16[8,64,768]{2,1,0:T(8,128)(2,1)S(1)}, u32[]{:S(2)}, u32[]{:S(2)}) async-start(bf16[8,64,768]{2,1,0:T(8,128)(2,1)} %bitcast.14), calls=%async_computation | async-start | bytes 1572864 | tf_op jit(solution)/shard_map/all_to_all | solution.py:362
  91.7 19.8 %all-to-all-done = bf16[8,64,768]{2,1,0:T(8,128)(2,1)S(1)} async-done(((bf16[8,64,768]{2,1,0:T(8,128)(2,1)}), bf16[8,64,768]{2,1,0:T(8,128)(2,1)S(1)}, u32[]{:S(2)}, u32[]{:S(2)}) %all-to-all-start) | async-done | bytes 786464 | tf_op jit(solution)/shard_map/all_to_all | solution.py:362
  112.1 1.4 collective-permute-start.10
  113.5 4.6 %collective-permute-start.9 = (bf16[256,768]{1,0:T(8,128)(2,1)S(1)}, bf16[256,768]{1,0:T(8,128)(2,1)S(1)}, u32[]{:S(2)}, u32[]{:S(2)}) collective-permute-start(bf16[256,768]{1,0:T(8,128)(2,1)S(1)} %get-tuple-element.25.high_ref.refs_11_), channel_id=1, source_target_pairs={{0,1},{1,2},{2,3},{3,4},{4,5},{5,6},{6,7},{8,9},{9,10},{10,11},{11... | collective-permute-start | bytes 1179656 | tf_op jit(solution)/shard_map/ppermute | solution.py:307
  118.6 6.0 %collective-permute-done.10.next_ref.refs_12_ = bf16[256,768]{1,0:T(8,128)(2,1)S(1)} collective-permute-done((bf16[256,768]{1,0:T(8,128)(2,1)S(1)}, bf16[256,768]{1,0:T(8,128)(2,1)S(1)}, u32[]{:S(2)}, u32[]{:S(2)}) %collective-permute-start.10) | collective-permute-done | bytes 393248 | tf_op jit(solution)/shard_map/ppermute | solution.py:308
  124.5 8.3 %collective-permute-done.9.prev_ref.refs_9_ = bf16[256,768]{1,0:T(8,128)(2,1)S(1)} collective-permute-done((bf16[256,768]{1,0:T(8,128)(2,1)S(1)}, bf16[256,768]{1,0:T(8,128)(2,1)S(1)}, u32[]{:S(2)}, u32[]{:S(2)}) %collective-permute-start.9) | collective-permute-done | bytes 393248 | tf_op jit(solution)/shard_map/ppermute | solution.py:307
  132.8 2.0 shard_map.136
  134.9 4.4 %collective-permute-start.11 = (bf16[128,768]{1,0:T(8,128)(2,1)S(1)}, bf16[128,768]{1,0:T(8,128)(2,1)S(1)}, u32[]{:S(2)}, u32[]{:S(2)}) collective-permute-start(bf16[128,768]{1,0:T(8,128)(2,1)S(1)} %get-tuple-element.28.refs_3_.high_ref), channel_id=1, source_target_pairs={{0,1},{1,2},{2,3},{3,4},{4,5},{5,6},{6,7},{8,9},{9,10},{10,11},{11... | collective-permute-start | bytes 589832 | tf_op jit(solution)/shard_map/ppermute | solution.py:307
  139.3 1.5 collective-permute-start.12
  140.9 6.9 %collective-permute-done.11.refs_1_.prev_ref = bf16[128,768]{1,0:T(8,128)(2,1)S(1)} collective-permute-done((bf16[128,768]{1,0:T(8,128)(2,1)S(1)}, bf16[128,768]{1,0:T(8,128)(2,1)S(1)}, u32[]{:S(2)}, u32[]{:S(2)}) %collective-permute-start.11) | collective-permute-done | bytes 196640 | tf_op jit(solution)/shard_map/ppermute | solution.py:307
  147.8 3.9 %shard_map.137 = (bf16[256,384]{1,0:T(8,128)(2,1)S(1)}, bf16[128,768]{1,0:T(8,128)(2,1)S(1)}, bf16[128,2048]{1,0:T(8,128)(2,1)S(1)}, bf16[128,768]{1,0:T(8,128)(...) custom-call(s32[2]{0:T(128)S(1)} %pad_add_fusion.1.refs_0_, ...), custom_call_target="tpu_custom_call" | custom-call | flops 1409286144 | bytes 9043976 | tf_op jit(solution)/shard_map/pallas_call | solution.py:55
  151.7 4.2 %shard_map.139 = (bf16[2,768,384]{2,1,0:T(8,128)(2,1)S(1)}, bf16[2,768,384]{2,1,0:T(8,128)(2,1)S(1)}) custom-call(s32[2]{0:T(128)S(1)} %pad_add_fusion.refs_0_.ids_ref, bf16[128,768]{1,0:T(8,128)(2,1)S(1)} %collective-permute-done.11.refs_1_.prev_ref, bf16[128,768]{1,0:T(8,128)(2,1)S(1)} %get-tuple-element.29.refs_2_.low_ref, ...), custom_call_target="tpu_custom_call" | custom-call | flops 905969664 | bytes 6094856 | tf_op jit(solution)/shard_map/pallas_call | solution.py:55
  156.0 4.4 %collective-permute-start.13 = (bf16[128,384]{1,0:T(8,128)(2,1)S(1)}, bf16[128,384]{1,0:T(8,128)(2,1)S(1)}, u32[]{:S(2)}, u32[]{:S(2)}) collective-permute-start(bf16[128,384]{1,0:T(8,128)(2,1)S(1)} %get-tuple-element.31.refs_3_.ghigh_ref), channel_id=1, source_target_pairs={{0,1},{1,2},{2,3},{3,4},{4,5},{5,6},{6,7},{8,9},{9,10},{10,11},{11... | collective-permute-start | bytes 294920 | tf_op jit(solution)/shard_map/ppermute | solution.py:307
  160.4 1.5 collective-permute-start.14
  161.9 2.7 %shard_map.140 = (bf16[2,768,512]{2,1,0:T(8,128)(2,1)S(1)}, bf16[2,768,512]{2,1,0:T(8,128)(2,1)}) custom-call(s32[2]{0:T(128)S(1)} %pad_add_fusion.refs_0_.ids_ref, bf16[128,768]{1,0:T(8,128)(2,1)S(1)} %get-tuple-element.41.second_ref, bf16[128,2048]{1,0:T(8,128)(2,1)S(1)} %get-tuple-element.42.logit_ref), custom_call_target="tpu_custom_call" | custom-call | flops 402653184 | bytes 3866632 | tf_op jit(solution)/shard_map/pallas_call | solution.py:55
  164.8 2.4 collective-permute-done.14.refs_4_
  167.2 8.7 %shard_map.138 = (f32[256,768]{1,0:T(8,128)}, bf16[2,768,384]{2,1,0:T(8,128)(2,1)S(1)}, bf16[2,768,384]{2,1,0:T(8,128)(2,1)}) custom-call(s32[2]{0:T(128)S(1)} %pad_add_fusion.refs_0_.ids_ref, bf16[128,384]{1,0:T(8,128)(2,1)S(1)} %collective-permute-done.13.refs_1_, bf16[128,384]{1,0:T(8,128)(2,1)S(1)} %get-tuple-element.32.refs_2_.glow_ref, ...), custom_call_target="tpu_custom_call" | custom-call | flops 3019898880 | bytes 11599880 | tf_op jit(solution)/shard_map/pallas_call | solution.py:55
  176.1 1.6 collective-permute-start.18
  177.6 14.2 %collective-permute-done.18 = bf16[768,384]{1,0:T(8,128)(2,1)S(1)} collective-permute-done((bf16[768,384]{1,0:T(8,128)(2,1)S(1)}, bf16[768,384]{1,0:T(8,128)(2,1)S(1)}, u32[]{:S(2)}, u32[]{:S(2)}) %collective-permute-start.18) | collective-permute-done | bytes 589856 | tf_op jit(solution)/shard_map/ppermute | solution.py:300
  191.9 1.1 fusion.1
  192.9 3.7 %all-to-all-start.2 = ((bf16[8,96,384]{2,1,0:T(8,128)(2,1)}), bf16[8,96,384]{2,1,0:T(8,128)(2,1)S(1)}, u32[]{:S(2)}, u32[]{:S(2)}) async-start(bf16[8,96,384]{2,1,0:T(8,128)(2,1)} %bitcast.80), calls=%async_computation.2 | async-start | bytes 1179648 | tf_op jit(solution)/shard_map/all_to_all | solution.py:319
  196.7 1.2 fusion.4
  197.9 1.5 collective-permute-start.16
  199.4 2.2 fusion.3
  202.2 12.0 %collective-permute-done.16 = bf16[768,384]{1,0:T(8,128)(2,1)S(1)} collective-permute-done((bf16[768,384]{1,0:T(8,128)(2,1)S(1)}, bf16[768,384]{1,0:T(8,128)(2,1)S(1)}, u32[]{:S(2)}, u32[]{:S(2)}) %collective-permute-start.16) | collective-permute-done | bytes 589856 | tf_op jit(solution)/shard_map/ppermute | solution.py:300
  214.2 2.1 fusion.2
  216.3 6.0 %all-to-all-start.1 = ((bf16[8,96,384]{2,1,0:T(8,128)(2,1)}), bf16[8,96,384]{2,1,0:T(8,128)(2,1)S(1)}, u32[]{:S(2)}, u32[]{:S(2)}) async-start(bf16[8,96,384]{2,1,0:T(8,128)(2,1)} %bitcast.81), calls=%async_computation.1 | async-start | bytes 1179648 | tf_op jit(solution)/shard_map/all_to_all | solution.py:319
  222.3 7.4 %collective-permute-done.20 = bf16[768,512]{1,0:T(8,128)(2,1)} collective-permute-done((bf16[768,512]{1,0:T(8,128)(2,1)}, bf16[768,512]{1,0:T(8,128)(2,1)}, u32[]{:S(2)}, u32[]{:S(2)}) %collective-permute-start.20) | collective-permute-done | bytes 786464 | tf_op jit(solution)/shard_map/ppermute | solution.py:300
  229.7 2.6 fusion
  232.5 2.3 all-to-all-done.1
  234.8 3.7 %all-to-all-start.3 = ((bf16[8,96,512]{2,1,0:T(8,128)(2,1)}), bf16[8,96,512]{2,1,0:T(8,128)(2,1)S(1)}, u32[]{:S(2)}, u32[]{:S(2)}) async-start(bf16[8,96,512]{2,1,0:T(8,128)(2,1)} %bitcast.39), calls=%async_computation.3 | async-start | bytes 1572864 | tf_op jit(solution)/shard_map/all_to_all | solution.py:319
  239.6 0.7 pad_maximum_fusion
  240.4 16.9 %all-to-all-done.3 = bf16[8,96,512]{2,1,0:T(8,128)(2,1)S(1)} async-done(((bf16[8,96,512]{2,1,0:T(8,128)(2,1)}), bf16[8,96,512]{2,1,0:T(8,128)(2,1)S(1)}, u32[]{:S(2)}, u32[]{:S(2)}) %all-to-all-start.3) | async-done | bytes 786464 | tf_op jit(solution)/shard_map/all_to_all | solution.py:319
  257.3 0.8 convert_reduce_fusion
  (66 shorter events, 6.1 us)
Async XLA Ops:
  0.6 66.3 %collective-permute-start.8 = (bf16[2048,768]{1,0:T(8,128)(2,1)}, bf16[2048,768]{1,0:T(8,128)(2,1)}, u32[]{:S(2)}, u32[]{:S(2)}) collective-permute-start(bf16[2048,768]{1,0:T(8,128)(2,1)} %refs_1_.1), channel_id=1, source_target_pairs={{0,8},{8,0},{16,24},{24,16},{1,9},{9,1},{17,25},{25,17},{2,10},{10... | collective-permute-start | bytes 9437192 | tf_op jit(solution)/shard_map/ppermute | solution.py:300
  1.1 59.3 %copy-start.2 = (bf16[2048,768]{1,0:T(8,128)(2,1)S(1)}, bf16[2048,768]{1,0:T(8,128)(2,1)}, u32[]{:S(2)}) copy-start(bf16[2048,768]{1,0:T(8,128)(2,1)} %refs_1_.1) | copy-start | bytes 9437188
  2.8 21.1 %collective-permute-start.3 = (bf16[512,768]{1,0:T(8,128)(2,1)S(1)}, bf16[512,768]{1,0:T(8,128)(2,1)}, u32[]{:S(2)}, u32[]{:S(2)}) collective-permute-start(bf16[512,768]{1,0:T(8,128)(2,1)S(1)} %get-tuple-element.48), channel_id=1, source_target_pairs={{0,16},{8,24},{16,0},{24,8},{1,17},{9,25},{17,1},{25,9},{2,18},{10... | collective-permute-start | bytes 2359304 | tf_op jit(solution)/shard_map/ppermute | solution.py:300
  5.4 35.1 %collective-permute-start = (bf16[512,768]{1,0:T(8,128)(2,1)S(1)}, bf16[512,768]{1,0:T(8,128)(2,1)}, u32[]{:S(2)}, u32[]{:S(2)}) collective-permute-start(bf16[512,768]{1,0:T(8,128)(2,1)S(1)} %get-tuple-element.49), channel_id=1, source_target_pairs={{0,16},{8,24},{16,0},{24,8},{1,17},{9,25},{17,1},{25,9},{2,18},{10... | collective-permute-start | bytes 2359304 | tf_op jit(solution)/shard_map/ppermute | solution.py:300
  23.9 19.4 %collective-permute-start.4 = (bf16[512,768]{1,0:T(8,128)(2,1)}, bf16[512,768]{1,0:T(8,128)(2,1)}, u32[]{:S(2)}, u32[]{:S(2)}) collective-permute-start(bf16[512,768]{1,0:T(8,128)(2,1)} %collective-permute-done.3.refs_2_), channel_id=1, source_target_pairs={{0,1},{1,0},{2,3},{3,2},{4,5},{5,4},{6,7},{7,6},{8,9},{9,8},{10,11... | collective-permute-start | bytes 2359304 | tf_op jit(solution)/shard_map/ppermute | solution.py:300
  40.5 19.6 %collective-permute-start.1 = (bf16[512,768]{1,0:T(8,128)(2,1)}, bf16[512,768]{1,0:T(8,128)(2,1)}, u32[]{:S(2)}, u32[]{:S(2)}) collective-permute-start(bf16[512,768]{1,0:T(8,128)(2,1)} %collective-permute-done.refs_2_), channel_id=1, source_target_pairs={{0,1},{1,0},{2,3},{3,2},{4,5},{5,4},{6,7},{7,6},{8,9},{9,8},{10,11... | collective-permute-start | bytes 2359304 | tf_op jit(solution)/shard_map/ppermute | solution.py:300
  42.3 29.7 %collective-permute-start.7 = (bf16[512,768]{1,0:T(8,128)(2,1)}, bf16[512,768]{1,0:T(8,128)(2,1)}, u32[]{:S(2)}, u32[]{:S(2)}) collective-permute-start(bf16[512,768]{1,0:T(8,128)(2,1)} %collective-permute-done.3.refs_2_), channel_id=1, source_target_pairs={{0,8},{8,0},{16,24},{24,16},{1,9},{9,1},{17,25},{25,17},{2,10},{10... | collective-permute-start | bytes 2359304 | tf_op jit(solution)/shard_map/ppermute | solution.py:300
  42.3 32.6 %collective-permute-start.6 = (bf16[512,768]{1,0:T(8,128)(2,1)}, bf16[512,768]{1,0:T(8,128)(2,1)}, u32[]{:S(2)}, u32[]{:S(2)}) collective-permute-start(bf16[512,768]{1,0:T(8,128)(2,1)} %collective-permute-done.refs_2_), channel_id=1, source_target_pairs={{0,8},{8,0},{16,24},{24,16},{1,9},{9,1},{17,25},{25,17},{2,10},{10... | collective-permute-start | bytes 2359304 | tf_op jit(solution)/shard_map/ppermute | solution.py:300
  43.3 34.5 %collective-permute-start.5 = (bf16[512,768]{1,0:T(8,128)(2,1)}, bf16[512,768]{1,0:T(8,128)(2,1)}, u32[]{:S(2)}, u32[]{:S(2)}) collective-permute-start(bf16[512,768]{1,0:T(8,128)(2,1)} %collective-permute-done.4.refs_2_), channel_id=1, source_target_pairs={{0,8},{8,0},{16,24},{24,16},{1,9},{9,1},{17,25},{25,17},{2,10},{10... | collective-permute-start | bytes 2359304 | tf_op jit(solution)/shard_map/ppermute | solution.py:300
  60.2 20.6 %collective-permute-start.2 = (bf16[512,768]{1,0:T(8,128)(2,1)}, bf16[512,768]{1,0:T(8,128)(2,1)}, u32[]{:S(2)}, u32[]{:S(2)}) collective-permute-start(bf16[512,768]{1,0:T(8,128)(2,1)} %collective-permute-done.1.refs_2_), channel_id=1, source_target_pairs={{0,8},{8,0},{16,24},{24,16},{1,9},{9,1},{17,25},{25,17},{2,10},{10... | collective-permute-start | bytes 2359304 | tf_op jit(solution)/shard_map/ppermute | solution.py:300
  60.4 3.4 %copy-start = (bf16[1,1,512,8192]{3,2,1,0:T(8,128)(2,1)S(1)}, bf16[1,1,512,8192]{3,2,1,0:T(8,128)(2,1)}, u32[]{:S(2)}) copy-start(bf16[1,1,512,8192]{3,2,1,0:T(8,128)(2,1)} %param.10) | copy-start | bytes 25165828
  63.8 3.4 %copy-start.1 = (bf16[1,1,512,8192]{3,2,1,0:T(8,128)(2,1)S(1)}, bf16[1,1,512,8192]{3,2,1,0:T(8,128)(2,1)}, u32[]{:S(2)}) copy-start(bf16[1,1,512,8192]{3,2,1,0:T(8,128)(2,1)} %param.10) | copy-start | bytes 25165828
  84.6 6.0 %copy-start.9 = (s32[1,8,8]{2,1,0:T(8,128)S(1)}, s32[1,8,8]{2,1,0:T(8,128)}, u32[]{:S(2)}) copy-start(s32[1,8,8]{2,1,0:T(8,128)} %param.11) | copy-start | bytes 772
  84.6 33.5 %copy-start.8 = (bf16[2,384,768]{2,1,0:T(8,128)(2,1)S(1)}, bf16[2,384,768]{2,1,0:T(8,128)(2,1)}, u32[]{:S(2)}) copy-start(bf16[2,384,768]{2,1,0:T(8,128)(2,1)} %param.16) | copy-start | bytes 3538948
  84.6 26.8 %all-to-all-start = ((bf16[8,64,768]{2,1,0:T(8,128)(2,1)}), bf16[8,64,768]{2,1,0:T(8,128)(2,1)S(1)}, u32[]{:S(2)}, u32[]{:S(2)}) async-start(bf16[8,64,768]{2,1,0:T(8,128)(2,1)} %bitcast.14), calls=%async_computation | async-start | bytes 1572864 | tf_op jit(solution)/shard_map/all_to_all | solution.py:362
  111.4 6.8 %copy-start.7 = (bf16[2,3,768,384]{3,2,1,0:T(8,128)(2,1)S(1)}, bf16[2,3,768,384]{3,2,1,0:T(8,128)(2,1)}, u32[]{:S(2)}) copy-start(bf16[2,3,768,384]{3,2,1,0:T(8,128)(2,1)} %param.15) | copy-start | bytes 10616836
  112.1 12.5 %collective-permute-start.10 = (bf16[256,768]{1,0:T(8,128)(2,1)S(1)}, bf16[256,768]{1,0:T(8,128)(2,1)S(1)}, u32[]{:S(2)}, u32[]{:S(2)}) collective-permute-start(bf16[256,768]{1,0:T(8,128)(2,1)S(1)} %get-tuple-element.26.low_ref.refs_10_), channel_id=1, source_target_pairs={{1,0},{2,1},{3,2},{4,3},{5,4},{6,5},{7,6},{9,8},{10,9},{11,10},{12... | collective-permute-start | bytes 1179656 | tf_op jit(solution)/shard_map/ppermute | solution.py:308
  113.5 19.3 %collective-permute-start.9 = (bf16[256,768]{1,0:T(8,128)(2,1)S(1)}, bf16[256,768]{1,0:T(8,128)(2,1)S(1)}, u32[]{:S(2)}, u32[]{:S(2)}) collective-permute-start(bf16[256,768]{1,0:T(8,128)(2,1)S(1)} %get-tuple-element.25.high_ref.refs_11_), channel_id=1, source_target_pairs={{0,1},{1,2},{2,3},{3,4},{4,5},{5,6},{6,7},{8,9},{9,10},{10,11},{11... | collective-permute-start | bytes 1179656 | tf_op jit(solution)/shard_map/ppermute | solution.py:307
  132.8 15.0 %copy-start.3 = (bf16[768,2048]{1,0:T(8,128)(2,1)S(1)}, bf16[768,2048]{1,0:T(8,128)(2,1)}, u32[]{:S(2)}) copy-start(bf16[768,2048]{1,0:T(8,128)(2,1)} %refs_8_.1) | copy-start | bytes 9437188
  132.8 15.0 %copy-start.6 = (s32[1,128,2048]{2,1,0:T(8,128)S(1)}, s32[1,128,2048]{2,1,0:T(8,128)}, u32[]{:S(2)}) copy-start(s32[1,128,2048]{2,1,0:T(8,128)} %param.13) | copy-start | bytes 3145732
  134.9 12.9 %collective-permute-start.11 = (bf16[128,768]{1,0:T(8,128)(2,1)S(1)}, bf16[128,768]{1,0:T(8,128)(2,1)S(1)}, u32[]{:S(2)}, u32[]{:S(2)}) collective-permute-start(bf16[128,768]{1,0:T(8,128)(2,1)S(1)} %get-tuple-element.28.refs_3_.high_ref), channel_id=1, source_target_pairs={{0,1},{1,2},{2,3},{3,4},{4,5},{5,6},{6,7},{8,9},{9,10},{10,11},{11... | collective-permute-start | bytes 589832 | tf_op jit(solution)/shard_map/ppermute | solution.py:307
  139.3 8.5 %collective-permute-start.12 = (bf16[128,768]{1,0:T(8,128)(2,1)S(1)}, bf16[128,768]{1,0:T(8,128)(2,1)S(1)}, u32[]{:S(2)}, u32[]{:S(2)}) collective-permute-start(bf16[128,768]{1,0:T(8,128)(2,1)S(1)} %get-tuple-element.29.refs_2_.low_ref), channel_id=1, source_target_pairs={{1,0},{2,1},{3,2},{4,3},{5,4},{6,5},{7,6},{9,8},{10,9},{11,10},{12... | collective-permute-start | bytes 589832 | tf_op jit(solution)/shard_map/ppermute | solution.py:308
  147.8 3.9 %copy-start.4 = (bf16[2,384,768]{2,1,0:T(8,128)(2,1)S(1)}, bf16[2,384,768]{2,1,0:T(8,128)(2,1)}, u32[]{:S(2)}) copy-start(bf16[2,384,768]{2,1,0:T(8,128)(2,1)} %constant.155.clone.refs_15_.spread_ref) | copy-start | bytes 3538948
  147.8 3.9 %copy-start.5 = (bf16[2,768,384]{2,1,0:T(8,128)(2,1)S(1)}, bf16[2,768,384]{2,1,0:T(8,128)(2,1)}, u32[]{:S(2)}) copy-start(bf16[2,768,384]{2,1,0:T(8,128)(2,1)} %constant.156.clone.refs_16_.split_ref) | copy-start | bytes 3538948
  155.9 20.0 %collective-permute-start.17 = (bf16[2,768,384]{2,1,0:T(8,128)(2,1)S(1)}, bf16[2,768,384]{2,1,0:T(8,128)(2,1)S(1)}, u32[]{:S(2)}, u32[]{:S(2)}) collective-permute-start(bf16[2,768,384]{2,1,0:T(8,128)(2,1)S(1)} %get-tuple-element.40), channel_id=1, source_target_pairs={{0,8},{8,0},{16,24},{24,16},{1,9},{9,1},{17,25},{25,17},{2,10},{10... | collective-permute-start | bytes 3538952 | tf_op jit(solution)/shard_map/ppermute | solution.py:300
  156.0 8.8 %collective-permute-start.13 = (bf16[128,384]{1,0:T(8,128)(2,1)S(1)}, bf16[128,384]{1,0:T(8,128)(2,1)S(1)}, u32[]{:S(2)}, u32[]{:S(2)}) collective-permute-start(bf16[128,384]{1,0:T(8,128)(2,1)S(1)} %get-tuple-element.31.refs_3_.ghigh_ref), channel_id=1, source_target_pairs={{0,1},{1,2},{2,3},{3,4},{4,5},{5,6},{6,7},{8,9},{9,10},{10,11},{11... | collective-permute-start | bytes 294920 | tf_op jit(solution)/shard_map/ppermute | solution.py:307
  160.4 6.8 %collective-permute-start.14 = (bf16[128,384]{1,0:T(8,128)(2,1)S(1)}, bf16[128,384]{1,0:T(8,128)(2,1)S(1)}, u32[]{:S(2)}, u32[]{:S(2)}) collective-permute-start(bf16[128,384]{1,0:T(8,128)(2,1)S(1)} %get-tuple-element.32.refs_2_.glow_ref), channel_id=1, source_target_pairs={{1,0},{2,1},{3,2},{4,3},{5,4},{6,5},{7,6},{9,8},{10,9},{11,10},{12... | collective-permute-start | bytes 294920 | tf_op jit(solution)/shard_map/ppermute | solution.py:308
  164.6 34.8 %collective-permute-start.19 = (bf16[2,768,512]{2,1,0:T(8,128)(2,1)}, bf16[2,768,512]{2,1,0:T(8,128)(2,1)}, u32[]{:S(2)}, u32[]{:S(2)}) collective-permute-start(bf16[2,768,512]{2,1,0:T(8,128)(2,1)} %get-tuple-element.44), channel_id=1, source_target_pairs={{0,8},{8,0},{16,24},{24,16},{1,9},{9,1},{17,25},{25,17},{2,10},{10... | collective-permute-start | bytes 4718600 | tf_op jit(solution)/shard_map/ppermute | solution.py:300
  175.9 20.8 %collective-permute-start.15 = (bf16[2,768,384]{2,1,0:T(8,128)(2,1)}, bf16[2,768,384]{2,1,0:T(8,128)(2,1)}, u32[]{:S(2)}, u32[]{:S(2)}) collective-permute-start(bf16[2,768,384]{2,1,0:T(8,128)(2,1)} %get-tuple-element.37), channel_id=1, source_target_pairs={{0,8},{8,0},{16,24},{24,16},{1,9},{9,1},{17,25},{25,17},{2,10},{10... | collective-permute-start | bytes 3538952 | tf_op jit(solution)/shard_map/ppermute | solution.py:300
  176.1 15.8 %collective-permute-start.18 = (bf16[768,384]{1,0:T(8,128)(2,1)S(1)}, bf16[768,384]{1,0:T(8,128)(2,1)S(1)}, u32[]{:S(2)}, u32[]{:S(2)}) collective-permute-start(bf16[768,384]{1,0:T(8,128)(2,1)S(1)} %fusion.5), channel_id=1, source_target_pairs={{0,16},{8,24},{16,0},{24,8},{1,17},{9,25},{17,1},{25,9},{2,18},{10... | collective-permute-start | bytes 1769480 | tf_op jit(solution)/shard_map/ppermute | solution.py:300
  192.9 23.4 %all-to-all-start.2 = ((bf16[8,96,384]{2,1,0:T(8,128)(2,1)}), bf16[8,96,384]{2,1,0:T(8,128)(2,1)S(1)}, u32[]{:S(2)}, u32[]{:S(2)}) async-start(bf16[8,96,384]{2,1,0:T(8,128)(2,1)} %bitcast.80), calls=%async_computation.2 | async-start | bytes 1179648 | tf_op jit(solution)/shard_map/all_to_all | solution.py:319
  197.9 16.3 %collective-permute-start.16 = (bf16[768,384]{1,0:T(8,128)(2,1)S(1)}, bf16[768,384]{1,0:T(8,128)(2,1)S(1)}, u32[]{:S(2)}, u32[]{:S(2)}) collective-permute-start(bf16[768,384]{1,0:T(8,128)(2,1)S(1)} %fusion.4), channel_id=1, source_target_pairs={{0,16},{8,24},{16,0},{24,8},{1,17},{9,25},{17,1},{25,9},{2,18},{10... | collective-permute-start | bytes 1769480 | tf_op jit(solution)/shard_map/ppermute | solution.py:300
  201.7 28.0 %collective-permute-start.20 = (bf16[768,512]{1,0:T(8,128)(2,1)}, bf16[768,512]{1,0:T(8,128)(2,1)}, u32[]{:S(2)}, u32[]{:S(2)}) collective-permute-start(bf16[768,512]{1,0:T(8,128)(2,1)} %fusion.3), channel_id=1, source_target_pairs={{0,16},{8,24},{16,0},{24,8},{1,17},{9,25},{17,1},{25,9},{2,18},{10... | collective-permute-start | bytes 2359304 | tf_op jit(solution)/shard_map/ppermute | solution.py:300
  216.3 18.5 %all-to-all-start.1 = ((bf16[8,96,384]{2,1,0:T(8,128)(2,1)}), bf16[8,96,384]{2,1,0:T(8,128)(2,1)S(1)}, u32[]{:S(2)}, u32[]{:S(2)}) async-start(bf16[8,96,384]{2,1,0:T(8,128)(2,1)} %bitcast.81), calls=%async_computation.1 | async-start | bytes 1179648 | tf_op jit(solution)/shard_map/all_to_all | solution.py:319
  234.8 22.5 %all-to-all-start.3 = ((bf16[8,96,512]{2,1,0:T(8,128)(2,1)}), bf16[8,96,512]{2,1,0:T(8,128)(2,1)S(1)}, u32[]{:S(2)}, u32[]{:S(2)}) async-start(bf16[8,96,512]{2,1,0:T(8,128)(2,1)} %bitcast.39), calls=%async_computation.3 | async-start | bytes 1572864 | tf_op jit(solution)/shard_map/all_to_all | solution.py:319

commit v2 on v1

--- a/solution.py
+++ b/solution.py
@@ -13,10 +13,11 @@
 SPREAD_COARSE = 128
 BF = jnp.bfloat16
 F32 = jnp.float32
-PIECES = 2
+PIECES = 4
 
 VMEM = pl.BlockSpec(memory_space=pltpu.VMEM)
 SMEM = pl.BlockSpec(memory_space=pltpu.SMEM)
+ANY = pl.BlockSpec(memory_space=pl.ANY)
 
 
 def params(mib):
@@ -50,12 +51,12 @@
     return lax.dot_general(a, b, (((0,), (0,)), ((), ())), preferred_element_type=F32)
 
 
-def call(body, inputs, outs, flops, mib, smem=0, scratch=()):
+def call(body, inputs, outs, flops, mib, smem=0, scratch=(), after=0):
     outs = [jax.ShapeDtypeStruct(s, d) for s, d in outs]
     return pl.pallas_call(
         body,
         out_shape=outs,
-        in_specs=[SMEM] * smem + [VMEM] * (len(inputs) - smem),
+        in_specs=[SMEM] * smem + [ANY] * after + [VMEM] * (len(inputs) - smem - after),
         out_specs=[VMEM] * len(outs),
         scratch_shapes=list(scratch),
         compiler_params=params(mib),
@@ -118,12 +119,12 @@
         grid_spec=pltpu.PrefetchScalarGridSpec(
             num_scalar_prefetch=1, grid=(steps,), in_specs=in_specs, out_specs=whole
         ),
-        compiler_params=params(24),
+        compiler_params=params(56),
         cost_estimate=cost(2 * row_count * depth * channels * count, list(weights) * 2 + [out]),
     )(jnp.stack(starts).astype(jnp.int32) // block, *inputs)
 
 
-def place_body(target_ref, received_ref, hidden_ref, low_ref, high_ref):
+def place_body(target_ref, received_ref, kernels_ref, hidden_ref, low_ref, high_ref, down_ref, up_ref):
     half = low_ref.shape[0]
     rows = received_ref[...]
     for h, out in enumerate((low_ref, high_ref)):
@@ -132,25 +133,29 @@
         placed = nn(pick, rows)
         hidden_ref[h * half : (h + 1) * half] = placed.astype(BF)
         out[...] = gelu(placed).astype(BF)
+    down_ref[...] = nn(low_ref[...], kernels_ref[0, 2]).astype(BF)
+    up_ref[...] = nn(high_ref[...], kernels_ref[0, 0]).astype(BF)
+
+
+def local_body(low_ref, high_ref, kernels_ref, inner_ref):
+    half = low_ref.shape[0]
+    low, high = low_ref[...], high_ref[...]
+    inner_ref[:half] = nn(low, kernels_ref[0, 1]) + nn(high, kernels_ref[0, 2])
+    inner_ref[half:] = nn(low, kernels_ref[0, 0]) + nn(high, kernels_ref[0, 1])
 
 
 def fine_body(
-    prev_ref, low_ref, high_ref, next_ref, hidden_ref, kernel_ref, mixer_ref,
-    inner_ref, gated_ref, first_ref, alow_ref, ahigh_ref,
+    prev_ref, next_ref, local_ref, hidden_ref, kernels_ref, mixers_ref,
+    inner_ref, gated_ref, first_ref, alow_ref, ahigh_ref, down_ref, up_ref,
 ):
-    half = low_ref.shape[0]
+    half = prev_ref.shape[0]
     slab = half // 4
-    taps = (prev_ref, low_ref, high_ref, next_ref)
-    for h, active in enumerate((alow_ref, ahigh_ref)):
-        inner = (
-            nn(taps[h + 1][...], kernel_ref[1])
-            + nn(taps[h][...], kernel_ref[0])
-            + nn(taps[h + 2][...], kernel_ref[2])
-        )
+    for h, (came, active) in enumerate(((prev_ref, alow_ref), (next_ref, ahigh_ref))):
+        inner = local_ref[h * half : (h + 1) * half] + came[...].astype(F32)
         inner_ref[h * half : (h + 1) * half] = inner
         gated = gelu(inner).astype(BF)
         gated_ref[h * half : (h + 1) * half] = gated
-        out = hidden_ref[h * half : (h + 1) * half].astype(F32) + nn(gated, mixer_ref[...])
+        out = hidden_ref[h * half : (h + 1) * half].astype(F32) + nn(gated, mixers_ref[0])
         for s in range(2):
             a = out[2 * s * slab : (2 * s + 1) * slab]
             b = out[(2 * s + 1) * slab : (2 * s + 2) * slab]
@@ -158,27 +163,27 @@
             start = h * half // 2 + s * slab
             first_ref[start : start + slab] = pooled
             active[s * slab : (s + 1) * slab] = gelu(pooled.astype(F32)).astype(BF)
+    down_ref[...] = nn(alow_ref[...], kernels_ref[1, 2]).astype(BF)
+    up_ref[...] = nn(ahigh_ref[...], kernels_ref[1, 0]).astype(BF)
 
 
 def coarse_body(
     scale, bins_per,
-    ids_ref, prev_ref, low_ref, high_ref, next_ref, first_ref, kernel_ref, mixer_ref, readout_ref, targets_ref,
+    ids_ref, prev_ref, low_ref, high_ref, next_ref, first_ref, kernels_ref, mixers_ref, readout_ref, targets_ref,
     gated_ref, second_ref, logit_ref, upper_ref, glow_ref, ghigh_ref,
 ):
     half = low_ref.shape[0]
     slab = half // 2
-    taps = (prev_ref, low_ref, high_ref, next_ref)
     slopes = []
-    for h in range(2):
+    for h, came in enumerate((prev_ref, next_ref)):
         inner = (
-            nn(taps[h + 1][...], kernel_ref[1])
-            + nn(taps[h][...], kernel_ref[0])
-            + nn(taps[h + 2][...], kernel_ref[2])
+            nn(low_ref[...], kernels_ref[1, 1 - h]) + nn(high_ref[...], kernels_ref[1, 2 - h])
+            + came[...].astype(F32)
         )
         slopes.append(gelu_slope(inner))
         gated = gelu(inner).astype(BF)
         gated_ref[h * half : (h + 1) * half] = gated
-        out = first_ref[h * half : (h + 1) * half].astype(F32) + nn(gated, mixer_ref[...])
+        out = first_ref[h * half : (h + 1) * half].astype(F32) + nn(gated, mixers_ref[1])
         second_ref[h * slab : (h + 1) * slab] = ((out[:slab] + out[slab:]) * 0.5).astype(BF)
     bins = second_ref.shape[0]
     tracks = readout_ref.shape[1]
@@ -199,14 +204,14 @@
         upper = upper + nt(grad, readout)
     upper = (upper * 0.5).astype(BF)
     upper_ref[...] = upper
-    back = nt(upper, mixer_ref[...])
+    back = nt(upper, mixers_ref[1])
     for h, out in enumerate((glow_ref, ghigh_ref)):
         piece = back[h * slab : (h + 1) * slab]
         for s in range(2):
             out[s * slab : (s + 1) * slab] = (piece * slopes[h][s * slab : (s + 1) * slab]).astype(BF)
 
 
-def readout_body(ids_ref, second_ref, logit_ref, keep_ref, send_ref):
+def readout_body(ids_ref, after_ref, before_ref, second_ref, logit_ref, keep_ref, send_ref):
     width = keep_ref.shape[2]
     second = second_ref[...]
     for k in range(4):
@@ -230,36 +235,33 @@
             send_ref[far] = block
 
 
-def weight_pieces(taps, grads, gated, upstream, spread_ref, split_ref):
-    pieces = []
-    for t in range(3):
-        pieces.append((tn(taps[t][...], grads[0]) + tn(taps[t + 1][...], grads[1])).astype(BF))
+def mixer_piece(gated, upstream, spread_ref, split_ref):
     mixed = 0.0
     for j in range(2):
         left = nn(gated, spread_ref[j]).astype(BF)
         right = nn(upstream, split_ref[j]).astype(BF)
         mixed = mixed + tn(left, right)
-    pieces.append(mixed.astype(BF))
-    return pieces
+    return mixed.astype(BF)
 
 
 def coarse_grad_body(
-    ids_ref, prev_ref, low_ref, high_ref, next_ref, glow_ref, ghigh_ref, gated_ref, upper_ref, spread_ref, split_ref,
-    keep_ref, send_ref,
+    ids_ref, after_ref, before_ref, low_ref, high_ref, gprev_ref, glow_ref, ghigh_ref, gnext_ref, gated_ref, upper_ref,
+    spread_ref, split_ref, keep_ref, send_ref,
 ):
     slab = low_ref.shape[0] // 2
     upper = upper_ref[...]
     rows = jnp.concatenate([upper[:slab], upper[:slab], upper[slab:], upper[slab:]], axis=0)
-    pieces = weight_pieces(
-        (prev_ref, low_ref, high_ref, next_ref), (glow_ref[...], ghigh_ref[...]), gated_ref[...], rows,
-        spread_ref, split_ref,
-    )
+    grads = (gprev_ref, glow_ref, ghigh_ref, gnext_ref)
+    pieces = []
+    for t in range(3):
+        pieces.append((tn(low_ref[...], grads[2 - t][...]) + tn(high_ref[...], grads[3 - t][...])).astype(BF))
+    pieces.append(mixer_piece(gated_ref[...], rows, spread_ref, split_ref))
     store_blocks(ids_ref, pieces, keep_ref, send_ref)
 
 
 def fine_grad_body(
     scale,
-    ids_ref, gprev_ref, glow_ref, ghigh_ref, gnext_ref, upper_ref, first_ref, kernel_ref, mixer_ref,
+    ids_ref, after_ref, gprev_ref, glow_ref, ghigh_ref, gnext_ref, upper_ref, first_ref, kernels_ref, mixers_ref,
     prev_ref, low_ref, high_ref, next_ref, inner_ref, gated_ref, spread_ref, split_ref,
     trunk_ref, keep_ref, send_ref, lanes_ref,
 ):
@@ -270,9 +272,9 @@
     inner_grads, rows = [], []
     for h in range(2):
         back = (
-            nt(grads[h + 2][...], kernel_ref[0])
-            + nt(grads[h + 1][...], kernel_ref[1])
-            + nt(grads[h][...], kernel_ref[2])
+            nt(grads[h + 2][...], kernels_ref[1, 0])
+            + nt(grads[h + 1][...], kernels_ref[1, 1])
+            + nt(grads[h][...], kernels_ref[1, 2])
         )
         slope = gelu_slope(first_ref[h * half : (h + 1) * half].astype(F32))
         base = upper[h * slab : (h + 1) * slab]
@@ -283,15 +285,16 @@
                 lanes_ref[t, pl.ds(s, slab, stride=2), :] = total[s * slab : (s + 1) * slab, cols] * scale
             trunk_ref[h * half : (h + 1) * half, cols] = lanes_ref[t]
         lower = (total * 0.5).astype(BF)
-        inner = nt(lower, mixer_ref[...])
+        inner = nt(lower, mixers_ref[0])
         spread_inner = jnp.concatenate([inner[:slab], inner[:slab], inner[slab:], inner[slab:]], axis=0)
         slope = gelu_slope(inner_ref[2 * h * half : 2 * (h + 1) * half])
         inner_grads.append((spread_inner * slope).astype(BF))
         rows += [lower[:slab], lower[:slab], lower[slab:], lower[slab:]]
-    pieces = weight_pieces(
-        (prev_ref, low_ref, high_ref, next_ref), inner_grads, gated_ref[...], jnp.concatenate(rows, axis=0),
-        spread_ref, split_ref,
-    )
+    taps = (prev_ref, low_ref, high_ref, next_ref)
+    pieces = []
+    for t in range(3):
+        pieces.append((tn(taps[t][...], inner_grads[0]) + tn(taps[t + 1][...], inner_grads[1])).astype(BF))
+    pieces.append(mixer_piece(gated_ref[...], jnp.concatenate(rows, axis=0), spread_ref, split_ref))
     store_blocks(ids_ref, pieces, keep_ref, send_ref)
 
 
@@ -309,16 +312,39 @@
     )
 
 
-def scatter_sum(keep, send):
+def core_sum(keep, send):
     came = swap(send, "dp", 1)
     away = (keep[1].astype(F32) + came[1].astype(F32)).astype(BF)
     here = keep[0].astype(F32) + came[0].astype(F32)
-    total = (here + swap(away, "dp", 2).astype(F32)).astype(BF)
+    return here, away
+
+
+def x_sum(here, away):
+    return (here + swap(away, "dp", 2).astype(F32)).astype(BF)
+
+
+def seq_sum(total):
     groups = lax.axis_size("seq")
     rows, columns = total.shape
     parts = lax.all_to_all(
         total.reshape(groups, rows // groups, columns), "seq", split_axis=0, concat_axis=0, tiled=True
     )
+    return parts.astype(F32).sum(axis=0)
+
+
+def side_first_sum(keep, send):
+    groups = lax.axis_size("seq")
+    side = lax.axis_index("seq") % 2
+    came = swap(send, "dp", 1)
+    blocks, rows, columns = keep.shape
+    total = keep.astype(F32) + came.astype(F32)
+    total = total.reshape(blocks, groups // 2, 2, rows // groups, columns)
+    other = lax.dynamic_index_in_dim(total, 1 - side, axis=2, keepdims=False).astype(BF)
+    own = lax.dynamic_index_in_dim(total, side, axis=2, keepdims=False)
+    total = own + swap(other, "seq", 1).astype(F32)
+    total = (total[0] + swap(total[1].astype(BF), "dp", 2).astype(F32)).astype(BF)
+    lines = [list(range(start, groups, 2)) for start in range(2)]
+    parts = lax.all_to_all(total, "seq", split_axis=0, concat_axis=0, axis_index_groups=lines, tiled=True)
     return parts.astype(F32).sum(axis=0)
 
 
@@ -341,22 +367,27 @@
     from_core = swap(projection, "dp", 1)
     mine = lax.dynamic_slice_in_dim(projection, side * share, share, axis=0)
     far = [swap(lax.slice_in_dim(mine, i * piece, (i + 1) * piece), "dp", 2) for i in range(PIECES)]
-    far_side = [swap(f, "seq", 1) for f in far]
-    far_core = [swap(f, "dp", 1) for f in far]
-    far_side_core = [swap(f, "dp", 1) for f in far_side]
+    near, away = (me ^ 2) * depth, (me ^ 3) * depth
     total = project(None, rows, [projection], [me * depth], False)
     total = project(total, rows, [from_core], [(me ^ 1) * depth], False)
+    weights, starts = [], []
     for i in range(PIECES):
+        if weights:
+            total = project(total, rows, weights, starts, False)
+        held, total = lax.optimization_barrier((far[i], total))
+        if i:
+            weights, starts = [side_piece, swap(side_piece, "dp", 1)], [near + side_at, away + side_at]
+        else:
+            weights, starts = [], []
         at = side * share + i * piece
-        total = project(
-            total, rows, [far[i], far_core[i]], [(me ^ 2) * depth + at, (me ^ 3) * depth + at], False
-        )
-    for i in range(PIECES):
-        at = (1 - side) * share + i * piece
-        total = project(
-            total, rows, [far_side[i], far_side_core[i]],
-            [(me ^ 2) * depth + at, (me ^ 3) * depth + at], i == PIECES - 1,
-        )
+        weights += [held, swap(held, "dp", 1)]
+        starts += [near + at, away + at]
+        side_piece = swap(held, "seq", 1)
+        side_at = (1 - side) * share + i * piece
+    total = project(total, rows, weights, starts, False)
+    total = project(
+        total, rows, [side_piece, swap(side_piece, "dp", 1)], [near + side_at, away + side_at], True
+    )
 
     block = row_count // groups
     received = lax.all_to_all(
@@ -367,19 +398,23 @@
     slot = (position // half) * half + (position % 4) * eighth + (position % half) // 4
     target = jnp.where(device * row_count + position < length, slot, -1).reshape(1, row_count)
 
-    hidden, low, high = call(
-        place_body, (target, received),
-        [((row_count, channels), BF), ((half, channels), BF), ((half, channels), BF)],
+    hidden, low, high, down, up = call(
+        place_body, (target, received, kernels),
+        [((row_count, channels), BF), ((half, channels), BF), ((half, channels), BF),
+         ((half, width), BF), ((half, width), BF)],
         2 * row_count * row_count * channels, 24,
     )
-    prev, nxt = halo(low, high)
-    inner, gated, first, alow, ahigh = call(
-        fine_body, (prev, low, high, nxt, hidden, kernels[0], mixers[0]),
+    fprev, fnext = halo(down, up)
+    local, = call(local_body, (low, high, kernels), [((row_count, width), F32)], 4 * row_count * width * channels, 24)
+    fprev, fnext, low_later, high_later = lax.optimization_barrier((fprev, fnext, low, high))
+    prev, nxt = halo(low_later, high_later)
+    inner, gated, first, alow, ahigh, adown, aup = call(
+        fine_body, (fprev, fnext, local, hidden, kernels, mixers),
         [((row_count, width), F32), ((row_count, width), BF), ((half, channels), BF),
-         ((quarter, channels), BF), ((quarter, channels), BF)],
-        8 * row_count * width * channels, 24,
-    )
-    aprev, anext = halo(alow, ahigh)
+         ((quarter, channels), BF), ((quarter, channels), BF), ((quarter, width), BF), ((quarter, width), BF)],
+        3 * row_count * width * channels, 24,
+    )
+    aprev, anext = halo(adown, aup)
     bins = quarter
     loss = 2.0 / math.sqrt(windows * groups * bins)
     ids = jnp.stack([device, length]).astype(jnp.int32)
@@ -389,17 +424,17 @@
         coarse_body(loss, bins, *refs)
 
     cgated, second, logit_grad, upper, glow, ghigh = call(
-        coarse, (ids, aprev, alow, ahigh, anext, first, kernels[1], mixers[1], readout, targets[0]),
+        coarse, (ids, aprev, alow, ahigh, anext, first, kernels, mixers, readout, targets[0]),
         [((half, width), BF), ((bins, channels), BF), ((bins, tracks), BF), ((bins, channels), BF),
          ((quarter, width), BF), ((quarter, width), BF)],
         8 * half * width * channels + 4 * bins * tracks * channels, 32, smem=1,
     )
     gprev, gnext = halo(glow, ghigh)
     track_keep, track_send = call(
-        readout_body, (place, second, logit_grad), [((2, channels, tracks // 4), BF)] * 2,
-        2 * bins * tracks * channels, 24, smem=1,
-    )
-    readout_total = scatter_sum(track_keep, track_send)
+        readout_body, (place, prev, nxt, second, logit_grad), [((2, channels, tracks // 4), BF)] * 2,
+        2 * bins * tracks * channels, 24, smem=1, after=2,
+    )
+    track_here, track_away = core_sum(track_keep, track_send)
 
     per = width // groups
     fold = np.zeros((2, width, channels), ml_dtypes.bfloat16)
@@ -412,24 +447,32 @@
             split[j, (b // piece_width) * 2 * piece_width + j * piece_width + b % piece_width, b] = 1
     fold, split = jnp.asarray(fold), jnp.asarray(split)
     pair = [((2, channels, width), BF)] * 2
-    coarse_keep, coarse_send = call(
-        coarse_grad_body, (place, aprev, alow, ahigh, anext, glow, ghigh, cgated, upper, fold, split), pair,
-        12 * half * width * channels, 32, smem=1,
-    )
-    coarse_total = scatter_sum(coarse_keep, coarse_send)
 
     def fine(*refs):
         fine_grad_body(math.sqrt(windows * groups * bins) * 0.5, *refs)
 
+    cut = channels // 2
+    track_first = swap(track_away[:cut], "dp", 2)
     trunk, fine_keep, fine_send = call(
         fine,
-        (place, gprev, glow, ghigh, gnext, upper, first, kernels[1], mixers[0],
+        (place, track_away, gprev, glow, ghigh, gnext, upper, first, kernels, mixers,
          prev, low, high, nxt, inner, gated, fold, split),
         [((half, channels), F32)] + pair,
-        20 * row_count * width * channels, 40, smem=1,
+        20 * row_count * width * channels, 40, smem=1, after=1,
         scratch=[pltpu.VMEM((channels // 128, quarter, 128), F32)],
     )
-    fine_total = scatter_sum(fine_keep, fine_send)
+    fine_send, track_first = lax.optimization_barrier((fine_send, track_first))
+    track_last = swap(track_away[cut:], "dp", 2)
+    track_total = (track_here + jnp.concatenate([track_first, track_last]).astype(F32)).astype(BF)
+    readout_total = seq_sum(track_total)
+    fine_here, fine_away = core_sum(fine_keep, fine_send)
+    coarse_keep, coarse_send = call(
+        coarse_grad_body,
+        (place, fine_away, track_total, alow, ahigh, gprev, glow, ghigh, gnext, cgated, upper, fold, split), pair,
+        12 * half * width * channels, 32, smem=1, after=2,
+    )
+    fine_total = seq_sum(x_sum(fine_here, fine_away))
+    coarse_total = side_first_sum(coarse_keep, coarse_send)
 
     cut = width // windows
     kernel_rows, mixer_rows = [], []

time: 259 us -> 255 us (0.985)
  waiting for transfers between devices: 146 us -> 107 us
  Pallas kernels: 42.6 us -> 58.2 us
  starting transfers between devices: 48.6 us -> 62.7 us
  local copies, waits for them, and re-layouts: 6.09 us -> 10.2 us
    ppermute x15 -> x25, waiting for transfers between devices: 84 us -> 39.7 us  [swap(): return lax.ppermute(value, axis, [(i, i ^ bit) for i in range(size)])]
    pallas_call x6 -> x7, Pallas kernels: 20.5 us -> 36.3 us  [project(): pl.pallas_call(body, out_shape=out, grid_spec=pltpu.PrefetchScalarGridSpe...]
    ppermute x15 -> x25, starting transfers between devices: 11.4 us -> 21.2 us  [swap(): return lax.ppermute(value, axis, [(i, i ^ bit) for i in range(size)])]
    convert_element_type x6, other arithmetic: 9.36 us -> 3.69 us  [the longest x2 1.49 us: shards(): (track_here + jnp.concatenate([track_first, track_last]).astype(F32)).ast...]
    all_to_all x3, waiting for transfers between devices: 19.2 us -> 23.7 us  [the longest x2 15.3 us: seq_sum(): lax.all_to_all(total.reshape(groups, rows // groups, columns), 'seq', spl...]
    unnamed x20 -> x56, local copies, waits for them, and re-layouts: 3.64 us -> 7.26 us
    ppermute x3 -> x4, starting transfers between devices: 13.4 us -> 16.8 us  [halo(): lax.ppermute(high, 'seq', up)]
    add x0 -> x3, other arithmetic: none -> 3.44 us  [the longest x1 1.6 us: side_first_sum(): total = keep.astype(F32) + came.astype(F32)]
  transfers between devices with their start and end apart: 25 -> 37, of which waited for: 14 -> 16; matrix products, arithmetic and copies ran while one was open for 6% -> 6% of each run, Pallas kernels for 11% -> 18%
where the time goes in v2:
time: 255 us; the launch traced here: 254 us
  waiting for transfers between devices  107 us (42%)
  starting transfers between devices  62.7 us (25%)
  Pallas kernels  58.2 us (23%)
  other arithmetic  14.3 us (6%)
  local copies, waits for them, and re-layouts  10.2 us (4%)
    ppermute x25, waiting for transfers between devices, swap(): return lax.ppermute(value, axis, [(i, i ^ bit) for i in range(size)])  39.7 us
    pallas_call x7, Pallas kernels, project(): pl.pallas_call(body, out_shape=out, grid_spec=pltpu.PrefetchScalarGridSpe...  36.3 us
    pallas_call x7, Pallas kernels, call(): pl.pallas_call(body, out_shape=outs, in_specs=[SMEM] * smem + [ANY] * aft...  21.9 us
    ppermute x25, starting transfers between devices, swap(): return lax.ppermute(value, axis, [(i, i ^ bit) for i in range(size)])  21.2 us
    all_to_all x1, waiting for transfers between devices, shards(): lax.all_to_all(total.reshape(groups, block, channels), 'seq', split_axis=...  19.8 us
    ppermute x4, starting transfers between devices, halo(): lax.ppermute(high, 'seq', up)  16.8 us
    ppermute x4, waiting for transfers between devices, halo(): lax.ppermute(high, 'seq', up)  15.9 us
    all_to_all x2, waiting for transfers between devices, seq_sum(): lax.all_to_all(total.reshape(groups, rows // groups, columns), 'seq', spl...  15.3 us
  transfers between devices with their start and end apart: 37, of which 16 were waited for; matrix products, arithmetic and copies ran while one was open for 6% of the time, Pallas kernels for 18%

profile of v2, /device:TPU:0, one launch (start us, length us, event | category | flops | bytes accessed | tf_op | source)
XLA Modules:
  0.0 253.8 jit_solution(13973087949132099117)
XLA Ops:
  1.1 2.4 constant_dynamic-slice_fusion.2
  3.5 2.5 collective-permute-start.2
  6.1 6.0 %shard_map.129.refs_2_ = f32[512,768]{1,0:T(8,128)} custom-call(s32[1]{0:T(128)S(6)} %select_n.119.starts_ref, bf16[512,8192]{1,0:T(8,128)(2,1)} %bitcast.80, bf16[2048,768]{1,0:T(8,128)(2,1)} %refs_1_.1), custom_call_target="tpu_custom_call" | custom-call | flops 1610612736 | bytes 7864320 | tf_op jit(solution)/shard_map/pallas_call | solution.py:116
  12.0 1.6 copy-done.9
  13.7 6.6 %shard_map.130.refs_4_ = f32[512,768]{1,0:T(8,128)} custom-call(s32[1]{0:T(128)S(6)} %select_n.118.starts_ref, bf16[512,8192]{1,0:T(8,128)(2,1)} %bitcast.81, bf16[2048,768]{1,0:T(8,128)(2,1)} %copy-done.9, f32[512,768]{1,0:T(8,128)} %shard_map.129.refs_2_), custom_call_target="tpu_custom_call" | custom-call | flops 1610612736 | bytes 7864320 | tf_op jit(solution)/shard_map/pallas_call | solution.py:116
  20.7 1.8 collective-permute-start.8
  23.9 4.3 %shard_map.131.refs_8_ = f32[512,768]{1,0:T(8,128)} custom-call(s32[2]{0:T(128)} %and_select_fusion.6.starts_ref, bf16[512,8192]{1,0:T(8,128)(2,1)} %bitcast.82, bf16[512,8192]{1,0:T(8,128)(2,1)} %bitcast.83, bf16[256,768]{1,0:T(8,128)(2,1)} %collective-permute-done.2.refs_2_, bf16[256,768]{1,0:T(8,128)(2,1)} %copy-done.26, f32[512,768]{1,0:T(8,128)} %shard_map.130.refs_4_), custom_call_target="tpu_custom_call" | custom-call | flops 402653184 | bytes 3145728 | tf_op jit(solution)/shard_map/pallas_call | solution.py:116
  28.1 3.9 %collective-permute-done.1.refs_6_ = bf16[256,768]{1,0:T(8,128)(2,1)S(1)} collective-permute-done((bf16[256,768]{1,0:T(8,128)(2,1)}, bf16[256,768]{1,0:T(8,128)(2,1)S(1)}, u32[]{:S(2)}, u32[]{:S(2)}) %collective-permute-start.1) | collective-permute-done | bytes 393248 | tf_op jit(solution)/shard_map/ppermute | solution.py:303
  32.6 1.7 collective-permute-start.7
  34.3 1.5 collective-permute-start.5
  38.0 5.0 %shard_map.132.refs_8_ = f32[512,768]{1,0:T(8,128)} custom-call(s32[4]{0:T(128)} %and_select_fusion.5.starts_ref, bf16[512,8192]{1,0:T(8,128)(2,1)} %bitcast.84, bf16[512,8192]{1,0:T(8,128)(2,1)} %bitcast.85, bf16[512,8192]{1,0:T(8,128)(2,1)} %bitcast.86, bf16[512,8192]{1,0:T(8,128)(2,1)} %bitcast.87, bf16[256,768]{1,0:T(8,128)(2,1)} %copy-done.17, ...), custom_call_target="tpu_custom_call" | custom-call | flops 805306368 | bytes 4718592 | tf_op jit(solution)/shard_map/pallas_call | solution.py:116
  46.5 1.5 collective-permute-start.14
  49.5 5.1 %shard_map.133.refs_8_ = f32[512,768]{1,0:T(8,128)} custom-call(s32[4]{0:T(128)} %and_select_fusion.7.starts_ref, bf16[512,8192]{1,0:T(8,128)(2,1)} %bitcast.88, bf16[512,8192]{1,0:T(8,128)(2,1)} %bitcast.89, bf16[512,8192]{1,0:T(8,128)(2,1)} %bitcast.90, bf16[512,8192]{1,0:T(8,128)(2,1)} %bitcast.91, bf16[256,768]{1,0:T(8,128)(2,1)} %copy-done.15, ...), custom_call_target="tpu_custom_call" | custom-call | flops 805306368 | bytes 4718592 | tf_op jit(solution)/shard_map/pallas_call | solution.py:116
  54.6 2.0 collective-permute-done.refs_6_
  56.5 1.5 collective-permute-start.12
  58.6 8.7 %collective-permute-done.12.refs_2_ = bf16[256,768]{1,0:T(8,128)(2,1)S(1)} collective-permute-done((bf16[256,768]{1,0:T(8,128)(2,1)S(1)}, bf16[256,768]{1,0:T(8,128)(2,1)S(1)}, u32[]{:S(2)}, u32[]{:S(2)}) %collective-permute-start.12) | collective-permute-done | bytes 393248 | tf_op jit(solution)/shard_map/ppermute | solution.py:303
  70.1 5.0 %shard_map.134.refs_4_ = f32[512,768]{1,0:T(8,128)} custom-call(s32[4]{0:T(128)} %and_select_fusion.4.starts_ref, bf16[512,8192]{1,0:T(8,128)(2,1)} %bitcast.92, bf16[512,8192]{1,0:T(8,128)(2,1)} %bitcast.93, bf16[512,8192]{1,0:T(8,128)(2,1)} %bitcast.94, bf16[512,8192]{1,0:T(8,128)(2,1)} %bitcast.95, bf16[256,768]{1,0:T(8,128)(2,1)} %copy-done.16, ...), custom_call_target="tpu_custom_call" | custom-call | flops 805306368 | bytes 4718592 | tf_op jit(solution)/shard_map/pallas_call | solution.py:116
  75.2 4.3 %shard_map.135 = bf16[512,768]{1,0:T(8,128)(2,1)} custom-call(s32[2]{0:T(128)} %and_select_fusion.8.starts_ref, bf16[512,8192]{1,0:T(8,128)(2,1)} %bitcast.96, bf16[512,8192]{1,0:T(8,128)(2,1)} %bitcast.97, bf16[256,768]{1,0:T(8,128)(2,1)} %copy-done.25, bf16[256,768]{1,0:T(8,128)(2,1)} %collective-permute-done.13.refs_3_, f32[512,768]{1,0:T(8,128)} %shard_map.134.refs_4_), custom_call_target="tpu_custom_call" | custom-call | flops 402653184 | bytes 2359296 | tf_op jit(solution)/shard_map/pallas_call | solution.py:116
  79.5 6.0 %all-to-all-start = ((bf16[8,64,768]{2,1,0:T(8,128)(2,1)}), bf16[8,64,768]{2,1,0:T(8,128)(2,1)}, u32[]{:S(2)}, u32[]{:S(2)}) async-start(bf16[8,64,768]{2,1,0:T(8,128)(2,1)} %bitcast.102), calls=%async_computation | async-start | bytes 1572864 | tf_op jit(solution)/shard_map/all_to_all | solution.py:393
  86.5 19.8 %all-to-all-done = bf16[8,64,768]{2,1,0:T(8,128)(2,1)} async-done(((bf16[8,64,768]{2,1,0:T(8,128)(2,1)}), bf16[8,64,768]{2,1,0:T(8,128)(2,1)}, u32[]{:S(2)}, u32[]{:S(2)}) %all-to-all-start) | async-done | bytes 786464 | tf_op jit(solution)/shard_map/all_to_all | solution.py:393
  106.3 2.2 shard_map.136
  108.5 3.3 %collective-permute-start.17 = (bf16[256,384]{1,0:T(8,128)(2,1)S(1)}, bf16[256,384]{1,0:T(8,128)(2,1)S(1)}, u32[]{:S(2)}, u32[]{:S(2)}) collective-permute-start(bf16[256,384]{1,0:T(8,128)(2,1)S(1)} %get-tuple-element.51), channel_id=1, source_target_pairs={{0,1},{1,2},{2,3},{3,4},{4,5},{5,6},{6,7},{8,9},{9,10},{10,11},{11... | collective-permute-start | bytes 589832 | tf_op jit(solution)/shard_map/ppermute | solution.py:310
  113.2 6.6 %collective-permute-done.17.prev_ref = bf16[256,384]{1,0:T(8,128)(2,1)S(1)} collective-permute-done((bf16[256,384]{1,0:T(8,128)(2,1)S(1)}, bf16[256,384]{1,0:T(8,128)(2,1)S(1)}, u32[]{:S(2)}, u32[]{:S(2)}) %collective-permute-start.17) | collective-permute-done | bytes 196640 | tf_op jit(solution)/shard_map/ppermute | solution.py:310
  119.7 4.4 %collective-permute-start.19 = (bf16[256,768]{1,0:T(8,128)(2,1)S(1)}, bf16[256,768]{1,0:T(8,128)(2,1)S(1)}, u32[]{:S(2)}, u32[]{:S(2)}) collective-permute-start(bf16[256,768]{1,0:T(8,128)(2,1)S(1)} %get-tuple-element.55.high_ref.refs_12_), channel_id=1, source_target_pairs={{0,1},{1,2},{2,3},{3,4},{4,5},{5,6},{6,7},{8,9},{9,10},{10,11},{11... | collective-permute-start | bytes 1179656 | tf_op jit(solution)/shard_map/ppermute | solution.py:310
  127.6 4.7 %collective-permute-start.21 = (bf16[128,384]{1,0:T(8,128)(2,1)S(1)}, bf16[128,384]{1,0:T(8,128)(2,1)S(1)}, u32[]{:S(2)}, u32[]{:S(2)}) collective-permute-start(bf16[128,384]{1,0:T(8,128)(2,1)S(1)} %get-tuple-element.60), channel_id=1, source_target_pairs={{0,1},{1,2},{2,3},{3,4},{4,5},{5,6},{6,7},{8,9},{9,10},{10,11},{11... | collective-permute-start | bytes 294920 | tf_op jit(solution)/shard_map/ppermute | solution.py:310
  132.3 1.5 collective-permute-start.22
  133.9 8.4 %collective-permute-done.21.refs_1_ = bf16[128,384]{1,0:T(8,128)(2,1)S(1)} collective-permute-done((bf16[128,384]{1,0:T(8,128)(2,1)S(1)}, bf16[128,384]{1,0:T(8,128)(2,1)S(1)}, u32[]{:S(2)}, u32[]{:S(2)}) %collective-permute-start.21) | collective-permute-done | bytes 98336 | tf_op jit(solution)/shard_map/ppermute | solution.py:310
  142.3 3.7 %shard_map.139 = (bf16[256,384]{1,0:T(8,128)(2,1)S(1)}, bf16[128,768]{1,0:T(8,128)(2,1)S(1)}, bf16[128,2048]{1,0:T(8,128)(2,1)S(1)}, bf16[128,768]{1,0:T(8,128)(...) custom-call(s32[2]{0:T(128)S(1)} %pad_add_fusion.6.refs_0_, ...), custom_call_target="tpu_custom_call" | custom-call | flops 1409286144 | bytes 11206664 | tf_op jit(solution)/shard_map/pallas_call | solution.py:56
  146.0 1.5 shard_map.140
  147.6 3.4 %collective-permute-done.23 = bf16[2,768,512]{2,1,0:T(8,128)(2,1)S(1)} collective-permute-done((bf16[2,768,512]{2,1,0:T(8,128)(2,1)S(1)}, bf16[2,768,512]{2,1,0:T(8,128)(2,1)S(1)}, u32[]{:S(2)}, u32[]{:S(2)}) %collective-permute-start.23) | collective-permute-done | bytes 1572896 | tf_op jit(solution)/shard_map/ppermute | solution.py:303
  151.9 4.4 %collective-permute-start.24 = (bf16[128,384]{1,0:T(8,128)(2,1)S(1)}, bf16[128,384]{1,0:T(8,128)(2,1)S(1)}, u32[]{:S(2)}, u32[]{:S(2)}) collective-permute-start(bf16[128,384]{1,0:T(8,128)(2,1)S(1)} %get-tuple-element.69.refs_4_.ghigh_ref), channel_id=1, source_target_pairs={{0,1},{1,2},{2,3},{3,4},{4,5},{5,6},{6,7},{8,9},{9,10},{10,11},{11... | collective-permute-start | bytes 294920 | tf_op jit(solution)/shard_map/ppermute | solution.py:310
  158.5 7.5 %collective-permute-done.25.refs_5_.gnext_ref = bf16[128,384]{1,0:T(8,128)(2,1)S(1)} collective-permute-done((bf16[128,384]{1,0:T(8,128)(2,1)S(1)}, bf16[128,384]{1,0:T(8,128)(2,1)S(1)}, u32[]{:S(2)}, u32[]{:S(2)}) %collective-permute-start.25) | collective-permute-done | bytes 98336 | tf_op jit(solution)/shard_map/ppermute | solution.py:311
  166.0 8.5 %shard_map.141 = (f32[256,768]{1,0:T(8,128)}, bf16[2,768,384]{2,1,0:T(8,128)(2,1)S(1)}, bf16[2,768,384]{2,1,0:T(8,128)(2,1)S(1)}) custom-call(s32[2]{0:T(128)S(1)} %pad_add_fusion.ids_ref.refs_0_, bf16[768,512]{1,0:T(8,128)(2,1)S(1)} %bitcast.78, bf16[128,384]{1,0:T(8,128)(2,1)S(1)} %collective-permute-done.24.refs_2_.gprev_ref, ...), custom_call_target="tpu_custom_call" | custom-call | flops 3019898880 | bytes 14745608 | tf_op jit(solution)/shard_map/pallas_call | solution.py:56
  174.5 1.7 collective-permute-start.29
  176.2 9.8 %collective-permute-done.29 = bf16[384,512]{1,0:T(8,128)(2,1)S(1)} collective-permute-done((bf16[384,512]{1,0:T(8,128)(2,1)S(1)}, bf16[384,512]{1,0:T(8,128)(2,1)S(1)}, u32[]{:S(2)}, u32[]{:S(2)}) %collective-permute-start.29) | collective-permute-done | bytes 393248 | tf_op jit(solution)/shard_map/ppermute | solution.py:303
  186.6 4.2 %shard_map.142 = (bf16[2,768,384]{2,1,0:T(8,128)(2,1)S(1)}, bf16[2,768,384]{2,1,0:T(8,128)(2,1)S(1)}) custom-call(s32[2]{0:T(128)S(1)} %pad_add_fusion.ids_ref.refs_0_, bf16[768,384]{1,0:T(8,128)(2,1)S(1)} %fusion.2.after_ref, bf16[768,512]{1,0:T(8,128)(2,1)S(1)} %fusion.before_ref, bf16[128,768]{1,0:T(8,128)(2,1)S(1)} %get-tuple-element.61.refs_2_.low_ref, ...), custom_call_target="tpu_custom_call" | custom-call | flops 905969664 | bytes 7274504 | tf_op jit(solution)/shard_map/pallas_call | solution.py:56
  192.2 6.2 %all-to-all-start.3 = ((bf16[8,96,512]{2,1,0:T(8,128)(2,1)}), bf16[8,96,512]{2,1,0:T(8,128)(2,1)}, u32[]{:S(2)}, u32[]{:S(2)}) async-start(bf16[8,96,512]{2,1,0:T(8,128)(2,1)} %add_convert_fusion), calls=%async_computation.3 | async-start | bytes 1572864 | tf_op jit(solution)/shard_map/all_to_all | solution.py:329
  198.4 1.7 collective-permute-start.28
  200.2 1.6 convert_add_fusion
  201.9 2.1 collective-permute-start.31
  203.9 9.9 %collective-permute-done.28 = bf16[768,384]{1,0:T(8,128)(2,1)S(1)} collective-permute-done((bf16[768,384]{1,0:T(8,128)(2,1)S(1)}, bf16[768,384]{1,0:T(8,128)(2,1)S(1)}, u32[]{:S(2)}, u32[]{:S(2)}) %collective-permute-start.28) | collective-permute-done | bytes 589856 | tf_op jit(solution)/shard_map/ppermute | solution.py:303
  214.9 4.4 %all-to-all-done.3 = bf16[8,96,512]{2,1,0:T(8,128)(2,1)} async-done(((bf16[8,96,512]{2,1,0:T(8,128)(2,1)}), bf16[8,96,512]{2,1,0:T(8,128)(2,1)}, u32[]{:S(2)}, u32[]{:S(2)}) %all-to-all-start.3) | async-done | bytes 786464 | tf_op jit(solution)/shard_map/all_to_all | solution.py:329
  219.3 3.7 %all-to-all-start.1 = ((bf16[8,96,384]{2,1,0:T(8,128)(2,1)}), bf16[8,96,384]{2,1,0:T(8,128)(2,1)S(1)}, u32[]{:S(2)}, u32[]{:S(2)}) async-start(bf16[8,96,384]{2,1,0:T(8,128)(2,1)} %bitcast.29), calls=%async_computation.1 | async-start | bytes 1179648 | tf_op jit(solution)/shard_map/all_to_all | solution.py:329
  224.5 1.8 collective-permute-start.32
  226.3 1.9 convert_reduce_fusion
  228.2 10.9 %all-to-all-done.1 = bf16[8,96,384]{2,1,0:T(8,128)(2,1)S(1)} async-done(((bf16[8,96,384]{2,1,0:T(8,128)(2,1)}), bf16[8,96,384]{2,1,0:T(8,128)(2,1)S(1)}, u32[]{:S(2)}, u32[]{:S(2)}) %all-to-all-start.1) | async-done | bytes 589856 | tf_op jit(solution)/shard_map/all_to_all | solution.py:329
  240.0 3.5 %all-to-all-start.2 = ((bf16[4,96,384]{2,1,0:T(8,128)(2,1)}), bf16[4,96,384]{2,1,0:T(8,128)(2,1)S(1)}, u32[]{:S(2)}, u32[]{:S(2)}) async-start(bf16[4,96,384]{2,1,0:T(8,128)(2,1)} %fusion.5), calls=%async_computation.2 | async-start | bytes 589824 | tf_op jit(solution)/shard_map/all_to_all | solution.py:347
  243.7 8.4 %all-to-all-done.2 = bf16[4,96,384]{2,1,0:T(8,128)(2,1)S(1)} async-done(((bf16[4,96,384]{2,1,0:T(8,128)(2,1)}), bf16[4,96,384]{2,1,0:T(8,128)(2,1)S(1)}, u32[]{:S(2)}, u32[]{:S(2)}) %all-to-all-start.2) | async-done | bytes 294944 | tf_op jit(solution)/shard_map/all_to_all | solution.py:347
  (131 shorter events, 29.1 us)
Async XLA Ops:
  0.6 11.4 %collective-permute-start.3 = (bf16[2048,768]{1,0:T(8,128)(2,1)}, bf16[2048,768]{1,0:T(8,128)(2,1)S(1)}, u32[]{:S(2)}, u32[]{:S(2)}) collective-permute-start(bf16[2048,768]{1,0:T(8,128)(2,1)} %refs_1_.1), channel_id=1, source_target_pairs={{0,8},{8,0},{16,24},{24,16},{1,9},{9,1},{17,25},{25,17},{2,10},{10... | collective-permute-start | bytes 9437192 | tf_op jit(solution)/shard_map/ppermute | solution.py:303
  3.5 16.7 %collective-permute-start.2 = (bf16[256,768]{1,0:T(8,128)(2,1)}, bf16[256,768]{1,0:T(8,128)(2,1)}, u32[]{:S(2)}, u32[]{:S(2)}) collective-permute-start(bf16[256,768]{1,0:T(8,128)(2,1)} %get-tuple-element.85), channel_id=1, source_target_pairs={{0,16},{8,24},{16,0},{24,8},{1,17},{9,25},{17,1},{25,9},{2,18},{10... | collective-permute-start | bytes 1179656 | tf_op jit(solution)/shard_map/ppermute | solution.py:303
  20.3 2.8 %collective-permute-start.4 = (bf16[256,768]{1,0:T(8,128)(2,1)}, bf16[256,768]{1,0:T(8,128)(2,1)S(1)}, u32[]{:S(2)}, u32[]{:S(2)}) collective-permute-start(bf16[256,768]{1,0:T(8,128)(2,1)} %collective-permute-done.2.refs_2_), channel_id=1, source_target_pairs={{0,8},{8,0},{16,24},{24,16},{1,9},{9,1},{17,25},{25,17},{2,10},{10... | collective-permute-start | bytes 1179656 | tf_op jit(solution)/shard_map/ppermute | solution.py:303
  20.4 11.6 %collective-permute-start.1 = (bf16[256,768]{1,0:T(8,128)(2,1)}, bf16[256,768]{1,0:T(8,128)(2,1)S(1)}, u32[]{:S(2)}, u32[]{:S(2)}) collective-permute-start(bf16[256,768]{1,0:T(8,128)(2,1)} %get-tuple-element.86), channel_id=1, source_target_pairs={{0,16},{8,24},{16,0},{24,8},{1,17},{9,25},{17,1},{25,9},{2,18},{10... | collective-permute-start | bytes 1179656 | tf_op jit(solution)/shard_map/ppermute | solution.py:303
  20.7 11.3 %collective-permute-start.8 = (bf16[256,768]{1,0:T(8,128)(2,1)}, bf16[256,768]{1,0:T(8,128)(2,1)S(1)}, u32[]{:S(2)}, u32[]{:S(2)}) collective-permute-start(bf16[256,768]{1,0:T(8,128)(2,1)} %collective-permute-done.2.refs_2_), channel_id=1, source_target_pairs={{0,1},{1,0},{2,3},{3,2},{4,5},{5,4},{6,7},{7,6},{8,9},{9,8},{10,11... | collective-permute-start | bytes 1179656 | tf_op jit(solution)/shard_map/ppermute | solution.py:303
  32.0 4.4 %collective-permute-start.9 = (bf16[256,768]{1,0:T(8,128)(2,1)S(1)}, bf16[256,768]{1,0:T(8,128)(2,1)S(1)}, u32[]{:S(2)}, u32[]{:S(2)}) collective-permute-start(bf16[256,768]{1,0:T(8,128)(2,1)S(1)} %collective-permute-done.8.refs_4_), channel_id=1, source_target_pairs={{0,8},{8,0},{16,24},{24,16},{1,9},{9,1},{17,25},{25,17},{2,10},{10... | collective-permute-start | bytes 1179656 | tf_op jit(solution)/shard_map/ppermute | solution.py:303
  32.1 4.4 %collective-permute-start.10 = (bf16[256,768]{1,0:T(8,128)(2,1)S(1)}, bf16[256,768]{1,0:T(8,128)(2,1)S(1)}, u32[]{:S(2)}, u32[]{:S(2)}) collective-permute-start(bf16[256,768]{1,0:T(8,128)(2,1)S(1)} %collective-permute-done.1.refs_6_), channel_id=1, source_target_pairs={{0,8},{8,0},{16,24},{24,16},{1,9},{9,1},{17,25},{25,17},{2,10},{10... | collective-permute-start | bytes 1179656 | tf_op jit(solution)/shard_map/ppermute | solution.py:303
  32.6 11.1 %collective-permute-start.7 = (bf16[256,768]{1,0:T(8,128)(2,1)S(1)}, bf16[256,768]{1,0:T(8,128)(2,1)S(1)}, u32[]{:S(2)}, u32[]{:S(2)}) collective-permute-start(bf16[256,768]{1,0:T(8,128)(2,1)S(1)} %copy-done.24), channel_id=1, source_target_pairs={{0,16},{8,24},{16,0},{24,8},{1,17},{9,25},{17,1},{25,9},{2,18},{10... | collective-permute-start | bytes 1179656 | tf_op jit(solution)/shard_map/ppermute | solution.py:303
  34.3 10.7 %collective-permute-start.5 = (bf16[256,768]{1,0:T(8,128)(2,1)S(1)}, bf16[256,768]{1,0:T(8,128)(2,1)S(1)}, u32[]{:S(2)}, u32[]{:S(2)}) collective-permute-start(bf16[256,768]{1,0:T(8,128)(2,1)S(1)} %collective-permute-done.1.refs_6_), channel_id=1, source_target_pairs={{0,1},{1,0},{2,3},{3,2},{4,5},{5,4},{6,7},{7,6},{8,9},{9,8},{10,11... | collective-permute-start | bytes 1179656 | tf_op jit(solution)/shard_map/ppermute | solution.py:303
  43.7 4.3 %collective-permute-start.11 = (bf16[256,768]{1,0:T(8,128)(2,1)S(1)}, bf16[256,768]{1,0:T(8,128)(2,1)S(1)}, u32[]{:S(2)}, u32[]{:S(2)}) collective-permute-start(bf16[256,768]{1,0:T(8,128)(2,1)S(1)} %collective-permute-done.7.refs_6_), channel_id=1, source_target_pairs={{0,8},{8,0},{16,24},{24,16},{1,9},{9,1},{17,25},{25,17},{2,10},{10... | collective-permute-start | bytes 1179656 | tf_op jit(solution)/shard_map/ppermute | solution.py:303
  45.0 3.0 %collective-permute-start.6 = (bf16[256,768]{1,0:T(8,128)(2,1)S(1)}, bf16[256,768]{1,0:T(8,128)(2,1)S(1)}, u32[]{:S(2)}, u32[]{:S(2)}) collective-permute-start(bf16[256,768]{1,0:T(8,128)(2,1)S(1)} %collective-permute-done.5.refs_4_), channel_id=1, source_target_pairs={{0,8},{8,0},{16,24},{24,16},{1,9},{9,1},{17,25},{25,17},{2,10},{10... | collective-permute-start | bytes 1179656 | tf_op jit(solution)/shard_map/ppermute | solution.py:303
  45.0 11.5 %collective-permute-start = (bf16[256,768]{1,0:T(8,128)(2,1)S(1)}, bf16[256,768]{1,0:T(8,128)(2,1)S(1)}, u32[]{:S(2)}, u32[]{:S(2)}) collective-permute-start(bf16[256,768]{1,0:T(8,128)(2,1)S(1)} %get-tuple-element.87), channel_id=1, source_target_pairs={{0,16},{8,24},{16,0},{24,8},{1,17},{9,25},{17,1},{25,9},{2,18},{10... | collective-permute-start | bytes 1179656 | tf_op jit(solution)/shard_map/ppermute | solution.py:303
  46.5 11.6 %collective-permute-start.14 = (bf16[256,768]{1,0:T(8,128)(2,1)S(1)}, bf16[256,768]{1,0:T(8,128)(2,1)S(1)}, u32[]{:S(2)}, u32[]{:S(2)}) collective-permute-start(bf16[256,768]{1,0:T(8,128)(2,1)S(1)} %collective-permute-done.7.refs_6_), channel_id=1, source_target_pairs={{0,1},{1,0},{2,3},{3,2},{4,5},{5,4},{6,7},{7,6},{8,9},{9,8},{10,11... | collective-permute-start | bytes 1179656 | tf_op jit(solution)/shard_map/ppermute | solution.py:303
  56.5 12.0 %copy-start.13 = (bf16[256,768]{1,0:T(8,128)(2,1)}, bf16[256,768]{1,0:T(8,128)(2,1)S(1)}, u32[]{:S(2)}) copy-start(bf16[256,768]{1,0:T(8,128)(2,1)S(1)} %collective-permute-done.refs_6_) | copy-start | bytes 1179652
  56.5 10.7 %collective-permute-start.12 = (bf16[256,768]{1,0:T(8,128)(2,1)S(1)}, bf16[256,768]{1,0:T(8,128)(2,1)S(1)}, u32[]{:S(2)}, u32[]{:S(2)}) collective-permute-start(bf16[256,768]{1,0:T(8,128)(2,1)S(1)} %collective-permute-done.refs_6_), channel_id=1, source_target_pairs={{0,1},{1,0},{2,3},{3,2},{4,5},{5,4},{6,7},{7,6},{8,9},{9,8},{10,11... | collective-permute-start | bytes 1179656 | tf_op jit(solution)/shard_map/ppermute | solution.py:303
  58.1 10.5 %copy-start.16 = (bf16[256,768]{1,0:T(8,128)(2,1)}, bf16[256,768]{1,0:T(8,128)(2,1)S(1)}, u32[]{:S(2)}) copy-start(bf16[256,768]{1,0:T(8,128)(2,1)S(1)} %collective-permute-done.14.refs_4_) | copy-start | bytes 1179652
  58.1 10.5 %collective-permute-start.15 = (bf16[256,768]{1,0:T(8,128)(2,1)S(1)}, bf16[256,768]{1,0:T(8,128)(2,1)S(1)}, u32[]{:S(2)}, u32[]{:S(2)}) collective-permute-start(bf16[256,768]{1,0:T(8,128)(2,1)S(1)} %collective-permute-done.14.refs_4_), channel_id=1, source_target_pairs={{0,8},{8,0},{16,24},{24,16},{1,9},{9,1},{17,25},{25,17},{2,10},{10... | collective-permute-start | bytes 1179656 | tf_op jit(solution)/shard_map/ppermute | solution.py:303
  58.1 10.5 %collective-permute-start.16 = (bf16[256,768]{1,0:T(8,128)(2,1)S(1)}, bf16[256,768]{1,0:T(8,128)(2,1)S(1)}, u32[]{:S(2)}, u32[]{:S(2)}) collective-permute-start(bf16[256,768]{1,0:T(8,128)(2,1)S(1)} %collective-permute-done.refs_6_), channel_id=1, source_target_pairs={{0,8},{8,0},{16,24},{24,16},{1,9},{9,1},{17,25},{25,17},{2,10},{10... | collective-permute-start | bytes 1179656 | tf_op jit(solution)/shard_map/ppermute | solution.py:303
  67.3 7.9 %collective-permute-start.13 = (bf16[256,768]{1,0:T(8,128)(2,1)S(1)}, bf16[256,768]{1,0:T(8,128)(2,1)}, u32[]{:S(2)}, u32[]{:S(2)}) collective-permute-start(bf16[256,768]{1,0:T(8,128)(2,1)S(1)} %collective-permute-done.12.refs_2_), channel_id=1, source_target_pairs={{0,8},{8,0},{16,24},{24,16},{1,9},{9,1},{17,25},{25,17},{2,10},{10... | collective-permute-start | bytes 1179656 | tf_op jit(solution)/shard_map/ppermute | solution.py:303
  75.2 31.2 %copy-start = (bf16[2,3,768,384]{3,2,1,0:T(8,128)(2,1)S(1)}, bf16[2,3,768,384]{3,2,1,0:T(8,128)(2,1)}, u32[]{:S(2)}) copy-start(bf16[2,3,768,384]{3,2,1,0:T(8,128)(2,1)} %refs_8_.3) | copy-start | bytes 10616836
  79.5 26.8 %all-to-all-start = ((bf16[8,64,768]{2,1,0:T(8,128)(2,1)}), bf16[8,64,768]{2,1,0:T(8,128)(2,1)}, u32[]{:S(2)}, u32[]{:S(2)}) async-start(bf16[8,64,768]{2,1,0:T(8,128)(2,1)} %bitcast.102), calls=%async_computation | async-start | bytes 1572864 | tf_op jit(solution)/shard_map/all_to_all | solution.py:393
  108.5 11.2 %collective-permute-start.17 = (bf16[256,384]{1,0:T(8,128)(2,1)S(1)}, bf16[256,384]{1,0:T(8,128)(2,1)S(1)}, u32[]{:S(2)}, u32[]{:S(2)}) collective-permute-start(bf16[256,384]{1,0:T(8,128)(2,1)S(1)} %get-tuple-element.51), channel_id=1, source_target_pairs={{0,1},{1,2},{2,3},{3,4},{4,5},{5,6},{6,7},{8,9},{9,10},{10,11},{11... | collective-permute-start | bytes 589832 | tf_op jit(solution)/shard_map/ppermute | solution.py:310
  111.9 7.9 %collective-permute-start.18 = (bf16[256,384]{1,0:T(8,128)(2,1)S(1)}, bf16[256,384]{1,0:T(8,128)(2,1)S(1)}, u32[]{:S(2)}, u32[]{:S(2)}) collective-permute-start(bf16[256,384]{1,0:T(8,128)(2,1)S(1)} %get-tuple-element.52), channel_id=1, source_target_pairs={{1,0},{2,1},{3,2},{4,3},{5,4},{6,5},{7,6},{9,8},{10,9},{11,10},{12... | collective-permute-start | bytes 589832 | tf_op jit(solution)/shard_map/ppermute | solution.py:311
  119.7 26.3 %collective-permute-start.19 = (bf16[256,768]{1,0:T(8,128)(2,1)S(1)}, bf16[256,768]{1,0:T(8,128)(2,1)S(1)}, u32[]{:S(2)}, u32[]{:S(2)}) collective-permute-start(bf16[256,768]{1,0:T(8,128)(2,1)S(1)} %get-tuple-element.55.high_ref.refs_12_), channel_id=1, source_target_pairs={{0,1},{1,2},{2,3},{3,4},{4,5},{5,6},{6,7},{8,9},{9,10},{10,11},{11... | collective-permute-start | bytes 1179656 | tf_op jit(solution)/shard_map/ppermute | solution.py:310
  124.1 21.9 %collective-permute-start.20 = (bf16[256,768]{1,0:T(8,128)(2,1)S(1)}, bf16[256,768]{1,0:T(8,128)(2,1)S(1)}, u32[]{:S(2)}, u32[]{:S(2)}) collective-permute-start(bf16[256,768]{1,0:T(8,128)(2,1)S(1)} %get-tuple-element.56.low_ref.refs_11_), channel_id=1, source_target_pairs={{1,0},{2,1},{3,2},{4,3},{5,4},{6,5},{7,6},{9,8},{10,9},{11,10},{12... | collective-permute-start | bytes 1179656 | tf_op jit(solution)/shard_map/ppermute | solution.py:311
  126.8 15.5 %copy-start.4 = (bf16[768,2048]{1,0:T(8,128)(2,1)S(1)}, bf16[768,2048]{1,0:T(8,128)(2,1)}, u32[]{:S(2)}) copy-start(bf16[768,2048]{1,0:T(8,128)(2,1)} %refs_8_.2) | copy-start | bytes 9437188
  126.8 15.5 %copy-start.7 = (s32[1,128,2048]{2,1,0:T(8,128)S(1)}, s32[1,128,2048]{2,1,0:T(8,128)}, u32[]{:S(2)}) copy-start(s32[1,128,2048]{2,1,0:T(8,128)} %param.13) | copy-start | bytes 3145732
  127.6 14.6 %collective-permute-start.21 = (bf16[128,384]{1,0:T(8,128)(2,1)S(1)}, bf16[128,384]{1,0:T(8,128)(2,1)S(1)}, u32[]{:S(2)}, u32[]{:S(2)}) collective-permute-start(bf16[128,384]{1,0:T(8,128)(2,1)S(1)} %get-tuple-element.60), channel_id=1, source_target_pairs={{0,1},{1,2},{2,3},{3,4},{4,5},{5,6},{6,7},{8,9},{9,10},{10,11},{11... | collective-permute-start | bytes 294920 | tf_op jit(solution)/shard_map/ppermute | solution.py:310
  132.3 9.9 %collective-permute-start.22 = (bf16[128,384]{1,0:T(8,128)(2,1)S(1)}, bf16[128,384]{1,0:T(8,128)(2,1)S(1)}, u32[]{:S(2)}, u32[]{:S(2)}) collective-permute-start(bf16[128,384]{1,0:T(8,128)(2,1)S(1)} %get-tuple-element.63), channel_id=1, source_target_pairs={{1,0},{2,1},{3,2},{4,3},{5,4},{6,5},{7,6},{9,8},{10,9},{11,10},{12... | collective-permute-start | bytes 294920 | tf_op jit(solution)/shard_map/ppermute | solution.py:311
  147.6 3.5 %collective-permute-start.23 = (bf16[2,768,512]{2,1,0:T(8,128)(2,1)S(1)}, bf16[2,768,512]{2,1,0:T(8,128)(2,1)S(1)}, u32[]{:S(2)}, u32[]{:S(2)}) collective-permute-start(bf16[2,768,512]{2,1,0:T(8,128)(2,1)S(1)} %get-tuple-element.68), channel_id=1, source_target_pairs={{0,8},{8,0},{16,24},{24,16},{1,9},{9,1},{17,25},{25,17},{2,10},{10... | collective-permute-start | bytes 4718600 | tf_op jit(solution)/shard_map/ppermute | solution.py:303
  151.0 14.9 %copy-start.3 = (bf16[2,384,768]{2,1,0:T(8,128)(2,1)S(1)}, bf16[2,384,768]{2,1,0:T(8,128)(2,1)}, u32[]{:S(2)}) copy-start(bf16[2,384,768]{2,1,0:T(8,128)(2,1)} %constant.173.clone.refs_16_.spread_ref) | copy-start | bytes 3538948
  151.5 14.5 %copy-start.2 = (bf16[2,768,384]{2,1,0:T(8,128)(2,1)S(1)}, bf16[2,768,384]{2,1,0:T(8,128)(2,1)}, u32[]{:S(2)}) copy-start(bf16[2,768,384]{2,1,0:T(8,128)(2,1)} %constant.174.clone.refs_17_.split_ref) | copy-start | bytes 3538948
  151.6 22.9 %collective-permute-start.26 = (bf16[384,512]{1,0:T(8,128)(2,1)S(1)}, bf16[384,512]{1,0:T(8,128)(2,1)S(1)}, u32[]{:S(2)}, u32[]{:S(2)}) collective-permute-start(bf16[384,512]{1,0:T(8,128)(2,1)S(1)} %get-tuple-element.89), channel_id=1, source_target_pairs={{0,16},{8,24},{16,0},{24,8},{1,17},{9,25},{17,1},{25,9},{2,18},{10... | collective-permute-start | bytes 1179656 | tf_op jit(solution)/shard_map/ppermute | solution.py:303
  151.9 6.6 %collective-permute-start.24 = (bf16[128,384]{1,0:T(8,128)(2,1)S(1)}, bf16[128,384]{1,0:T(8,128)(2,1)S(1)}, u32[]{:S(2)}, u32[]{:S(2)}) collective-permute-start(bf16[128,384]{1,0:T(8,128)(2,1)S(1)} %get-tuple-element.69.refs_4_.ghigh_ref), channel_id=1, source_target_pairs={{0,1},{1,2},{2,3},{3,4},{4,5},{5,6},{6,7},{8,9},{9,10},{10,11},{11... | collective-permute-start | bytes 294920 | tf_op jit(solution)/shard_map/ppermute | solution.py:310
  156.3 9.7 %collective-permute-start.25 = (bf16[128,384]{1,0:T(8,128)(2,1)S(1)}, bf16[128,384]{1,0:T(8,128)(2,1)S(1)}, u32[]{:S(2)}, u32[]{:S(2)}) collective-permute-start(bf16[128,384]{1,0:T(8,128)(2,1)S(1)} %get-tuple-element.70.refs_3_.glow_ref), channel_id=1, source_target_pairs={{1,0},{2,1},{3,2},{4,3},{5,4},{6,5},{7,6},{9,8},{10,9},{11,10},{12... | collective-permute-start | bytes 294920 | tf_op jit(solution)/shard_map/ppermute | solution.py:311
  174.5 11.9 %copy-start.5 = (bf16[2,768,384]{2,1,0:T(8,128)(2,1)}, bf16[2,768,384]{2,1,0:T(8,128)(2,1)S(1)}, u32[]{:S(2)}) copy-start(bf16[2,768,384]{2,1,0:T(8,128)(2,1)S(1)} %get-tuple-element.74) | copy-start | bytes 3538948
  174.5 11.9 %collective-permute-start.27 = (bf16[2,768,384]{2,1,0:T(8,128)(2,1)S(1)}, bf16[2,768,384]{2,1,0:T(8,128)(2,1)S(1)}, u32[]{:S(2)}, u32[]{:S(2)}) collective-permute-start(bf16[2,768,384]{2,1,0:T(8,128)(2,1)S(1)} %get-tuple-element.76), channel_id=1, source_target_pairs={{0,8},{8,0},{16,24},{24,16},{1,9},{9,1},{17,25},{25,17},{2,10},{10... | collective-permute-start | bytes 3538952 | tf_op jit(solution)/shard_map/ppermute | solution.py:303
  174.5 11.5 %collective-permute-start.29 = (bf16[384,512]{1,0:T(8,128)(2,1)S(1)}, bf16[384,512]{1,0:T(8,128)(2,1)S(1)}, u32[]{:S(2)}, u32[]{:S(2)}) collective-permute-start(bf16[384,512]{1,0:T(8,128)(2,1)S(1)} %get-tuple-element.88), channel_id=1, source_target_pairs={{0,16},{8,24},{16,0},{24,8},{1,17},{9,25},{17,1},{25,9},{2,18},{10... | collective-permute-start | bytes 1179656 | tf_op jit(solution)/shard_map/ppermute | solution.py:303
  190.8 9.4 %collective-permute-start.30 = (bf16[2,768,384]{2,1,0:T(8,128)(2,1)S(1)}, bf16[2,768,384]{2,1,0:T(8,128)(2,1)}, u32[]{:S(2)}, u32[]{:S(2)}) collective-permute-start(bf16[2,768,384]{2,1,0:T(8,128)(2,1)S(1)} %get-tuple-element.80), channel_id=1, source_target_pairs={{0,8},{8,0},{16,24},{24,16},{1,9},{9,1},{17,25},{25,17},{2,10},{10... | collective-permute-start | bytes 3538952 | tf_op jit(solution)/shard_map/ppermute | solution.py:303
  192.2 27.1 %all-to-all-start.3 = ((bf16[8,96,512]{2,1,0:T(8,128)(2,1)}), bf16[8,96,512]{2,1,0:T(8,128)(2,1)}, u32[]{:S(2)}, u32[]{:S(2)}) async-start(bf16[8,96,512]{2,1,0:T(8,128)(2,1)} %add_convert_fusion), calls=%async_computation.3 | async-start | bytes 1572864 | tf_op jit(solution)/shard_map/all_to_all | solution.py:329
  198.4 15.4 %collective-permute-start.28 = (bf16[768,384]{1,0:T(8,128)(2,1)S(1)}, bf16[768,384]{1,0:T(8,128)(2,1)S(1)}, u32[]{:S(2)}, u32[]{:S(2)}) collective-permute-start(bf16[768,384]{1,0:T(8,128)(2,1)S(1)} %fusion.2.after_ref), channel_id=1, source_target_pairs={{0,16},{8,24},{16,0},{24,8},{1,17},{9,25},{17,1},{25,9},{2,18},{10... | collective-permute-start | bytes 1769480 | tf_op jit(solution)/shard_map/ppermute | solution.py:303
  200.2 13.7 %copy-start.11 = (bf16[2,768,384]{2,1,0:T(8,128)(2,1)S(1)}, bf16[2,768,384]{2,1,0:T(8,128)(2,1)}, u32[]{:S(2)}) copy-start(bf16[2,768,384]{2,1,0:T(8,128)(2,1)} %copy-done.10) | copy-start | bytes 3538948
  201.8 12.1 %copy-start.8 = (f32[2,768,384]{2,1,0:T(8,128)}, f32[2,768,384]{2,1,0:T(8,128)S(1)}, u32[]{:S(2)}) copy-start(f32[2,768,384]{2,1,0:T(8,128)S(1)} %convert_add_fusion) | copy-start | bytes 7077892
  201.8 12.1 %copy-start.6 = (bf16[2,768,384]{2,1,0:T(8,128)(2,1)S(1)}, bf16[2,768,384]{2,1,0:T(8,128)(2,1)}, u32[]{:S(2)}) copy-start(bf16[2,768,384]{2,1,0:T(8,128)(2,1)} %copy-done.5) | copy-start | bytes 3538948
  201.9 21.2 %collective-permute-start.31 = (bf16[2,4,96,384]{3,2,1,0:T(8,128)(2,1)S(1)}, bf16[2,4,96,384]{3,2,1,0:T(8,128)(2,1)S(1)}, u32[]{:S(2)}, u32[]{:S(2)}) collective-permute-start(bf16[2,4,96,384]{3,2,1,0:T(8,128)(2,1)S(1)} %fusion.3), channel_id=1, source_target_pairs={{0,1},{1,0},{2,3},{3,2},{4,5},{5,4},{6,7},{7,6},{8,9},{9,8},{10,11... | collective-permute-start | bytes 1769480 | tf_op jit(solution)/shard_map/ppermute | solution.py:303
  219.3 19.8 %all-to-all-start.1 = ((bf16[8,96,384]{2,1,0:T(8,128)(2,1)}), bf16[8,96,384]{2,1,0:T(8,128)(2,1)S(1)}, u32[]{:S(2)}, u32[]{:S(2)}) async-start(bf16[8,96,384]{2,1,0:T(8,128)(2,1)} %bitcast.29), calls=%async_computation.1 | async-start | bytes 1179648 | tf_op jit(solution)/shard_map/all_to_all | solution.py:329
  224.5 14.7 %collective-permute-start.32 = (bf16[4,96,384]{2,1,0:T(8,128)(2,1)S(1)}, bf16[4,96,384]{2,1,0:T(8,128)(2,1)S(1)}, u32[]{:S(2)}, u32[]{:S(2)}) collective-permute-start(bf16[4,96,384]{2,1,0:T(8,128)(2,1)S(1)} %fusion.6), channel_id=1, source_target_pairs={{0,16},{8,24},{16,0},{24,8},{1,17},{9,25},{17,1},{25,9},{2,18},{10... | collective-permute-start | bytes 884744 | tf_op jit(solution)/shard_map/ppermute | solution.py:303
  240.0 12.0 %all-to-all-start.2 = ((bf16[4,96,384]{2,1,0:T(8,128)(2,1)}), bf16[4,96,384]{2,1,0:T(8,128)(2,1)S(1)}, u32[]{:S(2)}, u32[]{:S(2)}) async-start(bf16[4,96,384]{2,1,0:T(8,128)(2,1)} %fusion.5), calls=%async_computation.2 | async-start | bytes 589824 | tf_op jit(solution)/shard_map/all_to_all | solution.py:347
  (17 other events, 52.8 us)

commit v3 on v2

--- a/solution.py
+++ b/solution.py
@@ -15,6 +15,7 @@
 F32 = jnp.float32
 PIECES = 4
 
+CHEAP = pl.CostEstimate(flops=1024, bytes_accessed=1024, transcendentals=0)
 VMEM = pl.BlockSpec(memory_space=pltpu.VMEM)
 SMEM = pl.BlockSpec(memory_space=pltpu.SMEM)
 ANY = pl.BlockSpec(memory_space=pl.ANY)
@@ -22,11 +23,6 @@
 
 def params(mib):
     return pltpu.CompilerParams(vmem_limit_bytes=mib * 1024 * 1024)
-
-
-def cost(flops, arrays):
-    total = sum(int(np.prod(a.shape)) * a.dtype.itemsize for a in arrays)
-    return pl.CostEstimate(flops=int(flops), bytes_accessed=int(total), transcendentals=0)
 
 
 def gelu(v):
@@ -51,7 +47,7 @@
     return lax.dot_general(a, b, (((0,), (0,)), ((), ())), preferred_element_type=F32)
 
 
-def call(body, inputs, outs, flops, mib, smem=0, scratch=(), after=0):
+def call(body, inputs, outs, mib, smem=0, scratch=(), after=0):
     outs = [jax.ShapeDtypeStruct(s, d) for s, d in outs]
     return pl.pallas_call(
         body,
@@ -60,7 +56,7 @@
         out_specs=[VMEM] * len(outs),
         scratch_shapes=list(scratch),
         compiler_params=params(mib),
-        cost_estimate=cost(flops, list(inputs) + outs),
+        cost_estimate=CHEAP,
     )(*inputs)
 
 
@@ -120,8 +116,41 @@
             num_scalar_prefetch=1, grid=(steps,), in_specs=in_specs, out_specs=whole
         ),
         compiler_params=params(56),
-        cost_estimate=cost(2 * row_count * depth * channels * count, list(weights) * 2 + [out]),
+        cost_estimate=CHEAP,
     )(jnp.stack(starts).astype(jnp.int32) // block, *inputs)
+
+
+def absorb(total, rows, weights, starts, final):
+    count = len(weights)
+    row_count = rows.shape[0]
+    depth, channels = weights[0].shape
+
+    def body(starts_ref, rows_ref, old_ref, *refs):
+        weight_refs, (out_ref, held_ref, sems) = refs[:count], refs[count:]
+        copies = []
+        for k in range(count):
+            start = pl.multiple_of(starts_ref[k], depth)
+            copies.append(pltpu.make_async_copy(rows_ref.at[:, pl.ds(start, depth)], held_ref.at[k], sems.at[k]))
+            copies[-1].start()
+        for copy in copies:
+            copy.wait()
+        half = row_count // 2
+        for h in range(2):
+            part = slice(h * half, (h + 1) * half)
+            sums = old_ref[part]
+            for k in range(count):
+                sums = sums + nn(held_ref[k, part], weight_refs[k][...])
+            out_ref[part] = sums.astype(out_ref.dtype)
+
+    return pl.pallas_call(
+        body,
+        out_shape=jax.ShapeDtypeStruct((row_count, channels), BF if final else F32),
+        in_specs=[SMEM, ANY] + [VMEM] * (count + 1),
+        out_specs=VMEM,
+        scratch_shapes=[pltpu.VMEM((count, row_count, depth), BF), pltpu.SemaphoreType.DMA((count,))],
+        compiler_params=params(24),
+        cost_estimate=CHEAP,
+    )(jnp.stack(starts).astype(jnp.int32), rows, total, *weights)
 
 
 def place_body(target_ref, received_ref, kernels_ref, hidden_ref, low_ref, high_ref, down_ref, up_ref):
@@ -211,7 +240,7 @@
             out[s * slab : (s + 1) * slab] = (piece * slopes[h][s * slab : (s + 1) * slab]).astype(BF)
 
 
-def readout_body(ids_ref, after_ref, before_ref, second_ref, logit_ref, keep_ref, send_ref):
+def readout_body(ids_ref, second_ref, logit_ref, keep_ref, send_ref):
     width = keep_ref.shape[2]
     second = second_ref[...]
     for k in range(4):
@@ -244,33 +273,32 @@
     return mixed.astype(BF)
 
 
-def coarse_grad_body(
-    ids_ref, after_ref, before_ref, low_ref, high_ref, gprev_ref, glow_ref, ghigh_ref, gnext_ref, gated_ref, upper_ref,
+def weight_body(
+    slab, ids_ref, after_ref, low_ref, high_ref, gprev_ref, glow_ref, ghigh_ref, gnext_ref, gated_ref, up_ref,
     spread_ref, split_ref, keep_ref, send_ref,
 ):
-    slab = low_ref.shape[0] // 2
-    upper = upper_ref[...]
-    rows = jnp.concatenate([upper[:slab], upper[:slab], upper[slab:], upper[slab:]], axis=0)
+    up = up_ref[...]
+    rows = []
+    for s in range(up.shape[0] // slab):
+        rows += [up[s * slab : (s + 1) * slab]] * 2
     grads = (gprev_ref, glow_ref, ghigh_ref, gnext_ref)
     pieces = []
     for t in range(3):
         pieces.append((tn(low_ref[...], grads[2 - t][...]) + tn(high_ref[...], grads[3 - t][...])).astype(BF))
-    pieces.append(mixer_piece(gated_ref[...], rows, spread_ref, split_ref))
+    pieces.append(mixer_piece(gated_ref[...], jnp.concatenate(rows, axis=0), spread_ref, split_ref))
     store_blocks(ids_ref, pieces, keep_ref, send_ref)
 
 
-def fine_grad_body(
+def fine_back_body(
     scale,
-    ids_ref, after_ref, gprev_ref, glow_ref, ghigh_ref, gnext_ref, upper_ref, first_ref, kernels_ref, mixers_ref,
-    prev_ref, low_ref, high_ref, next_ref, inner_ref, gated_ref, spread_ref, split_ref,
-    trunk_ref, keep_ref, send_ref, lanes_ref,
+    after_ref, gprev_ref, glow_ref, ghigh_ref, gnext_ref, upper_ref, first_ref, kernels_ref, mixers_ref, inner_ref,
+    trunk_ref, lower_ref, ilow_ref, ihigh_ref, lanes_ref,
 ):
     half = glow_ref.shape[0]
     slab = half // 2
     grads = (gprev_ref, glow_ref, ghigh_ref, gnext_ref)
     upper = upper_ref[...].astype(F32)
-    inner_grads, rows = [], []
-    for h in range(2):
+    for h, out in enumerate((ilow_ref, ihigh_ref)):
         back = (
             nt(grads[h + 2][...], kernels_ref[1, 0])
             + nt(grads[h + 1][...], kernels_ref[1, 1])
@@ -285,17 +313,11 @@
                 lanes_ref[t, pl.ds(s, slab, stride=2), :] = total[s * slab : (s + 1) * slab, cols] * scale
             trunk_ref[h * half : (h + 1) * half, cols] = lanes_ref[t]
         lower = (total * 0.5).astype(BF)
+        lower_ref[h * half : (h + 1) * half] = lower
         inner = nt(lower, mixers_ref[0])
         spread_inner = jnp.concatenate([inner[:slab], inner[:slab], inner[slab:], inner[slab:]], axis=0)
         slope = gelu_slope(inner_ref[2 * h * half : 2 * (h + 1) * half])
-        inner_grads.append((spread_inner * slope).astype(BF))
-        rows += [lower[:slab], lower[:slab], lower[slab:], lower[slab:]]
-    taps = (prev_ref, low_ref, high_ref, next_ref)
-    pieces = []
-    for t in range(3):
-        pieces.append((tn(taps[t][...], inner_grads[0]) + tn(taps[t + 1][...], inner_grads[1])).astype(BF))
-    pieces.append(mixer_piece(gated_ref[...], jnp.concatenate(rows, axis=0), spread_ref, split_ref))
-    store_blocks(ids_ref, pieces, keep_ref, send_ref)
+        out[...] = (spread_inner * slope).astype(BF)
 
 
 def swap(value, axis, bit):
@@ -319,10 +341,6 @@
     return here, away
 
 
-def x_sum(here, away):
-    return (here + swap(away, "dp", 2).astype(F32)).astype(BF)
-
-
 def seq_sum(total):
     groups = lax.axis_size("seq")
     rows, columns = total.shape
@@ -332,20 +350,31 @@
     return parts.astype(F32).sum(axis=0)
 
 
-def side_first_sum(keep, send):
+def side_halves(total):
     groups = lax.axis_size("seq")
     side = lax.axis_index("seq") % 2
-    came = swap(send, "dp", 1)
-    blocks, rows, columns = keep.shape
-    total = keep.astype(F32) + came.astype(F32)
+    blocks, rows, columns = total.shape
     total = total.reshape(blocks, groups // 2, 2, rows // groups, columns)
-    other = lax.dynamic_index_in_dim(total, 1 - side, axis=2, keepdims=False).astype(BF)
-    own = lax.dynamic_index_in_dim(total, side, axis=2, keepdims=False)
-    total = own + swap(other, "seq", 1).astype(F32)
-    total = (total[0] + swap(total[1].astype(BF), "dp", 2).astype(F32)).astype(BF)
+    return (
+        lax.dynamic_index_in_dim(total, 1 - side, axis=2, keepdims=False).astype(BF),
+        lax.dynamic_index_in_dim(total, side, axis=2, keepdims=False),
+    )
+
+
+def crossed_sums(here, away, keep, send):
+    groups = lax.axis_size("seq")
+    other, own = side_halves(keep.astype(F32) + swap(send, "dp", 1).astype(F32))
+    x_came, side_came = swap(away, "dp", 2), swap(other, "seq", 1)
+    left_other, left_own = side_halves((here + x_came.astype(F32))[None])
+    right = own + side_came.astype(F32)
+    side_came, x_came = swap(left_other[0], "seq", 1), swap(right[1].astype(BF), "dp", 2)
+    left = left_own[0] + side_came.astype(F32)
+    right = right[0] + x_came.astype(F32)
+    both = jnp.concatenate([left, right], axis=2).astype(BF)
     lines = [list(range(start, groups, 2)) for start in range(2)]
-    parts = lax.all_to_all(total, "seq", split_axis=0, concat_axis=0, axis_index_groups=lines, tiled=True)
-    return parts.astype(F32).sum(axis=0)
+    parts = lax.all_to_all(both, "seq", split_axis=0, concat_axis=0, axis_index_groups=lines, tiled=True)
+    total = parts.astype(F32).sum(axis=0)
+    return total[:, : left.shape[2]], total[:, left.shape[2] :]
 
 
 def shards(embeddings, layout, lengths, targets, projection, kernels, mixers, readout):
@@ -368,26 +397,27 @@
     mine = lax.dynamic_slice_in_dim(projection, side * share, share, axis=0)
     far = [swap(lax.slice_in_dim(mine, i * piece, (i + 1) * piece), "dp", 2) for i in range(PIECES)]
     near, away = (me ^ 2) * depth, (me ^ 3) * depth
-    total = project(None, rows, [projection], [me * depth], False)
-    total = project(total, rows, [from_core], [(me ^ 1) * depth], False)
-    weights, starts = [], []
+    total = project(None, rows, [projection, from_core], [me * depth, (me ^ 1) * depth], False)
+    far_weights, far_starts, side_weights, side_starts = [], [], [], []
     for i in range(PIECES):
-        if weights:
-            total = project(total, rows, weights, starts, False)
-        held, total = lax.optimization_barrier((far[i], total))
-        if i:
-            weights, starts = [side_piece, swap(side_piece, "dp", 1)], [near + side_at, away + side_at]
-        else:
-            weights, starts = [], []
-        at = side * share + i * piece
-        weights += [held, swap(held, "dp", 1)]
-        starts += [near + at, away + at]
-        side_piece = swap(held, "seq", 1)
-        side_at = (1 - side) * share + i * piece
-    total = project(total, rows, weights, starts, False)
-    total = project(
-        total, rows, [side_piece, swap(side_piece, "dp", 1)], [near + side_at, away + side_at], True
-    )
+        held = far[i]
+        if i == 0:
+            held, total = lax.optimization_barrier((held, total))
+        if i == 2:
+            total = absorb(
+                total, rows, far_weights + side_weights[:2], far_starts + side_starts[:2], False
+            )
+            held, total = lax.optimization_barrier((held, total))
+            far_weights, far_starts = side_weights[2:], side_starts[2:]
+            side_weights, side_starts = [], []
+        crossed = swap(held, "seq", 1)
+        at, side_at = side * share + i * piece, (1 - side) * share + i * piece
+        far_weights += [held, swap(held, "dp", 1)]
+        far_starts += [near + at, away + at]
+        side_weights += [crossed, swap(crossed, "dp", 1)]
+        side_starts += [near + side_at, away + side_at]
+    total = absorb(total, rows, far_weights, far_starts, False)
+    total = absorb(total, rows, side_weights, side_starts, True)
 
     block = row_count // groups
     received = lax.all_to_all(
@@ -402,17 +432,15 @@
         place_body, (target, received, kernels),
         [((row_count, channels), BF), ((half, channels), BF), ((half, channels), BF),
          ((half, width), BF), ((half, width), BF)],
-        2 * row_count * row_count * channels, 24,
+        24,
     )
     fprev, fnext = halo(down, up)
-    local, = call(local_body, (low, high, kernels), [((row_count, width), F32)], 4 * row_count * width * channels, 24)
-    fprev, fnext, low_later, high_later = lax.optimization_barrier((fprev, fnext, low, high))
-    prev, nxt = halo(low_later, high_later)
+    local, = call(local_body, (low, high, kernels), [((row_count, width), F32)], 24)
     inner, gated, first, alow, ahigh, adown, aup = call(
         fine_body, (fprev, fnext, local, hidden, kernels, mixers),
         [((row_count, width), F32), ((row_count, width), BF), ((half, channels), BF),
          ((quarter, channels), BF), ((quarter, channels), BF), ((quarter, width), BF), ((quarter, width), BF)],
-        3 * row_count * width * channels, 24,
+        24,
     )
     aprev, anext = halo(adown, aup)
     bins = quarter
@@ -427,12 +455,12 @@
         coarse, (ids, aprev, alow, ahigh, anext, first, kernels, mixers, readout, targets[0]),
         [((half, width), BF), ((bins, channels), BF), ((bins, tracks), BF), ((bins, channels), BF),
          ((quarter, width), BF), ((quarter, width), BF)],
-        8 * half * width * channels + 4 * bins * tracks * channels, 32, smem=1,
+        32, smem=1,
     )
     gprev, gnext = halo(glow, ghigh)
     track_keep, track_send = call(
-        readout_body, (place, prev, nxt, second, logit_grad), [((2, channels, tracks // 4), BF)] * 2,
-        2 * bins * tracks * channels, 24, smem=1, after=2,
+        readout_body, (place, second, logit_grad), [((2, channels, tracks // 4), BF)] * 2,
+        24, smem=1,
     )
     track_here, track_away = core_sum(track_keep, track_send)
 
@@ -448,31 +476,32 @@
     fold, split = jnp.asarray(fold), jnp.asarray(split)
     pair = [((2, channels, width), BF)] * 2
 
-    def fine(*refs):
-        fine_grad_body(math.sqrt(windows * groups * bins) * 0.5, *refs)
-
-    cut = channels // 2
-    track_first = swap(track_away[:cut], "dp", 2)
-    trunk, fine_keep, fine_send = call(
-        fine,
-        (place, track_away, gprev, glow, ghigh, gnext, upper, first, kernels, mixers,
-         prev, low, high, nxt, inner, gated, fold, split),
-        [((half, channels), F32)] + pair,
-        20 * row_count * width * channels, 40, smem=1, after=1,
+    def fine_back(*refs):
+        fine_back_body(math.sqrt(windows * groups * bins) * 0.5, *refs)
+
+    def weights(*refs):
+        weight_body(eighth, *refs)
+
+    track_x = swap(track_away, "dp", 2)
+    trunk, lower, ilow, ihigh = call(
+        fine_back, (track_away, gprev, glow, ghigh, gnext, upper, first, kernels, mixers, inner),
+        [((half, channels), F32), ((half, channels), BF), ((half, width), BF), ((half, width), BF)],
+        32, after=1,
         scratch=[pltpu.VMEM((channels // 128, quarter, 128), F32)],
     )
-    fine_send, track_first = lax.optimization_barrier((fine_send, track_first))
-    track_last = swap(track_away[cut:], "dp", 2)
-    track_total = (track_here + jnp.concatenate([track_first, track_last]).astype(F32)).astype(BF)
-    readout_total = seq_sum(track_total)
-    fine_here, fine_away = core_sum(fine_keep, fine_send)
+    iprev, inext = halo(ilow, ihigh)
     coarse_keep, coarse_send = call(
-        coarse_grad_body,
-        (place, fine_away, track_total, alow, ahigh, gprev, glow, ghigh, gnext, cgated, upper, fold, split), pair,
-        12 * half * width * channels, 32, smem=1, after=2,
-    )
-    fine_total = seq_sum(x_sum(fine_here, fine_away))
-    coarse_total = side_first_sum(coarse_keep, coarse_send)
+        weights, (place, ilow, alow, ahigh, gprev, glow, ghigh, gnext, cgated, upper, fold, split), pair,
+        32, smem=1, after=1,
+    )
+    iprev, inext, coarse_send = lax.optimization_barrier((iprev, inext, coarse_send))
+    fine_keep, fine_send = call(
+        weights, (place, ilow, low, high, iprev, ilow, ihigh, inext, gated, lower, fold, split), pair,
+        32, smem=1, after=1,
+    )
+    fine_send, track_x = lax.optimization_barrier((fine_send, track_x))
+    readout_total = seq_sum((track_here + track_x.astype(F32)).astype(BF))
+    fine_total, coarse_total = crossed_sums(*core_sum(fine_keep, fine_send), coarse_keep, coarse_send)
 
     cut = width // windows
     kernel_rows, mixer_rows = [], []

time: 255 us -> 230 us (0.902)
  waiting for transfers between devices: 107 us -> 84.9 us
  Pallas kernels: 58.2 us -> 40.3 us
  local copies, waits for them, and re-layouts: 10.2 us -> 26.5 us
  starting transfers between devices: 62.7 us -> 59.7 us
    pallas_call x7 -> x1, Pallas kernels: 36.3 us -> 8.7 us  [project(): pl.pallas_call(body, out_shape=out, grid_spec=pltpu.PrefetchScalarGridSpe...]
    all_to_all x2 -> x1, waiting for transfers between devices: 15.3 us -> 0.01 us  [seq_sum(): lax.all_to_all(total.reshape(groups, rows // groups, columns), 'seq', spl...]
    unnamed x56 -> x58, local copies, waits for them, and re-layouts: 7.26 us -> 21.5 us
    ppermute x4, waiting for transfers between devices: 15.9 us -> 7.67 us  [halo(): lax.ppermute(high, 'seq', up)]
    pallas_call x0 -> x3, Pallas kernels: none -> 7.6 us  [absorb(): pl.pallas_call(body, out_shape=jax.ShapeDtypeStruct((row_count, channels)...]
    all_to_all x1, waiting for transfers between devices: 8.41 us -> 13.6 us  [crossed_sums(): lax.all_to_all(both, 'seq', split_axis=0, concat_axis=0, axis_index_group...]
    ppermute x25, waiting for transfers between devices: 39.7 us -> 34.8 us  [swap(): return lax.ppermute(value, axis, [(i, i ^ bit) for i in range(size)])]
    all_to_all x2 -> x1, starting transfers between devices: 9.93 us -> 5.56 us  [seq_sum(): lax.all_to_all(total.reshape(groups, rows // groups, columns), 'seq', spl...]
  transfers between devices with their start and end apart: 37 -> 36, of which waited for: 16 -> 20; matrix products, arithmetic and copies ran while one was open for 6% -> 8% of each run, Pallas kernels for 18% -> 13%
where the time goes in v3:
time: 230 us; the launch traced here: 229 us
  waiting for transfers between devices  84.9 us (37%)
  starting transfers between devices  59.7 us (26%)
  Pallas kernels  40.3 us (18%)
  local copies, waits for them, and re-layouts  26.5 us (12%)
  other arithmetic  16.2 us (7%)
    ppermute x25, waiting for transfers between devices, swap(): return lax.ppermute(value, axis, [(i, i ^ bit) for i in range(size)])  34.8 us
    pallas_call x8, Pallas kernels, call(): pl.pallas_call(body, out_shape=outs, in_specs=[SMEM] * smem + [ANY] * aft...  24 us
    ppermute x25, starting transfers between devices, swap(): return lax.ppermute(value, axis, [(i, i ^ bit) for i in range(size)])  22.2 us
    unnamed x58, local copies, waits for them, and re-layouts  21.5 us
    all_to_all x1, waiting for transfers between devices, shards(): lax.all_to_all(total.reshape(groups, block, channels), 'seq', split_axis=...  19.9 us
    ppermute x4, starting transfers between devices, halo(): lax.ppermute(high, 'seq', up)  14.9 us
    all_to_all x1, waiting for transfers between devices, crossed_sums(): lax.all_to_all(both, 'seq', split_axis=0, concat_axis=0, axis_index_group...  13.6 us
    ppermute x4, waiting for transfers between devices, halo(): lax.ppermute(low, 'seq', [(j, i) for i, j in up])  8.83 us
  transfers between devices with their start and end apart: 36, of which 20 were waited for; matrix products, arithmetic and copies ran while one was open for 8% of the time, Pallas kernels for 13%

profile of v3, /device:TPU:0, one launch (start us, length us, event | category | flops | bytes accessed | tf_op | source)
XLA Modules:
  0.0 229.2 jit_solution(547361433658026509)
XLA Ops:
  1.1 2.2 constant_dynamic-slice_fusion.2
  3.3 2.5 %collective-permute-start.1 = (bf16[256,768]{1,0:T(8,128)(2,1)S(1)}, bf16[256,768]{1,0:T(8,128)(2,1)S(1)}, u32[]{:S(2)}, u32[]{:S(2)}) collective-permute-start(bf16[256,768]{1,0:T(8,128)(2,1)S(1)} %get-tuple-element.80), channel_id=1, source_target_pairs={{0,16},{8,24},{16,0},{24,8},{1,17},{9,25},{17,1},{25,9},{2,18},{10... | collective-permute-start | bytes 1179656 | tf_op jit(solution)/shard_map/ppermute | solution.py:325
  6.8 8.7 %shard_map.129.old_ref = f32[512,768]{1,0:T(8,128)} custom-call(s32[2]{0:T(128)} %and_select_fusion.4.starts_ref, bf16[512,8192]{1,0:T(8,128)(2,1)} %bitcast.82, bf16[512,8192]{1,0:T(8,128)(2,1)} %bitcast.83, bf16[2048,768]{1,0:T(8,128)(2,1)} %refs_2_.1, bf16[2048,768]{1,0:T(8,128)(2,1)} %collective-permute-done.2.refs_3_), custom_call_target="tpu_custom_call" | custom-call | flops 1024 | bytes 1024 | tf_op jit(solution)/shard_map/pallas_call | solution.py:112
  15.8 2.5 %collective-permute-start.6 = (bf16[256,768]{1,0:T(8,128)(2,1)S(1)}, bf16[256,768]{1,0:T(8,128)(2,1)S(1)}, u32[]{:S(2)}, u32[]{:S(2)}) collective-permute-start(bf16[256,768]{1,0:T(8,128)(2,1)S(1)} %collective-permute-done.1.refs_0_), channel_id=1, source_target_pairs={{0,1},{1,0},{2,3},{3,2},{4,5},{5,4},{6,7},{7,6},{8,9},{9,8},{10,11... | collective-permute-start | bytes 1179656 | tf_op jit(solution)/shard_map/ppermute | solution.py:325
  18.4 1.5 collective-permute-start.11
  19.9 4.4 %collective-permute-done.4.refs_2_ = bf16[256,768]{1,0:T(8,128)(2,1)S(1)} collective-permute-done((bf16[256,768]{1,0:T(8,128)(2,1)S(1)}, bf16[256,768]{1,0:T(8,128)(2,1)S(1)}, u32[]{:S(2)}, u32[]{:S(2)}) %collective-permute-start.4) | collective-permute-done | bytes 393248 | tf_op jit(solution)/shard_map/ppermute | solution.py:325
  25.6 2.2 collective-permute-done.6.refs_4_
  28.5 1.7 collective-permute-start
  30.3 2.4 %collective-permute-done.11.refs_4_ = bf16[256,768]{1,0:T(8,128)(2,1)S(1)} collective-permute-done((bf16[256,768]{1,0:T(8,128)(2,1)S(1)}, bf16[256,768]{1,0:T(8,128)(2,1)S(1)}, u32[]{:S(2)}, u32[]{:S(2)}) %collective-permute-start.11) | collective-permute-done | bytes 393248 | tf_op jit(solution)/shard_map/ppermute | solution.py:325
  32.7 2.0 collective-permute-start.8
  37.0 3.4 %copy-done = bf16[1,1,512,8192]{3,2,1,0:T(8,128)(2,1)S(1)} copy-done((bf16[1,1,512,8192]{3,2,1,0:T(8,128)(2,1)S(1)}, bf16[1,1,512,8192]{3,2,1,0:T(8,128)(2,1)}, u32[]{:S(2)}) %copy-start) | copy-done | bytes 8388632
  46.8 2.2 shard_map.130.old_ref
  49.0 2.0 collective-permute-start.13
  52.8 7.6 %collective-permute-done.13.refs_0_ = bf16[256,768]{1,0:T(8,128)(2,1)} collective-permute-done((bf16[256,768]{1,0:T(8,128)(2,1)S(1)}, bf16[256,768]{1,0:T(8,128)(2,1)}, u32[]{:S(2)}, u32[]{:S(2)}) %collective-permute-start.13) | collective-permute-done | bytes 393248 | tf_op jit(solution)/shard_map/ppermute | solution.py:325
  60.5 3.4 %copy-done.1 = bf16[1,1,512,8192]{3,2,1,0:T(8,128)(2,1)S(1)} copy-done((bf16[1,1,512,8192]{3,2,1,0:T(8,128)(2,1)S(1)}, bf16[1,1,512,8192]{3,2,1,0:T(8,128)(2,1)}, u32[]{:S(2)}) %copy-start.1) | copy-done | bytes 8388632
  63.9 2.9 %shard_map.131.old_ref = f32[512,768]{1,0:T(8,128)S(1)} custom-call(s32[6]{0:T(128)S(1)} %stack.136.starts_ref, bf16[512,8192]{1,0:T(8,128)(2,1)S(1)} %bitcast.85, f32[512,768]{1,0:T(8,128)S(1)} %shard_map.130.old_ref, bf16[256,768]{1,0:T(8,128)(2,1)S(1)} %collective-permute-done.8.refs_0_, bf16[256,768]{1,0:T(8,128)(2,1)} %collective-permute-done.9.refs_1_, ...), custom_call_target="tpu_custom_call" | custom-call | flops 1024 | bytes 1024 | tf_op jit(solution)/shard_map/pallas_call | solution.py:145
  69.6 2.5 %shard_map.132 = bf16[512,768]{1,0:T(8,128)(2,1)S(1)} custom-call(s32[4]{0:T(128)S(1)} %pad_add_fusion.2.starts_ref, bf16[512,8192]{1,0:T(8,128)(2,1)S(1)} %bitcast.86, f32[512,768]{1,0:T(8,128)S(1)} %shard_map.131.old_ref, bf16[256,768]{1,0:T(8,128)(2,1)} %collective-permute-done.13.refs_0_, bf16[256,768]{1,0:T(8,128)(2,1)} %collective-permute-done.14.refs_1_, ...), custom_call_target="tpu_custom_call" | custom-call | flops 1024 | bytes 1024 | tf_op jit(solution)/shard_map/pallas_call | solution.py:145
  73.0 6.0 %all-to-all-start = ((bf16[8,64,768]{2,1,0:T(8,128)(2,1)}), bf16[8,64,768]{2,1,0:T(8,128)(2,1)}, u32[]{:S(2)}, u32[]{:S(2)}) async-start(bf16[8,64,768]{2,1,0:T(8,128)(2,1)} %bitcast.87), calls=%async_computation | async-start | bytes 1572864 | tf_op jit(solution)/shard_map/all_to_all | solution.py:423
  80.0 19.9 %all-to-all-done = bf16[8,64,768]{2,1,0:T(8,128)(2,1)} async-done(((bf16[8,64,768]{2,1,0:T(8,128)(2,1)}), bf16[8,64,768]{2,1,0:T(8,128)(2,1)}, u32[]{:S(2)}, u32[]{:S(2)}) %all-to-all-start) | async-done | bytes 786464 | tf_op jit(solution)/shard_map/all_to_all | solution.py:423
  99.9 2.2 shard_map.133
  102.1 3.3 %collective-permute-start.17 = (bf16[256,384]{1,0:T(8,128)(2,1)S(1)}, bf16[256,384]{1,0:T(8,128)(2,1)S(1)}, u32[]{:S(2)}, u32[]{:S(2)}) collective-permute-start(bf16[256,384]{1,0:T(8,128)(2,1)S(1)} %get-tuple-element.45), channel_id=1, source_target_pairs={{0,1},{1,2},{2,3},{3,4},{4,5},{5,6},{6,7},{8,9},{9,10},{10,11},{11... | collective-permute-start | bytes 589832 | tf_op jit(solution)/shard_map/ppermute | solution.py:332
  107.8 5.5 %collective-permute-done.17.prev_ref = bf16[256,384]{1,0:T(8,128)(2,1)S(1)} collective-permute-done((bf16[256,384]{1,0:T(8,128)(2,1)S(1)}, bf16[256,384]{1,0:T(8,128)(2,1)S(1)}, u32[]{:S(2)}, u32[]{:S(2)}) %collective-permute-start.17) | collective-permute-done | bytes 196640 | tf_op jit(solution)/shard_map/ppermute | solution.py:332
  114.2 4.5 %collective-permute-start.19 = (bf16[128,384]{1,0:T(8,128)(2,1)S(1)}, bf16[128,384]{1,0:T(8,128)(2,1)S(1)}, u32[]{:S(2)}, u32[]{:S(2)}) collective-permute-start(bf16[128,384]{1,0:T(8,128)(2,1)S(1)} %get-tuple-element.50), channel_id=1, source_target_pairs={{0,1},{1,2},{2,3},{3,4},{4,5},{5,6},{6,7},{8,9},{9,10},{10,11},{11... | collective-permute-start | bytes 294920 | tf_op jit(solution)/shard_map/ppermute | solution.py:332
  118.8 1.5 collective-permute-start.20
  121.0 4.3 %collective-permute-done.20.refs_4_ = bf16[128,384]{1,0:T(8,128)(2,1)S(1)} collective-permute-done((bf16[128,384]{1,0:T(8,128)(2,1)S(1)}, bf16[128,384]{1,0:T(8,128)(2,1)S(1)}, u32[]{:S(2)}, u32[]{:S(2)}) %collective-permute-start.20) | collective-permute-done | bytes 98336 | tf_op jit(solution)/shard_map/ppermute | solution.py:333
  125.3 3.7 %shard_map.136 = (bf16[256,384]{1,0:T(8,128)(2,1)S(1)}, bf16[128,768]{1,0:T(8,128)(2,1)S(1)}, bf16[128,2048]{1,0:T(8,128)(2,1)S(1)}, bf16[128,768]{1,0:T(8,128)(...) custom-call(s32[2]{0:T(128)S(1)} %pad_add_fusion.1.refs_0_, ...), custom_call_target="tpu_custom_call" | custom-call | flops 1024 | bytes 1024 | tf_op jit(solution)/shard_map/pallas_call | solution.py:52
  129.0 1.5 shard_map.137
  130.6 3.5 %collective-permute-done.21 = bf16[2,768,512]{2,1,0:T(8,128)(2,1)} collective-permute-done((bf16[2,768,512]{2,1,0:T(8,128)(2,1)S(1)}, bf16[2,768,512]{2,1,0:T(8,128)(2,1)}, u32[]{:S(2)}, u32[]{:S(2)}) %collective-permute-start.21) | collective-permute-done | bytes 1572896 | tf_op jit(solution)/shard_map/ppermute | solution.py:325
  135.5 1.6 collective-permute-start.26
  137.1 4.0 %collective-permute-start.22 = (bf16[128,384]{1,0:T(8,128)(2,1)S(1)}, bf16[128,384]{1,0:T(8,128)(2,1)S(1)}, u32[]{:S(2)}, u32[]{:S(2)}) collective-permute-start(bf16[128,384]{1,0:T(8,128)(2,1)S(1)} %get-tuple-element.59.refs_3_.refs_6_), channel_id=1, source_target_pairs={{0,1},{1,2},{2,3},{3,4},{4,5},{5,6},{6,7},{8,9},{9,10},{10,11},{11... | collective-permute-start | bytes 294920 | tf_op jit(solution)/shard_map/ppermute | solution.py:332
  143.2 4.3 %collective-permute-done.23.refs_4_.refs_7_ = bf16[128,384]{1,0:T(8,128)(2,1)S(1)} collective-permute-done((bf16[128,384]{1,0:T(8,128)(2,1)S(1)}, bf16[128,384]{1,0:T(8,128)(2,1)S(1)}, u32[]{:S(2)}, u32[]{:S(2)}) %collective-permute-start.23) | collective-permute-done | bytes 98336 | tf_op jit(solution)/shard_map/ppermute | solution.py:333
  147.5 2.5 %shard_map.138 = (f32[256,768]{1,0:T(8,128)}, bf16[256,768]{1,0:T(8,128)(2,1)S(1)}, bf16[256,384]{1,0:T(8,128)(2,1)S(1)}, bf16[256,384]{1,0:T(8,128)(2,1)S(1)}) custom-call(bf16[768,512]{1,0:T(8,128)(2,1)S(1)} %fusion.1.refs_0_, bf16[128,384]{1,0:T(8,128)(2,1)S(1)} %collective-permute-done.22.refs_1_.refs_4_, ...), custom_call_target="tpu_custom_call" | custom-call | flops 1024 | bytes 1024 | tf_op jit(solution)/shard_map/pallas_call | solution.py:52
  150.0 3.1 %collective-permute-start.24 = (bf16[256,384]{1,0:T(8,128)(2,1)S(1)}, bf16[256,384]{1,0:T(8,128)(2,1)S(1)}, u32[]{:S(2)}, u32[]{:S(2)}) collective-permute-start(bf16[256,384]{1,0:T(8,128)(2,1)S(1)} %get-tuple-element.64.refs_6_), channel_id=1, source_target_pairs={{0,1},{1,2},{2,3},{3,4},{4,5},{5,6},{6,7},{8,9},{9,10},{10,11},{11... | collective-permute-start | bytes 589832 | tf_op jit(solution)/shard_map/ppermute | solution.py:332
  154.4 5.5 %shard_map.139 = (bf16[2,768,384]{2,1,0:T(8,128)(2,1)S(1)}, bf16[2,768,384]{2,1,0:T(8,128)(2,1)}) custom-call(s32[2]{0:T(128)S(1)} %pad_add_fusion.ids_ref.refs_0_, bf16[256,384]{1,0:T(8,128)(2,1)S(1)} %get-tuple-element.63.refs_1_.refs_5_, bf16[128,768]{1,0:T(8,128)(2,1)S(1)} %get-tuple-element.51.refs_2_, bf16[128,768]{1,0:T(8,128)(2,1)S(1)} %get-tuple-element.52.refs_3_, ...), custom_call_target="tpu_custom_call" | custom-call | flops 1024 | bytes 1024 | tf_op jit(solution)/shard_map/pallas_call | solution.py:52
  160.7 6.8 %shard_map.140 = (bf16[2,768,384]{2,1,0:T(8,128)(2,1)S(1)}, bf16[2,768,384]{2,1,0:T(8,128)(2,1)}) custom-call(s32[2]{0:T(128)S(1)} %pad_add_fusion.ids_ref.refs_0_, bf16[256,384]{1,0:T(8,128)(2,1)S(1)} %get-tuple-element.63.refs_1_.refs_5_, bf16[256,768]{1,0:T(8,128)(2,1)S(1)} %get-tuple-element.47.low_ref.refs_2_, ...), custom_call_target="tpu_custom_call" | custom-call | flops 1024 | bytes 1024 | tf_op jit(solution)/shard_map/pallas_call | solution.py:52
  169.0 2.9 %convert_add_fusion = f32[2,768,384]{2,1,0:T(8,128)} fusion(bf16[2,768,384]{2,1,0:T(8,128)(2,1)} %collective-permute-done.30, bf16[2,768,384]{2,1,0:T(8,128)(2,1)S(1)} %get-tuple-element.74), kind=kLoop, calls=%fused_computation | loop fusion | flops 1769472 | bytes 4718592 | tf_op jit(solution)/shard_map/add | solution.py:366
  171.9 2.2 fusion.3
  174.1 2.3 collective-permute-start.31
  176.4 2.1 fusion.2
  179.0 2.3 %fusion = bf16[768,512]{1,0:T(8,128)(2,1)} fusion(bf16[768,512]{1,0:T(8,128)(2,1)S(1)} %copy-done.27, bf16[2,768,512]{2,1,0:T(8,128)(2,1)} %collective-permute-done.21, bf16[2,768,512]{2,1,0:T(8,128)(2,1)S(1)} %copy-done.10), kind=kLoop, calls=%fused_computation.2 | loop fusion | flops 2359296 | bytes 3145728 | tf_op jit(solution)/shard_map/convert_element_type | solution.py:503
  181.3 5.6 %all-to-all-start.2 = ((bf16[8,96,512]{2,1,0:T(8,128)(2,1)}), bf16[8,96,512]{2,1,0:T(8,128)(2,1)S(1)}, u32[]{:S(2)}, u32[]{:S(2)}) async-start(bf16[8,96,512]{2,1,0:T(8,128)(2,1)} %bitcast.47), calls=%async_computation.2 | async-start | bytes 1572864 | tf_op jit(solution)/shard_map/all_to_all | solution.py:347
  186.9 7.4 %collective-permute-done.31 = bf16[2,4,96,384]{3,2,1,0:T(8,128)(2,1)} collective-permute-done((bf16[2,4,96,384]{3,2,1,0:T(8,128)(2,1)}, bf16[2,4,96,384]{3,2,1,0:T(8,128)(2,1)}, u32[]{:S(2)}, u32[]{:S(2)}) %collective-permute-start.31) | collective-permute-done | bytes 589856 | tf_op jit(solution)/shard_map/ppermute | solution.py:325
  194.3 1.6 bitcast_add_fusion.1
  197.5 3.2 %collective-permute-start.29 = (bf16[4,96,384]{2,1,0:T(8,128)(2,1)S(1)}, bf16[4,96,384]{2,1,0:T(8,128)(2,1)S(1)}, u32[]{:S(2)}, u32[]{:S(2)}) collective-permute-start(bf16[4,96,384]{2,1,0:T(8,128)(2,1)S(1)} %fusion.7), channel_id=1, source_target_pairs={{0,1},{1,0},{2,3},{3,2},{4,5},{5,4},{6,7},{7,6},{8,9},{9,8},{10,11... | collective-permute-start | bytes 884744 | tf_op jit(solution)/shard_map/ppermute | solution.py:325
  200.7 2.0 collective-permute-done.32
  202.8 3.5 %collective-permute-done.29 = bf16[4,96,384]{2,1,0:T(8,128)(2,1)S(1)} collective-permute-done((bf16[4,96,384]{2,1,0:T(8,128)(2,1)S(1)}, bf16[4,96,384]{2,1,0:T(8,128)(2,1)S(1)}, u32[]{:S(2)}, u32[]{:S(2)}) %collective-permute-start.29) | collective-permute-done | bytes 294944 | tf_op jit(solution)/shard_map/ppermute | solution.py:325
  207.3 5.6 %all-to-all-start.1 = ((bf16[4,96,768]{2,1,0:T(8,128)(2,1)}), bf16[4,96,768]{2,1,0:T(8,128)(2,1)S(1)}, u32[]{:S(2)}, u32[]{:S(2)}) async-start(bf16[4,96,768]{2,1,0:T(8,128)(2,1)} %pad_maximum_fusion), calls=%async_computation.1 | async-start | bytes 1179648 | tf_op jit(solution)/shard_map/all_to_all | solution.py:375
  213.7 13.6 %all-to-all-done.1 = bf16[4,96,768]{2,1,0:T(8,128)(2,1)S(1)} async-done(((bf16[4,96,768]{2,1,0:T(8,128)(2,1)}), bf16[4,96,768]{2,1,0:T(8,128)(2,1)S(1)}, u32[]{:S(2)}, u32[]{:S(2)}) %all-to-all-start.1) | async-done | bytes 589856 | tf_op jit(solution)/shard_map/all_to_all | solution.py:375
  (125 shorter events, 35.3 us)
Async XLA Ops:
  0.6 6.1 %collective-permute-start.2 = (bf16[2048,768]{1,0:T(8,128)(2,1)}, bf16[2048,768]{1,0:T(8,128)(2,1)}, u32[]{:S(2)}, u32[]{:S(2)}) collective-permute-start(bf16[2048,768]{1,0:T(8,128)(2,1)} %refs_2_.1), channel_id=1, source_target_pairs={{0,8},{8,0},{16,24},{24,16},{1,9},{9,1},{17,25},{25,17},{2,10},{10... | collective-permute-start | bytes 9437192 | tf_op jit(solution)/shard_map/ppermute | solution.py:325
  3.3 12.5 %collective-permute-start.1 = (bf16[256,768]{1,0:T(8,128)(2,1)S(1)}, bf16[256,768]{1,0:T(8,128)(2,1)S(1)}, u32[]{:S(2)}, u32[]{:S(2)}) collective-permute-start(bf16[256,768]{1,0:T(8,128)(2,1)S(1)} %get-tuple-element.80), channel_id=1, source_target_pairs={{0,16},{8,24},{16,0},{24,8},{1,17},{9,25},{17,1},{25,9},{2,18},{10... | collective-permute-start | bytes 1179656 | tf_op jit(solution)/shard_map/ppermute | solution.py:325
  5.9 18.4 %collective-permute-start.4 = (bf16[256,768]{1,0:T(8,128)(2,1)S(1)}, bf16[256,768]{1,0:T(8,128)(2,1)S(1)}, u32[]{:S(2)}, u32[]{:S(2)}) collective-permute-start(bf16[256,768]{1,0:T(8,128)(2,1)S(1)} %get-tuple-element.79), channel_id=1, source_target_pairs={{0,16},{8,24},{16,0},{24,8},{1,17},{9,25},{17,1},{25,9},{2,18},{10... | collective-permute-start | bytes 1179656 | tf_op jit(solution)/shard_map/ppermute | solution.py:325
  15.8 11.9 %collective-permute-start.6 = (bf16[256,768]{1,0:T(8,128)(2,1)S(1)}, bf16[256,768]{1,0:T(8,128)(2,1)S(1)}, u32[]{:S(2)}, u32[]{:S(2)}) collective-permute-start(bf16[256,768]{1,0:T(8,128)(2,1)S(1)} %collective-permute-done.1.refs_0_), channel_id=1, source_target_pairs={{0,1},{1,0},{2,3},{3,2},{4,5},{5,4},{6,7},{7,6},{8,9},{9,8},{10,11... | collective-permute-start | bytes 1179656 | tf_op jit(solution)/shard_map/ppermute | solution.py:325
  18.4 14.3 %collective-permute-start.11 = (bf16[256,768]{1,0:T(8,128)(2,1)S(1)}, bf16[256,768]{1,0:T(8,128)(2,1)S(1)}, u32[]{:S(2)}, u32[]{:S(2)}) collective-permute-start(bf16[256,768]{1,0:T(8,128)(2,1)S(1)} %get-tuple-element.78), channel_id=1, source_target_pairs={{0,16},{8,24},{16,0},{24,8},{1,17},{9,25},{17,1},{25,9},{2,18},{10... | collective-permute-start | bytes 1179656 | tf_op jit(solution)/shard_map/ppermute | solution.py:325
  24.3 10.4 %collective-permute-start.5 = (bf16[256,768]{1,0:T(8,128)(2,1)S(1)}, bf16[256,768]{1,0:T(8,128)(2,1)S(1)}, u32[]{:S(2)}, u32[]{:S(2)}) collective-permute-start(bf16[256,768]{1,0:T(8,128)(2,1)S(1)} %collective-permute-done.4.refs_2_), channel_id=1, source_target_pairs={{0,8},{8,0},{16,24},{24,16},{1,9},{9,1},{17,25},{25,17},{2,10},{10... | collective-permute-start | bytes 1179656 | tf_op jit(solution)/shard_map/ppermute | solution.py:325
  24.3 11.2 %collective-permute-start.3 = (bf16[256,768]{1,0:T(8,128)(2,1)S(1)}, bf16[256,768]{1,0:T(8,128)(2,1)S(1)}, u32[]{:S(2)}, u32[]{:S(2)}) collective-permute-start(bf16[256,768]{1,0:T(8,128)(2,1)S(1)} %collective-permute-done.1.refs_0_), channel_id=1, source_target_pairs={{0,8},{8,0},{16,24},{24,16},{1,9},{9,1},{17,25},{25,17},{2,10},{10... | collective-permute-start | bytes 1179656 | tf_op jit(solution)/shard_map/ppermute | solution.py:325
  27.8 8.5 %collective-permute-start.7 = (bf16[256,768]{1,0:T(8,128)(2,1)S(1)}, bf16[256,768]{1,0:T(8,128)(2,1)S(1)}, u32[]{:S(2)}, u32[]{:S(2)}) collective-permute-start(bf16[256,768]{1,0:T(8,128)(2,1)S(1)} %collective-permute-done.6.refs_4_), channel_id=1, source_target_pairs={{0,8},{8,0},{16,24},{24,16},{1,9},{9,1},{17,25},{25,17},{2,10},{10... | collective-permute-start | bytes 1179656 | tf_op jit(solution)/shard_map/ppermute | solution.py:325
  28.5 20.5 %collective-permute-start = (bf16[256,768]{1,0:T(8,128)(2,1)}, bf16[256,768]{1,0:T(8,128)(2,1)S(1)}, u32[]{:S(2)}, u32[]{:S(2)}) collective-permute-start(bf16[256,768]{1,0:T(8,128)(2,1)} %get-tuple-element.81), channel_id=1, source_target_pairs={{0,16},{8,24},{16,0},{24,8},{1,17},{9,25},{17,1},{25,9},{2,18},{10... | collective-permute-start | bytes 1179656 | tf_op jit(solution)/shard_map/ppermute | solution.py:325
  32.7 18.4 %collective-permute-start.8 = (bf16[256,768]{1,0:T(8,128)(2,1)S(1)}, bf16[256,768]{1,0:T(8,128)(2,1)S(1)}, u32[]{:S(2)}, u32[]{:S(2)}) collective-permute-start(bf16[256,768]{1,0:T(8,128)(2,1)S(1)} %collective-permute-done.4.refs_2_), channel_id=1, source_target_pairs={{0,1},{1,0},{2,3},{3,2},{4,5},{5,4},{6,7},{7,6},{8,9},{9,8},{10,11... | collective-permute-start | bytes 1179656 | tf_op jit(solution)/shard_map/ppermute | solution.py:325
  35.4 17.3 %collective-permute-start.15 = (bf16[256,768]{1,0:T(8,128)(2,1)S(1)}, bf16[256,768]{1,0:T(8,128)(2,1)S(1)}, u32[]{:S(2)}, u32[]{:S(2)}) collective-permute-start(bf16[256,768]{1,0:T(8,128)(2,1)S(1)} %collective-permute-done.11.refs_4_), channel_id=1, source_target_pairs={{0,1},{1,0},{2,3},{3,2},{4,5},{5,4},{6,7},{7,6},{8,9},{9,8},{10,11... | collective-permute-start | bytes 1179656 | tf_op jit(solution)/shard_map/ppermute | solution.py:325
  49.0 11.3 %collective-permute-start.13 = (bf16[256,768]{1,0:T(8,128)(2,1)S(1)}, bf16[256,768]{1,0:T(8,128)(2,1)}, u32[]{:S(2)}, u32[]{:S(2)}) collective-permute-start(bf16[256,768]{1,0:T(8,128)(2,1)S(1)} %collective-permute-done.refs_2_), channel_id=1, source_target_pairs={{0,1},{1,0},{2,3},{3,2},{4,5},{5,4},{6,7},{7,6},{8,9},{9,8},{10,11... | collective-permute-start | bytes 1179656 | tf_op jit(solution)/shard_map/ppermute | solution.py:325
  51.1 9.4 %collective-permute-start.12 = (bf16[256,768]{1,0:T(8,128)(2,1)S(1)}, bf16[256,768]{1,0:T(8,128)(2,1)}, u32[]{:S(2)}, u32[]{:S(2)}) collective-permute-start(bf16[256,768]{1,0:T(8,128)(2,1)S(1)} %collective-permute-done.11.refs_4_), channel_id=1, source_target_pairs={{0,8},{8,0},{16,24},{24,16},{1,9},{9,1},{17,25},{25,17},{2,10},{10... | collective-permute-start | bytes 1179656 | tf_op jit(solution)/shard_map/ppermute | solution.py:325
  51.1 9.4 %collective-permute-start.9 = (bf16[256,768]{1,0:T(8,128)(2,1)S(1)}, bf16[256,768]{1,0:T(8,128)(2,1)}, u32[]{:S(2)}, u32[]{:S(2)}) collective-permute-start(bf16[256,768]{1,0:T(8,128)(2,1)S(1)} %collective-permute-done.8.refs_0_), channel_id=1, source_target_pairs={{0,8},{8,0},{16,24},{24,16},{1,9},{9,1},{17,25},{25,17},{2,10},{10... | collective-permute-start | bytes 1179656 | tf_op jit(solution)/shard_map/ppermute | solution.py:325
  51.6 8.9 %collective-permute-start.10 = (bf16[256,768]{1,0:T(8,128)(2,1)S(1)}, bf16[256,768]{1,0:T(8,128)(2,1)}, u32[]{:S(2)}, u32[]{:S(2)}) collective-permute-start(bf16[256,768]{1,0:T(8,128)(2,1)S(1)} %collective-permute-done.refs_2_), channel_id=1, source_target_pairs={{0,8},{8,0},{16,24},{24,16},{1,9},{9,1},{17,25},{25,17},{2,10},{10... | collective-permute-start | bytes 1179656 | tf_op jit(solution)/shard_map/ppermute | solution.py:325
  52.8 14.1 %copy-start.12 = (bf16[256,768]{1,0:T(8,128)(2,1)}, bf16[256,768]{1,0:T(8,128)(2,1)S(1)}, u32[]{:S(2)}) copy-start(bf16[256,768]{1,0:T(8,128)(2,1)S(1)} %collective-permute-done.15.refs_2_) | copy-start | bytes 1179652
  52.8 14.1 %collective-permute-start.16 = (bf16[256,768]{1,0:T(8,128)(2,1)S(1)}, bf16[256,768]{1,0:T(8,128)(2,1)S(1)}, u32[]{:S(2)}, u32[]{:S(2)}) collective-permute-start(bf16[256,768]{1,0:T(8,128)(2,1)S(1)} %collective-permute-done.15.refs_2_), channel_id=1, source_target_pairs={{0,8},{8,0},{16,24},{24,16},{1,9},{9,1},{17,25},{25,17},{2,10},{10... | collective-permute-start | bytes 1179656 | tf_op jit(solution)/shard_map/ppermute | solution.py:325
  60.3 7.3 %collective-permute-start.14 = (bf16[256,768]{1,0:T(8,128)(2,1)}, bf16[256,768]{1,0:T(8,128)(2,1)}, u32[]{:S(2)}, u32[]{:S(2)}) collective-permute-start(bf16[256,768]{1,0:T(8,128)(2,1)} %collective-permute-done.13.refs_0_), channel_id=1, source_target_pairs={{0,8},{8,0},{16,24},{24,16},{1,9},{9,1},{17,25},{25,17},{2,10},{10... | collective-permute-start | bytes 1179656 | tf_op jit(solution)/shard_map/ppermute | solution.py:325
  60.5 3.4 %copy-start.1 = (bf16[1,1,512,8192]{3,2,1,0:T(8,128)(2,1)S(1)}, bf16[1,1,512,8192]{3,2,1,0:T(8,128)(2,1)}, u32[]{:S(2)}) copy-start(bf16[1,1,512,8192]{3,2,1,0:T(8,128)(2,1)} %param.10) | copy-start | bytes 25165828
  69.6 30.3 %copy-start.2 = (bf16[2,3,768,384]{3,2,1,0:T(8,128)(2,1)S(1)}, bf16[2,3,768,384]{3,2,1,0:T(8,128)(2,1)}, u32[]{:S(2)}) copy-start(bf16[2,3,768,384]{3,2,1,0:T(8,128)(2,1)} %refs_7_.3) | copy-start | bytes 10616836
  73.0 6.7 %copy-start.28 = (s32[1,8,8]{2,1,0:T(8,128)S(1)}, s32[1,8,8]{2,1,0:T(8,128)}, u32[]{:S(2)}) copy-start(s32[1,8,8]{2,1,0:T(8,128)} %param.11) | copy-start | bytes 772
  73.0 26.9 %all-to-all-start = ((bf16[8,64,768]{2,1,0:T(8,128)(2,1)}), bf16[8,64,768]{2,1,0:T(8,128)(2,1)}, u32[]{:S(2)}, u32[]{:S(2)}) async-start(bf16[8,64,768]{2,1,0:T(8,128)(2,1)} %bitcast.87), calls=%async_computation | async-start | bytes 1572864 | tf_op jit(solution)/shard_map/all_to_all | solution.py:423
  102.1 11.3 %collective-permute-start.17 = (bf16[256,384]{1,0:T(8,128)(2,1)S(1)}, bf16[256,384]{1,0:T(8,128)(2,1)S(1)}, u32[]{:S(2)}, u32[]{:S(2)}) collective-permute-start(bf16[256,384]{1,0:T(8,128)(2,1)S(1)} %get-tuple-element.45), channel_id=1, source_target_pairs={{0,1},{1,2},{2,3},{3,4},{4,5},{5,6},{6,7},{8,9},{9,10},{10,11},{11... | collective-permute-start | bytes 589832 | tf_op jit(solution)/shard_map/ppermute | solution.py:332
  105.4 7.9 %collective-permute-start.18 = (bf16[256,384]{1,0:T(8,128)(2,1)S(1)}, bf16[256,384]{1,0:T(8,128)(2,1)S(1)}, u32[]{:S(2)}, u32[]{:S(2)}) collective-permute-start(bf16[256,384]{1,0:T(8,128)(2,1)S(1)} %get-tuple-element.46), channel_id=1, source_target_pairs={{1,0},{2,1},{3,2},{4,3},{5,4},{6,5},{7,6},{9,8},{10,9},{11,10},{12... | collective-permute-start | bytes 589832 | tf_op jit(solution)/shard_map/ppermute | solution.py:333
  106.8 6.5 %copy-start.3 = (bf16[2,384,768]{2,1,0:T(8,128)(2,1)S(1)}, bf16[2,384,768]{2,1,0:T(8,128)(2,1)}, u32[]{:S(2)}) copy-start(bf16[2,384,768]{2,1,0:T(8,128)(2,1)} %refs_8_.3) | copy-start | bytes 3538948
  113.4 11.9 %copy-start.7 = (bf16[768,2048]{1,0:T(8,128)(2,1)S(1)}, bf16[768,2048]{1,0:T(8,128)(2,1)}, u32[]{:S(2)}) copy-start(bf16[768,2048]{1,0:T(8,128)(2,1)} %refs_8_.2) | copy-start | bytes 9437188
  113.4 11.9 %copy-start.11 = (s32[1,128,2048]{2,1,0:T(8,128)S(1)}, s32[1,128,2048]{2,1,0:T(8,128)}, u32[]{:S(2)}) copy-start(s32[1,128,2048]{2,1,0:T(8,128)} %param.13) | copy-start | bytes 3145732
  114.2 6.7 %collective-permute-start.19 = (bf16[128,384]{1,0:T(8,128)(2,1)S(1)}, bf16[128,384]{1,0:T(8,128)(2,1)S(1)}, u32[]{:S(2)}, u32[]{:S(2)}) collective-permute-start(bf16[128,384]{1,0:T(8,128)(2,1)S(1)} %get-tuple-element.50), channel_id=1, source_target_pairs={{0,1},{1,2},{2,3},{3,4},{4,5},{5,6},{6,7},{8,9},{9,10},{10,11},{11... | collective-permute-start | bytes 294920 | tf_op jit(solution)/shard_map/ppermute | solution.py:332
  118.8 6.5 %collective-permute-start.20 = (bf16[128,384]{1,0:T(8,128)(2,1)S(1)}, bf16[128,384]{1,0:T(8,128)(2,1)S(1)}, u32[]{:S(2)}, u32[]{:S(2)}) collective-permute-start(bf16[128,384]{1,0:T(8,128)(2,1)S(1)} %get-tuple-element.53), channel_id=1, source_target_pairs={{1,0},{2,1},{3,2},{4,3},{5,4},{6,5},{7,6},{9,8},{10,9},{11,10},{12... | collective-permute-start | bytes 294920 | tf_op jit(solution)/shard_map/ppermute | solution.py:333
  130.5 5.0 %copy-start.9 = (bf16[2,768,512]{2,1,0:T(8,128)(2,1)}, bf16[2,768,512]{2,1,0:T(8,128)(2,1)S(1)}, u32[]{:S(2)}) copy-start(bf16[2,768,512]{2,1,0:T(8,128)(2,1)S(1)} %get-tuple-element.57) | copy-start | bytes 4718596
  130.5 3.6 %collective-permute-start.21 = (bf16[2,768,512]{2,1,0:T(8,128)(2,1)S(1)}, bf16[2,768,512]{2,1,0:T(8,128)(2,1)}, u32[]{:S(2)}, u32[]{:S(2)}) collective-permute-start(bf16[2,768,512]{2,1,0:T(8,128)(2,1)S(1)} %get-tuple-element.58), channel_id=1, source_target_pairs={{0,8},{8,0},{16,24},{24,16},{1,9},{9,1},{17,25},{25,17},{2,10},{10... | collective-permute-start | bytes 4718600 | tf_op jit(solution)/shard_map/ppermute | solution.py:325
  135.5 32.0 %collective-permute-start.26 = (bf16[768,512]{1,0:T(8,128)(2,1)S(1)}, bf16[768,512]{1,0:T(8,128)(2,1)S(1)}, u32[]{:S(2)}, u32[]{:S(2)}) collective-permute-start(bf16[768,512]{1,0:T(8,128)(2,1)S(1)} %fusion.1.refs_0_), channel_id=1, source_target_pairs={{0,16},{8,24},{16,0},{24,8},{1,17},{9,25},{17,1},{25,9},{2,18},{10... | collective-permute-start | bytes 2359304 | tf_op jit(solution)/shard_map/ppermute | solution.py:325
  137.1 6.2 %collective-permute-start.22 = (bf16[128,384]{1,0:T(8,128)(2,1)S(1)}, bf16[128,384]{1,0:T(8,128)(2,1)S(1)}, u32[]{:S(2)}, u32[]{:S(2)}) collective-permute-start(bf16[128,384]{1,0:T(8,128)(2,1)S(1)} %get-tuple-element.59.refs_3_.refs_6_), channel_id=1, source_target_pairs={{0,1},{1,2},{2,3},{3,4},{4,5},{5,6},{6,7},{8,9},{9,10},{10,11},{11... | collective-permute-start | bytes 294920 | tf_op jit(solution)/shard_map/ppermute | solution.py:332
  141.0 6.5 %collective-permute-start.23 = (bf16[128,384]{1,0:T(8,128)(2,1)S(1)}, bf16[128,384]{1,0:T(8,128)(2,1)S(1)}, u32[]{:S(2)}, u32[]{:S(2)}) collective-permute-start(bf16[128,384]{1,0:T(8,128)(2,1)S(1)} %get-tuple-element.60.refs_2_.refs_5_), channel_id=1, source_target_pairs={{1,0},{2,1},{3,2},{4,3},{5,4},{6,5},{7,6},{9,8},{10,9},{11,10},{12... | collective-permute-start | bytes 294920 | tf_op jit(solution)/shard_map/ppermute | solution.py:333
  147.5 6.9 %copy-start.5 = (bf16[2,768,384]{2,1,0:T(8,128)(2,1)S(1)}, bf16[2,768,384]{2,1,0:T(8,128)(2,1)}, u32[]{:S(2)}) copy-start(bf16[2,768,384]{2,1,0:T(8,128)(2,1)} %constant.123.clone.refs_11_) | copy-start | bytes 3538948
  147.5 6.9 %copy-start.6 = (bf16[2,384,768]{2,1,0:T(8,128)(2,1)S(1)}, bf16[2,384,768]{2,1,0:T(8,128)(2,1)}, u32[]{:S(2)}) copy-start(bf16[2,384,768]{2,1,0:T(8,128)(2,1)} %constant.122.clone.refs_10_) | copy-start | bytes 3538948
  150.0 10.5 %collective-permute-start.24 = (bf16[256,384]{1,0:T(8,128)(2,1)S(1)}, bf16[256,384]{1,0:T(8,128)(2,1)S(1)}, u32[]{:S(2)}, u32[]{:S(2)}) collective-permute-start(bf16[256,384]{1,0:T(8,128)(2,1)S(1)} %get-tuple-element.64.refs_6_), channel_id=1, source_target_pairs={{0,1},{1,2},{2,3},{3,4},{4,5},{5,6},{6,7},{8,9},{9,10},{10,11},{11... | collective-permute-start | bytes 589832 | tf_op jit(solution)/shard_map/ppermute | solution.py:332
  153.1 7.6 %collective-permute-start.25 = (bf16[256,384]{1,0:T(8,128)(2,1)S(1)}, bf16[256,384]{1,0:T(8,128)(2,1)S(1)}, u32[]{:S(2)}, u32[]{:S(2)}) collective-permute-start(bf16[256,384]{1,0:T(8,128)(2,1)S(1)} %get-tuple-element.63.refs_1_.refs_5_), channel_id=1, source_target_pairs={{1,0},{2,1},{3,2},{4,3},{5,4},{6,5},{7,6},{9,8},{10,9},{11,10},{12... | collective-permute-start | bytes 589832 | tf_op jit(solution)/shard_map/ppermute | solution.py:333
  160.7 8.3 %collective-permute-start.30 = (bf16[2,768,384]{2,1,0:T(8,128)(2,1)}, bf16[2,768,384]{2,1,0:T(8,128)(2,1)}, u32[]{:S(2)}, u32[]{:S(2)}) collective-permute-start(bf16[2,768,384]{2,1,0:T(8,128)(2,1)} %get-tuple-element.75), channel_id=1, source_target_pairs={{0,8},{8,0},{16,24},{24,16},{1,9},{9,1},{17,25},{25,17},{2,10},{10... | collective-permute-start | bytes 3538952 | tf_op jit(solution)/shard_map/ppermute | solution.py:325
  168.4 8.0 %collective-permute-start.27 = (bf16[2,768,384]{2,1,0:T(8,128)(2,1)}, bf16[2,768,384]{2,1,0:T(8,128)(2,1)}, u32[]{:S(2)}, u32[]{:S(2)}) collective-permute-start(bf16[2,768,384]{2,1,0:T(8,128)(2,1)} %get-tuple-element.73), channel_id=1, source_target_pairs={{0,8},{8,0},{16,24},{24,16},{1,9},{9,1},{17,25},{25,17},{2,10},{10... | collective-permute-start | bytes 3538952 | tf_op jit(solution)/shard_map/ppermute | solution.py:325
  171.9 7.1 %copy-start.27 = (bf16[768,512]{1,0:T(8,128)(2,1)S(1)}, bf16[768,512]{1,0:T(8,128)(2,1)}, u32[]{:S(2)}) copy-start(bf16[768,512]{1,0:T(8,128)(2,1)} %copy-done.26) | copy-start | bytes 2359300
  174.1 4.9 %copy-start.10 = (bf16[2,768,512]{2,1,0:T(8,128)(2,1)S(1)}, bf16[2,768,512]{2,1,0:T(8,128)(2,1)}, u32[]{:S(2)}) copy-start(bf16[2,768,512]{2,1,0:T(8,128)(2,1)} %copy-done.9) | copy-start | bytes 4718596
  174.1 20.2 %collective-permute-start.31 = (bf16[2,4,96,384]{3,2,1,0:T(8,128)(2,1)}, bf16[2,4,96,384]{3,2,1,0:T(8,128)(2,1)}, u32[]{:S(2)}, u32[]{:S(2)}) collective-permute-start(bf16[2,4,96,384]{3,2,1,0:T(8,128)(2,1)} %fusion.3), channel_id=1, source_target_pairs={{0,1},{1,0},{2,3},{3,2},{4,5},{5,4},{6,7},{7,6},{8,9},{9,8},{10,11... | collective-permute-start | bytes 1769480 | tf_op jit(solution)/shard_map/ppermute | solution.py:325
  178.5 17.6 %collective-permute-start.28 = (bf16[768,384]{1,0:T(8,128)(2,1)}, bf16[768,384]{1,0:T(8,128)(2,1)}, u32[]{:S(2)}, u32[]{:S(2)}) collective-permute-start(bf16[768,384]{1,0:T(8,128)(2,1)} %fusion.2), channel_id=1, source_target_pairs={{0,16},{8,24},{16,0},{24,8},{1,17},{9,25},{17,1},{25,9},{2,18},{10... | collective-permute-start | bytes 1769480 | tf_op jit(solution)/shard_map/ppermute | solution.py:325
  181.3 26.0 %all-to-all-start.2 = ((bf16[8,96,512]{2,1,0:T(8,128)(2,1)}), bf16[8,96,512]{2,1,0:T(8,128)(2,1)S(1)}, u32[]{:S(2)}, u32[]{:S(2)}) async-start(bf16[8,96,512]{2,1,0:T(8,128)(2,1)} %bitcast.47), calls=%async_computation.2 | async-start | bytes 1572864 | tf_op jit(solution)/shard_map/all_to_all | solution.py:347
  195.9 6.8 %collective-permute-start.32 = (bf16[4,96,384]{2,1,0:T(8,128)(2,1)S(1)}, bf16[4,96,384]{2,1,0:T(8,128)(2,1)S(1)}, u32[]{:S(2)}, u32[]{:S(2)}) collective-permute-start(bf16[4,96,384]{2,1,0:T(8,128)(2,1)S(1)} %fusion.8), channel_id=1, source_target_pairs={{0,16},{8,24},{16,0},{24,8},{1,17},{9,25},{17,1},{25,9},{2,18},{10... | collective-permute-start | bytes 884744 | tf_op jit(solution)/shard_map/ppermute | solution.py:325
  197.5 8.8 %collective-permute-start.29 = (bf16[4,96,384]{2,1,0:T(8,128)(2,1)S(1)}, bf16[4,96,384]{2,1,0:T(8,128)(2,1)S(1)}, u32[]{:S(2)}, u32[]{:S(2)}) collective-permute-start(bf16[4,96,384]{2,1,0:T(8,128)(2,1)S(1)} %fusion.7), channel_id=1, source_target_pairs={{0,1},{1,0},{2,3},{3,2},{4,5},{5,4},{6,7},{7,6},{8,9},{9,8},{10,11... | collective-permute-start | bytes 884744 | tf_op jit(solution)/shard_map/ppermute | solution.py:325
  207.3 20.1 %all-to-all-start.1 = ((bf16[4,96,768]{2,1,0:T(8,128)(2,1)}), bf16[4,96,768]{2,1,0:T(8,128)(2,1)S(1)}, u32[]{:S(2)}, u32[]{:S(2)}) async-start(bf16[4,96,768]{2,1,0:T(8,128)(2,1)} %pad_maximum_fusion), calls=%async_computation.1 | async-start | bytes 1179648 | tf_op jit(solution)/shard_map/all_to_all | solution.py:375
  (17 other events, 18.1 us)

commit v4 on v3

--- a/solution.py
+++ b/solution.py
@@ -13,11 +13,11 @@
 SPREAD_COARSE = 128
 BF = jnp.bfloat16
 F32 = jnp.float32
-PIECES = 4
 
 CHEAP = pl.CostEstimate(flops=1024, bytes_accessed=1024, transcendentals=0)
 VMEM = pl.BlockSpec(memory_space=pltpu.VMEM)
 SMEM = pl.BlockSpec(memory_space=pltpu.SMEM)
+HBM = pl.BlockSpec(memory_space=pltpu.HBM)
 ANY = pl.BlockSpec(memory_space=pl.ANY)
 
 
@@ -60,108 +60,70 @@
     )(*inputs)
 
 
-def project(total, rows, weights, starts, final):
+def absorb(total, column, rows, weights, starts, final, after=()):
     count = len(weights)
     row_count = rows.shape[0]
-    depth, channels = weights[0].shape
+    depth, columns = weights[0].shape
     block = min(512, depth)
-    steps = depth // block
-
-    def body(starts_ref, *refs):
-        row_refs, weight_refs = refs[:count], refs[count : 2 * count]
-        rest = refs[2 * count :]
-        step = pl.program_id(0)
-        part = nn(row_refs[0][...], weight_refs[0][...])
-        for r, w in zip(row_refs[1:], weight_refs[1:]):
-            part = part + nn(r[...], w[...])
-        if total is None:
-            out_ref = rest[0]
-
-            @pl.when(step == 0)
-            def _():
-                out_ref[...] = part
-
-            @pl.when(step > 0)
-            def _():
-                out_ref[...] += part
-        else:
-            old_ref, out_ref = rest
-            if steps == 1:
-                out_ref[...] = (old_ref[...] + part).astype(out_ref.dtype)
-            else:
-
-                @pl.when(step == 0)
-                def _():
-                    out_ref[...] = old_ref[...] + part
-
-                @pl.when(step > 0)
-                def _():
-                    out_ref[...] += part
-
-    def row_map(k):
-        return lambda i, s: (0, s[k] + i)
-
-    whole = pl.BlockSpec((row_count, channels), lambda i, s: (0, 0))
-    in_specs = [pl.BlockSpec((row_count, block), row_map(k)) for k in range(count)]
-    in_specs += [pl.BlockSpec((block, channels), lambda i, s: (i, 0)) for _ in range(count)]
-    inputs = [rows] * count + list(weights)
-    if total is not None:
-        in_specs.append(whole)
-        inputs.append(total)
-    out = jax.ShapeDtypeStruct((row_count, channels), BF if final else F32)
-    return pl.pallas_call(
-        body,
-        out_shape=out,
-        grid_spec=pltpu.PrefetchScalarGridSpec(
-            num_scalar_prefetch=1, grid=(steps,), in_specs=in_specs, out_specs=whole
-        ),
-        compiler_params=params(56),
-        cost_estimate=CHEAP,
-    )(jnp.stack(starts).astype(jnp.int32) // block, *inputs)
-
-
-def absorb(total, rows, weights, starts, final):
-    count = len(weights)
-    row_count = rows.shape[0]
-    depth, channels = weights[0].shape
-
-    def body(starts_ref, rows_ref, old_ref, *refs):
-        weight_refs, (out_ref, held_ref, sems) = refs[:count], refs[count:]
+    blocks = [(k, at) for k in range(count) for at in range(0, depth, block)]
+    first = total is None
+    fixed = 2 if first else 3
+
+    def body(*refs):
+        starts_ref, rows_ref, old_ref = refs[0], refs[1], refs[2]
+        weight_refs = refs[fixed : fixed + count]
+        out_ref, held_ref, sems, *more = refs[fixed + count + len(after) :]
         copies = []
-        for k in range(count):
-            start = pl.multiple_of(starts_ref[k], depth)
-            copies.append(pltpu.make_async_copy(rows_ref.at[:, pl.ds(start, depth)], held_ref.at[k], sems.at[k]))
-            copies[-1].start()
-        for copy in copies:
-            copy.wait()
+        for n, (k, at) in enumerate(blocks):
+            start = pl.multiple_of(starts_ref[k] + at, block)
+            batch = [pltpu.make_async_copy(rows_ref.at[:, pl.ds(start, block)], held_ref.at[n], sems.at[0, n])]
+            if first:
+                batch.append(
+                    pltpu.make_async_copy(weight_refs[k].at[pl.ds(at, block)], more[0].at[n], sems.at[1, n])
+                )
+            for copy in batch:
+                copy.start()
+            copies.append(batch)
         half = row_count // 2
         for h in range(2):
             part = slice(h * half, (h + 1) * half)
-            sums = old_ref[part]
-            for k in range(count):
-                sums = sums + nn(held_ref[k, part], weight_refs[k][...])
+            sums = 0.0 if first else old_ref[part, column : column + columns]
+            for n, (k, at) in enumerate(blocks):
+                if h == 0:
+                    for copy in copies[n]:
+                        copy.wait()
+                piece = more[0][n] if first else weight_refs[k][at : at + block]
+                sums = sums + nn(held_ref[n, part], piece)
             out_ref[part] = sums.astype(out_ref.dtype)
 
+    scratch = [
+        pltpu.VMEM((len(blocks), row_count, block), BF),
+        pltpu.SemaphoreType.DMA((2, len(blocks))),
+    ]
+    if first:
+        scratch.append(pltpu.VMEM((len(blocks), block, columns), BF))
     return pl.pallas_call(
         body,
-        out_shape=jax.ShapeDtypeStruct((row_count, channels), BF if final else F32),
-        in_specs=[SMEM, ANY] + [VMEM] * (count + 1),
+        out_shape=jax.ShapeDtypeStruct((row_count, columns), BF if final else F32),
+        in_specs=[SMEM, HBM] + ([] if first else [VMEM]) + [HBM if first else VMEM] * count + [ANY] * len(after),
         out_specs=VMEM,
-        scratch_shapes=[pltpu.VMEM((count, row_count, depth), BF), pltpu.SemaphoreType.DMA((count,))],
-        compiler_params=params(24),
+        scratch_shapes=scratch,
+        compiler_params=params(49),
         cost_estimate=CHEAP,
-    )(jnp.stack(starts).astype(jnp.int32), rows, total, *weights)
-
-
-def place_body(target_ref, received_ref, kernels_ref, hidden_ref, low_ref, high_ref, down_ref, up_ref):
+    )(jnp.stack(starts).astype(jnp.int32), rows, *([] if first else [total]), *weights, *after)
+
+
+def place_body(target_ref, left_ref, right_ref, kernels_ref, hidden_ref, low_ref, high_ref, down_ref, up_ref):
     half = low_ref.shape[0]
-    rows = received_ref[...]
+    row_count, columns = left_ref.shape
     for h, out in enumerate((low_ref, high_ref)):
-        order = lax.broadcasted_iota(jnp.int32, (half, rows.shape[0]), 0) + h * half
+        order = lax.broadcasted_iota(jnp.int32, (half, row_count), 0) + h * half
         pick = jnp.where(order == target_ref[...], 1.0, 0.0).astype(BF)
-        placed = nn(pick, rows)
-        hidden_ref[h * half : (h + 1) * half] = placed.astype(BF)
-        out[...] = gelu(placed).astype(BF)
+        for n, rows_ref in enumerate((left_ref, right_ref)):
+            placed = nn(pick, rows_ref[...])
+            cols = slice(n * columns, (n + 1) * columns)
+            hidden_ref[h * half : (h + 1) * half, cols] = placed.astype(BF)
+            out[:, cols] = gelu(placed).astype(BF)
     down_ref[...] = nn(low_ref[...], kernels_ref[0, 2]).astype(BF)
     up_ref[...] = nn(high_ref[...], kernels_ref[0, 0]).astype(BF)
 
@@ -264,12 +226,15 @@
             send_ref[far] = block
 
 
-def mixer_piece(gated, upstream, spread_ref, split_ref):
+def mixer_piece(slab, gated, up, spread_ref, split_ref):
     mixed = 0.0
     for j in range(2):
         left = nn(gated, spread_ref[j]).astype(BF)
-        right = nn(upstream, split_ref[j]).astype(BF)
-        mixed = mixed + tn(left, right)
+        right = nn(up, split_ref[j]).astype(BF)
+        rows = []
+        for s in range(up.shape[0] // slab):
+            rows += [right[s * slab : (s + 1) * slab]] * 2
+        mixed = mixed + tn(left, jnp.concatenate(rows, axis=0))
     return mixed.astype(BF)
 
 
@@ -277,15 +242,11 @@
     slab, ids_ref, after_ref, low_ref, high_ref, gprev_ref, glow_ref, ghigh_ref, gnext_ref, gated_ref, up_ref,
     spread_ref, split_ref, keep_ref, send_ref,
 ):
-    up = up_ref[...]
-    rows = []
-    for s in range(up.shape[0] // slab):
-        rows += [up[s * slab : (s + 1) * slab]] * 2
     grads = (gprev_ref, glow_ref, ghigh_ref, gnext_ref)
     pieces = []
     for t in range(3):
         pieces.append((tn(low_ref[...], grads[2 - t][...]) + tn(high_ref[...], grads[3 - t][...])).astype(BF))
-    pieces.append(mixer_piece(gated_ref[...], jnp.concatenate(rows, axis=0), spread_ref, split_ref))
+    pieces.append(mixer_piece(slab, gated_ref[...], up_ref[...], spread_ref, split_ref))
     store_blocks(ids_ref, pieces, keep_ref, send_ref)
 
 
@@ -350,26 +311,32 @@
     return parts.astype(F32).sum(axis=0)
 
 
-def side_halves(total):
+def side_rows(value, side):
+    groups = lax.axis_size("seq")
+    *blocks, rows, columns = value.shape
+    value = value.reshape(*blocks, groups // 2, 2, rows // groups, columns)
+    return lax.dynamic_index_in_dim(value, side, axis=len(blocks) + 1, keepdims=False).astype(F32)
+
+
+def crossed_sums(left_keep, left_send, right_keep, right_send):
     groups = lax.axis_size("seq")
     side = lax.axis_index("seq") % 2
-    blocks, rows, columns = total.shape
-    total = total.reshape(blocks, groups // 2, 2, rows // groups, columns)
-    return (
-        lax.dynamic_index_in_dim(total, 1 - side, axis=2, keepdims=False).astype(BF),
-        lax.dynamic_index_in_dim(total, side, axis=2, keepdims=False),
-    )
-
-
-def crossed_sums(here, away, keep, send):
-    groups = lax.axis_size("seq")
-    other, own = side_halves(keep.astype(F32) + swap(send, "dp", 1).astype(F32))
-    x_came, side_came = swap(away, "dp", 2), swap(other, "seq", 1)
-    left_other, left_own = side_halves((here + x_came.astype(F32))[None])
-    right = own + side_came.astype(F32)
-    side_came, x_came = swap(left_other[0], "seq", 1), swap(right[1].astype(BF), "dp", 2)
-    left = left_own[0] + side_came.astype(F32)
-    right = right[0] + x_came.astype(F32)
+    right_came = swap(right_send, "dp", 1)
+    left_came = swap(left_send, "dp", 1)
+    x_came = swap((left_keep[1].astype(F32) + left_came[1].astype(F32)).astype(BF), "dp", 2)
+    other = side_rows(right_keep, 1 - side) + side_rows(right_came, 1 - side)
+    side_came = swap(other.astype(BF), "seq", 1)
+
+    def left_half(at):
+        return side_rows(left_keep[0], at) + side_rows(left_came[0], at) + side_rows(x_came, at)
+
+    def right_half(at):
+        return side_rows(right_keep[at], side) + side_rows(right_came[at], side) + side_came[at].astype(F32)
+
+    left = swap(left_half(1 - side).astype(BF), "seq", 1)
+    right = swap(right_half(1).astype(BF), "dp", 2)
+    left = left_half(side) + left.astype(F32)
+    right = right_half(0) + right.astype(F32)
     both = jnp.concatenate([left, right], axis=2).astype(BF)
     lines = [list(range(start, groups, 2)) for start in range(2)]
     parts = lax.all_to_all(both, "seq", split_axis=0, concat_axis=0, axis_index_groups=lines, tiled=True)
@@ -392,44 +359,45 @@
 
     side = device % 2
     share = depth // 2
-    piece = share // PIECES
+    piece = share // 2
+    columns = channels // 2
+    block = row_count // groups
     from_core = swap(projection, "dp", 1)
     mine = lax.dynamic_slice_in_dim(projection, side * share, share, axis=0)
-    far = [swap(lax.slice_in_dim(mine, i * piece, (i + 1) * piece), "dp", 2) for i in range(PIECES)]
+    far = [
+        [swap(mine[i * piece : (i + 1) * piece, n * columns : (n + 1) * columns], "dp", 2) for i in range(2)]
+        for n in range(2)
+    ]
     near, away = (me ^ 2) * depth, (me ^ 3) * depth
-    total = project(None, rows, [projection, from_core], [me * depth, (me ^ 1) * depth], False)
-    far_weights, far_starts, side_weights, side_starts = [], [], [], []
-    for i in range(PIECES):
-        held = far[i]
-        if i == 0:
-            held, total = lax.optimization_barrier((held, total))
-        if i == 2:
-            total = absorb(
-                total, rows, far_weights + side_weights[:2], far_starts + side_starts[:2], False
-            )
-            held, total = lax.optimization_barrier((held, total))
-            far_weights, far_starts = side_weights[2:], side_starts[2:]
-            side_weights, side_starts = [], []
-        crossed = swap(held, "seq", 1)
-        at, side_at = side * share + i * piece, (1 - side) * share + i * piece
-        far_weights += [held, swap(held, "dp", 1)]
-        far_starts += [near + at, away + at]
-        side_weights += [crossed, swap(crossed, "dp", 1)]
-        side_starts += [near + side_at, away + side_at]
-    total = absorb(total, rows, far_weights, far_starts, False)
-    total = absorb(total, rows, side_weights, side_starts, True)
-
-    block = row_count // groups
-    received = lax.all_to_all(
-        total.reshape(groups, block, channels), "seq", split_axis=0, concat_axis=0, tiled=True
-    ).reshape(row_count, channels)
+    total = absorb(None, 0, rows, [projection, from_core], [me * depth, (me ^ 1) * depth], False)
+    received = []
+    for n in range(2):
+        far_weights, far_starts, side_weights, side_starts = [], [], [], []
+        for i in range(2):
+            held = far[n][i]
+            if n == 0 and i == 0:
+                held, total = lax.optimization_barrier((held, total))
+            crossed = swap(held, "seq", 1)
+            at, side_at = side * share + i * piece, (1 - side) * share + i * piece
+            far_weights += [held, swap(held, "dp", 1)]
+            far_starts += [near + at, away + at]
+            side_weights += [crossed, swap(crossed, "dp", 1)]
+            side_starts += [near + side_at, away + side_at]
+        sums = absorb(total, n * columns, rows, far_weights, far_starts, False)
+        sums = absorb(sums, 0, rows, side_weights, side_starts, True, received)
+        received.append(
+            lax.all_to_all(
+                sums.reshape(groups, block, columns), "seq", split_axis=0, concat_axis=0, tiled=True
+            ).reshape(row_count, columns)
+        )
+
     column = lax.dynamic_index_in_dim(layout[0], device, axis=1, keepdims=True)
     position = column * block + jnp.arange(block, dtype=jnp.int32)[None, :]
     slot = (position // half) * half + (position % 4) * eighth + (position % half) // 4
     target = jnp.where(device * row_count + position < length, slot, -1).reshape(1, row_count)
 
     hidden, low, high, down, up = call(
-        place_body, (target, received, kernels),
+        place_body, (target, *received, kernels),
         [((row_count, channels), BF), ((half, channels), BF), ((half, channels), BF),
          ((half, width), BF), ((half, width), BF)],
         24,
@@ -501,7 +469,7 @@
     )
     fine_send, track_x = lax.optimization_barrier((fine_send, track_x))
     readout_total = seq_sum((track_here + track_x.astype(F32)).astype(BF))
-    fine_total, coarse_total = crossed_sums(*core_sum(fine_keep, fine_send), coarse_keep, coarse_send)
+    fine_total, coarse_total = crossed_sums(fine_keep, fine_send, coarse_keep, coarse_send)
 
     cut = width // windows
     kernel_rows, mixer_rows = [], []

time: 230 us -> 223 us (0.970)
  local copies, waits for them, and re-layouts: 26.5 us -> 18.4 us
  other arithmetic: 16.2 us -> 8.46 us
  Pallas kernels: 40.3 us -> 46.6 us
    unnamed x58 -> x52, local copies, waits for them, and re-layouts: 21.5 us -> 11.9 us
    pallas_call x4 -> x5, Pallas kernels: 16.3 us -> 24.4 us  [absorb(): pl.pallas_call(body, out_shape=jax.ShapeDtypeStruct((row_count, columns),...]
    ppermute x25, waiting for transfers between devices: 34.8 us -> 41.6 us  [swap(): return lax.ppermute(value, axis, [(i, i ^ bit) for i in range(size)])]
    all_to_all x1 -> x2, starting transfers between devices: 6.01 us -> 12.4 us  [shards(): lax.all_to_all(sums.reshape(groups, block, columns), 'seq', split_axis=0,...]
    all_to_all x1 -> x2, waiting for transfers between devices: 19.9 us -> 13.6 us  [shards(): lax.all_to_all(sums.reshape(groups, block, columns), 'seq', split_axis=0,...]
    add x3 -> x0, other arithmetic: 5.9 us -> none  [the longest x1 2.91 us: crossed_sums(): other, own = side_halves(keep.astype(F32) + swap(send, 'dp', 1).astype(F32))]
    slice x1 -> x5, local copies, waits for them, and re-layouts: 2.2 us -> 6.23 us  [the longest x1 2.41 us: shards(): mine[i * piece:(i + 1) * piece, n * columns:(n + 1) * columns]]
    convert_element_type x2 -> x1, other arithmetic: 3.41 us -> 0.21 us  [core_sum(): away = (keep[1].astype(F32) + came[1].astype(F32)).astype(BF)]
  transfers between devices with their start and end apart: 36 -> 37, of which waited for: 20 -> 19; matrix products, arithmetic and copies ran while one was open for 8% -> 6% of each run, Pallas kernels for 13% -> 15%
where the time goes in v4:
time: 223 us; the launch traced here: 222 us
  waiting for transfers between devices  85.1 us (38%)
  starting transfers between devices  61.3 us (27%)
  Pallas kernels  46.6 us (21%)
  local copies, waits for them, and re-layouts  18.4 us (8%)
  other arithmetic  8.46 us (4%)
    ppermute x25, waiting for transfers between devices, swap(): return lax.ppermute(value, axis, [(i, i ^ bit) for i in range(size)])  41.6 us
    pallas_call x5, Pallas kernels, absorb(): pl.pallas_call(body, out_shape=jax.ShapeDtypeStruct((row_count, columns),...  24.4 us
    pallas_call x8, Pallas kernels, call(): pl.pallas_call(body, out_shape=outs, in_specs=[SMEM] * smem + [ANY] * aft...  22.2 us
    ppermute x25, starting transfers between devices, swap(): return lax.ppermute(value, axis, [(i, i ^ bit) for i in range(size)])  19.6 us
    ppermute x4, starting transfers between devices, halo(): lax.ppermute(high, 'seq', up)  14.9 us
    all_to_all x2, waiting for transfers between devices, shards(): lax.all_to_all(sums.reshape(groups, block, columns), 'seq', split_axis=0,...  13.6 us
    all_to_all x2, starting transfers between devices, shards(): lax.all_to_all(sums.reshape(groups, block, columns), 'seq', split_axis=0,...  12.4 us
    all_to_all x1, waiting for transfers between devices, crossed_sums(): lax.all_to_all(both, 'seq', split_axis=0, concat_axis=0, axis_index_group...  12.1 us
  transfers between devices with their start and end apart: 37, of which 19 were waited for; matrix products, arithmetic and copies ran while one was open for 6% of the time, Pallas kernels for 15%

profile of v4, /device:TPU:0, one launch (start us, length us, event | category | flops | bytes accessed | tf_op | source)
XLA Modules:
  0.0 221.6 jit_solution(12950716632486520040)
XLA Ops:
  1.1 2.4 %fusion.9 = (bf16[512,384]{1,0:T(8,128)(2,1)}, bf16[512,384]{1,0:T(8,128)(2,1)}, bf16[512,384]{1,0:T(8,128)(2,1)S(1)}, bf16[512,384]{1,0:T(8,128)(2,1)}) fusion(bf16[2048,768]{1,0:T(8,128)(2,1)} %refs_2_.1, s32[]{:T(128)S(6)} %add.284, s32[]{:T(128)S(6)} %add.285, s32[]{:T(128)S(6)} %select_n.98), kind=kLoop, calls=%fused_computation.55 | loop fusion | bytes 3145740 | tf_op jit(solution)/shard_map/slice | solution.py:368
  3.6 2.5 %collective-permute-start.3 = (bf16[512,384]{1,0:T(8,128)(2,1)S(1)}, bf16[512,384]{1,0:T(8,128)(2,1)S(1)}, u32[]{:S(2)}, u32[]{:S(2)}) collective-permute-start(bf16[512,384]{1,0:T(8,128)(2,1)S(1)} %get-tuple-element.76), channel_id=1, source_target_pairs={{0,16},{8,24},{16,0},{24,8},{1,17},{9,25},{17,1},{25,9},{2,18},{10... | collective-permute-start | bytes 1179656 | tf_op jit(solution)/shard_map/ppermute | solution.py:286
  6.1 2.0 collective-permute-start.9
  8.2 7.9 %collective-permute-done.3.refs_5_ = bf16[512,384]{1,0:T(8,128)(2,1)S(1)} collective-permute-done((bf16[512,384]{1,0:T(8,128)(2,1)S(1)}, bf16[512,384]{1,0:T(8,128)(2,1)S(1)}, u32[]{:S(2)}, u32[]{:S(2)}) %collective-permute-start.3) | collective-permute-done | bytes 393248 | tf_op jit(solution)/shard_map/ppermute | solution.py:286
  16.1 2.0 collective-permute-start.7
  18.0 1.9 copy-done.2
  19.9 8.3 %shard_map.129.refs_2_ = f32[512,768]{1,0:T(8,128)S(1)} custom-call(s32[2]{0:T(128)S(1)} %pad_add_fusion.4.refs_0_, bf16[512,8192]{1,0:T(8,128)(2,1)} %bitcast.104, bf16[2048,768]{1,0:T(8,128)(2,1)S(1)} %copy-done.2, bf16[2048,768]{1,0:T(8,128)(2,1)} %collective-permute-done.1.refs_3_), custom_call_target="tpu_custom_call" | custom-call | flops 1024 | bytes 1024 | tf_op jit(solution)/shard_map/pallas_call | solution.py:105
  28.4 2.0 collective-permute-start.11
  30.4 2.6 %collective-permute-done.9.refs_3_ = bf16[512,384]{1,0:T(8,128)(2,1)S(1)} collective-permute-done((bf16[512,384]{1,0:T(8,128)(2,1)}, bf16[512,384]{1,0:T(8,128)(2,1)S(1)}, u32[]{:S(2)}, u32[]{:S(2)}) %collective-permute-start.9) | collective-permute-done | bytes 393248 | tf_op jit(solution)/shard_map/ppermute | solution.py:286
  33.4 5.0 %collective-permute-done.5.refs_3_ = bf16[512,384]{1,0:T(8,128)(2,1)} collective-permute-done((bf16[512,384]{1,0:T(8,128)(2,1)S(1)}, bf16[512,384]{1,0:T(8,128)(2,1)}, u32[]{:S(2)}, u32[]{:S(2)}) %collective-permute-start.5) | collective-permute-done | bytes 393248 | tf_op jit(solution)/shard_map/ppermute | solution.py:286
  38.4 2.7 %collective-permute-done.11.refs_5_ = bf16[512,384]{1,0:T(8,128)(2,1)S(1)} collective-permute-done((bf16[512,384]{1,0:T(8,128)(2,1)}, bf16[512,384]{1,0:T(8,128)(2,1)S(1)}, u32[]{:S(2)}, u32[]{:S(2)}) %collective-permute-start.11) | collective-permute-done | bytes 393248 | tf_op jit(solution)/shard_map/ppermute | solution.py:286
  41.1 1.8 collective-permute-start.13
  43.2 3.9 %shard_map.130.refs_2_ = f32[512,384]{1,0:T(8,128)S(1)} custom-call(s32[4]{0:T(128)S(1)} %get-tuple-element.93.refs_0_, bf16[512,8192]{1,0:T(8,128)(2,1)} %bitcast.105, f32[512,768]{1,0:T(8,128)S(1)} %shard_map.129.refs_2_, bf16[512,384]{1,0:T(8,128)(2,1)S(1)} %collective-permute-done.refs_3_, bf16[512,384]{1,0:T(8,128)(2,1)} %collective-permute-done.2.refs_4_, ...), custom_call_target="tpu_custom_call" | custom-call | flops 1024 | bytes 1024 | tf_op jit(solution)/shard_map/pallas_call | solution.py:105
  47.2 4.8 %shard_map.131 = bf16[512,384]{1,0:T(8,128)(2,1)} custom-call(s32[4]{0:T(128)S(1)} %get-tuple-element.92.refs_0_, bf16[512,8192]{1,0:T(8,128)(2,1)} %bitcast.106, f32[512,384]{1,0:T(8,128)S(1)} %shard_map.130.refs_2_, bf16[512,384]{1,0:T(8,128)(2,1)} %collective-permute-done.5.refs_3_, bf16[512,384]{1,0:T(8,128)(2,1)} %collective-permute-done.6.refs_4_, ...), custom_call_target="tpu_custom_call" | custom-call | flops 1024 | bytes 1024 | tf_op jit(solution)/shard_map/pallas_call | solution.py:105
  51.9 6.1 %all-to-all-start = ((bf16[8,64,384]{2,1,0:T(8,128)(2,1)}), bf16[8,64,384]{2,1,0:T(8,128)(2,1)S(1)}, u32[]{:S(2)}, u32[]{:S(2)}) async-start(bf16[8,64,384]{2,1,0:T(8,128)(2,1)} %bitcast.14), calls=%async_computation | async-start | bytes 786432 | tf_op jit(solution)/shard_map/all_to_all | solution.py:389
  58.6 2.4 %collective-permute-done.15.refs_5_ = bf16[512,384]{1,0:T(8,128)(2,1)} collective-permute-done((bf16[512,384]{1,0:T(8,128)(2,1)S(1)}, bf16[512,384]{1,0:T(8,128)(2,1)}, u32[]{:S(2)}, u32[]{:S(2)}) %collective-permute-start.15) | collective-permute-done | bytes 393248 | tf_op jit(solution)/shard_map/ppermute | solution.py:286
  61.1 3.3 %shard_map.132.refs_2_ = f32[512,384]{1,0:T(8,128)S(1)} custom-call(s32[4]{0:T(128)S(1)} %get-tuple-element.93.refs_0_, bf16[512,8192]{1,0:T(8,128)(2,1)} %bitcast.107, f32[512,768]{1,0:T(8,128)S(1)} %shard_map.129.refs_2_, bf16[512,384]{1,0:T(8,128)(2,1)S(1)} %collective-permute-done.9.refs_3_, bf16[512,384]{1,0:T(8,128)(2,1)S(1)} %collective-permute-done.10.refs_4_, ...), custom_call_target="tpu_custom_call" | custom-call | flops 1024 | bytes 1024 | tf_op jit(solution)/shard_map/pallas_call | solution.py:105
  66.8 2.2 all-to-all-done
  73.9 4.1 %shard_map.133 = bf16[512,384]{1,0:T(8,128)(2,1)S(1)} custom-call(s32[4]{0:T(128)S(1)} %get-tuple-element.92.refs_0_, bf16[512,8192]{1,0:T(8,128)(2,1)} %bitcast.108, f32[512,384]{1,0:T(8,128)S(1)} %copy-done.10, bf16[512,384]{1,0:T(8,128)(2,1)} %collective-permute-done.13.refs_3_, bf16[512,384]{1,0:T(8,128)(2,1)S(1)} %copy-done.16, ...), custom_call_target="tpu_custom_call" | custom-call | flops 1024 | bytes 1024 | tf_op jit(solution)/shard_map/pallas_call | solution.py:105
  78.8 6.3 %all-to-all-start.1 = ((bf16[8,64,384]{2,1,0:T(8,128)(2,1)}), bf16[8,64,384]{2,1,0:T(8,128)(2,1)}, u32[]{:S(2)}, u32[]{:S(2)}) async-start(bf16[8,64,384]{2,1,0:T(8,128)(2,1)} %bitcast.102), calls=%async_computation.1 | async-start | bytes 786432 | tf_op jit(solution)/shard_map/all_to_all | solution.py:389
  86.1 11.4 %all-to-all-done.1 = bf16[8,64,384]{2,1,0:T(8,128)(2,1)} async-done(((bf16[8,64,384]{2,1,0:T(8,128)(2,1)}), bf16[8,64,384]{2,1,0:T(8,128)(2,1)}, u32[]{:S(2)}, u32[]{:S(2)}) %all-to-all-start.1) | async-done | bytes 393248 | tf_op jit(solution)/shard_map/all_to_all | solution.py:389
  98.5 2.1 shard_map.134
  100.7 3.4 %collective-permute-start.17 = (bf16[256,384]{1,0:T(8,128)(2,1)S(1)}, bf16[256,384]{1,0:T(8,128)(2,1)S(1)}, u32[]{:S(2)}, u32[]{:S(2)}) collective-permute-start(bf16[256,384]{1,0:T(8,128)(2,1)S(1)} %get-tuple-element.41), channel_id=1, source_target_pairs={{0,1},{1,2},{2,3},{3,4},{4,5},{5,6},{6,7},{8,9},{9,10},{10,11},{11... | collective-permute-start | bytes 589832 | tf_op jit(solution)/shard_map/ppermute | solution.py:293
  106.5 5.5 %collective-permute-done.17.prev_ref = bf16[256,384]{1,0:T(8,128)(2,1)S(1)} collective-permute-done((bf16[256,384]{1,0:T(8,128)(2,1)S(1)}, bf16[256,384]{1,0:T(8,128)(2,1)S(1)}, u32[]{:S(2)}, u32[]{:S(2)}) %collective-permute-start.17) | collective-permute-done | bytes 196640 | tf_op jit(solution)/shard_map/ppermute | solution.py:293
  112.9 4.5 %collective-permute-start.19 = (bf16[128,384]{1,0:T(8,128)(2,1)S(1)}, bf16[128,384]{1,0:T(8,128)(2,1)S(1)}, u32[]{:S(2)}, u32[]{:S(2)}) collective-permute-start(bf16[128,384]{1,0:T(8,128)(2,1)S(1)} %get-tuple-element.46), channel_id=1, source_target_pairs={{0,1},{1,2},{2,3},{3,4},{4,5},{5,6},{6,7},{8,9},{9,10},{10,11},{11... | collective-permute-start | bytes 294920 | tf_op jit(solution)/shard_map/ppermute | solution.py:293
  119.6 4.3 %collective-permute-done.20.refs_4_ = bf16[128,384]{1,0:T(8,128)(2,1)S(1)} collective-permute-done((bf16[128,384]{1,0:T(8,128)(2,1)S(1)}, bf16[128,384]{1,0:T(8,128)(2,1)S(1)}, u32[]{:S(2)}, u32[]{:S(2)}) %collective-permute-start.20) | collective-permute-done | bytes 98336 | tf_op jit(solution)/shard_map/ppermute | solution.py:294
  123.9 3.7 %shard_map.137 = (bf16[256,384]{1,0:T(8,128)(2,1)S(1)}, bf16[128,768]{1,0:T(8,128)(2,1)S(1)}, bf16[128,2048]{1,0:T(8,128)(2,1)S(1)}, bf16[128,768]{1,0:T(8,128)(...) custom-call(s32[2]{0:T(128)S(1)} %pad_add_fusion.1.refs_0_, ...), custom_call_target="tpu_custom_call" | custom-call | flops 1024 | bytes 1024 | tf_op jit(solution)/shard_map/pallas_call | solution.py:52
  127.6 1.5 shard_map.138
  129.2 3.4 %collective-permute-done.21 = bf16[2,768,512]{2,1,0:T(8,128)(2,1)S(1)} collective-permute-done((bf16[2,768,512]{2,1,0:T(8,128)(2,1)S(1)}, bf16[2,768,512]{2,1,0:T(8,128)(2,1)S(1)}, u32[]{:S(2)}, u32[]{:S(2)}) %collective-permute-start.21) | collective-permute-done | bytes 1572896 | tf_op jit(solution)/shard_map/ppermute | solution.py:286
  132.9 1.6 collective-permute-start.26
  134.4 4.0 %collective-permute-start.22 = (bf16[128,384]{1,0:T(8,128)(2,1)S(1)}, bf16[128,384]{1,0:T(8,128)(2,1)S(1)}, u32[]{:S(2)}, u32[]{:S(2)}) collective-permute-start(bf16[128,384]{1,0:T(8,128)(2,1)S(1)} %get-tuple-element.55.refs_3_.refs_6_), channel_id=1, source_target_pairs={{0,1},{1,2},{2,3},{3,4},{4,5},{5,6},{6,7},{8,9},{9,10},{10,11},{11... | collective-permute-start | bytes 294920 | tf_op jit(solution)/shard_map/ppermute | solution.py:293
  140.6 4.3 %collective-permute-done.23.refs_4_.refs_7_ = bf16[128,384]{1,0:T(8,128)(2,1)S(1)} collective-permute-done((bf16[128,384]{1,0:T(8,128)(2,1)S(1)}, bf16[128,384]{1,0:T(8,128)(2,1)S(1)}, u32[]{:S(2)}, u32[]{:S(2)}) %collective-permute-start.23) | collective-permute-done | bytes 98336 | tf_op jit(solution)/shard_map/ppermute | solution.py:294
  144.9 2.4 %shard_map.139 = (f32[256,768]{1,0:T(8,128)}, bf16[256,768]{1,0:T(8,128)(2,1)S(1)}, bf16[256,384]{1,0:T(8,128)(2,1)S(1)}, bf16[256,384]{1,0:T(8,128)(2,1)S(1)}) custom-call(bf16[768,512]{1,0:T(8,128)(2,1)S(1)} %fusion.1.refs_0_, bf16[128,384]{1,0:T(8,128)(2,1)S(1)} %collective-permute-done.22.refs_1_.refs_4_, ...), custom_call_target="tpu_custom_call" | custom-call | flops 1024 | bytes 1024 | tf_op jit(solution)/shard_map/pallas_call | solution.py:52
  147.4 3.0 %collective-permute-start.24 = (bf16[256,384]{1,0:T(8,128)(2,1)S(1)}, bf16[256,384]{1,0:T(8,128)(2,1)S(1)}, u32[]{:S(2)}, u32[]{:S(2)}) collective-permute-start(bf16[256,384]{1,0:T(8,128)(2,1)S(1)} %get-tuple-element.60.refs_6_), channel_id=1, source_target_pairs={{0,1},{1,2},{2,3},{3,4},{4,5},{5,6},{6,7},{8,9},{9,10},{10,11},{11... | collective-permute-start | bytes 589832 | tf_op jit(solution)/shard_map/ppermute | solution.py:293
  151.8 4.2 %shard_map.140 = (bf16[2,768,384]{2,1,0:T(8,128)(2,1)S(1)}, bf16[2,768,384]{2,1,0:T(8,128)(2,1)S(1)}) custom-call(s32[2]{0:T(128)S(1)} %pad_add_fusion.ids_ref.refs_0_, bf16[256,384]{1,0:T(8,128)(2,1)S(1)} %get-tuple-element.59.refs_1_.refs_5_, bf16[128,768]{1,0:T(8,128)(2,1)S(1)} %get-tuple-element.47.refs_2_, ...), custom_call_target="tpu_custom_call" | custom-call | flops 1024 | bytes 1024 | tf_op jit(solution)/shard_map/pallas_call | solution.py:52
  156.0 2.0 collective-permute-done.25.refs_7_
  158.0 6.3 %shard_map.141 = (bf16[2,768,384]{2,1,0:T(8,128)(2,1)S(1)}, bf16[2,768,384]{2,1,0:T(8,128)(2,1)}) custom-call(s32[2]{0:T(128)S(1)} %pad_add_fusion.ids_ref.refs_0_, bf16[256,384]{1,0:T(8,128)(2,1)S(1)} %get-tuple-element.59.refs_1_.refs_5_, bf16[256,768]{1,0:T(8,128)(2,1)S(1)} %get-tuple-element.43.low_ref.refs_2_, ...), custom_call_target="tpu_custom_call" | custom-call | flops 1024 | bytes 1024 | tf_op jit(solution)/shard_map/pallas_call | solution.py:52
  167.0 1.3 fusion.3
  168.3 2.6 %collective-permute-start.31 = (bf16[2,4,96,384]{3,2,1,0:T(8,128)(2,1)S(1)}, bf16[2,4,96,384]{3,2,1,0:T(8,128)(2,1)S(1)}, u32[]{:S(2)}, u32[]{:S(2)}) collective-permute-start(bf16[2,4,96,384]{3,2,1,0:T(8,128)(2,1)S(1)} %fusion.3), channel_id=1, source_target_pairs={{0,1},{1,0},{2,3},{3,2},{4,5},{5,4},{6,7},{7,6},{8,9},{9,8},{10,11... | collective-permute-start | bytes 1769480 | tf_op jit(solution)/shard_map/ppermute | solution.py:286
  172.2 4.7 %all-to-all-start.3 = ((bf16[8,96,512]{2,1,0:T(8,128)(2,1)}), bf16[8,96,512]{2,1,0:T(8,128)(2,1)S(1)}, u32[]{:S(2)}, u32[]{:S(2)}) async-start(bf16[8,96,512]{2,1,0:T(8,128)(2,1)} %bitcast.48), calls=%async_computation.3 | async-start | bytes 1572864 | tf_op jit(solution)/shard_map/all_to_all | solution.py:308
  178.7 1.4 fusion.11
  180.0 9.9 %collective-permute-done.31 = bf16[2,4,96,384]{3,2,1,0:T(8,128)(2,1)S(1)} collective-permute-done((bf16[2,4,96,384]{3,2,1,0:T(8,128)(2,1)S(1)}, bf16[2,4,96,384]{3,2,1,0:T(8,128)(2,1)S(1)}, u32[]{:S(2)}, u32[]{:S(2)}) %collective-permute-start.31) | collective-permute-done | bytes 589856 | tf_op jit(solution)/shard_map/ppermute | solution.py:286
  191.9 2.5 %collective-permute-done.28 = bf16[768,384]{1,0:T(8,128)(2,1)S(1)} collective-permute-done((bf16[768,384]{1,0:T(8,128)(2,1)S(1)}, bf16[768,384]{1,0:T(8,128)(2,1)S(1)}, u32[]{:S(2)}, u32[]{:S(2)}) %collective-permute-start.28) | collective-permute-done | bytes 589856 | tf_op jit(solution)/shard_map/ppermute | solution.py:286
  194.5 1.4 collective-permute-start.29
  195.9 3.2 %collective-permute-done.32 = bf16[4,96,384]{2,1,0:T(8,128)(2,1)S(1)} collective-permute-done((bf16[4,96,384]{2,1,0:T(8,128)(2,1)S(1)}, bf16[4,96,384]{2,1,0:T(8,128)(2,1)S(1)}, u32[]{:S(2)}, u32[]{:S(2)}) %collective-permute-start.32) | collective-permute-done | bytes 294944 | tf_op jit(solution)/shard_map/ppermute | solution.py:286
  199.3 2.0 collective-permute-done.29
  202.3 4.5 %all-to-all-start.2 = ((bf16[4,96,768]{2,1,0:T(8,128)(2,1)}), bf16[4,96,768]{2,1,0:T(8,128)(2,1)S(1)}, u32[]{:S(2)}, u32[]{:S(2)}) async-start(bf16[4,96,768]{2,1,0:T(8,128)(2,1)} %pad_maximum_fusion), calls=%async_computation.2 | async-start | bytes 1179648 | tf_op jit(solution)/shard_map/all_to_all | solution.py:342
  207.6 12.1 %all-to-all-done.2 = bf16[4,96,768]{2,1,0:T(8,128)(2,1)S(1)} async-done(((bf16[4,96,768]{2,1,0:T(8,128)(2,1)}), bf16[4,96,768]{2,1,0:T(8,128)(2,1)S(1)}, u32[]{:S(2)}, u32[]{:S(2)}) %all-to-all-start.2) | async-done | bytes 589856 | tf_op jit(solution)/shard_map/all_to_all | solution.py:342
  (123 shorter events, 32.4 us)
Async XLA Ops:
  0.6 17.4 %collective-permute-start.1 = (bf16[2048,768]{1,0:T(8,128)(2,1)}, bf16[2048,768]{1,0:T(8,128)(2,1)}, u32[]{:S(2)}, u32[]{:S(2)}) collective-permute-start(bf16[2048,768]{1,0:T(8,128)(2,1)} %refs_2_.1), channel_id=1, source_target_pairs={{0,8},{8,0},{16,24},{24,16},{1,9},{9,1},{17,25},{25,17},{2,10},{10... | collective-permute-start | bytes 9437192 | tf_op jit(solution)/shard_map/ppermute | solution.py:286
  3.6 12.5 %collective-permute-start.3 = (bf16[512,384]{1,0:T(8,128)(2,1)S(1)}, bf16[512,384]{1,0:T(8,128)(2,1)S(1)}, u32[]{:S(2)}, u32[]{:S(2)}) collective-permute-start(bf16[512,384]{1,0:T(8,128)(2,1)S(1)} %get-tuple-element.76), channel_id=1, source_target_pairs={{0,16},{8,24},{16,0},{24,8},{1,17},{9,25},{17,1},{25,9},{2,18},{10... | collective-permute-start | bytes 1179656 | tf_op jit(solution)/shard_map/ppermute | solution.py:286
  6.1 22.2 %collective-permute-start = (bf16[512,384]{1,0:T(8,128)(2,1)}, bf16[512,384]{1,0:T(8,128)(2,1)S(1)}, u32[]{:S(2)}, u32[]{:S(2)}) collective-permute-start(bf16[512,384]{1,0:T(8,128)(2,1)} %get-tuple-element.77), channel_id=1, source_target_pairs={{0,16},{8,24},{16,0},{24,8},{1,17},{9,25},{17,1},{25,9},{2,18},{10... | collective-permute-start | bytes 1179656 | tf_op jit(solution)/shard_map/ppermute | solution.py:286
  6.1 26.8 %collective-permute-start.9 = (bf16[512,384]{1,0:T(8,128)(2,1)}, bf16[512,384]{1,0:T(8,128)(2,1)S(1)}, u32[]{:S(2)}, u32[]{:S(2)}) collective-permute-start(bf16[512,384]{1,0:T(8,128)(2,1)} %get-tuple-element.75), channel_id=1, source_target_pairs={{0,16},{8,24},{16,0},{24,8},{1,17},{9,25},{17,1},{25,9},{2,18},{10... | collective-permute-start | bytes 1179656 | tf_op jit(solution)/shard_map/ppermute | solution.py:286
  16.1 16.9 %collective-permute-start.7 = (bf16[512,384]{1,0:T(8,128)(2,1)S(1)}, bf16[512,384]{1,0:T(8,128)(2,1)S(1)}, u32[]{:S(2)}, u32[]{:S(2)}) collective-permute-start(bf16[512,384]{1,0:T(8,128)(2,1)S(1)} %collective-permute-done.3.refs_5_), channel_id=1, source_target_pairs={{0,1},{1,0},{2,3},{3,2},{4,5},{5,4},{6,7},{7,6},{8,9},{9,8},{10,11... | collective-permute-start | bytes 1179656 | tf_op jit(solution)/shard_map/ppermute | solution.py:286
  28.3 10.2 %collective-permute-start.5 = (bf16[512,384]{1,0:T(8,128)(2,1)S(1)}, bf16[512,384]{1,0:T(8,128)(2,1)}, u32[]{:S(2)}, u32[]{:S(2)}) collective-permute-start(bf16[512,384]{1,0:T(8,128)(2,1)S(1)} %collective-permute-done.refs_3_), channel_id=1, source_target_pairs={{0,1},{1,0},{2,3},{3,2},{4,5},{5,4},{6,7},{7,6},{8,9},{9,8},{10,11... | collective-permute-start | bytes 1179656 | tf_op jit(solution)/shard_map/ppermute | solution.py:286
  28.4 12.7 %collective-permute-start.11 = (bf16[512,384]{1,0:T(8,128)(2,1)}, bf16[512,384]{1,0:T(8,128)(2,1)S(1)}, u32[]{:S(2)}, u32[]{:S(2)}) collective-permute-start(bf16[512,384]{1,0:T(8,128)(2,1)} %get-tuple-element.74), channel_id=1, source_target_pairs={{0,16},{8,24},{16,0},{24,8},{1,17},{9,25},{17,1},{25,9},{2,18},{10... | collective-permute-start | bytes 1179656 | tf_op jit(solution)/shard_map/ppermute | solution.py:286
  30.4 12.5 %collective-permute-start.4 = (bf16[512,384]{1,0:T(8,128)(2,1)S(1)}, bf16[512,384]{1,0:T(8,128)(2,1)}, u32[]{:S(2)}, u32[]{:S(2)}) collective-permute-start(bf16[512,384]{1,0:T(8,128)(2,1)S(1)} %collective-permute-done.3.refs_5_), channel_id=1, source_target_pairs={{0,8},{8,0},{16,24},{24,16},{1,9},{9,1},{17,25},{25,17},{2,10},{10... | collective-permute-start | bytes 1179656 | tf_op jit(solution)/shard_map/ppermute | solution.py:286
  32.9 10.3 %collective-permute-start.2 = (bf16[512,384]{1,0:T(8,128)(2,1)S(1)}, bf16[512,384]{1,0:T(8,128)(2,1)}, u32[]{:S(2)}, u32[]{:S(2)}) collective-permute-start(bf16[512,384]{1,0:T(8,128)(2,1)S(1)} %collective-permute-done.refs_3_), channel_id=1, source_target_pairs={{0,8},{8,0},{16,24},{24,16},{1,9},{9,1},{17,25},{25,17},{2,10},{10... | collective-permute-start | bytes 1179656 | tf_op jit(solution)/shard_map/ppermute | solution.py:286
  32.9 14.2 %collective-permute-start.8 = (bf16[512,384]{1,0:T(8,128)(2,1)S(1)}, bf16[512,384]{1,0:T(8,128)(2,1)}, u32[]{:S(2)}, u32[]{:S(2)}) collective-permute-start(bf16[512,384]{1,0:T(8,128)(2,1)S(1)} %collective-permute-done.7.refs_5_), channel_id=1, source_target_pairs={{0,8},{8,0},{16,24},{24,16},{1,9},{9,1},{17,25},{25,17},{2,10},{10... | collective-permute-start | bytes 1179656 | tf_op jit(solution)/shard_map/ppermute | solution.py:286
  38.4 8.7 %collective-permute-start.6 = (bf16[512,384]{1,0:T(8,128)(2,1)}, bf16[512,384]{1,0:T(8,128)(2,1)}, u32[]{:S(2)}, u32[]{:S(2)}) collective-permute-start(bf16[512,384]{1,0:T(8,128)(2,1)} %collective-permute-done.5.refs_3_), channel_id=1, source_target_pairs={{0,8},{8,0},{16,24},{24,16},{1,9},{9,1},{17,25},{25,17},{2,10},{10... | collective-permute-start | bytes 1179656 | tf_op jit(solution)/shard_map/ppermute | solution.py:286
  41.1 17.4 %collective-permute-start.13 = (bf16[512,384]{1,0:T(8,128)(2,1)S(1)}, bf16[512,384]{1,0:T(8,128)(2,1)}, u32[]{:S(2)}, u32[]{:S(2)}) collective-permute-start(bf16[512,384]{1,0:T(8,128)(2,1)S(1)} %collective-permute-done.9.refs_3_), channel_id=1, source_target_pairs={{0,1},{1,0},{2,3},{3,2},{4,5},{5,4},{6,7},{7,6},{8,9},{9,8},{10,11... | collective-permute-start | bytes 1179656 | tf_op jit(solution)/shard_map/ppermute | solution.py:286
  42.9 18.2 %collective-permute-start.15 = (bf16[512,384]{1,0:T(8,128)(2,1)S(1)}, bf16[512,384]{1,0:T(8,128)(2,1)}, u32[]{:S(2)}, u32[]{:S(2)}) collective-permute-start(bf16[512,384]{1,0:T(8,128)(2,1)S(1)} %collective-permute-done.11.refs_5_), channel_id=1, source_target_pairs={{0,1},{1,0},{2,3},{3,2},{4,5},{5,4},{6,7},{7,6},{8,9},{9,8},{10,11... | collective-permute-start | bytes 1179656 | tf_op jit(solution)/shard_map/ppermute | solution.py:286
  51.9 17.1 %all-to-all-start = ((bf16[8,64,384]{2,1,0:T(8,128)(2,1)}), bf16[8,64,384]{2,1,0:T(8,128)(2,1)S(1)}, u32[]{:S(2)}, u32[]{:S(2)}) async-start(bf16[8,64,384]{2,1,0:T(8,128)(2,1)} %bitcast.14), calls=%async_computation | async-start | bytes 786432 | tf_op jit(solution)/shard_map/all_to_all | solution.py:389
  58.0 3.0 %collective-permute-start.10 = (bf16[512,384]{1,0:T(8,128)(2,1)S(1)}, bf16[512,384]{1,0:T(8,128)(2,1)S(1)}, u32[]{:S(2)}, u32[]{:S(2)}) collective-permute-start(bf16[512,384]{1,0:T(8,128)(2,1)S(1)} %collective-permute-done.9.refs_3_), channel_id=1, source_target_pairs={{0,8},{8,0},{16,24},{24,16},{1,9},{9,1},{17,25},{25,17},{2,10},{10... | collective-permute-start | bytes 1179656 | tf_op jit(solution)/shard_map/ppermute | solution.py:286
  58.1 3.0 %collective-permute-start.12 = (bf16[512,384]{1,0:T(8,128)(2,1)S(1)}, bf16[512,384]{1,0:T(8,128)(2,1)S(1)}, u32[]{:S(2)}, u32[]{:S(2)}) collective-permute-start(bf16[512,384]{1,0:T(8,128)(2,1)S(1)} %collective-permute-done.11.refs_5_), channel_id=1, source_target_pairs={{0,8},{8,0},{16,24},{24,16},{1,9},{9,1},{17,25},{25,17},{2,10},{10... | collective-permute-start | bytes 1179656 | tf_op jit(solution)/shard_map/ppermute | solution.py:286
  58.6 6.7 %collective-permute-start.14 = (bf16[512,384]{1,0:T(8,128)(2,1)}, bf16[512,384]{1,0:T(8,128)(2,1)S(1)}, u32[]{:S(2)}, u32[]{:S(2)}) collective-permute-start(bf16[512,384]{1,0:T(8,128)(2,1)} %collective-permute-done.13.refs_3_), channel_id=1, source_target_pairs={{0,8},{8,0},{16,24},{24,16},{1,9},{9,1},{17,25},{25,17},{2,10},{10... | collective-permute-start | bytes 1179656 | tf_op jit(solution)/shard_map/ppermute | solution.py:286
  61.1 5.0 %collective-permute-start.16 = (bf16[512,384]{1,0:T(8,128)(2,1)}, bf16[512,384]{1,0:T(8,128)(2,1)S(1)}, u32[]{:S(2)}, u32[]{:S(2)}) collective-permute-start(bf16[512,384]{1,0:T(8,128)(2,1)} %collective-permute-done.15.refs_5_), channel_id=1, source_target_pairs={{0,8},{8,0},{16,24},{24,16},{1,9},{9,1},{17,25},{25,17},{2,10},{10... | collective-permute-start | bytes 1179656 | tf_op jit(solution)/shard_map/ppermute | solution.py:286
  73.9 11.9 %copy-start.25 = (s32[1,8,8]{2,1,0:T(8,128)S(1)}, s32[1,8,8]{2,1,0:T(8,128)}, u32[]{:S(2)}) copy-start(s32[1,8,8]{2,1,0:T(8,128)} %param.11) | copy-start | bytes 772
  73.9 23.6 %copy-start = (bf16[2,3,768,384]{3,2,1,0:T(8,128)(2,1)S(1)}, bf16[2,3,768,384]{3,2,1,0:T(8,128)(2,1)}, u32[]{:S(2)}) copy-start(bf16[2,3,768,384]{3,2,1,0:T(8,128)(2,1)} %refs_7_.3) | copy-start | bytes 10616836
  78.8 18.8 %all-to-all-start.1 = ((bf16[8,64,384]{2,1,0:T(8,128)(2,1)}), bf16[8,64,384]{2,1,0:T(8,128)(2,1)}, u32[]{:S(2)}, u32[]{:S(2)}) async-start(bf16[8,64,384]{2,1,0:T(8,128)(2,1)} %bitcast.102), calls=%async_computation.1 | async-start | bytes 786432 | tf_op jit(solution)/shard_map/all_to_all | solution.py:389
  100.7 11.3 %collective-permute-start.17 = (bf16[256,384]{1,0:T(8,128)(2,1)S(1)}, bf16[256,384]{1,0:T(8,128)(2,1)S(1)}, u32[]{:S(2)}, u32[]{:S(2)}) collective-permute-start(bf16[256,384]{1,0:T(8,128)(2,1)S(1)} %get-tuple-element.41), channel_id=1, source_target_pairs={{0,1},{1,2},{2,3},{3,4},{4,5},{5,6},{6,7},{8,9},{9,10},{10,11},{11... | collective-permute-start | bytes 589832 | tf_op jit(solution)/shard_map/ppermute | solution.py:293
  104.1 7.9 %collective-permute-start.18 = (bf16[256,384]{1,0:T(8,128)(2,1)S(1)}, bf16[256,384]{1,0:T(8,128)(2,1)S(1)}, u32[]{:S(2)}, u32[]{:S(2)}) collective-permute-start(bf16[256,384]{1,0:T(8,128)(2,1)S(1)} %get-tuple-element.42), channel_id=1, source_target_pairs={{1,0},{2,1},{3,2},{4,3},{5,4},{6,5},{7,6},{9,8},{10,9},{11,10},{12... | collective-permute-start | bytes 589832 | tf_op jit(solution)/shard_map/ppermute | solution.py:294
  105.5 6.5 %copy-start.1 = (bf16[2,384,768]{2,1,0:T(8,128)(2,1)S(1)}, bf16[2,384,768]{2,1,0:T(8,128)(2,1)}, u32[]{:S(2)}) copy-start(bf16[2,384,768]{2,1,0:T(8,128)(2,1)} %refs_8_.3) | copy-start | bytes 3538948
  112.0 11.9 %copy-start.8 = (bf16[768,2048]{1,0:T(8,128)(2,1)S(1)}, bf16[768,2048]{1,0:T(8,128)(2,1)}, u32[]{:S(2)}) copy-start(bf16[768,2048]{1,0:T(8,128)(2,1)} %refs_8_.2) | copy-start | bytes 9437188
  112.0 11.9 %copy-start.14 = (s32[1,128,2048]{2,1,0:T(8,128)S(1)}, s32[1,128,2048]{2,1,0:T(8,128)}, u32[]{:S(2)}) copy-start(s32[1,128,2048]{2,1,0:T(8,128)} %param.13) | copy-start | bytes 3145732
  112.9 6.7 %collective-permute-start.19 = (bf16[128,384]{1,0:T(8,128)(2,1)S(1)}, bf16[128,384]{1,0:T(8,128)(2,1)S(1)}, u32[]{:S(2)}, u32[]{:S(2)}) collective-permute-start(bf16[128,384]{1,0:T(8,128)(2,1)S(1)} %get-tuple-element.46), channel_id=1, source_target_pairs={{0,1},{1,2},{2,3},{3,4},{4,5},{5,6},{6,7},{8,9},{9,10},{10,11},{11... | collective-permute-start | bytes 294920 | tf_op jit(solution)/shard_map/ppermute | solution.py:293
  117.4 6.5 %collective-permute-start.20 = (bf16[128,384]{1,0:T(8,128)(2,1)S(1)}, bf16[128,384]{1,0:T(8,128)(2,1)S(1)}, u32[]{:S(2)}, u32[]{:S(2)}) collective-permute-start(bf16[128,384]{1,0:T(8,128)(2,1)S(1)} %get-tuple-element.49), channel_id=1, source_target_pairs={{1,0},{2,1},{3,2},{4,3},{5,4},{6,5},{7,6},{9,8},{10,9},{11,10},{12... | collective-permute-start | bytes 294920 | tf_op jit(solution)/shard_map/ppermute | solution.py:294
  129.2 3.5 %collective-permute-start.21 = (bf16[2,768,512]{2,1,0:T(8,128)(2,1)S(1)}, bf16[2,768,512]{2,1,0:T(8,128)(2,1)S(1)}, u32[]{:S(2)}, u32[]{:S(2)}) collective-permute-start(bf16[2,768,512]{2,1,0:T(8,128)(2,1)S(1)} %get-tuple-element.54), channel_id=1, source_target_pairs={{0,8},{8,0},{16,24},{24,16},{1,9},{9,1},{17,25},{25,17},{2,10},{10... | collective-permute-start | bytes 4718600 | tf_op jit(solution)/shard_map/ppermute | solution.py:286
  132.6 12.3 %copy-start.19 = (bf16[2,768,512]{2,1,0:T(8,128)(2,1)}, bf16[2,768,512]{2,1,0:T(8,128)(2,1)S(1)}, u32[]{:S(2)}) copy-start(bf16[2,768,512]{2,1,0:T(8,128)(2,1)S(1)} %collective-permute-done.21) | copy-start | bytes 4718596
  132.9 31.4 %collective-permute-start.26 = (bf16[768,512]{1,0:T(8,128)(2,1)S(1)}, bf16[768,512]{1,0:T(8,128)(2,1)S(1)}, u32[]{:S(2)}, u32[]{:S(2)}) collective-permute-start(bf16[768,512]{1,0:T(8,128)(2,1)S(1)} %fusion.1.refs_0_), channel_id=1, source_target_pairs={{0,16},{8,24},{16,0},{24,8},{1,17},{9,25},{17,1},{25,9},{2,18},{10... | collective-permute-start | bytes 2359304 | tf_op jit(solution)/shard_map/ppermute | solution.py:286
  134.4 6.2 %collective-permute-start.22 = (bf16[128,384]{1,0:T(8,128)(2,1)S(1)}, bf16[128,384]{1,0:T(8,128)(2,1)S(1)}, u32[]{:S(2)}, u32[]{:S(2)}) collective-permute-start(bf16[128,384]{1,0:T(8,128)(2,1)S(1)} %get-tuple-element.55.refs_3_.refs_6_), channel_id=1, source_target_pairs={{0,1},{1,2},{2,3},{3,4},{4,5},{5,6},{6,7},{8,9},{9,10},{10,11},{11... | collective-permute-start | bytes 294920 | tf_op jit(solution)/shard_map/ppermute | solution.py:293
  138.4 6.5 %collective-permute-start.23 = (bf16[128,384]{1,0:T(8,128)(2,1)S(1)}, bf16[128,384]{1,0:T(8,128)(2,1)S(1)}, u32[]{:S(2)}, u32[]{:S(2)}) collective-permute-start(bf16[128,384]{1,0:T(8,128)(2,1)S(1)} %get-tuple-element.56.refs_2_.refs_5_), channel_id=1, source_target_pairs={{1,0},{2,1},{3,2},{4,3},{5,4},{6,5},{7,6},{9,8},{10,9},{11,10},{12... | collective-permute-start | bytes 294920 | tf_op jit(solution)/shard_map/ppermute | solution.py:294
  144.9 6.8 %copy-start.3 = (bf16[2,384,768]{2,1,0:T(8,128)(2,1)S(1)}, bf16[2,384,768]{2,1,0:T(8,128)(2,1)}, u32[]{:S(2)}) copy-start(bf16[2,384,768]{2,1,0:T(8,128)(2,1)} %constant.122.clone.refs_10_) | copy-start | bytes 3538948
  144.9 6.8 %copy-start.4 = (bf16[2,768,384]{2,1,0:T(8,128)(2,1)S(1)}, bf16[2,768,384]{2,1,0:T(8,128)(2,1)}, u32[]{:S(2)}) copy-start(bf16[2,768,384]{2,1,0:T(8,128)(2,1)} %constant.123.clone.refs_11_) | copy-start | bytes 3538948
  147.4 8.6 %collective-permute-start.24 = (bf16[256,384]{1,0:T(8,128)(2,1)S(1)}, bf16[256,384]{1,0:T(8,128)(2,1)S(1)}, u32[]{:S(2)}, u32[]{:S(2)}) collective-permute-start(bf16[256,384]{1,0:T(8,128)(2,1)S(1)} %get-tuple-element.60.refs_6_), channel_id=1, source_target_pairs={{0,1},{1,2},{2,3},{3,4},{4,5},{5,6},{6,7},{8,9},{9,10},{10,11},{11... | collective-permute-start | bytes 589832 | tf_op jit(solution)/shard_map/ppermute | solution.py:293
  150.4 7.6 %collective-permute-start.25 = (bf16[256,384]{1,0:T(8,128)(2,1)S(1)}, bf16[256,384]{1,0:T(8,128)(2,1)S(1)}, u32[]{:S(2)}, u32[]{:S(2)}) collective-permute-start(bf16[256,384]{1,0:T(8,128)(2,1)S(1)} %get-tuple-element.59.refs_1_.refs_5_), channel_id=1, source_target_pairs={{1,0},{2,1},{3,2},{4,3},{5,4},{6,5},{7,6},{9,8},{10,9},{11,10},{12... | collective-permute-start | bytes 589832 | tf_op jit(solution)/shard_map/ppermute | solution.py:294
  158.0 9.0 %collective-permute-start.30 = (bf16[2,768,384]{2,1,0:T(8,128)(2,1)S(1)}, bf16[2,768,384]{2,1,0:T(8,128)(2,1)}, u32[]{:S(2)}, u32[]{:S(2)}) collective-permute-start(bf16[2,768,384]{2,1,0:T(8,128)(2,1)S(1)} %get-tuple-element.71), channel_id=1, source_target_pairs={{0,8},{8,0},{16,24},{24,16},{1,9},{9,1},{17,25},{25,17},{2,10},{10... | collective-permute-start | bytes 3538952 | tf_op jit(solution)/shard_map/ppermute | solution.py:286
  165.2 11.6 %collective-permute-start.27 = (bf16[2,768,384]{2,1,0:T(8,128)(2,1)}, bf16[2,768,384]{2,1,0:T(8,128)(2,1)}, u32[]{:S(2)}, u32[]{:S(2)}) collective-permute-start(bf16[2,768,384]{2,1,0:T(8,128)(2,1)} %get-tuple-element.69), channel_id=1, source_target_pairs={{0,8},{8,0},{16,24},{24,16},{1,9},{9,1},{17,25},{25,17},{2,10},{10... | collective-permute-start | bytes 3538952 | tf_op jit(solution)/shard_map/ppermute | solution.py:286
  165.8 5.2 %copy-start.24 = (bf16[768,512]{1,0:T(8,128)(2,1)S(1)}, bf16[768,512]{1,0:T(8,128)(2,1)}, u32[]{:S(2)}) copy-start(bf16[768,512]{1,0:T(8,128)(2,1)} %copy-done.23) | copy-start | bytes 2359300
  168.3 21.6 %collective-permute-start.31 = (bf16[2,4,96,384]{3,2,1,0:T(8,128)(2,1)S(1)}, bf16[2,4,96,384]{3,2,1,0:T(8,128)(2,1)S(1)}, u32[]{:S(2)}, u32[]{:S(2)}) collective-permute-start(bf16[2,4,96,384]{3,2,1,0:T(8,128)(2,1)S(1)} %fusion.3), channel_id=1, source_target_pairs={{0,1},{1,0},{2,3},{3,2},{4,5},{5,4},{6,7},{7,6},{8,9},{9,8},{10,11... | collective-permute-start | bytes 1769480 | tf_op jit(solution)/shard_map/ppermute | solution.py:286
  172.2 30.2 %all-to-all-start.3 = ((bf16[8,96,512]{2,1,0:T(8,128)(2,1)}), bf16[8,96,512]{2,1,0:T(8,128)(2,1)S(1)}, u32[]{:S(2)}, u32[]{:S(2)}) async-start(bf16[8,96,512]{2,1,0:T(8,128)(2,1)} %bitcast.48), calls=%async_computation.3 | async-start | bytes 1572864 | tf_op jit(solution)/shard_map/all_to_all | solution.py:308
  178.1 11.8 %copy-start.22 = (bf16[1,768,384]{2,1,0:T(8,128)(2,1)S(1)}, bf16[1,768,384]{2,1,0:T(8,128)(2,1)}, u32[]{:S(2)}) copy-start(bf16[1,768,384]{2,1,0:T(8,128)(2,1)} %get-tuple-element.79) | copy-start | bytes 1769476
  178.1 16.3 %collective-permute-start.28 = (bf16[768,384]{1,0:T(8,128)(2,1)S(1)}, bf16[768,384]{1,0:T(8,128)(2,1)S(1)}, u32[]{:S(2)}, u32[]{:S(2)}) collective-permute-start(bf16[768,384]{1,0:T(8,128)(2,1)S(1)} %fusion.2), channel_id=1, source_target_pairs={{0,16},{8,24},{16,0},{24,8},{1,17},{9,25},{17,1},{25,9},{2,18},{10... | collective-permute-start | bytes 1769480 | tf_op jit(solution)/shard_map/ppermute | solution.py:286
  190.0 9.1 %collective-permute-start.32 = (bf16[4,96,384]{2,1,0:T(8,128)(2,1)S(1)}, bf16[4,96,384]{2,1,0:T(8,128)(2,1)S(1)}, u32[]{:S(2)}, u32[]{:S(2)}) collective-permute-start(bf16[4,96,384]{2,1,0:T(8,128)(2,1)S(1)} %fusion.4), channel_id=1, source_target_pairs={{0,16},{8,24},{16,0},{24,8},{1,17},{9,25},{17,1},{25,9},{2,18},{10... | collective-permute-start | bytes 884744 | tf_op jit(solution)/shard_map/ppermute | solution.py:286
  190.7 8.5 %copy-start.21 = (bf16[1,768,384]{2,1,0:T(8,128)(2,1)S(1)}, bf16[1,768,384]{2,1,0:T(8,128)(2,1)}, u32[]{:S(2)}) copy-start(bf16[1,768,384]{2,1,0:T(8,128)(2,1)} %get-tuple-element.78) | copy-start | bytes 1769476
  194.5 6.8 %collective-permute-start.29 = (bf16[4,96,384]{2,1,0:T(8,128)(2,1)S(1)}, bf16[4,96,384]{2,1,0:T(8,128)(2,1)S(1)}, u32[]{:S(2)}, u32[]{:S(2)}) collective-permute-start(bf16[4,96,384]{2,1,0:T(8,128)(2,1)S(1)} %fusion.8), channel_id=1, source_target_pairs={{0,1},{1,0},{2,3},{3,2},{4,5},{5,4},{6,7},{7,6},{8,9},{9,8},{10,11... | collective-permute-start | bytes 884744 | tf_op jit(solution)/shard_map/ppermute | solution.py:286
  202.3 17.4 %all-to-all-start.2 = ((bf16[4,96,768]{2,1,0:T(8,128)(2,1)}), bf16[4,96,768]{2,1,0:T(8,128)(2,1)S(1)}, u32[]{:S(2)}, u32[]{:S(2)}) async-start(bf16[4,96,768]{2,1,0:T(8,128)(2,1)} %pad_maximum_fusion), calls=%async_computation.2 | async-start | bytes 1179648 | tf_op jit(solution)/shard_map/all_to_all | solution.py:342
  (15 other events, 24.6 us)

commit v5 on v4

--- a/solution.py
+++ b/solution.py
@@ -108,7 +108,7 @@
         in_specs=[SMEM, HBM] + ([] if first else [VMEM]) + [HBM if first else VMEM] * count + [ANY] * len(after),
         out_specs=VMEM,
         scratch_shapes=scratch,
-        compiler_params=params(49),
+        compiler_params=params(20 if first else 14),
         cost_estimate=CHEAP,
     )(jnp.stack(starts).astype(jnp.int32), rows, *([] if first else [total]), *weights, *after)
 
@@ -281,6 +281,19 @@
         out[...] = (spread_inner * slope).astype(BF)
 
 
+def output_body(parts_ref, kernels_ref, mixers_ref):
+    total = parts_ref[0].astype(F32)
+    for g in range(1, parts_ref.shape[0]):
+        total = total + parts_ref[g].astype(F32)
+    cut, per = kernels_ref.shape[3], mixers_ref.shape[1]
+    for n in range(2):
+        start = 4 * n * cut
+        for t in range(3):
+            kernels_ref[n, t] = total[:, start + t * cut : start + (t + 1) * cut]
+        tail = total[:, start + 3 * cut : start + 4 * cut]
+        mixers_ref[n] = jnp.concatenate([tail[:per], tail[per:]], axis=1)
+
+
 def swap(value, axis, bit):
     size = lax.axis_size(axis)
     return lax.ppermute(value, axis, [(i, i ^ bit) for i in range(size)])
@@ -302,13 +315,12 @@
     return here, away
 
 
-def seq_sum(total):
+def seq_parts(total):
     groups = lax.axis_size("seq")
     rows, columns = total.shape
-    parts = lax.all_to_all(
+    return lax.all_to_all(
         total.reshape(groups, rows // groups, columns), "seq", split_axis=0, concat_axis=0, tiled=True
     )
-    return parts.astype(F32).sum(axis=0)
 
 
 def side_rows(value, side):
@@ -318,12 +330,14 @@
     return lax.dynamic_index_in_dim(value, side, axis=len(blocks) + 1, keepdims=False).astype(F32)
 
 
-def crossed_sums(left_keep, left_send, right_keep, right_send):
+def crossed_sums(left_keep, left_send, right_keep, right_send, first, first_came):
     groups = lax.axis_size("seq")
     side = lax.axis_index("seq") % 2
     right_came = swap(right_send, "dp", 1)
     left_came = swap(left_send, "dp", 1)
-    x_came = swap((left_keep[1].astype(F32) + left_came[1].astype(F32)).astype(BF), "dp", 2)
+    left_away = (left_keep[1].astype(F32) + left_came[1].astype(F32)).astype(BF)
+    left_away, first_came = lax.optimization_barrier((left_away, first_came))
+    x_came = swap(left_away, "dp", 2)
     other = side_rows(right_keep, 1 - side) + side_rows(right_came, 1 - side)
     side_came = swap(other.astype(BF), "seq", 1)
 
@@ -338,10 +352,11 @@
     left = left_half(side) + left.astype(F32)
     right = right_half(0) + right.astype(F32)
     both = jnp.concatenate([left, right], axis=2).astype(BF)
+    first = seq_parts((first + first_came.astype(F32)).astype(BF))
+    both, first = lax.optimization_barrier((both, first))
     lines = [list(range(start, groups, 2)) for start in range(2)]
     parts = lax.all_to_all(both, "seq", split_axis=0, concat_axis=0, axis_index_groups=lines, tiled=True)
-    total = parts.astype(F32).sum(axis=0)
-    return total[:, : left.shape[2]], total[:, left.shape[2] :]
+    return parts, first.astype(F32).sum(axis=0)
 
 
 def shards(embeddings, layout, lengths, targets, projection, kernels, mixers, readout):
@@ -370,26 +385,27 @@
     ]
     near, away = (me ^ 2) * depth, (me ^ 3) * depth
     total = absorb(None, 0, rows, [projection, from_core], [me * depth, (me ^ 1) * depth], False)
-    received = []
+    weights, starts = [], []
     for n in range(2):
-        far_weights, far_starts, side_weights, side_starts = [], [], [], []
         for i in range(2):
             held = far[n][i]
             if n == 0 and i == 0:
                 held, total = lax.optimization_barrier((held, total))
             crossed = swap(held, "seq", 1)
             at, side_at = side * share + i * piece, (1 - side) * share + i * piece
-            far_weights += [held, swap(held, "dp", 1)]
-            far_starts += [near + at, away + at]
-            side_weights += [crossed, swap(crossed, "dp", 1)]
-            side_starts += [near + side_at, away + side_at]
-        sums = absorb(total, n * columns, rows, far_weights, far_starts, False)
-        sums = absorb(sums, 0, rows, side_weights, side_starts, True, received)
-        received.append(
-            lax.all_to_all(
-                sums.reshape(groups, block, columns), "seq", split_axis=0, concat_axis=0, tiled=True
-            ).reshape(row_count, columns)
-        )
+            weights.append([held, swap(held, "dp", 1), crossed, swap(crossed, "dp", 1)])
+            starts.append([near + at, away + at, near + side_at, away + side_at])
+
+    def send(sums):
+        return lax.all_to_all(
+            sums.reshape(groups, block, columns), "seq", split_axis=0, concat_axis=0, tiled=True
+        ).reshape(row_count, columns)
+
+    left = send(absorb(total, 0, rows, weights[0] + weights[1], starts[0] + starts[1], True, [weights[2][2]]))
+    right = absorb(
+        total, columns, rows, weights[2] + weights[3][:2], starts[2] + starts[3][:2], False
+    )
+    right = send(absorb(right, 0, rows, weights[3][2:], starts[3][2:], True, [left]))
 
     column = lax.dynamic_index_in_dim(layout[0], device, axis=1, keepdims=True)
     position = column * block + jnp.arange(block, dtype=jnp.int32)[None, :]
@@ -397,7 +413,7 @@
     target = jnp.where(device * row_count + position < length, slot, -1).reshape(1, row_count)
 
     hidden, low, high, down, up = call(
-        place_body, (target, *received, kernels),
+        place_body, (target, left, right, kernels),
         [((row_count, channels), BF), ((half, channels), BF), ((half, channels), BF),
          ((half, width), BF), ((half, width), BF)],
         24,
@@ -431,6 +447,7 @@
         24, smem=1,
     )
     track_here, track_away = core_sum(track_keep, track_send)
+    track_away, gprev, gnext = lax.optimization_barrier((track_away, gprev, gnext))
 
     per = width // groups
     fold = np.zeros((2, width, channels), ml_dtypes.bfloat16)
@@ -468,16 +485,13 @@
         32, smem=1, after=1,
     )
     fine_send, track_x = lax.optimization_barrier((fine_send, track_x))
-    readout_total = seq_sum((track_here + track_x.astype(F32)).astype(BF))
-    fine_total, coarse_total = crossed_sums(fine_keep, fine_send, coarse_keep, coarse_send)
-
+    both, readout_total = crossed_sums(fine_keep, fine_send, coarse_keep, coarse_send, track_here, track_x)
     cut = width // windows
-    kernel_rows, mixer_rows = [], []
-    for value in (fine_total, coarse_total):
-        kernel_rows.append(jnp.stack([value[:, t * cut : (t + 1) * cut] for t in range(3)]))
-        tail = value[:, 3 * cut :]
-        mixer_rows.append(jnp.concatenate([tail[:per], tail[per:]], axis=1))
-    return (jnp.stack(kernel_rows), jnp.stack(mixer_rows), readout_total, trunk[None])
+    kernel_total, mixer_total = call(
+        output_body, (both,),
+        [((2, 3, channels // groups, cut), F32), ((2, per, 2 * cut), F32)], 16,
+    )
+    return (kernel_total, mixer_total, readout_total, trunk[None])
 
 
 def solution(mesh):

time: 223 us -> 234 us (1.049)
  local copies, waits for them, and re-layouts: 18.4 us -> 33.1 us
  Pallas kernels: 46.6 us -> 44.2 us
    unnamed x52 -> x60, local copies, waits for them, and re-layouts: 11.9 us -> 26.5 us
    pallas_call x5 -> x4, Pallas kernels: 24.4 us -> 21.3 us  [absorb(): pl.pallas_call(body, out_shape=jax.ShapeDtypeStruct((row_count, columns),...]
    all_to_all x3, waiting for transfers between devices: 13.6 us -> 11.1 us  [the longest x2 11.1 us: send(): lax.all_to_all(sums.reshape(groups, block, columns), 'seq', split_axis=0,...]
    ppermute x25, waiting for transfers between devices: 41.6 us -> 44 us  [swap(): return lax.ppermute(value, axis, [(i, i ^ bit) for i in range(size)])]
    pallas_call x8 -> x9, Pallas kernels: 22.2 us -> 22.8 us  [call(): pl.pallas_call(body, out_shape=outs, in_specs=[SMEM] * smem + [ANY] * aft...]
  transfers between devices with their start and end apart: 37 -> 37, of which waited for: 19 -> 17; matrix products, arithmetic and copies ran while one was open for 6% -> 7% of each run, Pallas kernels for 15% -> 14%
where the time goes in v5:
time: 234 us; the launch traced here: 233 us
  waiting for transfers between devices  85.1 us (36%)
  starting transfers between devices  59.6 us (25%)
  Pallas kernels  44.2 us (19%)
  local copies, waits for them, and re-layouts  33.1 us (14%)
  other arithmetic  9.48 us (4%)
    ppermute x25, waiting for transfers between devices, swap(): return lax.ppermute(value, axis, [(i, i ^ bit) for i in range(size)])  44 us
    unnamed x60, local copies, waits for them, and re-layouts  26.5 us
    pallas_call x9, Pallas kernels, call(): pl.pallas_call(body, out_shape=outs, in_specs=[SMEM] * smem + [ANY] * aft...  22.8 us
    pallas_call x4, Pallas kernels, absorb(): pl.pallas_call(body, out_shape=jax.ShapeDtypeStruct((row_count, columns),...  21.3 us
    ppermute x25, starting transfers between devices, swap(): return lax.ppermute(value, axis, [(i, i ^ bit) for i in range(size)])  18.8 us
    ppermute x4, starting transfers between devices, halo(): lax.ppermute(high, 'seq', up)  15.1 us
    all_to_all x1, waiting for transfers between devices, crossed_sums(): lax.all_to_all(both, 'seq', split_axis=0, concat_axis=0, axis_index_group...  12 us
    all_to_all x2, waiting for transfers between devices, send(): lax.all_to_all(sums.reshape(groups, block, columns), 'seq', split_axis=0,...  11.1 us
  transfers between devices with their start and end apart: 37, of which 17 were waited for; matrix products, arithmetic and copies ran while one was open for 7% of the time, Pallas kernels for 14%

profile of v5, /device:TPU:0, one launch (start us, length us, event | category | flops | bytes accessed | tf_op | source)
XLA Modules:
  0.0 233.1 jit_solution(17087263101702323625)
XLA Ops:
  1.1 2.5 %fusion.9 = (bf16[512,384]{1,0:T(8,128)(2,1)}, bf16[512,384]{1,0:T(8,128)(2,1)}, bf16[512,384]{1,0:T(8,128)(2,1)}, bf16[512,384]{1,0:T(8,128)(2,1)}) fusion(bf16[2048,768]{1,0:T(8,128)(2,1)} %refs_2_.1, s32[]{:T(128)S(6)} %add.279, s32[]{:T(128)S(6)} %add.280, s32[]{:T(128)S(6)} %select_n.98), kind=kLoop, calls=%fused_computation.41 | loop fusion | bytes 3145740 | tf_op jit(solution)/shard_map/slice | solution.py:383
  3.7 2.5 %collective-permute-start.5 = (bf16[512,384]{1,0:T(8,128)(2,1)}, bf16[512,384]{1,0:T(8,128)(2,1)}, u32[]{:S(2)}, u32[]{:S(2)}) collective-permute-start(bf16[512,384]{1,0:T(8,128)(2,1)} %get-tuple-element.94), channel_id=1, source_target_pairs={{0,16},{8,24},{16,0},{24,8},{1,17},{9,25},{17,1},{25,9},{2,18},{10... | collective-permute-start | bytes 1179656 | tf_op jit(solution)/shard_map/ppermute | solution.py:299
  6.2 2.0 collective-permute-start.9
  8.4 8.1 %collective-permute-done.5.refs_7_ = bf16[512,384]{1,0:T(8,128)(2,1)} collective-permute-done((bf16[512,384]{1,0:T(8,128)(2,1)}, bf16[512,384]{1,0:T(8,128)(2,1)}, u32[]{:S(2)}, u32[]{:S(2)}) %collective-permute-start.5) | collective-permute-done | bytes 393248 | tf_op jit(solution)/shard_map/ppermute | solution.py:299
  16.5 2.0 collective-permute-start.7
  18.5 1.6 copy-done.13
  20.1 3.4 %copy-done = bf16[1,1,512,8192]{3,2,1,0:T(8,128)(2,1)S(1)} copy-done((bf16[1,1,512,8192]{3,2,1,0:T(8,128)(2,1)S(1)}, bf16[1,1,512,8192]{3,2,1,0:T(8,128)(2,1)}, u32[]{:S(2)}) %copy-start) | copy-done | bytes 8388632
  23.5 1.9 copy-done.6
  25.4 1.9 copy-done.14
  27.3 8.3 %shard_map.129.refs_2_ = f32[512,768]{1,0:T(8,128)S(1)} custom-call(s32[2]{0:T(128)S(1)} %pad_add_fusion.2.refs_0_, bf16[512,8192]{1,0:T(8,128)(2,1)S(1)} %bitcast.85, bf16[2048,768]{1,0:T(8,128)(2,1)S(1)} %copy-done.6, bf16[2048,768]{1,0:T(8,128)(2,1)S(1)} %copy-done.14), custom_call_target="tpu_custom_call" | custom-call | flops 1024 | bytes 1024 | tf_op jit(solution)/shard_map/pallas_call | solution.py:105
  35.7 1.9 collective-permute-start.10
  37.9 3.7 %collective-permute-done.13.refs_7_ = bf16[512,384]{1,0:T(8,128)(2,1)} collective-permute-done((bf16[512,384]{1,0:T(8,128)(2,1)}, bf16[512,384]{1,0:T(8,128)(2,1)}, u32[]{:S(2)}, u32[]{:S(2)}) %collective-permute-start.13) | collective-permute-done | bytes 393248 | tf_op jit(solution)/shard_map/ppermute | solution.py:299
  41.5 6.3 %collective-permute-done.3.refs_5_ = bf16[512,384]{1,0:T(8,128)(2,1)S(1)} collective-permute-done((bf16[512,384]{1,0:T(8,128)(2,1)}, bf16[512,384]{1,0:T(8,128)(2,1)S(1)}, u32[]{:S(2)}, u32[]{:S(2)}) %collective-permute-start.3) | collective-permute-done | bytes 393248 | tf_op jit(solution)/shard_map/ppermute | solution.py:299
  48.0 8.3 %collective-permute-done.10.refs_11_.refs_5_ = bf16[512,384]{1,0:T(8,128)(2,1)S(1)} collective-permute-done((bf16[512,384]{1,0:T(8,128)(2,1)S(1)}, bf16[512,384]{1,0:T(8,128)(2,1)S(1)}, u32[]{:S(2)}, u32[]{:S(2)}) %collective-permute-start.10) | collective-permute-done | bytes 393248 | tf_op jit(solution)/shard_map/ppermute | solution.py:299
  56.3 3.4 %copy-done.1 = bf16[1,1,512,8192]{3,2,1,0:T(8,128)(2,1)S(1)} copy-done((bf16[1,1,512,8192]{3,2,1,0:T(8,128)(2,1)S(1)}, bf16[1,1,512,8192]{3,2,1,0:T(8,128)(2,1)}, u32[]{:S(2)}) %copy-start.1) | copy-done | bytes 8388632
  59.7 6.5 %shard_map.130 = bf16[512,384]{1,0:T(8,128)(2,1)} custom-call(s32[8]{0:T(128)S(1)} %stack.75.refs_0_, bf16[512,8192]{1,0:T(8,128)(2,1)S(1)} %bitcast.86, f32[512,768]{1,0:T(8,128)S(1)} %shard_map.129.refs_2_, bf16[512,384]{1,0:T(8,128)(2,1)} %collective-permute-done.refs_3_, bf16[512,384]{1,0:T(8,128)(2,1)} %collective-permute-done.2.refs_4_, ...), custom_call_target="tpu_custom_call" | custom-call | flops 1024 | bytes 1024 | tf_op jit(solution)/shard_map/pallas_call | solution.py:105
  66.2 4.9 %all-to-all-start = ((bf16[8,64,384]{2,1,0:T(8,128)(2,1)}), bf16[8,64,384]{2,1,0:T(8,128)(2,1)S(1)}, u32[]{:S(2)}, u32[]{:S(2)}) async-start(bf16[8,64,384]{2,1,0:T(8,128)(2,1)} %bitcast.14), calls=%async_computation | async-start | bytes 786432 | tf_op jit(solution)/shard_map/all_to_all | solution.py:400
  74.3 3.4 %copy-done.2 = bf16[1,1,512,8192]{3,2,1,0:T(8,128)(2,1)S(1)} copy-done((bf16[1,1,512,8192]{3,2,1,0:T(8,128)(2,1)S(1)}, bf16[1,1,512,8192]{3,2,1,0:T(8,128)(2,1)}, u32[]{:S(2)}) %copy-start.2) | copy-done | bytes 8388632
  77.7 4.4 %shard_map.131.refs_2_ = f32[512,384]{1,0:T(8,128)S(1)} custom-call(s32[6]{0:T(128)S(1)} %stack.80.refs_0_, bf16[512,8192]{1,0:T(8,128)(2,1)S(1)} %bitcast.87, f32[512,768]{1,0:T(8,128)S(1)} %shard_map.129.refs_2_, bf16[512,384]{1,0:T(8,128)(2,1)S(1)} %collective-permute-done.9.refs_3_, bf16[512,384]{1,0:T(8,128)(2,1)S(1)} %collective-permute-done.11.refs_4_, ...), custom_call_target="tpu_custom_call" | custom-call | flops 1024 | bytes 1024 | tf_op jit(solution)/shard_map/pallas_call | solution.py:105
  83.7 3.4 %copy-done.3 = bf16[1,1,512,8192]{3,2,1,0:T(8,128)(2,1)S(1)} copy-done((bf16[1,1,512,8192]{3,2,1,0:T(8,128)(2,1)S(1)}, bf16[1,1,512,8192]{3,2,1,0:T(8,128)(2,1)}, u32[]{:S(2)}) %copy-start.3) | copy-done | bytes 8388632
  90.2 2.2 shard_map.132
  93.2 5.8 %all-to-all-start.1 = ((bf16[8,64,384]{2,1,0:T(8,128)(2,1)}), bf16[8,64,384]{2,1,0:T(8,128)(2,1)}, u32[]{:S(2)}, u32[]{:S(2)}) async-start(bf16[8,64,384]{2,1,0:T(8,128)(2,1)} %bitcast.92), calls=%async_computation.1 | async-start | bytes 786432 | tf_op jit(solution)/shard_map/all_to_all | solution.py:400
  100.0 11.1 %all-to-all-done.1 = bf16[8,64,384]{2,1,0:T(8,128)(2,1)} async-done(((bf16[8,64,384]{2,1,0:T(8,128)(2,1)}), bf16[8,64,384]{2,1,0:T(8,128)(2,1)}, u32[]{:S(2)}, u32[]{:S(2)}) %all-to-all-start.1) | async-done | bytes 393248 | tf_op jit(solution)/shard_map/all_to_all | solution.py:400
  112.1 2.1 shard_map.133
  114.3 3.4 %collective-permute-start.17 = (bf16[256,384]{1,0:T(8,128)(2,1)S(1)}, bf16[256,384]{1,0:T(8,128)(2,1)S(1)}, u32[]{:S(2)}, u32[]{:S(2)}) collective-permute-start(bf16[256,384]{1,0:T(8,128)(2,1)S(1)} %get-tuple-element.50), channel_id=1, source_target_pairs={{0,1},{1,2},{2,3},{3,4},{4,5},{5,6},{6,7},{8,9},{9,10},{10,11},{11... | collective-permute-start | bytes 589832 | tf_op jit(solution)/shard_map/ppermute | solution.py:306
  120.0 5.3 %collective-permute-done.17.prev_ref = bf16[256,384]{1,0:T(8,128)(2,1)S(1)} collective-permute-done((bf16[256,384]{1,0:T(8,128)(2,1)S(1)}, bf16[256,384]{1,0:T(8,128)(2,1)S(1)}, u32[]{:S(2)}, u32[]{:S(2)}) %collective-permute-start.17) | collective-permute-done | bytes 196640 | tf_op jit(solution)/shard_map/ppermute | solution.py:306
  126.2 4.5 %collective-permute-start.19 = (bf16[128,384]{1,0:T(8,128)(2,1)S(1)}, bf16[128,384]{1,0:T(8,128)(2,1)S(1)}, u32[]{:S(2)}, u32[]{:S(2)}) collective-permute-start(bf16[128,384]{1,0:T(8,128)(2,1)S(1)} %get-tuple-element.55), channel_id=1, source_target_pairs={{0,1},{1,2},{2,3},{3,4},{4,5},{5,6},{6,7},{8,9},{9,10},{10,11},{11... | collective-permute-start | bytes 294920 | tf_op jit(solution)/shard_map/ppermute | solution.py:306
  132.9 4.3 %collective-permute-done.20.refs_4_ = bf16[128,384]{1,0:T(8,128)(2,1)S(1)} collective-permute-done((bf16[128,384]{1,0:T(8,128)(2,1)S(1)}, bf16[128,384]{1,0:T(8,128)(2,1)S(1)}, u32[]{:S(2)}, u32[]{:S(2)}) %collective-permute-start.20) | collective-permute-done | bytes 98336 | tf_op jit(solution)/shard_map/ppermute | solution.py:307
  137.2 3.7 %shard_map.136 = (bf16[256,384]{1,0:T(8,128)(2,1)S(1)}, bf16[128,768]{1,0:T(8,128)(2,1)S(1)}, bf16[128,2048]{1,0:T(8,128)(2,1)S(1)}, bf16[128,768]{1,0:T(8,128)(...) custom-call(s32[2]{0:T(128)S(1)} %get-tuple-element.101.refs_0_, ...), custom_call_target="tpu_custom_call" | custom-call | flops 1024 | bytes 1024 | tf_op jit(solution)/shard_map/pallas_call | solution.py:52
  140.9 1.5 shard_map.137
  142.5 4.0 %collective-permute-start.22 = (bf16[128,384]{1,0:T(8,128)(2,1)S(1)}, bf16[128,384]{1,0:T(8,128)(2,1)S(1)}, u32[]{:S(2)}, u32[]{:S(2)}) collective-permute-start(bf16[128,384]{1,0:T(8,128)(2,1)S(1)} %get-tuple-element.64.refs_3_.refs_6_), channel_id=1, source_target_pairs={{0,1},{1,2},{2,3},{3,4},{4,5},{5,6},{6,7},{8,9},{9,10},{10,11},{11... | collective-permute-start | bytes 294920 | tf_op jit(solution)/shard_map/ppermute | solution.py:306
  146.5 1.5 collective-permute-start.23
  149.2 4.1 %collective-permute-done.23.refs_4_.refs_7_ = bf16[128,384]{1,0:T(8,128)(2,1)S(1)} collective-permute-done((bf16[128,384]{1,0:T(8,128)(2,1)S(1)}, bf16[128,384]{1,0:T(8,128)(2,1)S(1)}, u32[]{:S(2)}, u32[]{:S(2)}) %collective-permute-start.23) | collective-permute-done | bytes 98336 | tf_op jit(solution)/shard_map/ppermute | solution.py:307
  153.3 1.5 collective-permute-start.26
  154.8 2.4 %shard_map.138 = (f32[256,768]{1,0:T(8,128)}, bf16[256,768]{1,0:T(8,128)(2,1)S(1)}, bf16[256,384]{1,0:T(8,128)(2,1)S(1)}, bf16[256,384]{1,0:T(8,128)(2,1)S(1)}) custom-call(bf16[768,512]{1,0:T(8,128)(2,1)S(1)} %fusion.1.refs_0_, bf16[128,384]{1,0:T(8,128)(2,1)S(1)} %collective-permute-done.22.refs_1_.refs_4_, ...), custom_call_target="tpu_custom_call" | custom-call | flops 1024 | bytes 1024 | tf_op jit(solution)/shard_map/pallas_call | solution.py:52
  157.3 3.2 %collective-permute-start.24 = (bf16[256,384]{1,0:T(8,128)(2,1)S(1)}, bf16[256,384]{1,0:T(8,128)(2,1)S(1)}, u32[]{:S(2)}, u32[]{:S(2)}) collective-permute-start(bf16[256,384]{1,0:T(8,128)(2,1)S(1)} %get-tuple-element.72.refs_6_), channel_id=1, source_target_pairs={{0,1},{1,2},{2,3},{3,4},{4,5},{5,6},{6,7},{8,9},{9,10},{10,11},{11... | collective-permute-start | bytes 589832 | tf_op jit(solution)/shard_map/ppermute | solution.py:306
  161.8 4.0 %shard_map.139 = (bf16[2,768,384]{2,1,0:T(8,128)(2,1)S(1)}, bf16[2,768,384]{2,1,0:T(8,128)(2,1)S(1)}) custom-call(s32[2]{0:T(128)S(1)} %get-tuple-element.100.ids_ref.refs_0_, bf16[256,384]{1,0:T(8,128)(2,1)S(1)} %get-tuple-element.71.refs_1_.refs_5_, bf16[128,768]{1,0:T(8,128)(2,1)S(1)} %get-tuple-element.56.refs_2_, ...), custom_call_target="tpu_custom_call" | custom-call | flops 1024 | bytes 1024 | tf_op jit(solution)/shard_map/pallas_call | solution.py:52
  165.8 2.4 %collective-permute-done.25.refs_7_ = bf16[256,384]{1,0:T(8,128)(2,1)S(1)} collective-permute-done((bf16[256,384]{1,0:T(8,128)(2,1)S(1)}, bf16[256,384]{1,0:T(8,128)(2,1)S(1)}, u32[]{:S(2)}, u32[]{:S(2)}) %collective-permute-start.25) | collective-permute-done | bytes 196640 | tf_op jit(solution)/shard_map/ppermute | solution.py:307
  168.2 6.3 %shard_map.140 = (bf16[2,768,384]{2,1,0:T(8,128)(2,1)S(1)}, bf16[2,768,384]{2,1,0:T(8,128)(2,1)}) custom-call(s32[2]{0:T(128)S(1)} %get-tuple-element.100.ids_ref.refs_0_, bf16[256,384]{1,0:T(8,128)(2,1)S(1)} %get-tuple-element.71.refs_1_.refs_5_, bf16[256,768]{1,0:T(8,128)(2,1)S(1)} %get-tuple-element.52.low_ref.refs_2_, ...), custom_call_target="tpu_custom_call" | custom-call | flops 1024 | bytes 1024 | tf_op jit(solution)/shard_map/pallas_call | solution.py:52
  177.2 2.1 fusion.3
  179.4 2.6 %collective-permute-start.31 = (bf16[2,4,96,384]{3,2,1,0:T(8,128)(2,1)}, bf16[2,4,96,384]{3,2,1,0:T(8,128)(2,1)S(1)}, u32[]{:S(2)}, u32[]{:S(2)}) collective-permute-start(bf16[2,4,96,384]{3,2,1,0:T(8,128)(2,1)} %fusion.3), channel_id=1, source_target_pairs={{0,1},{1,0},{2,3},{3,2},{4,5},{5,4},{6,7},{7,6},{8,9},{9,8},{10,11... | collective-permute-start | bytes 1769480 | tf_op jit(solution)/shard_map/ppermute | solution.py:299
  185.0 4.4 %all-to-all-start.2 = ((bf16[8,96,512]{2,1,0:T(8,128)(2,1)}), bf16[8,96,512]{2,1,0:T(8,128)(2,1)S(1)}, u32[]{:S(2)}, u32[]{:S(2)}) async-start(bf16[8,96,512]{2,1,0:T(8,128)(2,1)} %bitcast.38), calls=%async_computation.2 | async-start | bytes 1572864 | tf_op jit(solution)/shard_map/all_to_all | solution.py:321
  190.9 10.3 %collective-permute-done.31 = bf16[2,4,96,384]{3,2,1,0:T(8,128)(2,1)S(1)} collective-permute-done((bf16[2,4,96,384]{3,2,1,0:T(8,128)(2,1)}, bf16[2,4,96,384]{3,2,1,0:T(8,128)(2,1)S(1)}, u32[]{:S(2)}, u32[]{:S(2)}) %collective-permute-start.31) | collective-permute-done | bytes 589856 | tf_op jit(solution)/shard_map/ppermute | solution.py:299
  204.3 2.4 %collective-permute-start.29 = (bf16[4,96,384]{2,1,0:T(8,128)(2,1)S(1)}, bf16[4,96,384]{2,1,0:T(8,128)(2,1)S(1)}, u32[]{:S(2)}, u32[]{:S(2)}) collective-permute-start(bf16[4,96,384]{2,1,0:T(8,128)(2,1)S(1)} %fusion.8), channel_id=1, source_target_pairs={{0,1},{1,0},{2,3},{3,2},{4,5},{5,4},{6,7},{7,6},{8,9},{9,8},{10,11... | collective-permute-start | bytes 884744 | tf_op jit(solution)/shard_map/ppermute | solution.py:299
  206.8 1.5 collective-permute-done.32
  208.4 3.8 %collective-permute-done.29 = bf16[4,96,384]{2,1,0:T(8,128)(2,1)S(1)} collective-permute-done((bf16[4,96,384]{2,1,0:T(8,128)(2,1)S(1)}, bf16[4,96,384]{2,1,0:T(8,128)(2,1)S(1)}, u32[]{:S(2)}, u32[]{:S(2)}) %collective-permute-start.29) | collective-permute-done | bytes 294944 | tf_op jit(solution)/shard_map/ppermute | solution.py:299
  214.1 5.3 %all-to-all-start.3 = ((bf16[4,96,768]{2,1,0:T(8,128)(2,1)}), bf16[4,96,768]{2,1,0:T(8,128)(2,1)S(1)}, u32[]{:S(2)}, u32[]{:S(2)}) async-start(bf16[4,96,768]{2,1,0:T(8,128)(2,1)} %pad_maximum_fusion), calls=%async_computation.3 | async-start | bytes 1179648 | tf_op jit(solution)/shard_map/all_to_all | solution.py:358
  220.2 12.0 %all-to-all-done.3.parts_ref = bf16[4,96,768]{2,1,0:T(8,128)(2,1)S(1)} async-done(((bf16[4,96,768]{2,1,0:T(8,128)(2,1)}), bf16[4,96,768]{2,1,0:T(8,128)(2,1)S(1)}, u32[]{:S(2)}, u32[]{:S(2)}) %all-to-all-start.3) | async-done | bytes 589856 | tf_op jit(solution)/shard_map/all_to_all | solution.py:358
  (123 shorter events, 33.3 us)
Async XLA Ops:
  0.6 17.8 %collective-permute-start.1 = (bf16[2048,768]{1,0:T(8,128)(2,1)}, bf16[2048,768]{1,0:T(8,128)(2,1)S(1)}, u32[]{:S(2)}, u32[]{:S(2)}) collective-permute-start(bf16[2048,768]{1,0:T(8,128)(2,1)} %refs_2_.1), channel_id=1, source_target_pairs={{0,8},{8,0},{16,24},{24,16},{1,9},{9,1},{17,25},{25,17},{2,10},{10... | collective-permute-start | bytes 9437192 | tf_op jit(solution)/shard_map/ppermute | solution.py:299
  3.7 12.8 %collective-permute-start.5 = (bf16[512,384]{1,0:T(8,128)(2,1)}, bf16[512,384]{1,0:T(8,128)(2,1)}, u32[]{:S(2)}, u32[]{:S(2)}) collective-permute-start(bf16[512,384]{1,0:T(8,128)(2,1)} %get-tuple-element.94), channel_id=1, source_target_pairs={{0,16},{8,24},{16,0},{24,8},{1,17},{9,25},{17,1},{25,9},{2,18},{10... | collective-permute-start | bytes 1179656 | tf_op jit(solution)/shard_map/ppermute | solution.py:299
  6.2 29.3 %collective-permute-start = (bf16[512,384]{1,0:T(8,128)(2,1)}, bf16[512,384]{1,0:T(8,128)(2,1)}, u32[]{:S(2)}, u32[]{:S(2)}) collective-permute-start(bf16[512,384]{1,0:T(8,128)(2,1)} %get-tuple-element.95), channel_id=1, source_target_pairs={{0,16},{8,24},{16,0},{24,8},{1,17},{9,25},{17,1},{25,9},{2,18},{10... | collective-permute-start | bytes 1179656 | tf_op jit(solution)/shard_map/ppermute | solution.py:299
  6.2 29.5 %collective-permute-start.9 = (bf16[512,384]{1,0:T(8,128)(2,1)}, bf16[512,384]{1,0:T(8,128)(2,1)S(1)}, u32[]{:S(2)}, u32[]{:S(2)}) collective-permute-start(bf16[512,384]{1,0:T(8,128)(2,1)} %get-tuple-element.93), channel_id=1, source_target_pairs={{0,16},{8,24},{16,0},{24,8},{1,17},{9,25},{17,1},{25,9},{2,18},{10... | collective-permute-start | bytes 1179656 | tf_op jit(solution)/shard_map/ppermute | solution.py:299
  8.2 33.3 %collective-permute-start.13 = (bf16[512,384]{1,0:T(8,128)(2,1)}, bf16[512,384]{1,0:T(8,128)(2,1)}, u32[]{:S(2)}, u32[]{:S(2)}) collective-permute-start(bf16[512,384]{1,0:T(8,128)(2,1)} %get-tuple-element.92), channel_id=1, source_target_pairs={{0,16},{8,24},{16,0},{24,8},{1,17},{9,25},{17,1},{25,9},{2,18},{10... | collective-permute-start | bytes 1179656 | tf_op jit(solution)/shard_map/ppermute | solution.py:299
  16.5 21.2 %collective-permute-start.7 = (bf16[512,384]{1,0:T(8,128)(2,1)}, bf16[512,384]{1,0:T(8,128)(2,1)}, u32[]{:S(2)}, u32[]{:S(2)}) collective-permute-start(bf16[512,384]{1,0:T(8,128)(2,1)} %collective-permute-done.5.refs_7_), channel_id=1, source_target_pairs={{0,1},{1,0},{2,3},{3,2},{4,5},{5,4},{6,7},{7,6},{8,9},{9,8},{10,11... | collective-permute-start | bytes 1179656 | tf_op jit(solution)/shard_map/ppermute | solution.py:299
  35.5 12.3 %collective-permute-start.3 = (bf16[512,384]{1,0:T(8,128)(2,1)}, bf16[512,384]{1,0:T(8,128)(2,1)S(1)}, u32[]{:S(2)}, u32[]{:S(2)}) collective-permute-start(bf16[512,384]{1,0:T(8,128)(2,1)} %collective-permute-done.refs_3_), channel_id=1, source_target_pairs={{0,1},{1,0},{2,3},{3,2},{4,5},{5,4},{6,7},{7,6},{8,9},{9,8},{10,11... | collective-permute-start | bytes 1179656 | tf_op jit(solution)/shard_map/ppermute | solution.py:299
  35.7 12.2 %collective-permute-start.6 = (bf16[512,384]{1,0:T(8,128)(2,1)}, bf16[512,384]{1,0:T(8,128)(2,1)S(1)}, u32[]{:S(2)}, u32[]{:S(2)}) collective-permute-start(bf16[512,384]{1,0:T(8,128)(2,1)} %collective-permute-done.5.refs_7_), channel_id=1, source_target_pairs={{0,8},{8,0},{16,24},{24,16},{1,9},{9,1},{17,25},{25,17},{2,10},{10... | collective-permute-start | bytes 1179656 | tf_op jit(solution)/shard_map/ppermute | solution.py:299
  35.7 20.6 %collective-permute-start.10 = (bf16[512,384]{1,0:T(8,128)(2,1)S(1)}, bf16[512,384]{1,0:T(8,128)(2,1)S(1)}, u32[]{:S(2)}, u32[]{:S(2)}) collective-permute-start(bf16[512,384]{1,0:T(8,128)(2,1)S(1)} %collective-permute-done.9.refs_3_), channel_id=1, source_target_pairs={{0,1},{1,0},{2,3},{3,2},{4,5},{5,4},{6,7},{7,6},{8,9},{9,8},{10,11... | collective-permute-start | bytes 1179656 | tf_op jit(solution)/shard_map/ppermute | solution.py:299
  37.6 18.7 %collective-permute-start.8 = (bf16[512,384]{1,0:T(8,128)(2,1)}, bf16[512,384]{1,0:T(8,128)(2,1)}, u32[]{:S(2)}, u32[]{:S(2)}) collective-permute-start(bf16[512,384]{1,0:T(8,128)(2,1)} %collective-permute-done.7.refs_9_), channel_id=1, source_target_pairs={{0,8},{8,0},{16,24},{24,16},{1,9},{9,1},{17,25},{25,17},{2,10},{10... | collective-permute-start | bytes 1179656 | tf_op jit(solution)/shard_map/ppermute | solution.py:299
  41.5 14.8 %collective-permute-start.2 = (bf16[512,384]{1,0:T(8,128)(2,1)}, bf16[512,384]{1,0:T(8,128)(2,1)}, u32[]{:S(2)}, u32[]{:S(2)}) collective-permute-start(bf16[512,384]{1,0:T(8,128)(2,1)} %collective-permute-done.refs_3_), channel_id=1, source_target_pairs={{0,8},{8,0},{16,24},{24,16},{1,9},{9,1},{17,25},{25,17},{2,10},{10... | collective-permute-start | bytes 1179656 | tf_op jit(solution)/shard_map/ppermute | solution.py:299
  47.9 8.4 %collective-permute-start.4 = (bf16[512,384]{1,0:T(8,128)(2,1)S(1)}, bf16[512,384]{1,0:T(8,128)(2,1)}, u32[]{:S(2)}, u32[]{:S(2)}) collective-permute-start(bf16[512,384]{1,0:T(8,128)(2,1)S(1)} %collective-permute-done.3.refs_5_), channel_id=1, source_target_pairs={{0,8},{8,0},{16,24},{24,16},{1,9},{9,1},{17,25},{25,17},{2,10},{10... | collective-permute-start | bytes 1179656 | tf_op jit(solution)/shard_map/ppermute | solution.py:299
  47.9 23.8 %collective-permute-start.15 = (bf16[512,384]{1,0:T(8,128)(2,1)}, bf16[512,384]{1,0:T(8,128)(2,1)S(1)}, u32[]{:S(2)}, u32[]{:S(2)}) collective-permute-start(bf16[512,384]{1,0:T(8,128)(2,1)} %collective-permute-done.13.refs_7_), channel_id=1, source_target_pairs={{0,1},{1,0},{2,3},{3,2},{4,5},{5,4},{6,7},{7,6},{8,9},{9,8},{10,11... | collective-permute-start | bytes 1179656 | tf_op jit(solution)/shard_map/ppermute | solution.py:299
  66.2 16.7 %all-to-all-start = ((bf16[8,64,384]{2,1,0:T(8,128)(2,1)}), bf16[8,64,384]{2,1,0:T(8,128)(2,1)S(1)}, u32[]{:S(2)}, u32[]{:S(2)}) async-start(bf16[8,64,384]{2,1,0:T(8,128)(2,1)} %bitcast.14), calls=%async_computation | async-start | bytes 786432 | tf_op jit(solution)/shard_map/all_to_all | solution.py:400
  71.1 1.7 collective-permute-start.11
  71.1 3.2 %collective-permute-start.14 = (bf16[512,384]{1,0:T(8,128)(2,1)}, bf16[512,384]{1,0:T(8,128)(2,1)}, u32[]{:S(2)}, u32[]{:S(2)}) collective-permute-start(bf16[512,384]{1,0:T(8,128)(2,1)} %collective-permute-done.13.refs_7_), channel_id=1, source_target_pairs={{0,8},{8,0},{16,24},{24,16},{1,9},{9,1},{17,25},{25,17},{2,10},{10... | collective-permute-start | bytes 1179656 | tf_op jit(solution)/shard_map/ppermute | solution.py:299
  71.6 2.7 %collective-permute-start.12 = (bf16[512,384]{1,0:T(8,128)(2,1)S(1)}, bf16[512,384]{1,0:T(8,128)(2,1)}, u32[]{:S(2)}, u32[]{:S(2)}) collective-permute-start(bf16[512,384]{1,0:T(8,128)(2,1)S(1)} %collective-permute-done.10.refs_11_.refs_5_), channel_id=1, source_target_pairs={{0,8},{8,0},{16,24},{24,16},{1,9},{9,1},{17,25},{25,17},{2,10},{10... | collective-permute-start | bytes 1179656 | tf_op jit(solution)/shard_map/ppermute | solution.py:299
  71.7 10.4 %copy-start.21 = (bf16[512,384]{1,0:T(8,128)(2,1)}, bf16[512,384]{1,0:T(8,128)(2,1)S(1)}, u32[]{:S(2)}) copy-start(bf16[512,384]{1,0:T(8,128)(2,1)S(1)} %collective-permute-done.15.refs_3_) | copy-start | bytes 1179652
  71.7 11.2 %collective-permute-start.16 = (bf16[512,384]{1,0:T(8,128)(2,1)S(1)}, bf16[512,384]{1,0:T(8,128)(2,1)}, u32[]{:S(2)}, u32[]{:S(2)}) collective-permute-start(bf16[512,384]{1,0:T(8,128)(2,1)S(1)} %collective-permute-done.15.refs_3_), channel_id=1, source_target_pairs={{0,8},{8,0},{16,24},{24,16},{1,9},{9,1},{17,25},{25,17},{2,10},{10... | collective-permute-start | bytes 1179656 | tf_op jit(solution)/shard_map/ppermute | solution.py:299
  90.2 9.4 %copy-start.29 = (s32[1,8,8]{2,1,0:T(8,128)S(1)}, s32[1,8,8]{2,1,0:T(8,128)}, u32[]{:S(2)}) copy-start(s32[1,8,8]{2,1,0:T(8,128)} %param.11) | copy-start | bytes 772
  90.2 20.9 %copy-start.4 = (bf16[2,3,768,384]{3,2,1,0:T(8,128)(2,1)S(1)}, bf16[2,3,768,384]{3,2,1,0:T(8,128)(2,1)}, u32[]{:S(2)}) copy-start(bf16[2,3,768,384]{3,2,1,0:T(8,128)(2,1)} %refs_7_.3) | copy-start | bytes 10616836
  93.2 17.9 %all-to-all-start.1 = ((bf16[8,64,384]{2,1,0:T(8,128)(2,1)}), bf16[8,64,384]{2,1,0:T(8,128)(2,1)}, u32[]{:S(2)}, u32[]{:S(2)}) async-start(bf16[8,64,384]{2,1,0:T(8,128)(2,1)} %bitcast.92), calls=%async_computation.1 | async-start | bytes 786432 | tf_op jit(solution)/shard_map/all_to_all | solution.py:400
  114.3 11.0 %collective-permute-start.17 = (bf16[256,384]{1,0:T(8,128)(2,1)S(1)}, bf16[256,384]{1,0:T(8,128)(2,1)S(1)}, u32[]{:S(2)}, u32[]{:S(2)}) collective-permute-start(bf16[256,384]{1,0:T(8,128)(2,1)S(1)} %get-tuple-element.50), channel_id=1, source_target_pairs={{0,1},{1,2},{2,3},{3,4},{4,5},{5,6},{6,7},{8,9},{9,10},{10,11},{11... | collective-permute-start | bytes 589832 | tf_op jit(solution)/shard_map/ppermute | solution.py:306
  117.7 7.7 %collective-permute-start.18 = (bf16[256,384]{1,0:T(8,128)(2,1)S(1)}, bf16[256,384]{1,0:T(8,128)(2,1)S(1)}, u32[]{:S(2)}, u32[]{:S(2)}) collective-permute-start(bf16[256,384]{1,0:T(8,128)(2,1)S(1)} %get-tuple-element.51), channel_id=1, source_target_pairs={{1,0},{2,1},{3,2},{4,3},{5,4},{6,5},{7,6},{9,8},{10,9},{11,10},{12... | collective-permute-start | bytes 589832 | tf_op jit(solution)/shard_map/ppermute | solution.py:307
  125.3 11.9 %copy-start.12 = (bf16[768,2048]{1,0:T(8,128)(2,1)S(1)}, bf16[768,2048]{1,0:T(8,128)(2,1)}, u32[]{:S(2)}) copy-start(bf16[768,2048]{1,0:T(8,128)(2,1)} %refs_8_.2) | copy-start | bytes 9437188
  125.3 11.9 %copy-start.20 = (s32[1,128,2048]{2,1,0:T(8,128)S(1)}, s32[1,128,2048]{2,1,0:T(8,128)}, u32[]{:S(2)}) copy-start(s32[1,128,2048]{2,1,0:T(8,128)} %param.13) | copy-start | bytes 3145732
  126.2 6.7 %collective-permute-start.19 = (bf16[128,384]{1,0:T(8,128)(2,1)S(1)}, bf16[128,384]{1,0:T(8,128)(2,1)S(1)}, u32[]{:S(2)}, u32[]{:S(2)}) collective-permute-start(bf16[128,384]{1,0:T(8,128)(2,1)S(1)} %get-tuple-element.55), channel_id=1, source_target_pairs={{0,1},{1,2},{2,3},{3,4},{4,5},{5,6},{6,7},{8,9},{9,10},{10,11},{11... | collective-permute-start | bytes 294920 | tf_op jit(solution)/shard_map/ppermute | solution.py:306
  130.7 6.5 %collective-permute-start.20 = (bf16[128,384]{1,0:T(8,128)(2,1)S(1)}, bf16[128,384]{1,0:T(8,128)(2,1)S(1)}, u32[]{:S(2)}, u32[]{:S(2)}) collective-permute-start(bf16[128,384]{1,0:T(8,128)(2,1)S(1)} %get-tuple-element.58), channel_id=1, source_target_pairs={{1,0},{2,1},{3,2},{4,3},{5,4},{6,5},{7,6},{9,8},{10,9},{11,10},{12... | collective-permute-start | bytes 294920 | tf_op jit(solution)/shard_map/ppermute | solution.py:307
  142.5 5.6 %collective-permute-start.21 = (bf16[2,768,512]{2,1,0:T(8,128)(2,1)S(1)}, bf16[2,768,512]{2,1,0:T(8,128)(2,1)S(1)}, u32[]{:S(2)}, u32[]{:S(2)}) collective-permute-start(bf16[2,768,512]{2,1,0:T(8,128)(2,1)S(1)} %get-tuple-element.63), channel_id=1, source_target_pairs={{0,8},{8,0},{16,24},{24,16},{1,9},{9,1},{17,25},{25,17},{2,10},{10... | collective-permute-start | bytes 4718600 | tf_op jit(solution)/shard_map/ppermute | solution.py:299
  142.5 6.7 %collective-permute-start.22 = (bf16[128,384]{1,0:T(8,128)(2,1)S(1)}, bf16[128,384]{1,0:T(8,128)(2,1)S(1)}, u32[]{:S(2)}, u32[]{:S(2)}) collective-permute-start(bf16[128,384]{1,0:T(8,128)(2,1)S(1)} %get-tuple-element.64.refs_3_.refs_6_), channel_id=1, source_target_pairs={{0,1},{1,2},{2,3},{3,4},{4,5},{5,6},{6,7},{8,9},{9,10},{10,11},{11... | collective-permute-start | bytes 294920 | tf_op jit(solution)/shard_map/ppermute | solution.py:306
  146.5 6.8 %collective-permute-start.23 = (bf16[128,384]{1,0:T(8,128)(2,1)S(1)}, bf16[128,384]{1,0:T(8,128)(2,1)S(1)}, u32[]{:S(2)}, u32[]{:S(2)}) collective-permute-start(bf16[128,384]{1,0:T(8,128)(2,1)S(1)} %get-tuple-element.65.refs_2_.refs_5_), channel_id=1, source_target_pairs={{1,0},{2,1},{3,2},{4,3},{5,4},{6,5},{7,6},{9,8},{10,9},{11,10},{12... | collective-permute-start | bytes 294920 | tf_op jit(solution)/shard_map/ppermute | solution.py:307
  148.1 6.8 %copy-start.23 = (bf16[2,768,512]{2,1,0:T(8,128)(2,1)}, bf16[2,768,512]{2,1,0:T(8,128)(2,1)S(1)}, u32[]{:S(2)}) copy-start(bf16[2,768,512]{2,1,0:T(8,128)(2,1)S(1)} %collective-permute-done.21) | copy-start | bytes 4718596
  153.3 21.2 %collective-permute-start.26 = (bf16[768,512]{1,0:T(8,128)(2,1)S(1)}, bf16[768,512]{1,0:T(8,128)(2,1)S(1)}, u32[]{:S(2)}, u32[]{:S(2)}) collective-permute-start(bf16[768,512]{1,0:T(8,128)(2,1)S(1)} %fusion.1.refs_0_), channel_id=1, source_target_pairs={{0,16},{8,24},{16,0},{24,8},{1,17},{9,25},{17,1},{25,9},{2,18},{10... | collective-permute-start | bytes 2359304 | tf_op jit(solution)/shard_map/ppermute | solution.py:299
  154.8 7.0 %copy-start.7 = (bf16[2,384,768]{2,1,0:T(8,128)(2,1)S(1)}, bf16[2,384,768]{2,1,0:T(8,128)(2,1)}, u32[]{:S(2)}) copy-start(bf16[2,384,768]{2,1,0:T(8,128)(2,1)} %constant.122.clone.refs_10_) | copy-start | bytes 3538948
  154.8 7.0 %copy-start.8 = (bf16[2,768,384]{2,1,0:T(8,128)(2,1)S(1)}, bf16[2,768,384]{2,1,0:T(8,128)(2,1)}, u32[]{:S(2)}) copy-start(bf16[2,768,384]{2,1,0:T(8,128)(2,1)} %constant.123.clone.refs_11_) | copy-start | bytes 3538948
  157.3 8.5 %collective-permute-start.24 = (bf16[256,384]{1,0:T(8,128)(2,1)S(1)}, bf16[256,384]{1,0:T(8,128)(2,1)S(1)}, u32[]{:S(2)}, u32[]{:S(2)}) collective-permute-start(bf16[256,384]{1,0:T(8,128)(2,1)S(1)} %get-tuple-element.72.refs_6_), channel_id=1, source_target_pairs={{0,1},{1,2},{2,3},{3,4},{4,5},{5,6},{6,7},{8,9},{9,10},{10,11},{11... | collective-permute-start | bytes 589832 | tf_op jit(solution)/shard_map/ppermute | solution.py:306
  160.5 7.7 %collective-permute-start.25 = (bf16[256,384]{1,0:T(8,128)(2,1)S(1)}, bf16[256,384]{1,0:T(8,128)(2,1)S(1)}, u32[]{:S(2)}, u32[]{:S(2)}) collective-permute-start(bf16[256,384]{1,0:T(8,128)(2,1)S(1)} %get-tuple-element.71.refs_1_.refs_5_), channel_id=1, source_target_pairs={{1,0},{2,1},{3,2},{4,3},{5,4},{6,5},{7,6},{9,8},{10,9},{11,10},{12... | collective-permute-start | bytes 589832 | tf_op jit(solution)/shard_map/ppermute | solution.py:307
  168.2 9.0 %collective-permute-start.30 = (bf16[2,768,384]{2,1,0:T(8,128)(2,1)S(1)}, bf16[2,768,384]{2,1,0:T(8,128)(2,1)}, u32[]{:S(2)}, u32[]{:S(2)}) collective-permute-start(bf16[2,768,384]{2,1,0:T(8,128)(2,1)S(1)} %get-tuple-element.85), channel_id=1, source_target_pairs={{0,8},{8,0},{16,24},{24,16},{1,9},{9,1},{17,25},{25,17},{2,10},{10... | collective-permute-start | bytes 3538952 | tf_op jit(solution)/shard_map/ppermute | solution.py:299
  175.5 6.5 %collective-permute-start.27 = (bf16[2,768,384]{2,1,0:T(8,128)(2,1)}, bf16[2,768,384]{2,1,0:T(8,128)(2,1)}, u32[]{:S(2)}, u32[]{:S(2)}) collective-permute-start(bf16[2,768,384]{2,1,0:T(8,128)(2,1)} %get-tuple-element.81), channel_id=1, source_target_pairs={{0,8},{8,0},{16,24},{24,16},{1,9},{9,1},{17,25},{25,17},{2,10},{10... | collective-permute-start | bytes 3538952 | tf_op jit(solution)/shard_map/ppermute | solution.py:299
  176.0 7.8 %copy-start.28 = (bf16[768,512]{1,0:T(8,128)(2,1)S(1)}, bf16[768,512]{1,0:T(8,128)(2,1)}, u32[]{:S(2)}) copy-start(bf16[768,512]{1,0:T(8,128)(2,1)} %copy-done.27) | copy-start | bytes 2359300
  177.2 6.5 %copy-start.24 = (bf16[2,768,512]{2,1,0:T(8,128)(2,1)S(1)}, bf16[2,768,512]{2,1,0:T(8,128)(2,1)}, u32[]{:S(2)}) copy-start(bf16[2,768,512]{2,1,0:T(8,128)(2,1)} %copy-done.23) | copy-start | bytes 4718596
  179.4 21.9 %collective-permute-start.31 = (bf16[2,4,96,384]{3,2,1,0:T(8,128)(2,1)}, bf16[2,4,96,384]{3,2,1,0:T(8,128)(2,1)S(1)}, u32[]{:S(2)}, u32[]{:S(2)}) collective-permute-start(bf16[2,4,96,384]{3,2,1,0:T(8,128)(2,1)} %fusion.3), channel_id=1, source_target_pairs={{0,1},{1,0},{2,3},{3,2},{4,5},{5,4},{6,7},{7,6},{8,9},{9,8},{10,11... | collective-permute-start | bytes 1769480 | tf_op jit(solution)/shard_map/ppermute | solution.py:299
  183.2 20.1 %collective-permute-start.28 = (bf16[768,384]{1,0:T(8,128)(2,1)S(1)}, bf16[768,384]{1,0:T(8,128)(2,1)}, u32[]{:S(2)}, u32[]{:S(2)}) collective-permute-start(bf16[768,384]{1,0:T(8,128)(2,1)S(1)} %fusion.2), channel_id=1, source_target_pairs={{0,16},{8,24},{16,0},{24,8},{1,17},{9,25},{17,1},{25,9},{2,18},{10... | collective-permute-start | bytes 1769480 | tf_op jit(solution)/shard_map/ppermute | solution.py:299
  185.0 29.1 %all-to-all-start.2 = ((bf16[8,96,512]{2,1,0:T(8,128)(2,1)}), bf16[8,96,512]{2,1,0:T(8,128)(2,1)S(1)}, u32[]{:S(2)}, u32[]{:S(2)}) async-start(bf16[8,96,512]{2,1,0:T(8,128)(2,1)} %bitcast.38), calls=%async_computation.2 | async-start | bytes 1572864 | tf_op jit(solution)/shard_map/all_to_all | solution.py:321
  189.5 11.8 %copy-start.26 = (bf16[1,768,384]{2,1,0:T(8,128)(2,1)S(1)}, bf16[1,768,384]{2,1,0:T(8,128)(2,1)}, u32[]{:S(2)}) copy-start(bf16[1,768,384]{2,1,0:T(8,128)(2,1)} %get-tuple-element.97) | copy-start | bytes 1769476
  201.4 6.9 %collective-permute-start.32 = (bf16[4,96,384]{2,1,0:T(8,128)(2,1)S(1)}, bf16[4,96,384]{2,1,0:T(8,128)(2,1)S(1)}, u32[]{:S(2)}, u32[]{:S(2)}) collective-permute-start(bf16[4,96,384]{2,1,0:T(8,128)(2,1)S(1)} %fusion.4), channel_id=1, source_target_pairs={{0,16},{8,24},{16,0},{24,8},{1,17},{9,25},{17,1},{25,9},{2,18},{10... | collective-permute-start | bytes 884744 | tf_op jit(solution)/shard_map/ppermute | solution.py:299
  204.3 7.9 %collective-permute-start.29 = (bf16[4,96,384]{2,1,0:T(8,128)(2,1)S(1)}, bf16[4,96,384]{2,1,0:T(8,128)(2,1)S(1)}, u32[]{:S(2)}, u32[]{:S(2)}) collective-permute-start(bf16[4,96,384]{2,1,0:T(8,128)(2,1)S(1)} %fusion.8), channel_id=1, source_target_pairs={{0,1},{1,0},{2,3},{3,2},{4,5},{5,4},{6,7},{7,6},{8,9},{9,8},{10,11... | collective-permute-start | bytes 884744 | tf_op jit(solution)/shard_map/ppermute | solution.py:299
  214.1 18.1 %all-to-all-start.3 = ((bf16[4,96,768]{2,1,0:T(8,128)(2,1)}), bf16[4,96,768]{2,1,0:T(8,128)(2,1)S(1)}, u32[]{:S(2)}, u32[]{:S(2)}) async-start(bf16[4,96,768]{2,1,0:T(8,128)(2,1)} %pad_maximum_fusion), calls=%async_computation.3 | async-start | bytes 1179648 | tf_op jit(solution)/shard_map/all_to_all | solution.py:358
  (19 other events, 49.2 us)

commit v6 on v5

--- a/solution.py
+++ b/solution.py
@@ -60,57 +60,80 @@
     )(*inputs)
 
 
-def absorb(total, column, rows, weights, starts, final, after=()):
-    count = len(weights)
+def product(rows, weights, starts, later, block):
+    count, spare = len(weights), len(later)
     row_count = rows.shape[0]
     depth, columns = weights[0].shape
-    block = min(512, depth)
     blocks = [(k, at) for k in range(count) for at in range(0, depth, block)]
-    first = total is None
-    fixed = 2 if first else 3
-
-    def body(*refs):
-        starts_ref, rows_ref, old_ref = refs[0], refs[1], refs[2]
-        weight_refs = refs[fixed : fixed + count]
-        out_ref, held_ref, sems, *more = refs[fixed + count + len(after) :]
+
+    def body(starts_ref, rows_ref, *refs):
+        weight_refs, out_ref, later_refs = refs[:count], refs[count], refs[count + 1 : count + 1 + spare]
+        held_ref, piece_ref, sems, later_sems = refs[count + 1 + spare :]
         copies = []
         for n, (k, at) in enumerate(blocks):
             start = pl.multiple_of(starts_ref[k] + at, block)
-            batch = [pltpu.make_async_copy(rows_ref.at[:, pl.ds(start, block)], held_ref.at[n], sems.at[0, n])]
-            if first:
-                batch.append(
-                    pltpu.make_async_copy(weight_refs[k].at[pl.ds(at, block)], more[0].at[n], sems.at[1, n])
-                )
-            for copy in batch:
+            copies.append((
+                pltpu.make_async_copy(rows_ref.at[:, pl.ds(start, block)], held_ref.at[n], sems.at[0, n]),
+                pltpu.make_async_copy(weight_refs[k].at[pl.ds(at, block)], piece_ref.at[n], sems.at[1, n]),
+            ))
+            for copy in copies[-1]:
                 copy.start()
-            copies.append(batch)
+        rest = []
+        for n in range(spare):
+            start = pl.multiple_of(starts_ref[count + n], block)
+            rest.append(
+                pltpu.make_async_copy(rows_ref.at[:, pl.ds(start, block)], later_refs[n], later_sems.at[n])
+            )
+            rest[-1].start()
         half = row_count // 2
         for h in range(2):
             part = slice(h * half, (h + 1) * half)
-            sums = 0.0 if first else old_ref[part, column : column + columns]
-            for n, (k, at) in enumerate(blocks):
+            sums = 0.0
+            for n in range(len(blocks)):
                 if h == 0:
                     for copy in copies[n]:
                         copy.wait()
-                piece = more[0][n] if first else weight_refs[k][at : at + block]
-                sums = sums + nn(held_ref[n, part], piece)
-            out_ref[part] = sums.astype(out_ref.dtype)
-
-    scratch = [
-        pltpu.VMEM((len(blocks), row_count, block), BF),
-        pltpu.SemaphoreType.DMA((2, len(blocks))),
-    ]
-    if first:
-        scratch.append(pltpu.VMEM((len(blocks), block, columns), BF))
+                sums = sums + nn(held_ref[n, part], piece_ref[n])
+            out_ref[part] = sums
+        for copy in rest:
+            copy.wait()
+
+    out = [jax.ShapeDtypeStruct((row_count, columns), F32)]
+    out += [jax.ShapeDtypeStruct((row_count, block), BF)] * spare
     return pl.pallas_call(
         body,
-        out_shape=jax.ShapeDtypeStruct((row_count, columns), BF if final else F32),
-        in_specs=[SMEM, HBM] + ([] if first else [VMEM]) + [HBM if first else VMEM] * count + [ANY] * len(after),
-        out_specs=VMEM,
-        scratch_shapes=scratch,
-        compiler_params=params(20 if first else 14),
+        out_shape=out,
+        in_specs=[SMEM] + [HBM] * (count + 1),
+        out_specs=[VMEM] * (1 + spare),
+        scratch_shapes=[
+            pltpu.VMEM((len(blocks), row_count, block), BF),
+            pltpu.VMEM((len(blocks), block, columns), BF),
+            pltpu.SemaphoreType.DMA((2, len(blocks))),
+            pltpu.SemaphoreType.DMA((spare,)),
+        ],
+        compiler_params=params(49),
         cost_estimate=CHEAP,
-    )(jnp.stack(starts).astype(jnp.int32), rows, *([] if first else [total]), *weights, *after)
+    )(jnp.stack(starts + later).astype(jnp.int32), rows, *weights)
+
+
+def absorb(total, column, blocks, weights, final):
+    count = len(weights)
+    row_count = total.shape[0]
+    columns = weights[0].shape[1]
+
+    def body(old_ref, *refs):
+        out_ref = refs[2 * count]
+        half = row_count // 2
+        for h in range(2):
+            part = slice(h * half, (h + 1) * half)
+            sums = old_ref[part, column : column + columns]
+            for k in range(count):
+                sums = sums + nn(refs[k][part], refs[count + k][...])
+            out_ref[part] = sums.astype(out_ref.dtype)
+
+    return call(
+        body, (total, *blocks, *weights), [((row_count, columns), BF if final else F32)], 20
+    )[0]
 
 
 def place_body(target_ref, left_ref, right_ref, kernels_ref, hidden_ref, low_ref, high_ref, down_ref, up_ref):
@@ -384,28 +407,29 @@
         for n in range(2)
     ]
     near, away = (me ^ 2) * depth, (me ^ 3) * depth
-    total = absorb(None, 0, rows, [projection, from_core], [me * depth, (me ^ 1) * depth], False)
-    weights, starts = [], []
+    later = []
+    for i in range(2):
+        at, side_at = side * share + i * piece, (1 - side) * share + i * piece
+        later += [near + at, away + at, near + side_at, away + side_at]
+    total, *blocks = product(rows, [projection, from_core], [me * depth, (me ^ 1) * depth], later, piece)
+    weights = []
     for n in range(2):
         for i in range(2):
             held = far[n][i]
             if n == 0 and i == 0:
                 held, total = lax.optimization_barrier((held, total))
             crossed = swap(held, "seq", 1)
-            at, side_at = side * share + i * piece, (1 - side) * share + i * piece
             weights.append([held, swap(held, "dp", 1), crossed, swap(crossed, "dp", 1)])
-            starts.append([near + at, away + at, near + side_at, away + side_at])
 
     def send(sums):
         return lax.all_to_all(
             sums.reshape(groups, block, columns), "seq", split_axis=0, concat_axis=0, tiled=True
         ).reshape(row_count, columns)
 
-    left = send(absorb(total, 0, rows, weights[0] + weights[1], starts[0] + starts[1], True, [weights[2][2]]))
-    right = absorb(
-        total, columns, rows, weights[2] + weights[3][:2], starts[2] + starts[3][:2], False
-    )
-    right = send(absorb(right, 0, rows, weights[3][2:], starts[3][2:], True, [left]))
+    left = send(absorb(total, 0, blocks, weights[0] + weights[1], True))
+    right = absorb(total, columns, blocks[:6], weights[2] + weights[3][:2], False)
+    left, last = lax.optimization_barrier((left, weights[3][2]))
+    right = send(absorb(right, 0, blocks[6:], [last, weights[3][3]], True))
 
     column = lax.dynamic_index_in_dim(layout[0], device, axis=1, keepdims=True)
     position = column * block + jnp.arange(block, dtype=jnp.int32)[None, :]

time: 234 us -> 220 us (0.940)
  local copies, waits for them, and re-layouts: 33.1 us -> 20.4 us
  starting transfers between devices: 59.6 us -> 63.5 us
  Pallas kernels: 44.2 us -> 41.4 us
  waiting for transfers between devices: 85.1 us -> 82.5 us
    unnamed x60 -> x68, local copies, waits for them, and re-layouts: 26.5 us -> 14.1 us
    pallas_call x4 -> x1, Pallas kernels: 21.3 us -> 10.4 us  [product(): pl.pallas_call(body, out_shape=out, in_specs=[SMEM] + [HBM] * (count + 1)...]
    pallas_call x9 -> x12, Pallas kernels: 22.8 us -> 31 us  [call(): pl.pallas_call(body, out_shape=outs, in_specs=[SMEM] * smem + [ANY] * aft...]
    ppermute x25, waiting for transfers between devices: 44 us -> 41.3 us  [swap(): return lax.ppermute(value, axis, [(i, i ^ bit) for i in range(size)])]
  transfers between devices with their start and end apart: 37 -> 37, of which waited for: 17 -> 16; matrix products, arithmetic and copies ran while one was open for 7% -> 7% of each run, Pallas kernels for 14% -> 14%
where the time goes in v6:
time: 220 us; the launch traced here: 219 us
  waiting for transfers between devices  82.5 us (38%)
  starting transfers between devices  63.5 us (29%)
  Pallas kernels  41.4 us (19%)
  local copies, waits for them, and re-layouts  20.4 us (9%)
  other arithmetic  9.33 us (4%)
    ppermute x25, waiting for transfers between devices, swap(): return lax.ppermute(value, axis, [(i, i ^ bit) for i in range(size)])  41.3 us
    pallas_call x12, Pallas kernels, call(): pl.pallas_call(body, out_shape=outs, in_specs=[SMEM] * smem + [ANY] * aft...  31 us
    ppermute x25, starting transfers between devices, swap(): return lax.ppermute(value, axis, [(i, i ^ bit) for i in range(size)])  20.5 us
    ppermute x4, starting transfers between devices, halo(): lax.ppermute(high, 'seq', up)  15 us
    unnamed x68, local copies, waits for them, and re-layouts  14.1 us
    all_to_all x2, starting transfers between devices, send(): lax.all_to_all(sums.reshape(groups, block, columns), 'seq', split_axis=0,...  12.5 us
    all_to_all x1, waiting for transfers between devices, crossed_sums(): lax.all_to_all(both, 'seq', split_axis=0, concat_axis=0, axis_index_group...  12 us
    all_to_all x2, waiting for transfers between devices, send(): lax.all_to_all(sums.reshape(groups, block, columns), 'seq', split_axis=0,...  11.4 us
  transfers between devices with their start and end apart: 37, of which 16 were waited for; matrix products, arithmetic and copies ran while one was open for 7% of the time, Pallas kernels for 14%

profile of v6, /device:TPU:0, one launch (start us, length us, event | category | flops | bytes accessed | tf_op | source)
XLA Modules:
  0.0 218.9 jit_solution(11553222175487635075)
XLA Ops:
  1.1 2.3 %fusion.9 = (bf16[512,384]{1,0:T(8,128)(2,1)S(1)}, bf16[512,384]{1,0:T(8,128)(2,1)S(1)}, bf16[512,384]{1,0:T(8,128)(2,1)S(1)}, bf16[512,384]{1,0:T(8,128)(2,1)}) fusion(bf16[2048,768]{1,0:T(8,128)(2,1)} %refs_0_.1, s32[]{:T(128)S(6)} %select_n.98, s32[]{:T(128)S(6)} %add.269, s32[]{:T(128)S(6)} %add.267), kind=kLoop, calls=%fused_computation.39 | loop fusion | bytes 3145740 | tf_op jit(solution)/shard_map/slice | solution.py:406
  3.4 2.5 %collective-permute-start.5 = (bf16[512,384]{1,0:T(8,128)(2,1)S(1)}, bf16[512,384]{1,0:T(8,128)(2,1)S(1)}, u32[]{:S(2)}, u32[]{:S(2)}) collective-permute-start(bf16[512,384]{1,0:T(8,128)(2,1)S(1)} %get-tuple-element.116), channel_id=1, source_target_pairs={{0,16},{8,24},{16,0},{24,8},{1,17},{9,25},{17,1},{25,9},{2,18},{10... | collective-permute-start | bytes 1179656 | tf_op jit(solution)/shard_map/ppermute | solution.py:322
  6.0 2.0 collective-permute-start.9
  8.1 7.9 %collective-permute-done.5.refs_12_ = bf16[512,384]{1,0:T(8,128)(2,1)S(1)} collective-permute-done((bf16[512,384]{1,0:T(8,128)(2,1)S(1)}, bf16[512,384]{1,0:T(8,128)(2,1)S(1)}, u32[]{:S(2)}, u32[]{:S(2)}) %collective-permute-start.5) | collective-permute-done | bytes 393248 | tf_op jit(solution)/shard_map/ppermute | solution.py:322
  15.9 2.0 collective-permute-start.7
  17.9 10.4 %shard_map.129 = (f32[512,768]{1,0:T(8,128)}, bf16[512,512]{1,0:T(8,128)(2,1)S(1)}, bf16[512,512]{1,0:T(8,128)(2,1)S(1)}, bf16[512,512]{1,0:T(8,128)(2,1)S(1)}, ...) custom-call(s32[10]{0:T(128)S(1)} %stack.60.starts_ref, ...), custom_call_target="tpu_custom_call" | custom-call | flops 1024 | bytes 1024 | tf_op jit(solution)/shard_map/pallas_call | solution.py:103
  28.5 2.0 collective-permute-start.11
  31.0 1.9 collective-permute-done.9.refs_10_
  33.6 4.8 %collective-permute-done.3.refs_10_ = bf16[512,384]{1,0:T(8,128)(2,1)S(1)} collective-permute-done((bf16[512,384]{1,0:T(8,128)(2,1)S(1)}, bf16[512,384]{1,0:T(8,128)(2,1)S(1)}, u32[]{:S(2)}, u32[]{:S(2)}) %collective-permute-start.3) | collective-permute-done | bytes 393248 | tf_op jit(solution)/shard_map/ppermute | solution.py:322
  38.5 2.6 %collective-permute-done.11.refs_6_ = bf16[512,384]{1,0:T(8,128)(2,1)} collective-permute-done((bf16[512,384]{1,0:T(8,128)(2,1)S(1)}, bf16[512,384]{1,0:T(8,128)(2,1)}, u32[]{:S(2)}, u32[]{:S(2)}) %collective-permute-start.11) | collective-permute-done | bytes 393248 | tf_op jit(solution)/shard_map/ppermute | solution.py:322
  41.1 1.8 collective-permute-start.13
  43.1 1.4 copy-done.2
  45.5 3.1 %shard_map.130 = bf16[512,384]{1,0:T(8,128)(2,1)} custom-call(f32[512,768]{1,0:T(8,128)S(1)} %copy-done.2, bf16[512,512]{1,0:T(8,128)(2,1)S(1)} %get-tuple-element.61.refs_0_, bf16[512,512]{1,0:T(8,128)(2,1)S(1)} %get-tuple-element.62.refs_1_, bf16[512,512]{1,0:T(8,128)(2,1)S(1)} %get-tuple-element.63.refs_2_, ...), custom_call_target="tpu_custom_call" | custom-call | flops 1024 | bytes 1024 | tf_op jit(solution)/shard_map/pallas_call | solution.py:52
  48.6 6.1 %all-to-all-start = ((bf16[8,64,384]{2,1,0:T(8,128)(2,1)}), bf16[8,64,384]{2,1,0:T(8,128)(2,1)S(1)}, u32[]{:S(2)}, u32[]{:S(2)}) async-start(bf16[8,64,384]{2,1,0:T(8,128)(2,1)} %bitcast.14), calls=%async_computation | async-start | bytes 786432 | tf_op jit(solution)/shard_map/all_to_all | solution.py:425
  55.3 8.6 %collective-permute-done.10.refs_2_ = bf16[512,384]{1,0:T(8,128)(2,1)} collective-permute-done((bf16[512,384]{1,0:T(8,128)(2,1)}, bf16[512,384]{1,0:T(8,128)(2,1)}, u32[]{:S(2)}, u32[]{:S(2)}) %collective-permute-start.10) | collective-permute-done | bytes 393248 | tf_op jit(solution)/shard_map/ppermute | solution.py:322
  67.0 3.0 %shard_map.131.old_ref = f32[512,384]{1,0:T(8,128)S(1)} custom-call(f32[512,768]{1,0:T(8,128)S(1)} %copy-done.3, bf16[512,512]{1,0:T(8,128)(2,1)S(1)} %get-tuple-element.61.refs_0_, bf16[512,512]{1,0:T(8,128)(2,1)S(1)} %get-tuple-element.62.refs_1_, bf16[512,512]{1,0:T(8,128)(2,1)S(1)} %get-tuple-element.63.refs_2_, bf16[512,512]{1,0:T(8,128)(2,1)S(1)} %copy-done.14, ...), custom_call_target="tpu_custom_call" | custom-call | flops 1024 | bytes 1024 | tf_op jit(solution)/shard_map/pallas_call | solution.py:52
  75.1 1.8 shard_map.132
  77.7 6.4 %all-to-all-start.1 = ((bf16[8,64,384]{2,1,0:T(8,128)(2,1)}), bf16[8,64,384]{2,1,0:T(8,128)(2,1)}, u32[]{:S(2)}, u32[]{:S(2)}) async-start(bf16[8,64,384]{2,1,0:T(8,128)(2,1)} %bitcast.86), calls=%async_computation.1 | async-start | bytes 786432 | tf_op jit(solution)/shard_map/all_to_all | solution.py:425
  85.1 11.4 %all-to-all-done.1 = bf16[8,64,384]{2,1,0:T(8,128)(2,1)} async-done(((bf16[8,64,384]{2,1,0:T(8,128)(2,1)}), bf16[8,64,384]{2,1,0:T(8,128)(2,1)}, u32[]{:S(2)}, u32[]{:S(2)}) %all-to-all-start.1) | async-done | bytes 393248 | tf_op jit(solution)/shard_map/all_to_all | solution.py:425
  97.5 2.1 shard_map.133
  99.7 3.4 %collective-permute-start.17 = (bf16[256,384]{1,0:T(8,128)(2,1)S(1)}, bf16[256,384]{1,0:T(8,128)(2,1)S(1)}, u32[]{:S(2)}, u32[]{:S(2)}) collective-permute-start(bf16[256,384]{1,0:T(8,128)(2,1)S(1)} %get-tuple-element.72), channel_id=1, source_target_pairs={{0,1},{1,2},{2,3},{3,4},{4,5},{5,6},{6,7},{8,9},{9,10},{10,11},{11... | collective-permute-start | bytes 589832 | tf_op jit(solution)/shard_map/ppermute | solution.py:329
  103.1 1.5 collective-permute-start.18
  105.5 5.4 %collective-permute-done.17.prev_ref = bf16[256,384]{1,0:T(8,128)(2,1)S(1)} collective-permute-done((bf16[256,384]{1,0:T(8,128)(2,1)S(1)}, bf16[256,384]{1,0:T(8,128)(2,1)S(1)}, u32[]{:S(2)}, u32[]{:S(2)}) %collective-permute-start.17) | collective-permute-done | bytes 196640 | tf_op jit(solution)/shard_map/ppermute | solution.py:329
  111.8 4.5 %collective-permute-start.19 = (bf16[128,384]{1,0:T(8,128)(2,1)S(1)}, bf16[128,384]{1,0:T(8,128)(2,1)S(1)}, u32[]{:S(2)}, u32[]{:S(2)}) collective-permute-start(bf16[128,384]{1,0:T(8,128)(2,1)S(1)} %get-tuple-element.77), channel_id=1, source_target_pairs={{0,1},{1,2},{2,3},{3,4},{4,5},{5,6},{6,7},{8,9},{9,10},{10,11},{11... | collective-permute-start | bytes 294920 | tf_op jit(solution)/shard_map/ppermute | solution.py:329
  116.4 1.3 collective-permute-start.20
  118.6 4.3 %collective-permute-done.20.refs_4_ = bf16[128,384]{1,0:T(8,128)(2,1)S(1)} collective-permute-done((bf16[128,384]{1,0:T(8,128)(2,1)S(1)}, bf16[128,384]{1,0:T(8,128)(2,1)S(1)}, u32[]{:S(2)}, u32[]{:S(2)}) %collective-permute-start.20) | collective-permute-done | bytes 98336 | tf_op jit(solution)/shard_map/ppermute | solution.py:330
  122.9 3.7 %shard_map.136 = (bf16[256,384]{1,0:T(8,128)(2,1)S(1)}, bf16[128,768]{1,0:T(8,128)(2,1)S(1)}, bf16[128,2048]{1,0:T(8,128)(2,1)S(1)}, bf16[128,768]{1,0:T(8,128)(...) custom-call(s32[2]{0:T(128)S(1)} %get-tuple-element.123.refs_0_, ...), custom_call_target="tpu_custom_call" | custom-call | flops 1024 | bytes 1024 | tf_op jit(solution)/shard_map/pallas_call | solution.py:52
  126.6 1.5 shard_map.137
  128.2 4.0 %collective-permute-start.22 = (bf16[128,384]{1,0:T(8,128)(2,1)S(1)}, bf16[128,384]{1,0:T(8,128)(2,1)S(1)}, u32[]{:S(2)}, u32[]{:S(2)}) collective-permute-start(bf16[128,384]{1,0:T(8,128)(2,1)S(1)} %get-tuple-element.86.refs_3_.refs_6_), channel_id=1, source_target_pairs={{0,1},{1,2},{2,3},{3,4},{4,5},{5,6},{6,7},{8,9},{9,10},{10,11},{11... | collective-permute-start | bytes 294920 | tf_op jit(solution)/shard_map/ppermute | solution.py:329
  132.2 1.3 collective-permute-start.23
  134.9 4.1 %collective-permute-done.23.refs_4_.refs_7_ = bf16[128,384]{1,0:T(8,128)(2,1)S(1)} collective-permute-done((bf16[128,384]{1,0:T(8,128)(2,1)S(1)}, bf16[128,384]{1,0:T(8,128)(2,1)S(1)}, u32[]{:S(2)}, u32[]{:S(2)}) %collective-permute-start.23) | collective-permute-done | bytes 98336 | tf_op jit(solution)/shard_map/ppermute | solution.py:330
  139.0 1.5 collective-permute-start.26
  140.5 2.4 %shard_map.138 = (f32[256,768]{1,0:T(8,128)}, bf16[256,768]{1,0:T(8,128)(2,1)S(1)}, bf16[256,384]{1,0:T(8,128)(2,1)S(1)}, bf16[256,384]{1,0:T(8,128)(2,1)S(1)}) custom-call(bf16[768,512]{1,0:T(8,128)(2,1)S(1)} %fusion.1.refs_0_, bf16[128,384]{1,0:T(8,128)(2,1)S(1)} %collective-permute-done.22.refs_1_.refs_4_, ...), custom_call_target="tpu_custom_call" | custom-call | flops 1024 | bytes 1024 | tf_op jit(solution)/shard_map/pallas_call | solution.py:52
  143.0 3.1 %collective-permute-start.24 = (bf16[256,384]{1,0:T(8,128)(2,1)S(1)}, bf16[256,384]{1,0:T(8,128)(2,1)S(1)}, u32[]{:S(2)}, u32[]{:S(2)}) collective-permute-start(bf16[256,384]{1,0:T(8,128)(2,1)S(1)} %get-tuple-element.94.refs_6_), channel_id=1, source_target_pairs={{0,1},{1,2},{2,3},{3,4},{4,5},{5,6},{6,7},{8,9},{9,10},{10,11},{11... | collective-permute-start | bytes 589832 | tf_op jit(solution)/shard_map/ppermute | solution.py:329
  146.1 1.3 collective-permute-start.25
  147.4 4.2 %shard_map.139 = (bf16[2,768,384]{2,1,0:T(8,128)(2,1)S(1)}, bf16[2,768,384]{2,1,0:T(8,128)(2,1)S(1)}) custom-call(s32[2]{0:T(128)S(1)} %get-tuple-element.122.ids_ref.refs_0_, bf16[256,384]{1,0:T(8,128)(2,1)S(1)} %get-tuple-element.93.refs_1_.refs_5_, bf16[128,768]{1,0:T(8,128)(2,1)S(1)} %get-tuple-element.78.refs_2_, ...), custom_call_target="tpu_custom_call" | custom-call | flops 1024 | bytes 1024 | tf_op jit(solution)/shard_map/pallas_call | solution.py:52
  151.6 2.0 collective-permute-done.25.refs_7_
  153.7 6.3 %shard_map.140 = (bf16[2,768,384]{2,1,0:T(8,128)(2,1)S(1)}, bf16[2,768,384]{2,1,0:T(8,128)(2,1)}) custom-call(s32[2]{0:T(128)S(1)} %get-tuple-element.122.ids_ref.refs_0_, bf16[256,384]{1,0:T(8,128)(2,1)S(1)} %get-tuple-element.93.refs_1_.refs_5_, bf16[256,768]{1,0:T(8,128)(2,1)S(1)} %get-tuple-element.74.low_ref.refs_2_, ...), custom_call_target="tpu_custom_call" | custom-call | flops 1024 | bytes 1024 | tf_op jit(solution)/shard_map/pallas_call | solution.py:52
  162.7 2.1 fusion.3
  164.8 2.6 %collective-permute-start.31 = (bf16[2,4,96,384]{3,2,1,0:T(8,128)(2,1)}, bf16[2,4,96,384]{3,2,1,0:T(8,128)(2,1)S(1)}, u32[]{:S(2)}, u32[]{:S(2)}) collective-permute-start(bf16[2,4,96,384]{3,2,1,0:T(8,128)(2,1)} %fusion.3), channel_id=1, source_target_pairs={{0,1},{1,0},{2,3},{3,2},{4,5},{5,4},{6,7},{7,6},{8,9},{9,8},{10,11... | collective-permute-start | bytes 1769480 | tf_op jit(solution)/shard_map/ppermute | solution.py:322
  170.5 4.7 %all-to-all-start.2 = ((bf16[8,96,512]{2,1,0:T(8,128)(2,1)}), bf16[8,96,512]{2,1,0:T(8,128)(2,1)S(1)}, u32[]{:S(2)}, u32[]{:S(2)}) async-start(bf16[8,96,512]{2,1,0:T(8,128)(2,1)} %bitcast.38), calls=%async_computation.2 | async-start | bytes 1572864 | tf_op jit(solution)/shard_map/all_to_all | solution.py:344
  175.2 1.4 fusion.11
  176.6 10.1 %collective-permute-done.31 = bf16[2,4,96,384]{3,2,1,0:T(8,128)(2,1)S(1)} collective-permute-done((bf16[2,4,96,384]{3,2,1,0:T(8,128)(2,1)}, bf16[2,4,96,384]{3,2,1,0:T(8,128)(2,1)S(1)}, u32[]{:S(2)}, u32[]{:S(2)}) %collective-permute-start.31) | collective-permute-done | bytes 589856 | tf_op jit(solution)/shard_map/ppermute | solution.py:322
  189.6 2.6 %collective-permute-start.29 = (bf16[4,96,384]{2,1,0:T(8,128)(2,1)S(1)}, bf16[4,96,384]{2,1,0:T(8,128)(2,1)S(1)}, u32[]{:S(2)}, u32[]{:S(2)}) collective-permute-start(bf16[4,96,384]{2,1,0:T(8,128)(2,1)S(1)} %fusion.8), channel_id=1, source_target_pairs={{0,1},{1,0},{2,3},{3,2},{4,5},{5,4},{6,7},{7,6},{8,9},{9,8},{10,11... | collective-permute-start | bytes 884744 | tf_op jit(solution)/shard_map/ppermute | solution.py:322
  192.2 1.4 collective-permute-done.32
  193.8 4.0 %collective-permute-done.29 = bf16[4,96,384]{2,1,0:T(8,128)(2,1)S(1)} collective-permute-done((bf16[4,96,384]{2,1,0:T(8,128)(2,1)S(1)}, bf16[4,96,384]{2,1,0:T(8,128)(2,1)S(1)}, u32[]{:S(2)}, u32[]{:S(2)}) %collective-permute-start.29) | collective-permute-done | bytes 294944 | tf_op jit(solution)/shard_map/ppermute | solution.py:322
  199.8 5.4 %all-to-all-start.3 = ((bf16[4,96,768]{2,1,0:T(8,128)(2,1)}), bf16[4,96,768]{2,1,0:T(8,128)(2,1)S(1)}, u32[]{:S(2)}, u32[]{:S(2)}) async-start(bf16[4,96,768]{2,1,0:T(8,128)(2,1)} %pad_maximum_fusion), calls=%async_computation.3 | async-start | bytes 1179648 | tf_op jit(solution)/shard_map/all_to_all | solution.py:381
  206.0 12.0 %all-to-all-done.3.parts_ref = bf16[4,96,768]{2,1,0:T(8,128)(2,1)S(1)} async-done(((bf16[4,96,768]{2,1,0:T(8,128)(2,1)}), bf16[4,96,768]{2,1,0:T(8,128)(2,1)S(1)}, u32[]{:S(2)}, u32[]{:S(2)}) %all-to-all-start.3) | async-done | bytes 589856 | tf_op jit(solution)/shard_map/all_to_all | solution.py:381
  (128 shorter events, 30.9 us)
Async XLA Ops:
  0.6 17.3 %collective-permute-start.1 = (bf16[2048,768]{1,0:T(8,128)(2,1)}, bf16[2048,768]{1,0:T(8,128)(2,1)}, u32[]{:S(2)}, u32[]{:S(2)}) collective-permute-start(bf16[2048,768]{1,0:T(8,128)(2,1)} %refs_0_.1), channel_id=1, source_target_pairs={{0,8},{8,0},{16,24},{24,16},{1,9},{9,1},{17,25},{25,17},{2,10},{10... | collective-permute-start | bytes 9437192 | tf_op jit(solution)/shard_map/ppermute | solution.py:322
  3.4 12.5 %collective-permute-start.5 = (bf16[512,384]{1,0:T(8,128)(2,1)S(1)}, bf16[512,384]{1,0:T(8,128)(2,1)S(1)}, u32[]{:S(2)}, u32[]{:S(2)}) collective-permute-start(bf16[512,384]{1,0:T(8,128)(2,1)S(1)} %get-tuple-element.116), channel_id=1, source_target_pairs={{0,16},{8,24},{16,0},{24,8},{1,17},{9,25},{17,1},{25,9},{2,18},{10... | collective-permute-start | bytes 1179656 | tf_op jit(solution)/shard_map/ppermute | solution.py:322
  6.0 22.5 %collective-permute-start = (bf16[512,384]{1,0:T(8,128)(2,1)}, bf16[512,384]{1,0:T(8,128)(2,1)S(1)}, u32[]{:S(2)}, u32[]{:S(2)}) collective-permute-start(bf16[512,384]{1,0:T(8,128)(2,1)} %get-tuple-element.117), channel_id=1, source_target_pairs={{0,16},{8,24},{16,0},{24,8},{1,17},{9,25},{17,1},{25,9},{2,18},{10... | collective-permute-start | bytes 1179656 | tf_op jit(solution)/shard_map/ppermute | solution.py:322
  6.0 26.9 %collective-permute-start.9 = (bf16[512,384]{1,0:T(8,128)(2,1)S(1)}, bf16[512,384]{1,0:T(8,128)(2,1)}, u32[]{:S(2)}, u32[]{:S(2)}) collective-permute-start(bf16[512,384]{1,0:T(8,128)(2,1)S(1)} %get-tuple-element.115), channel_id=1, source_target_pairs={{0,16},{8,24},{16,0},{24,8},{1,17},{9,25},{17,1},{25,9},{2,18},{10... | collective-permute-start | bytes 1179656 | tf_op jit(solution)/shard_map/ppermute | solution.py:322
  15.9 14.6 %collective-permute-start.7 = (bf16[512,384]{1,0:T(8,128)(2,1)S(1)}, bf16[512,384]{1,0:T(8,128)(2,1)S(1)}, u32[]{:S(2)}, u32[]{:S(2)}) collective-permute-start(bf16[512,384]{1,0:T(8,128)(2,1)S(1)} %collective-permute-done.5.refs_12_), channel_id=1, source_target_pairs={{0,1},{1,0},{2,3},{3,2},{4,5},{5,4},{6,7},{7,6},{8,9},{9,8},{10,11... | collective-permute-start | bytes 1179656 | tf_op jit(solution)/shard_map/ppermute | solution.py:322
  28.4 20.3 %copy-start.9 = (bf16[512,512]{1,0:T(8,128)(2,1)}, bf16[512,512]{1,0:T(8,128)(2,1)S(1)}, u32[]{:S(2)}) copy-start(bf16[512,512]{1,0:T(8,128)(2,1)S(1)} %get-tuple-element.67.refs_6_.refs_0_) | copy-start | bytes 1572868
  28.4 20.2 %copy-start.11 = (bf16[512,512]{1,0:T(8,128)(2,1)}, bf16[512,512]{1,0:T(8,128)(2,1)S(1)}, u32[]{:S(2)}) copy-start(bf16[512,512]{1,0:T(8,128)(2,1)S(1)} %get-tuple-element.68.refs_7_.refs_1_) | copy-start | bytes 1572868
  28.4 20.2 %copy-start.13 = (bf16[512,512]{1,0:T(8,128)(2,1)}, bf16[512,512]{1,0:T(8,128)(2,1)S(1)}, u32[]{:S(2)}) copy-start(bf16[512,512]{1,0:T(8,128)(2,1)S(1)} %get-tuple-element.64.refs_3_) | copy-start | bytes 1572868
  28.4 20.2 %copy-start.15 = (bf16[512,512]{1,0:T(8,128)(2,1)}, bf16[512,512]{1,0:T(8,128)(2,1)S(1)}, u32[]{:S(2)}) copy-start(bf16[512,512]{1,0:T(8,128)(2,1)S(1)} %get-tuple-element.65.refs_4_) | copy-start | bytes 1572868
  28.4 20.2 %copy-start.17 = (bf16[512,512]{1,0:T(8,128)(2,1)}, bf16[512,512]{1,0:T(8,128)(2,1)S(1)}, u32[]{:S(2)}) copy-start(bf16[512,512]{1,0:T(8,128)(2,1)S(1)} %get-tuple-element.66.refs_5_) | copy-start | bytes 1572868
  28.4 10.0 %collective-permute-start.3 = (bf16[512,384]{1,0:T(8,128)(2,1)S(1)}, bf16[512,384]{1,0:T(8,128)(2,1)S(1)}, u32[]{:S(2)}, u32[]{:S(2)}) collective-permute-start(bf16[512,384]{1,0:T(8,128)(2,1)S(1)} %collective-permute-done.refs_8_), channel_id=1, source_target_pairs={{0,1},{1,0},{2,3},{3,2},{4,5},{5,4},{6,7},{7,6},{8,9},{9,8},{10,11... | collective-permute-start | bytes 1179656 | tf_op jit(solution)/shard_map/ppermute | solution.py:322
  28.5 12.5 %collective-permute-start.11 = (bf16[512,384]{1,0:T(8,128)(2,1)S(1)}, bf16[512,384]{1,0:T(8,128)(2,1)}, u32[]{:S(2)}, u32[]{:S(2)}) collective-permute-start(bf16[512,384]{1,0:T(8,128)(2,1)S(1)} %get-tuple-element.114), channel_id=1, source_target_pairs={{0,16},{8,24},{16,0},{24,8},{1,17},{9,25},{17,1},{25,9},{2,18},{10... | collective-permute-start | bytes 1179656 | tf_op jit(solution)/shard_map/ppermute | solution.py:322
  30.5 12.4 %collective-permute-start.6 = (bf16[512,384]{1,0:T(8,128)(2,1)S(1)}, bf16[512,384]{1,0:T(8,128)(2,1)S(1)}, u32[]{:S(2)}, u32[]{:S(2)}) collective-permute-start(bf16[512,384]{1,0:T(8,128)(2,1)S(1)} %collective-permute-done.5.refs_12_), channel_id=1, source_target_pairs={{0,8},{8,0},{16,24},{24,16},{1,9},{9,1},{17,25},{25,17},{2,10},{10... | collective-permute-start | bytes 1179656 | tf_op jit(solution)/shard_map/ppermute | solution.py:322
  30.5 12.6 %collective-permute-start.8 = (bf16[512,384]{1,0:T(8,128)(2,1)S(1)}, bf16[512,384]{1,0:T(8,128)(2,1)S(1)}, u32[]{:S(2)}, u32[]{:S(2)}) collective-permute-start(bf16[512,384]{1,0:T(8,128)(2,1)S(1)} %collective-permute-done.7.refs_14_), channel_id=1, source_target_pairs={{0,8},{8,0},{16,24},{24,16},{1,9},{9,1},{17,25},{25,17},{2,10},{10... | collective-permute-start | bytes 1179656 | tf_op jit(solution)/shard_map/ppermute | solution.py:322
  32.9 10.2 %collective-permute-start.2 = (bf16[512,384]{1,0:T(8,128)(2,1)S(1)}, bf16[512,384]{1,0:T(8,128)(2,1)S(1)}, u32[]{:S(2)}, u32[]{:S(2)}) collective-permute-start(bf16[512,384]{1,0:T(8,128)(2,1)S(1)} %collective-permute-done.refs_8_), channel_id=1, source_target_pairs={{0,8},{8,0},{16,24},{24,16},{1,9},{9,1},{17,25},{25,17},{2,10},{10... | collective-permute-start | bytes 1179656 | tf_op jit(solution)/shard_map/ppermute | solution.py:322
  38.5 4.6 %collective-permute-start.4 = (bf16[512,384]{1,0:T(8,128)(2,1)S(1)}, bf16[512,384]{1,0:T(8,128)(2,1)S(1)}, u32[]{:S(2)}, u32[]{:S(2)}) collective-permute-start(bf16[512,384]{1,0:T(8,128)(2,1)S(1)} %collective-permute-done.3.refs_10_), channel_id=1, source_target_pairs={{0,8},{8,0},{16,24},{24,16},{1,9},{9,1},{17,25},{25,17},{2,10},{10... | collective-permute-start | bytes 1179656 | tf_op jit(solution)/shard_map/ppermute | solution.py:322
  41.1 14.2 %collective-permute-start.13 = (bf16[512,384]{1,0:T(8,128)(2,1)}, bf16[512,384]{1,0:T(8,128)(2,1)}, u32[]{:S(2)}, u32[]{:S(2)}) collective-permute-start(bf16[512,384]{1,0:T(8,128)(2,1)} %collective-permute-done.11.refs_6_), channel_id=1, source_target_pairs={{0,1},{1,0},{2,3},{3,2},{4,5},{5,4},{6,7},{7,6},{8,9},{9,8},{10,11... | collective-permute-start | bytes 1179656 | tf_op jit(solution)/shard_map/ppermute | solution.py:322
  42.9 21.0 %collective-permute-start.10 = (bf16[512,384]{1,0:T(8,128)(2,1)}, bf16[512,384]{1,0:T(8,128)(2,1)}, u32[]{:S(2)}, u32[]{:S(2)}) collective-permute-start(bf16[512,384]{1,0:T(8,128)(2,1)} %collective-permute-done.9.refs_10_), channel_id=1, source_target_pairs={{0,1},{1,0},{2,3},{3,2},{4,5},{5,4},{6,7},{7,6},{8,9},{9,8},{10,11... | collective-permute-start | bytes 1179656 | tf_op jit(solution)/shard_map/ppermute | solution.py:322
  45.5 18.4 %copy-start.3 = (f32[512,768]{1,0:T(8,128)S(1)}, f32[512,768]{1,0:T(8,128)}, u32[]{:S(2)}) copy-start(f32[512,768]{1,0:T(8,128)} %get-tuple-element.60.old_ref) | copy-start | bytes 4718596
  48.6 22.3 %all-to-all-start = ((bf16[8,64,384]{2,1,0:T(8,128)(2,1)}), bf16[8,64,384]{2,1,0:T(8,128)(2,1)S(1)}, u32[]{:S(2)}, u32[]{:S(2)}) async-start(bf16[8,64,384]{2,1,0:T(8,128)(2,1)} %bitcast.14), calls=%async_computation | async-start | bytes 786432 | tf_op jit(solution)/shard_map/all_to_all | solution.py:425
  54.7 9.1 %collective-permute-start.12 = (bf16[512,384]{1,0:T(8,128)(2,1)}, bf16[512,384]{1,0:T(8,128)(2,1)S(1)}, u32[]{:S(2)}, u32[]{:S(2)}) collective-permute-start(bf16[512,384]{1,0:T(8,128)(2,1)} %collective-permute-done.11.refs_6_), channel_id=1, source_target_pairs={{0,8},{8,0},{16,24},{24,16},{1,9},{9,1},{17,25},{25,17},{2,10},{10... | collective-permute-start | bytes 1179656 | tf_op jit(solution)/shard_map/ppermute | solution.py:322
  54.7 9.1 %collective-permute-start.15 = (bf16[512,384]{1,0:T(8,128)(2,1)}, bf16[512,384]{1,0:T(8,128)(2,1)S(1)}, u32[]{:S(2)}, u32[]{:S(2)}) collective-permute-start(bf16[512,384]{1,0:T(8,128)(2,1)} %collective-permute-done.9.refs_10_), channel_id=1, source_target_pairs={{0,8},{8,0},{16,24},{24,16},{1,9},{9,1},{17,25},{25,17},{2,10},{10... | collective-permute-start | bytes 1179656 | tf_op jit(solution)/shard_map/ppermute | solution.py:322
  55.2 8.6 %collective-permute-start.14 = (bf16[512,384]{1,0:T(8,128)(2,1)}, bf16[512,384]{1,0:T(8,128)(2,1)S(1)}, u32[]{:S(2)}, u32[]{:S(2)}) collective-permute-start(bf16[512,384]{1,0:T(8,128)(2,1)} %collective-permute-done.13.refs_8_), channel_id=1, source_target_pairs={{0,8},{8,0},{16,24},{24,16},{1,9},{9,1},{17,25},{25,17},{2,10},{10... | collective-permute-start | bytes 1179656 | tf_op jit(solution)/shard_map/ppermute | solution.py:322
  63.9 7.8 %collective-permute-start.16 = (bf16[512,384]{1,0:T(8,128)(2,1)}, bf16[512,384]{1,0:T(8,128)(2,1)}, u32[]{:S(2)}, u32[]{:S(2)}) collective-permute-start(bf16[512,384]{1,0:T(8,128)(2,1)} %collective-permute-done.10.refs_2_), channel_id=1, source_target_pairs={{0,8},{8,0},{16,24},{24,16},{1,9},{9,1},{17,25},{25,17},{2,10},{10... | collective-permute-start | bytes 1179656 | tf_op jit(solution)/shard_map/ppermute | solution.py:322
  71.7 24.8 %copy-start = (bf16[2,3,768,384]{3,2,1,0:T(8,128)(2,1)S(1)}, bf16[2,3,768,384]{3,2,1,0:T(8,128)(2,1)}, u32[]{:S(2)}) copy-start(bf16[2,3,768,384]{3,2,1,0:T(8,128)(2,1)} %refs_7_.3) | copy-start | bytes 10616836
  75.1 9.7 %copy-start.33 = (s32[1,8,8]{2,1,0:T(8,128)S(1)}, s32[1,8,8]{2,1,0:T(8,128)}, u32[]{:S(2)}) copy-start(s32[1,8,8]{2,1,0:T(8,128)} %param.11) | copy-start | bytes 772
  77.7 18.9 %all-to-all-start.1 = ((bf16[8,64,384]{2,1,0:T(8,128)(2,1)}), bf16[8,64,384]{2,1,0:T(8,128)(2,1)}, u32[]{:S(2)}, u32[]{:S(2)}) async-start(bf16[8,64,384]{2,1,0:T(8,128)(2,1)} %bitcast.86), calls=%async_computation.1 | async-start | bytes 786432 | tf_op jit(solution)/shard_map/all_to_all | solution.py:425
  99.7 11.3 %collective-permute-start.17 = (bf16[256,384]{1,0:T(8,128)(2,1)S(1)}, bf16[256,384]{1,0:T(8,128)(2,1)S(1)}, u32[]{:S(2)}, u32[]{:S(2)}) collective-permute-start(bf16[256,384]{1,0:T(8,128)(2,1)S(1)} %get-tuple-element.72), channel_id=1, source_target_pairs={{0,1},{1,2},{2,3},{3,4},{4,5},{5,6},{6,7},{8,9},{9,10},{10,11},{11... | collective-permute-start | bytes 589832 | tf_op jit(solution)/shard_map/ppermute | solution.py:329
  103.1 7.9 %collective-permute-start.18 = (bf16[256,384]{1,0:T(8,128)(2,1)S(1)}, bf16[256,384]{1,0:T(8,128)(2,1)S(1)}, u32[]{:S(2)}, u32[]{:S(2)}) collective-permute-start(bf16[256,384]{1,0:T(8,128)(2,1)S(1)} %get-tuple-element.73), channel_id=1, source_target_pairs={{1,0},{2,1},{3,2},{4,3},{5,4},{6,5},{7,6},{9,8},{10,9},{11,10},{12... | collective-permute-start | bytes 589832 | tf_op jit(solution)/shard_map/ppermute | solution.py:330
  111.0 11.9 %copy-start.6 = (bf16[768,2048]{1,0:T(8,128)(2,1)S(1)}, bf16[768,2048]{1,0:T(8,128)(2,1)}, u32[]{:S(2)}) copy-start(bf16[768,2048]{1,0:T(8,128)(2,1)} %refs_8_.2) | copy-start | bytes 9437188
  111.0 11.9 %copy-start.24 = (s32[1,128,2048]{2,1,0:T(8,128)S(1)}, s32[1,128,2048]{2,1,0:T(8,128)}, u32[]{:S(2)}) copy-start(s32[1,128,2048]{2,1,0:T(8,128)} %param.13) | copy-start | bytes 3145732
  111.8 6.7 %collective-permute-start.19 = (bf16[128,384]{1,0:T(8,128)(2,1)S(1)}, bf16[128,384]{1,0:T(8,128)(2,1)S(1)}, u32[]{:S(2)}, u32[]{:S(2)}) collective-permute-start(bf16[128,384]{1,0:T(8,128)(2,1)S(1)} %get-tuple-element.77), channel_id=1, source_target_pairs={{0,1},{1,2},{2,3},{3,4},{4,5},{5,6},{6,7},{8,9},{9,10},{10,11},{11... | collective-permute-start | bytes 294920 | tf_op jit(solution)/shard_map/ppermute | solution.py:329
  116.4 6.5 %collective-permute-start.20 = (bf16[128,384]{1,0:T(8,128)(2,1)S(1)}, bf16[128,384]{1,0:T(8,128)(2,1)S(1)}, u32[]{:S(2)}, u32[]{:S(2)}) collective-permute-start(bf16[128,384]{1,0:T(8,128)(2,1)S(1)} %get-tuple-element.80), channel_id=1, source_target_pairs={{1,0},{2,1},{3,2},{4,3},{5,4},{6,5},{7,6},{9,8},{10,9},{11,10},{12... | collective-permute-start | bytes 294920 | tf_op jit(solution)/shard_map/ppermute | solution.py:330
  128.2 5.4 %collective-permute-start.21 = (bf16[2,768,512]{2,1,0:T(8,128)(2,1)S(1)}, bf16[2,768,512]{2,1,0:T(8,128)(2,1)S(1)}, u32[]{:S(2)}, u32[]{:S(2)}) collective-permute-start(bf16[2,768,512]{2,1,0:T(8,128)(2,1)S(1)} %get-tuple-element.85), channel_id=1, source_target_pairs={{0,8},{8,0},{16,24},{24,16},{1,9},{9,1},{17,25},{25,17},{2,10},{10... | collective-permute-start | bytes 4718600 | tf_op jit(solution)/shard_map/ppermute | solution.py:322
  128.2 6.7 %collective-permute-start.22 = (bf16[128,384]{1,0:T(8,128)(2,1)S(1)}, bf16[128,384]{1,0:T(8,128)(2,1)S(1)}, u32[]{:S(2)}, u32[]{:S(2)}) collective-permute-start(bf16[128,384]{1,0:T(8,128)(2,1)S(1)} %get-tuple-element.86.refs_3_.refs_6_), channel_id=1, source_target_pairs={{0,1},{1,2},{2,3},{3,4},{4,5},{5,6},{6,7},{8,9},{9,10},{10,11},{11... | collective-permute-start | bytes 294920 | tf_op jit(solution)/shard_map/ppermute | solution.py:329
  132.2 6.8 %collective-permute-start.23 = (bf16[128,384]{1,0:T(8,128)(2,1)S(1)}, bf16[128,384]{1,0:T(8,128)(2,1)S(1)}, u32[]{:S(2)}, u32[]{:S(2)}) collective-permute-start(bf16[128,384]{1,0:T(8,128)(2,1)S(1)} %get-tuple-element.87.refs_2_.refs_5_), channel_id=1, source_target_pairs={{1,0},{2,1},{3,2},{4,3},{5,4},{6,5},{7,6},{9,8},{10,9},{11,10},{12... | collective-permute-start | bytes 294920 | tf_op jit(solution)/shard_map/ppermute | solution.py:330
  139.0 20.9 %collective-permute-start.26 = (bf16[768,512]{1,0:T(8,128)(2,1)S(1)}, bf16[768,512]{1,0:T(8,128)(2,1)S(1)}, u32[]{:S(2)}, u32[]{:S(2)}) collective-permute-start(bf16[768,512]{1,0:T(8,128)(2,1)S(1)} %fusion.1.refs_0_), channel_id=1, source_target_pairs={{0,16},{8,24},{16,0},{24,8},{1,17},{9,25},{17,1},{25,9},{2,18},{10... | collective-permute-start | bytes 2359304 | tf_op jit(solution)/shard_map/ppermute | solution.py:322
  143.0 8.6 %collective-permute-start.24 = (bf16[256,384]{1,0:T(8,128)(2,1)S(1)}, bf16[256,384]{1,0:T(8,128)(2,1)S(1)}, u32[]{:S(2)}, u32[]{:S(2)}) collective-permute-start(bf16[256,384]{1,0:T(8,128)(2,1)S(1)} %get-tuple-element.94.refs_6_), channel_id=1, source_target_pairs={{0,1},{1,2},{2,3},{3,4},{4,5},{5,6},{6,7},{8,9},{9,10},{10,11},{11... | collective-permute-start | bytes 589832 | tf_op jit(solution)/shard_map/ppermute | solution.py:329
  146.1 7.6 %collective-permute-start.25 = (bf16[256,384]{1,0:T(8,128)(2,1)S(1)}, bf16[256,384]{1,0:T(8,128)(2,1)S(1)}, u32[]{:S(2)}, u32[]{:S(2)}) collective-permute-start(bf16[256,384]{1,0:T(8,128)(2,1)S(1)} %get-tuple-element.93.refs_1_.refs_5_), channel_id=1, source_target_pairs={{1,0},{2,1},{3,2},{4,3},{5,4},{6,5},{7,6},{9,8},{10,9},{11,10},{12... | collective-permute-start | bytes 589832 | tf_op jit(solution)/shard_map/ppermute | solution.py:330
  153.7 9.0 %collective-permute-start.30 = (bf16[2,768,384]{2,1,0:T(8,128)(2,1)S(1)}, bf16[2,768,384]{2,1,0:T(8,128)(2,1)}, u32[]{:S(2)}, u32[]{:S(2)}) collective-permute-start(bf16[2,768,384]{2,1,0:T(8,128)(2,1)S(1)} %get-tuple-element.107), channel_id=1, source_target_pairs={{0,8},{8,0},{16,24},{24,16},{1,9},{9,1},{17,25},{25,17},{2,10},{10... | collective-permute-start | bytes 3538952 | tf_op jit(solution)/shard_map/ppermute | solution.py:322
  161.0 6.5 %collective-permute-start.27 = (bf16[2,768,384]{2,1,0:T(8,128)(2,1)}, bf16[2,768,384]{2,1,0:T(8,128)(2,1)}, u32[]{:S(2)}, u32[]{:S(2)}) collective-permute-start(bf16[2,768,384]{2,1,0:T(8,128)(2,1)} %get-tuple-element.103), channel_id=1, source_target_pairs={{0,8},{8,0},{16,24},{24,16},{1,9},{9,1},{17,25},{25,17},{2,10},{10... | collective-permute-start | bytes 3538952 | tf_op jit(solution)/shard_map/ppermute | solution.py:322
  164.8 21.9 %collective-permute-start.31 = (bf16[2,4,96,384]{3,2,1,0:T(8,128)(2,1)}, bf16[2,4,96,384]{3,2,1,0:T(8,128)(2,1)S(1)}, u32[]{:S(2)}, u32[]{:S(2)}) collective-permute-start(bf16[2,4,96,384]{3,2,1,0:T(8,128)(2,1)} %fusion.3), channel_id=1, source_target_pairs={{0,1},{1,0},{2,3},{3,2},{4,5},{5,4},{6,7},{7,6},{8,9},{9,8},{10,11... | collective-permute-start | bytes 1769480 | tf_op jit(solution)/shard_map/ppermute | solution.py:322
  168.6 19.9 %collective-permute-start.28 = (bf16[768,384]{1,0:T(8,128)(2,1)S(1)}, bf16[768,384]{1,0:T(8,128)(2,1)}, u32[]{:S(2)}, u32[]{:S(2)}) collective-permute-start(bf16[768,384]{1,0:T(8,128)(2,1)S(1)} %fusion.2), channel_id=1, source_target_pairs={{0,16},{8,24},{16,0},{24,8},{1,17},{9,25},{17,1},{25,9},{2,18},{10... | collective-permute-start | bytes 1769480 | tf_op jit(solution)/shard_map/ppermute | solution.py:322
  170.5 29.3 %all-to-all-start.2 = ((bf16[8,96,512]{2,1,0:T(8,128)(2,1)}), bf16[8,96,512]{2,1,0:T(8,128)(2,1)S(1)}, u32[]{:S(2)}, u32[]{:S(2)}) async-start(bf16[8,96,512]{2,1,0:T(8,128)(2,1)} %bitcast.38), calls=%async_computation.2 | async-start | bytes 1572864 | tf_op jit(solution)/shard_map/all_to_all | solution.py:344
  175.2 11.5 %copy-start.30 = (bf16[1,768,384]{2,1,0:T(8,128)(2,1)S(1)}, bf16[1,768,384]{2,1,0:T(8,128)(2,1)}, u32[]{:S(2)}) copy-start(bf16[1,768,384]{2,1,0:T(8,128)(2,1)} %get-tuple-element.119) | copy-start | bytes 1769476
  186.8 6.8 %collective-permute-start.32 = (bf16[4,96,384]{2,1,0:T(8,128)(2,1)S(1)}, bf16[4,96,384]{2,1,0:T(8,128)(2,1)S(1)}, u32[]{:S(2)}, u32[]{:S(2)}) collective-permute-start(bf16[4,96,384]{2,1,0:T(8,128)(2,1)S(1)} %fusion.4), channel_id=1, source_target_pairs={{0,16},{8,24},{16,0},{24,8},{1,17},{9,25},{17,1},{25,9},{2,18},{10... | collective-permute-start | bytes 884744 | tf_op jit(solution)/shard_map/ppermute | solution.py:322
  189.6 8.2 %collective-permute-start.29 = (bf16[4,96,384]{2,1,0:T(8,128)(2,1)S(1)}, bf16[4,96,384]{2,1,0:T(8,128)(2,1)S(1)}, u32[]{:S(2)}, u32[]{:S(2)}) collective-permute-start(bf16[4,96,384]{2,1,0:T(8,128)(2,1)S(1)} %fusion.8), channel_id=1, source_target_pairs={{0,1},{1,0},{2,3},{3,2},{4,5},{5,4},{6,7},{7,6},{8,9},{9,8},{10,11... | collective-permute-start | bytes 884744 | tf_op jit(solution)/shard_map/ppermute | solution.py:322
  199.8 18.2 %all-to-all-start.3 = ((bf16[4,96,768]{2,1,0:T(8,128)(2,1)}), bf16[4,96,768]{2,1,0:T(8,128)(2,1)S(1)}, u32[]{:S(2)}, u32[]{:S(2)}) async-start(bf16[4,96,768]{2,1,0:T(8,128)(2,1)} %pad_maximum_fusion), calls=%async_computation.3 | async-start | bytes 1179648 | tf_op jit(solution)/shard_map/all_to_all | solution.py:381
  (23 other events, 71.8 us)

commit v7 on v6

--- a/solution.py
+++ b/solution.py
@@ -132,7 +132,7 @@
             out_ref[part] = sums.astype(out_ref.dtype)
 
     return call(
-        body, (total, *blocks, *weights), [((row_count, columns), BF if final else F32)], 20
+        body, (total, *blocks, *weights), [((row_count, columns), BF if final else F32)], 60
     )[0]
 
 
@@ -346,35 +346,53 @@
     )
 
 
-def side_rows(value, side):
+def far_body(keep_ref, came_ref, away_ref, here_ref):
+    away_ref[...] = (keep_ref[1].astype(F32) + came_ref[1].astype(F32)).astype(BF)
+    here_ref[...] = keep_ref[0].astype(F32) + came_ref[0].astype(F32)
+
+
+def side_body(ids_ref, held_ref, came_ref, other_ref, own_ref):
+    side = ids_ref[1] & 1
+    lead = (slice(None),) * (len(held_ref.shape) - 3)
+
+    def total(at):
+        place = (*lead, at)
+        return held_ref[place].astype(F32) + came_ref[place].astype(F32)
+
+    other_ref[...] = total(1 - side).astype(BF)
+    own_ref[...] = total(side)
+
+
+def both_body(left_ref, left_came_ref, right_ref, right_came_ref, both_ref):
+    columns = left_ref.shape[2]
+    both_ref[:, :, :columns] = (left_ref[...] + left_came_ref[...].astype(F32)).astype(BF)
+    both_ref[:, :, columns:] = (right_ref[...] + right_came_ref[...].astype(F32)).astype(BF)
+
+
+def crossed_sums(place, left_keep, left_send, right_keep, right_send, first, first_came):
     groups = lax.axis_size("seq")
-    *blocks, rows, columns = value.shape
-    value = value.reshape(*blocks, groups // 2, 2, rows // groups, columns)
-    return lax.dynamic_index_in_dim(value, side, axis=len(blocks) + 1, keepdims=False).astype(F32)
-
-
-def crossed_sums(left_keep, left_send, right_keep, right_send, first, first_came):
-    groups = lax.axis_size("seq")
-    side = lax.axis_index("seq") % 2
+    blocks, rows, columns = left_keep.shape
+    pairs = (groups // 2, 2, rows // groups, columns)
+    half = (groups // 2, rows // groups, columns)
     right_came = swap(right_send, "dp", 1)
     left_came = swap(left_send, "dp", 1)
-    left_away = (left_keep[1].astype(F32) + left_came[1].astype(F32)).astype(BF)
-    left_away, first_came = lax.optimization_barrier((left_away, first_came))
-    x_came = swap(left_away, "dp", 2)
-    other = side_rows(right_keep, 1 - side) + side_rows(right_came, 1 - side)
-    side_came = swap(other.astype(BF), "seq", 1)
-
-    def left_half(at):
-        return side_rows(left_keep[0], at) + side_rows(left_came[0], at) + side_rows(x_came, at)
-
-    def right_half(at):
-        return side_rows(right_keep[at], side) + side_rows(right_came[at], side) + side_came[at].astype(F32)
-
-    left = swap(left_half(1 - side).astype(BF), "seq", 1)
-    right = swap(right_half(1).astype(BF), "dp", 2)
-    left = left_half(side) + left.astype(F32)
-    right = right_half(0) + right.astype(F32)
-    both = jnp.concatenate([left, right], axis=2).astype(BF)
+    other, own = call(
+        side_body, (place, right_keep.reshape(blocks, *pairs), right_came.reshape(blocks, *pairs)),
+        [((blocks, *half), BF), ((blocks, *half), F32)], 20, smem=1,
+    )
+    side_came = swap(other, "seq", 1)
+    away, here = call(far_body, (left_keep, left_came), [((rows, columns), BF), ((rows, columns), F32)], 20)
+    away, first_came = lax.optimization_barrier((away, first_came))
+    x_came = swap(away, "dp", 2)
+    other, left = call(
+        side_body, (place, here.reshape(pairs), x_came.reshape(pairs)), [(half, BF), (half, F32)], 20, smem=1
+    )
+    left_came = swap(other, "seq", 1)
+    away, right = call(far_body, (own, side_came), [(half, BF), (half, F32)], 20)
+    right_came = swap(away, "dp", 2)
+    both, = call(
+        both_body, (left, left_came, right, right_came), [((groups // 2, rows // groups, 2 * columns), BF)], 20
+    )
     first = seq_parts((first + first_came.astype(F32)).astype(BF))
     both, first = lax.optimization_barrier((both, first))
     lines = [list(range(start, groups, 2)) for start in range(2)]
@@ -509,7 +527,9 @@
         32, smem=1, after=1,
     )
     fine_send, track_x = lax.optimization_barrier((fine_send, track_x))
-    both, readout_total = crossed_sums(fine_keep, fine_send, coarse_keep, coarse_send, track_here, track_x)
+    both, readout_total = crossed_sums(
+        place, fine_keep, fine_send, coarse_keep, coarse_send, track_here, track_x
+    )
     cut = width // windows
     kernel_total, mixer_total = call(
         output_body, (both,),

time: 220 us -> 228 us (1.036)
  waiting for transfers between devices: 82.5 us -> 94.8 us
  Pallas kernels: 41.4 us -> 52 us
  other arithmetic: 9.33 us -> 3.73 us
  local copies, waits for them, and re-layouts: 20.4 us -> 15.2 us
  starting transfers between devices: 63.5 us -> 60.2 us
    ppermute x25, waiting for transfers between devices: 41.3 us -> 53.5 us  [swap(): return lax.ppermute(value, axis, [(i, i ^ bit) for i in range(size)])]
    pallas_call x12 -> x17, Pallas kernels: 31 us -> 41.5 us  [call(): pl.pallas_call(body, out_shape=outs, in_specs=[SMEM] * smem + [ANY] * aft...]
    convert_element_type x4 -> x0, other arithmetic: 4.55 us -> none  [the longest x1 2.14 us: crossed_sums(): side_came = swap(other.astype(BF), 'seq', 1)]
    slice x4 -> x0, local copies, waits for them, and re-layouts: 3.9 us -> none  [the longest x1 1.42 us: right_half(): right_came[at]]
    ppermute x25, starting transfers between devices: 20.5 us -> 18 us  [swap(): return lax.ppermute(value, axis, [(i, i ^ bit) for i in range(size)])]
    unnamed x68 -> x66, local copies, waits for them, and re-layouts: 14.1 us -> 12.4 us
  transfers between devices with their start and end apart: 37 -> 37, of which waited for: 16 -> 15; matrix products, arithmetic and copies ran while one was open for 7% -> 3% of each run, Pallas kernels for 14% -> 17%
where the time goes in v7:
time: 228 us
  waiting for transfers between devices  94.8 us (42%)
  starting transfers between devices  60.2 us (26%)
  Pallas kernels  52 us (23%)
  local copies, waits for them, and re-layouts  15.2 us (7%)
  other arithmetic  3.73 us (2%)
    ppermute x25, waiting for transfers between devices, swap(): return lax.ppermute(value, axis, [(i, i ^ bit) for i in range(size)])  53.5 us
    pallas_call x17, Pallas kernels, call(): pl.pallas_call(body, out_shape=outs, in_specs=[SMEM] * smem + [ANY] * aft...  41.5 us
    ppermute x25, starting transfers between devices, swap(): return lax.ppermute(value, axis, [(i, i ^ bit) for i in range(size)])  18 us
    ppermute x4, starting transfers between devices, halo(): lax.ppermute(high, 'seq', up)  15 us
    all_to_all x1, waiting for transfers between devices, crossed_sums(): lax.all_to_all(both, 'seq', split_axis=0, concat_axis=0, axis_index_group...  13 us
    unnamed x66, local copies, waits for them, and re-layouts  12.4 us
    all_to_all x2, starting transfers between devices, send(): lax.all_to_all(sums.reshape(groups, block, columns), 'seq', split_axis=0,...  11.4 us
    all_to_all x2, waiting for transfers between devices, send(): lax.all_to_all(sums.reshape(groups, block, columns), 'seq', split_axis=0,...  11.4 us
  transfers between devices with their start and end apart: 37, of which 15 were waited for; matrix products, arithmetic and copies ran while one was open for 3% of the time, Pallas kernels for 17%

profile of v7, /device:TPU:0, one launch (start us, length us, event | category | flops | bytes accessed | tf_op | source)
XLA Modules:
  0.0 227.5 jit_solution(400711629939940491)
XLA Ops:
  1.1 2.6 %fusion.2 = (bf16[512,384]{1,0:T(8,128)(2,1)}, bf16[512,384]{1,0:T(8,128)(2,1)}, bf16[512,384]{1,0:T(8,128)(2,1)}, bf16[512,384]{1,0:T(8,128)(2,1)}) fusion(bf16[2048,768]{1,0:T(8,128)(2,1)} %refs_0_.1, s32[]{:T(128)S(6)} %select_n.78, s32[]{:T(128)S(6)} %add.182, s32[]{:T(128)S(6)} %add.180), kind=kLoop, calls=%fused_computation.23 | loop fusion | bytes 3145740 | tf_op jit(solution)/shard_map/slice | solution.py:424
  3.7 2.5 %collective-permute-start.5 = (bf16[512,384]{1,0:T(8,128)(2,1)}, bf16[512,384]{1,0:T(8,128)(2,1)S(1)}, u32[]{:S(2)}, u32[]{:S(2)}) collective-permute-start(bf16[512,384]{1,0:T(8,128)(2,1)} %get-tuple-element.132), channel_id=1, source_target_pairs={{0,16},{8,24},{16,0},{24,8},{1,17},{9,25},{17,1},{25,9},{2,18},{10... | collective-permute-start | bytes 1179656 | tf_op jit(solution)/shard_map/ppermute | solution.py:322
  6.3 2.0 collective-permute-start.11
  8.3 8.1 %collective-permute-done.5.refs_12_ = bf16[512,384]{1,0:T(8,128)(2,1)S(1)} collective-permute-done((bf16[512,384]{1,0:T(8,128)(2,1)}, bf16[512,384]{1,0:T(8,128)(2,1)S(1)}, u32[]{:S(2)}, u32[]{:S(2)}) %collective-permute-start.5) | collective-permute-done | bytes 393248 | tf_op jit(solution)/shard_map/ppermute | solution.py:322
  16.4 2.0 collective-permute-start.7
  18.4 1.6 copy-done.18
  20.0 10.5 %shard_map.129 = (f32[512,768]{1,0:T(8,128)}, bf16[512,512]{1,0:T(8,128)(2,1)S(1)}, bf16[512,512]{1,0:T(8,128)(2,1)S(1)}, bf16[512,512]{1,0:T(8,128)(2,1)S(1)}, ...) custom-call(s32[10]{0:T(128)S(1)} %stack.60.starts_ref, ...), custom_call_target="tpu_custom_call" | custom-call | flops 1024 | bytes 1024 | tf_op jit(solution)/shard_map/pallas_call | solution.py:103
  37.1 1.9 collective-permute-start.9
  39.6 7.6 %collective-permute-done.3.refs_10_ = bf16[512,384]{1,0:T(8,128)(2,1)S(1)} collective-permute-done((bf16[512,384]{1,0:T(8,128)(2,1)}, bf16[512,384]{1,0:T(8,128)(2,1)S(1)}, u32[]{:S(2)}, u32[]{:S(2)}) %collective-permute-start.3) | collective-permute-done | bytes 393248 | tf_op jit(solution)/shard_map/ppermute | solution.py:322
  47.2 1.5 collective-permute-start.13
  50.3 6.6 %shard_map.130 = bf16[512,384]{1,0:T(8,128)(2,1)} custom-call(f32[512,768]{1,0:T(8,128)} %get-tuple-element.68.old_ref, bf16[512,512]{1,0:T(8,128)(2,1)} %copy-done.7, bf16[512,512]{1,0:T(8,128)(2,1)} %copy-done.8, bf16[512,512]{1,0:T(8,128)(2,1)} %copy-done.9, bf16[512,512]{1,0:T(8,128)(2,1)} %copy-done.10, bf16[512,512]{1,0:T(8,128)(2,1)} %copy-done.11, ...), custom_call_target="tpu_custom_call" | custom-call | flops 1024 | bytes 1024 | tf_op jit(solution)/shard_map/pallas_call | solution.py:52
  56.9 5.8 %all-to-all-start = ((bf16[8,64,384]{2,1,0:T(8,128)(2,1)}), bf16[8,64,384]{2,1,0:T(8,128)(2,1)S(1)}, u32[]{:S(2)}, u32[]{:S(2)}) async-start(bf16[8,64,384]{2,1,0:T(8,128)(2,1)} %bitcast.40), calls=%async_computation | async-start | bytes 786432 | tf_op jit(solution)/shard_map/all_to_all | solution.py:443
  63.3 7.0 %collective-permute-done.10.refs_2_ = bf16[512,384]{1,0:T(8,128)(2,1)} collective-permute-done((bf16[512,384]{1,0:T(8,128)(2,1)S(1)}, bf16[512,384]{1,0:T(8,128)(2,1)}, u32[]{:S(2)}, u32[]{:S(2)}) %collective-permute-start.10) | collective-permute-done | bytes 393248 | tf_op jit(solution)/shard_map/ppermute | solution.py:322
  71.9 5.7 %shard_map.131.old_ref = f32[512,384]{1,0:T(8,128)} custom-call(f32[512,768]{1,0:T(8,128)} %get-tuple-element.68.old_ref, bf16[512,512]{1,0:T(8,128)(2,1)} %copy-done.7, bf16[512,512]{1,0:T(8,128)(2,1)} %copy-done.8, bf16[512,512]{1,0:T(8,128)(2,1)} %copy-done.9, bf16[512,512]{1,0:T(8,128)(2,1)} %copy-done.10, bf16[512,512]{1,0:T(8,128)(2,1)} %copy-done.11, ...), custom_call_target="tpu_custom_call" | custom-call | flops 1024 | bytes 1024 | tf_op jit(solution)/shard_map/pallas_call | solution.py:52
  78.4 3.3 %shard_map.132 = bf16[512,384]{1,0:T(8,128)(2,1)} custom-call(f32[512,384]{1,0:T(8,128)} %shard_map.131.old_ref, bf16[512,512]{1,0:T(8,128)(2,1)} %copy-done.5, bf16[512,512]{1,0:T(8,128)(2,1)} %copy-done.6, bf16[512,384]{1,0:T(8,128)(2,1)} %collective-permute-done.10.refs_2_, bf16[512,384]{1,0:T(8,128)(2,1)} %collective-permute-done.16.refs_3_), custom_call_target="tpu_custom_call" | custom-call | flops 1024 | bytes 1024 | tf_op jit(solution)/shard_map/pallas_call | solution.py:52
  81.7 5.7 %all-to-all-start.1 = ((bf16[8,64,384]{2,1,0:T(8,128)(2,1)}), bf16[8,64,384]{2,1,0:T(8,128)(2,1)}, u32[]{:S(2)}, u32[]{:S(2)}) async-start(bf16[8,64,384]{2,1,0:T(8,128)(2,1)} %bitcast.41), calls=%async_computation.1 | async-start | bytes 786432 | tf_op jit(solution)/shard_map/all_to_all | solution.py:443
  88.4 11.4 %all-to-all-done.1 = bf16[8,64,384]{2,1,0:T(8,128)(2,1)} async-done(((bf16[8,64,384]{2,1,0:T(8,128)(2,1)}), bf16[8,64,384]{2,1,0:T(8,128)(2,1)}, u32[]{:S(2)}, u32[]{:S(2)}) %all-to-all-start.1) | async-done | bytes 393248 | tf_op jit(solution)/shard_map/all_to_all | solution.py:443
  99.8 1.0 copy-done.14
  100.8 2.1 shard_map.133
  103.0 3.4 %collective-permute-start.17 = (bf16[256,384]{1,0:T(8,128)(2,1)S(1)}, bf16[256,384]{1,0:T(8,128)(2,1)S(1)}, u32[]{:S(2)}, u32[]{:S(2)}) collective-permute-start(bf16[256,384]{1,0:T(8,128)(2,1)S(1)} %get-tuple-element.80), channel_id=1, source_target_pairs={{0,1},{1,2},{2,3},{3,4},{4,5},{5,6},{6,7},{8,9},{9,10},{10,11},{11... | collective-permute-start | bytes 589832 | tf_op jit(solution)/shard_map/ppermute | solution.py:329
  106.3 1.5 collective-permute-start.18
  108.8 5.4 %collective-permute-done.17.prev_ref = bf16[256,384]{1,0:T(8,128)(2,1)S(1)} collective-permute-done((bf16[256,384]{1,0:T(8,128)(2,1)S(1)}, bf16[256,384]{1,0:T(8,128)(2,1)S(1)}, u32[]{:S(2)}, u32[]{:S(2)}) %collective-permute-start.17) | collective-permute-done | bytes 196640 | tf_op jit(solution)/shard_map/ppermute | solution.py:329
  115.1 4.5 %collective-permute-start.19 = (bf16[128,384]{1,0:T(8,128)(2,1)S(1)}, bf16[128,384]{1,0:T(8,128)(2,1)S(1)}, u32[]{:S(2)}, u32[]{:S(2)}) collective-permute-start(bf16[128,384]{1,0:T(8,128)(2,1)S(1)} %get-tuple-element.85), channel_id=1, source_target_pairs={{0,1},{1,2},{2,3},{3,4},{4,5},{5,6},{6,7},{8,9},{9,10},{10,11},{11... | collective-permute-start | bytes 294920 | tf_op jit(solution)/shard_map/ppermute | solution.py:329
  119.7 1.3 collective-permute-start.20
  121.9 4.3 %collective-permute-done.20.refs_4_ = bf16[128,384]{1,0:T(8,128)(2,1)S(1)} collective-permute-done((bf16[128,384]{1,0:T(8,128)(2,1)S(1)}, bf16[128,384]{1,0:T(8,128)(2,1)S(1)}, u32[]{:S(2)}, u32[]{:S(2)}) %collective-permute-start.20) | collective-permute-done | bytes 98336 | tf_op jit(solution)/shard_map/ppermute | solution.py:330
  126.2 3.7 %shard_map.136 = (bf16[256,384]{1,0:T(8,128)(2,1)S(1)}, bf16[128,768]{1,0:T(8,128)(2,1)S(1)}, bf16[128,2048]{1,0:T(8,128)(2,1)S(1)}, bf16[128,768]{1,0:T(8,128)(...) custom-call(s32[2]{0:T(128)S(1)} %get-tuple-element.135.refs_0_, ...), custom_call_target="tpu_custom_call" | custom-call | flops 1024 | bytes 1024 | tf_op jit(solution)/shard_map/pallas_call | solution.py:52
  129.9 1.5 shard_map.137
  131.5 4.0 %collective-permute-start.22 = (bf16[128,384]{1,0:T(8,128)(2,1)S(1)}, bf16[128,384]{1,0:T(8,128)(2,1)S(1)}, u32[]{:S(2)}, u32[]{:S(2)}) collective-permute-start(bf16[128,384]{1,0:T(8,128)(2,1)S(1)} %get-tuple-element.94.refs_3_.refs_6_), channel_id=1, source_target_pairs={{0,1},{1,2},{2,3},{3,4},{4,5},{5,6},{6,7},{8,9},{9,10},{10,11},{11... | collective-permute-start | bytes 294920 | tf_op jit(solution)/shard_map/ppermute | solution.py:329
  135.5 1.3 collective-permute-start.23
  137.0 1.2 collective-permute-done.22.refs_1_.refs_4_
  138.2 4.1 %collective-permute-done.23.refs_4_.refs_7_ = bf16[128,384]{1,0:T(8,128)(2,1)S(1)} collective-permute-done((bf16[128,384]{1,0:T(8,128)(2,1)S(1)}, bf16[128,384]{1,0:T(8,128)(2,1)S(1)}, u32[]{:S(2)}, u32[]{:S(2)}) %collective-permute-start.23) | collective-permute-done | bytes 98336 | tf_op jit(solution)/shard_map/ppermute | solution.py:330
  142.3 1.5 collective-permute-start.26
  143.8 2.5 %shard_map.138 = (f32[256,768]{1,0:T(8,128)}, bf16[256,768]{1,0:T(8,128)(2,1)S(1)}, bf16[256,384]{1,0:T(8,128)(2,1)S(1)}, bf16[256,384]{1,0:T(8,128)(2,1)S(1)}) custom-call(bf16[768,512]{1,0:T(8,128)(2,1)S(1)} %fusion.1.refs_0_, bf16[128,384]{1,0:T(8,128)(2,1)S(1)} %collective-permute-done.22.refs_1_.refs_4_, ...), custom_call_target="tpu_custom_call" | custom-call | flops 1024 | bytes 1024 | tf_op jit(solution)/shard_map/pallas_call | solution.py:52
  146.3 3.1 %collective-permute-start.24 = (bf16[256,384]{1,0:T(8,128)(2,1)S(1)}, bf16[256,384]{1,0:T(8,128)(2,1)S(1)}, u32[]{:S(2)}, u32[]{:S(2)}) collective-permute-start(bf16[256,384]{1,0:T(8,128)(2,1)S(1)} %get-tuple-element.102.refs_6_), channel_id=1, source_target_pairs={{0,1},{1,2},{2,3},{3,4},{4,5},{5,6},{6,7},{8,9},{9,10},{10,11},{11... | collective-permute-start | bytes 589832 | tf_op jit(solution)/shard_map/ppermute | solution.py:329
  149.4 1.3 collective-permute-start.25
  150.7 5.2 %shard_map.139 = (bf16[2,768,384]{2,1,0:T(8,128)(2,1)S(1)}, bf16[2,768,384]{2,1,0:T(8,128)(2,1)}) custom-call(s32[2]{0:T(128)S(1)} %get-tuple-element.134.ids_ref.refs_0_, bf16[256,384]{1,0:T(8,128)(2,1)S(1)} %get-tuple-element.101.refs_1_.refs_5_, bf16[128,768]{1,0:T(8,128)(2,1)S(1)} %get-tuple-element.86.refs_2_, ...), custom_call_target="tpu_custom_call" | custom-call | flops 1024 | bytes 1024 | tf_op jit(solution)/shard_map/pallas_call | solution.py:52
  155.9 1.0 collective-permute-done.25.refs_7_
  157.0 5.3 %shard_map.140 = (bf16[2,768,384]{2,1,0:T(8,128)(2,1)S(1)}, bf16[2,768,384]{2,1,0:T(8,128)(2,1)S(1)}) custom-call(s32[2]{0:T(128)S(1)} %get-tuple-element.134.ids_ref.refs_0_, bf16[256,384]{1,0:T(8,128)(2,1)S(1)} %get-tuple-element.101.refs_1_.refs_5_, bf16[256,768]{1,0:T(8,128)(2,1)S(1)} %get-tuple-element.82.low_ref.refs_2_, ...), custom_call_target="tpu_custom_call" | custom-call | flops 1024 | bytes 1024 | tf_op jit(solution)/shard_map/pallas_call | solution.py:52
  162.8 3.2 %collective-permute-done.27.came_ref = bf16[2,768,384]{2,1,0:T(8,128)(2,1)S(1)} collective-permute-done((bf16[2,768,384]{2,1,0:T(8,128)(2,1)S(1)}, bf16[2,768,384]{2,1,0:T(8,128)(2,1)S(1)}, u32[]{:S(2)}, u32[]{:S(2)}) %collective-permute-start.27) | collective-permute-done | bytes 1179680 | tf_op jit(solution)/shard_map/ppermute | solution.py:322
  166.3 1.2 fusion
  167.5 5.8 %all-to-all-start.2 = ((bf16[8,96,512]{2,1,0:T(8,128)(2,1)}), bf16[8,96,512]{2,1,0:T(8,128)(2,1)}, u32[]{:S(2)}, u32[]{:S(2)}) async-start(bf16[8,96,512]{2,1,0:T(8,128)(2,1)} %bitcast.39), calls=%async_computation.2 | async-start | bytes 1572864 | tf_op jit(solution)/shard_map/all_to_all | solution.py:344
  174.2 2.1 collective-permute-start.31
  176.8 20.3 %collective-permute-done.31.came_ref = bf16[2,4,96,384]{3,2,1,0:T(8,128)(2,1)S(1)} collective-permute-done((bf16[2,4,96,384]{3,2,1,0:T(8,128)(2,1)S(1)}, bf16[2,4,96,384]{3,2,1,0:T(8,128)(2,1)S(1)}, u32[]{:S(2)}, u32[]{:S(2)}) %collective-permute-start.31) | collective-permute-done | bytes 589856 | tf_op jit(solution)/shard_map/ppermute | solution.py:322
  198.8 6.3 %collective-permute-done.32.right_came_ref = bf16[4,96,384]{2,1,0:T(8,128)(2,1)S(1)} collective-permute-done((bf16[4,96,384]{2,1,0:T(8,128)(2,1)S(1)}, bf16[4,96,384]{2,1,0:T(8,128)(2,1)S(1)}, u32[]{:S(2)}, u32[]{:S(2)}) %collective-permute-start.32) | collective-permute-done | bytes 294944 | tf_op jit(solution)/shard_map/ppermute | solution.py:322
  205.1 1.0 collective-permute-done.29.left_came_ref
  207.1 4.7 %all-to-all-start.3 = ((bf16[4,96,768]{2,1,0:T(8,128)(2,1)}), bf16[4,96,768]{2,1,0:T(8,128)(2,1)S(1)}, u32[]{:S(2)}, u32[]{:S(2)}) async-start(bf16[4,96,768]{2,1,0:T(8,128)(2,1)} %shard_map.145), calls=%async_computation.3 | async-start | bytes 1179648 | tf_op jit(solution)/shard_map/all_to_all | solution.py:399
  211.7 1.9 convert_reduce_fusion
  213.6 13.0 %all-to-all-done.3.parts_ref = bf16[4,96,768]{2,1,0:T(8,128)(2,1)S(1)} async-done(((bf16[4,96,768]{2,1,0:T(8,128)(2,1)}), bf16[4,96,768]{2,1,0:T(8,128)(2,1)S(1)}, u32[]{:S(2)}, u32[]{:S(2)}) %all-to-all-start.3) | async-done | bytes 589856 | tf_op jit(solution)/shard_map/all_to_all | solution.py:399
  (120 shorter events, 21.5 us)
Async XLA Ops:
  0.6 17.8 %collective-permute-start.1 = (bf16[2048,768]{1,0:T(8,128)(2,1)}, bf16[2048,768]{1,0:T(8,128)(2,1)S(1)}, u32[]{:S(2)}, u32[]{:S(2)}) collective-permute-start(bf16[2048,768]{1,0:T(8,128)(2,1)} %refs_0_.1), channel_id=1, source_target_pairs={{0,8},{8,0},{16,24},{24,16},{1,9},{9,1},{17,25},{25,17},{2,10},{10... | collective-permute-start | bytes 9437192 | tf_op jit(solution)/shard_map/ppermute | solution.py:322
  3.7 12.7 %collective-permute-start.5 = (bf16[512,384]{1,0:T(8,128)(2,1)}, bf16[512,384]{1,0:T(8,128)(2,1)S(1)}, u32[]{:S(2)}, u32[]{:S(2)}) collective-permute-start(bf16[512,384]{1,0:T(8,128)(2,1)} %get-tuple-element.132), channel_id=1, source_target_pairs={{0,16},{8,24},{16,0},{24,8},{1,17},{9,25},{17,1},{25,9},{2,18},{10... | collective-permute-start | bytes 1179656 | tf_op jit(solution)/shard_map/ppermute | solution.py:322
  6.2 30.7 %collective-permute-start = (bf16[512,384]{1,0:T(8,128)(2,1)}, bf16[512,384]{1,0:T(8,128)(2,1)}, u32[]{:S(2)}, u32[]{:S(2)}) collective-permute-start(bf16[512,384]{1,0:T(8,128)(2,1)} %get-tuple-element.133), channel_id=1, source_target_pairs={{0,16},{8,24},{16,0},{24,8},{1,17},{9,25},{17,1},{25,9},{2,18},{10... | collective-permute-start | bytes 1179656 | tf_op jit(solution)/shard_map/ppermute | solution.py:322
  6.3 33.2 %collective-permute-start.11 = (bf16[512,384]{1,0:T(8,128)(2,1)}, bf16[512,384]{1,0:T(8,128)(2,1)}, u32[]{:S(2)}, u32[]{:S(2)}) collective-permute-start(bf16[512,384]{1,0:T(8,128)(2,1)} %get-tuple-element.130), channel_id=1, source_target_pairs={{0,16},{8,24},{16,0},{24,8},{1,17},{9,25},{17,1},{25,9},{2,18},{10... | collective-permute-start | bytes 1179656 | tf_op jit(solution)/shard_map/ppermute | solution.py:322
  16.4 22.5 %copy-start.19 = (bf16[512,384]{1,0:T(8,128)(2,1)}, bf16[512,384]{1,0:T(8,128)(2,1)S(1)}, u32[]{:S(2)}) copy-start(bf16[512,384]{1,0:T(8,128)(2,1)S(1)} %collective-permute-done.5.refs_12_) | copy-start | bytes 1179652
  16.4 22.5 %collective-permute-start.7 = (bf16[512,384]{1,0:T(8,128)(2,1)S(1)}, bf16[512,384]{1,0:T(8,128)(2,1)S(1)}, u32[]{:S(2)}, u32[]{:S(2)}) collective-permute-start(bf16[512,384]{1,0:T(8,128)(2,1)S(1)} %collective-permute-done.5.refs_12_), channel_id=1, source_target_pairs={{0,1},{1,0},{2,3},{3,2},{4,5},{5,4},{6,7},{7,6},{8,9},{9,8},{10,11... | collective-permute-start | bytes 1179656 | tf_op jit(solution)/shard_map/ppermute | solution.py:322
  20.0 17.0 %copy-start.26 = (bf16[512,384]{1,0:T(8,128)(2,1)S(1)}, bf16[512,384]{1,0:T(8,128)(2,1)}, u32[]{:S(2)}) copy-start(bf16[512,384]{1,0:T(8,128)(2,1)} %get-tuple-element.131) | copy-start | bytes 1179652
  36.9 10.2 %collective-permute-start.3 = (bf16[512,384]{1,0:T(8,128)(2,1)}, bf16[512,384]{1,0:T(8,128)(2,1)S(1)}, u32[]{:S(2)}, u32[]{:S(2)}) collective-permute-start(bf16[512,384]{1,0:T(8,128)(2,1)} %collective-permute-done.refs_8_), channel_id=1, source_target_pairs={{0,1},{1,0},{2,3},{3,2},{4,5},{5,4},{6,7},{7,6},{8,9},{9,8},{10,11... | collective-permute-start | bytes 1179656 | tf_op jit(solution)/shard_map/ppermute | solution.py:322
  37.1 10.1 %collective-permute-start.9 = (bf16[512,384]{1,0:T(8,128)(2,1)S(1)}, bf16[512,384]{1,0:T(8,128)(2,1)S(1)}, u32[]{:S(2)}, u32[]{:S(2)}) collective-permute-start(bf16[512,384]{1,0:T(8,128)(2,1)S(1)} %copy-done.26), channel_id=1, source_target_pairs={{0,16},{8,24},{16,0},{24,8},{1,17},{9,25},{17,1},{25,9},{2,18},{10... | collective-permute-start | bytes 1179656 | tf_op jit(solution)/shard_map/ppermute | solution.py:322
  39.0 9.7 %collective-permute-start.6 = (bf16[512,384]{1,0:T(8,128)(2,1)S(1)}, bf16[512,384]{1,0:T(8,128)(2,1)S(1)}, u32[]{:S(2)}, u32[]{:S(2)}) collective-permute-start(bf16[512,384]{1,0:T(8,128)(2,1)S(1)} %collective-permute-done.5.refs_12_), channel_id=1, source_target_pairs={{0,8},{8,0},{16,24},{24,16},{1,9},{9,1},{17,25},{25,17},{2,10},{10... | collective-permute-start | bytes 1179656 | tf_op jit(solution)/shard_map/ppermute | solution.py:322
  39.0 10.3 %copy-start.20 = (bf16[512,384]{1,0:T(8,128)(2,1)}, bf16[512,384]{1,0:T(8,128)(2,1)S(1)}, u32[]{:S(2)}) copy-start(bf16[512,384]{1,0:T(8,128)(2,1)S(1)} %collective-permute-done.7.refs_14_) | copy-start | bytes 1179652
  39.0 10.3 %collective-permute-start.8 = (bf16[512,384]{1,0:T(8,128)(2,1)S(1)}, bf16[512,384]{1,0:T(8,128)(2,1)S(1)}, u32[]{:S(2)}, u32[]{:S(2)}) collective-permute-start(bf16[512,384]{1,0:T(8,128)(2,1)S(1)} %collective-permute-done.7.refs_14_), channel_id=1, source_target_pairs={{0,8},{8,0},{16,24},{24,16},{1,9},{9,1},{17,25},{25,17},{2,10},{10... | collective-permute-start | bytes 1179656 | tf_op jit(solution)/shard_map/ppermute | solution.py:322
  39.5 9.8 %collective-permute-start.2 = (bf16[512,384]{1,0:T(8,128)(2,1)}, bf16[512,384]{1,0:T(8,128)(2,1)S(1)}, u32[]{:S(2)}, u32[]{:S(2)}) collective-permute-start(bf16[512,384]{1,0:T(8,128)(2,1)} %collective-permute-done.refs_8_), channel_id=1, source_target_pairs={{0,8},{8,0},{16,24},{24,16},{1,9},{9,1},{17,25},{25,17},{2,10},{10... | collective-permute-start | bytes 1179656 | tf_op jit(solution)/shard_map/ppermute | solution.py:322
  47.1 2.1 collective-permute-start.4
  47.2 15.5 %copy-start.27 = (bf16[512,384]{1,0:T(8,128)(2,1)}, bf16[512,384]{1,0:T(8,128)(2,1)S(1)}, u32[]{:S(2)}) copy-start(bf16[512,384]{1,0:T(8,128)(2,1)S(1)} %collective-permute-done.9.refs_10_) | copy-start | bytes 1179652
  47.2 16.0 %collective-permute-start.13 = (bf16[512,384]{1,0:T(8,128)(2,1)}, bf16[512,384]{1,0:T(8,128)(2,1)S(1)}, u32[]{:S(2)}, u32[]{:S(2)}) collective-permute-start(bf16[512,384]{1,0:T(8,128)(2,1)} %collective-permute-done.11.refs_6_), channel_id=1, source_target_pairs={{0,1},{1,0},{2,3},{3,2},{4,5},{5,4},{6,7},{7,6},{8,9},{9,8},{10,11... | collective-permute-start | bytes 1179656 | tf_op jit(solution)/shard_map/ppermute | solution.py:322
  48.7 21.6 %collective-permute-start.10 = (bf16[512,384]{1,0:T(8,128)(2,1)S(1)}, bf16[512,384]{1,0:T(8,128)(2,1)}, u32[]{:S(2)}, u32[]{:S(2)}) collective-permute-start(bf16[512,384]{1,0:T(8,128)(2,1)S(1)} %collective-permute-done.9.refs_10_), channel_id=1, source_target_pairs={{0,1},{1,0},{2,3},{3,2},{4,5},{5,4},{6,7},{7,6},{8,9},{9,8},{10,11... | collective-permute-start | bytes 1179656 | tf_op jit(solution)/shard_map/ppermute | solution.py:322
  56.9 20.7 %all-to-all-start = ((bf16[8,64,384]{2,1,0:T(8,128)(2,1)}), bf16[8,64,384]{2,1,0:T(8,128)(2,1)S(1)}, u32[]{:S(2)}, u32[]{:S(2)}) async-start(bf16[8,64,384]{2,1,0:T(8,128)(2,1)} %bitcast.40), calls=%async_computation | async-start | bytes 786432 | tf_op jit(solution)/shard_map/all_to_all | solution.py:443
  62.7 7.6 %collective-permute-start.12 = (bf16[512,384]{1,0:T(8,128)(2,1)}, bf16[512,384]{1,0:T(8,128)(2,1)S(1)}, u32[]{:S(2)}, u32[]{:S(2)}) collective-permute-start(bf16[512,384]{1,0:T(8,128)(2,1)} %collective-permute-done.11.refs_6_), channel_id=1, source_target_pairs={{0,8},{8,0},{16,24},{24,16},{1,9},{9,1},{17,25},{25,17},{2,10},{10... | collective-permute-start | bytes 1179656 | tf_op jit(solution)/shard_map/ppermute | solution.py:322
  62.7 7.6 %collective-permute-start.15 = (bf16[512,384]{1,0:T(8,128)(2,1)S(1)}, bf16[512,384]{1,0:T(8,128)(2,1)S(1)}, u32[]{:S(2)}, u32[]{:S(2)}) collective-permute-start(bf16[512,384]{1,0:T(8,128)(2,1)S(1)} %collective-permute-done.9.refs_10_), channel_id=1, source_target_pairs={{0,8},{8,0},{16,24},{24,16},{1,9},{9,1},{17,25},{25,17},{2,10},{10... | collective-permute-start | bytes 1179656 | tf_op jit(solution)/shard_map/ppermute | solution.py:322
  63.2 7.1 %copy-start.28 = (bf16[512,384]{1,0:T(8,128)(2,1)}, bf16[512,384]{1,0:T(8,128)(2,1)S(1)}, u32[]{:S(2)}) copy-start(bf16[512,384]{1,0:T(8,128)(2,1)S(1)} %collective-permute-done.13.refs_8_) | copy-start | bytes 1179652
  63.2 7.1 %collective-permute-start.14 = (bf16[512,384]{1,0:T(8,128)(2,1)S(1)}, bf16[512,384]{1,0:T(8,128)(2,1)S(1)}, u32[]{:S(2)}, u32[]{:S(2)}) collective-permute-start(bf16[512,384]{1,0:T(8,128)(2,1)S(1)} %collective-permute-done.13.refs_8_), channel_id=1, source_target_pairs={{0,8},{8,0},{16,24},{24,16},{1,9},{9,1},{17,25},{25,17},{2,10},{10... | collective-permute-start | bytes 1179656 | tf_op jit(solution)/shard_map/ppermute | solution.py:322
  70.3 8.1 %collective-permute-start.16 = (bf16[512,384]{1,0:T(8,128)(2,1)}, bf16[512,384]{1,0:T(8,128)(2,1)}, u32[]{:S(2)}, u32[]{:S(2)}) collective-permute-start(bf16[512,384]{1,0:T(8,128)(2,1)} %collective-permute-done.10.refs_2_), channel_id=1, source_target_pairs={{0,8},{8,0},{16,24},{24,16},{1,9},{9,1},{17,25},{25,17},{2,10},{10... | collective-permute-start | bytes 1179656 | tf_op jit(solution)/shard_map/ppermute | solution.py:322
  78.4 9.0 %copy-start.32 = (s32[1,8,8]{2,1,0:T(8,128)S(1)}, s32[1,8,8]{2,1,0:T(8,128)}, u32[]{:S(2)}) copy-start(s32[1,8,8]{2,1,0:T(8,128)} %param.11) | copy-start | bytes 772
  78.4 21.4 %copy-start = (bf16[2,3,768,384]{3,2,1,0:T(8,128)(2,1)S(1)}, bf16[2,3,768,384]{3,2,1,0:T(8,128)(2,1)}, u32[]{:S(2)}) copy-start(bf16[2,3,768,384]{3,2,1,0:T(8,128)(2,1)} %refs_7_.3) | copy-start | bytes 10616836
  81.7 18.1 %all-to-all-start.1 = ((bf16[8,64,384]{2,1,0:T(8,128)(2,1)}), bf16[8,64,384]{2,1,0:T(8,128)(2,1)}, u32[]{:S(2)}, u32[]{:S(2)}) async-start(bf16[8,64,384]{2,1,0:T(8,128)(2,1)} %bitcast.41), calls=%async_computation.1 | async-start | bytes 786432 | tf_op jit(solution)/shard_map/all_to_all | solution.py:443
  103.0 11.3 %collective-permute-start.17 = (bf16[256,384]{1,0:T(8,128)(2,1)S(1)}, bf16[256,384]{1,0:T(8,128)(2,1)S(1)}, u32[]{:S(2)}, u32[]{:S(2)}) collective-permute-start(bf16[256,384]{1,0:T(8,128)(2,1)S(1)} %get-tuple-element.80), channel_id=1, source_target_pairs={{0,1},{1,2},{2,3},{3,4},{4,5},{5,6},{6,7},{8,9},{9,10},{10,11},{11... | collective-permute-start | bytes 589832 | tf_op jit(solution)/shard_map/ppermute | solution.py:329
  106.3 7.9 %collective-permute-start.18 = (bf16[256,384]{1,0:T(8,128)(2,1)S(1)}, bf16[256,384]{1,0:T(8,128)(2,1)S(1)}, u32[]{:S(2)}, u32[]{:S(2)}) collective-permute-start(bf16[256,384]{1,0:T(8,128)(2,1)S(1)} %get-tuple-element.81), channel_id=1, source_target_pairs={{1,0},{2,1},{3,2},{4,3},{5,4},{6,5},{7,6},{9,8},{10,9},{11,10},{12... | collective-permute-start | bytes 589832 | tf_op jit(solution)/shard_map/ppermute | solution.py:330
  114.3 11.9 %copy-start.4 = (bf16[768,2048]{1,0:T(8,128)(2,1)S(1)}, bf16[768,2048]{1,0:T(8,128)(2,1)}, u32[]{:S(2)}) copy-start(bf16[768,2048]{1,0:T(8,128)(2,1)} %refs_8_.2) | copy-start | bytes 9437188
  114.3 11.9 %copy-start.15 = (s32[1,128,2048]{2,1,0:T(8,128)S(1)}, s32[1,128,2048]{2,1,0:T(8,128)}, u32[]{:S(2)}) copy-start(s32[1,128,2048]{2,1,0:T(8,128)} %param.13) | copy-start | bytes 3145732
  115.1 6.7 %collective-permute-start.19 = (bf16[128,384]{1,0:T(8,128)(2,1)S(1)}, bf16[128,384]{1,0:T(8,128)(2,1)S(1)}, u32[]{:S(2)}, u32[]{:S(2)}) collective-permute-start(bf16[128,384]{1,0:T(8,128)(2,1)S(1)} %get-tuple-element.85), channel_id=1, source_target_pairs={{0,1},{1,2},{2,3},{3,4},{4,5},{5,6},{6,7},{8,9},{9,10},{10,11},{11... | collective-permute-start | bytes 294920 | tf_op jit(solution)/shard_map/ppermute | solution.py:329
  119.7 6.5 %collective-permute-start.20 = (bf16[128,384]{1,0:T(8,128)(2,1)S(1)}, bf16[128,384]{1,0:T(8,128)(2,1)S(1)}, u32[]{:S(2)}, u32[]{:S(2)}) collective-permute-start(bf16[128,384]{1,0:T(8,128)(2,1)S(1)} %get-tuple-element.88), channel_id=1, source_target_pairs={{1,0},{2,1},{3,2},{4,3},{5,4},{6,5},{7,6},{9,8},{10,9},{11,10},{12... | collective-permute-start | bytes 294920 | tf_op jit(solution)/shard_map/ppermute | solution.py:330
  131.4 5.4 %collective-permute-start.21 = (bf16[2,768,512]{2,1,0:T(8,128)(2,1)S(1)}, bf16[2,768,512]{2,1,0:T(8,128)(2,1)S(1)}, u32[]{:S(2)}, u32[]{:S(2)}) collective-permute-start(bf16[2,768,512]{2,1,0:T(8,128)(2,1)S(1)} %get-tuple-element.93), channel_id=1, source_target_pairs={{0,8},{8,0},{16,24},{24,16},{1,9},{9,1},{17,25},{25,17},{2,10},{10... | collective-permute-start | bytes 4718600 | tf_op jit(solution)/shard_map/ppermute | solution.py:322
  131.5 6.7 %collective-permute-start.22 = (bf16[128,384]{1,0:T(8,128)(2,1)S(1)}, bf16[128,384]{1,0:T(8,128)(2,1)S(1)}, u32[]{:S(2)}, u32[]{:S(2)}) collective-permute-start(bf16[128,384]{1,0:T(8,128)(2,1)S(1)} %get-tuple-element.94.refs_3_.refs_6_), channel_id=1, source_target_pairs={{0,1},{1,2},{2,3},{3,4},{4,5},{5,6},{6,7},{8,9},{9,10},{10,11},{11... | collective-permute-start | bytes 294920 | tf_op jit(solution)/shard_map/ppermute | solution.py:329
  135.5 6.8 %collective-permute-start.23 = (bf16[128,384]{1,0:T(8,128)(2,1)S(1)}, bf16[128,384]{1,0:T(8,128)(2,1)S(1)}, u32[]{:S(2)}, u32[]{:S(2)}) collective-permute-start(bf16[128,384]{1,0:T(8,128)(2,1)S(1)} %get-tuple-element.95.refs_2_.refs_5_), channel_id=1, source_target_pairs={{1,0},{2,1},{3,2},{4,3},{5,4},{6,5},{7,6},{9,8},{10,9},{11,10},{12... | collective-permute-start | bytes 294920 | tf_op jit(solution)/shard_map/ppermute | solution.py:330
  142.3 19.9 %collective-permute-start.26 = (bf16[768,512]{1,0:T(8,128)(2,1)S(1)}, bf16[768,512]{1,0:T(8,128)(2,1)S(1)}, u32[]{:S(2)}, u32[]{:S(2)}) collective-permute-start(bf16[768,512]{1,0:T(8,128)(2,1)S(1)} %fusion.1.refs_0_), channel_id=1, source_target_pairs={{0,16},{8,24},{16,0},{24,8},{1,17},{9,25},{17,1},{25,9},{2,18},{10... | collective-permute-start | bytes 2359304 | tf_op jit(solution)/shard_map/ppermute | solution.py:322
  143.8 6.9 %copy-start.2 = (bf16[2,384,768]{2,1,0:T(8,128)(2,1)S(1)}, bf16[2,384,768]{2,1,0:T(8,128)(2,1)}, u32[]{:S(2)}) copy-start(bf16[2,384,768]{2,1,0:T(8,128)(2,1)} %constant.91.clone.refs_10_) | copy-start | bytes 3538948
  143.8 6.9 %copy-start.3 = (bf16[2,768,384]{2,1,0:T(8,128)(2,1)S(1)}, bf16[2,768,384]{2,1,0:T(8,128)(2,1)}, u32[]{:S(2)}) copy-start(bf16[2,768,384]{2,1,0:T(8,128)(2,1)} %constant.92.clone.refs_11_) | copy-start | bytes 3538948
  146.3 9.6 %collective-permute-start.24 = (bf16[256,384]{1,0:T(8,128)(2,1)S(1)}, bf16[256,384]{1,0:T(8,128)(2,1)S(1)}, u32[]{:S(2)}, u32[]{:S(2)}) collective-permute-start(bf16[256,384]{1,0:T(8,128)(2,1)S(1)} %get-tuple-element.102.refs_6_), channel_id=1, source_target_pairs={{0,1},{1,2},{2,3},{3,4},{4,5},{5,6},{6,7},{8,9},{9,10},{10,11},{11... | collective-permute-start | bytes 589832 | tf_op jit(solution)/shard_map/ppermute | solution.py:329
  149.4 7.6 %collective-permute-start.25 = (bf16[256,384]{1,0:T(8,128)(2,1)S(1)}, bf16[256,384]{1,0:T(8,128)(2,1)S(1)}, u32[]{:S(2)}, u32[]{:S(2)}) collective-permute-start(bf16[256,384]{1,0:T(8,128)(2,1)S(1)} %get-tuple-element.101.refs_1_.refs_5_), channel_id=1, source_target_pairs={{1,0},{2,1},{3,2},{4,3},{5,4},{6,5},{7,6},{9,8},{10,9},{11,10},{12... | collective-permute-start | bytes 589832 | tf_op jit(solution)/shard_map/ppermute | solution.py:330
  162.2 3.8 %collective-permute-start.27 = (bf16[2,768,384]{2,1,0:T(8,128)(2,1)S(1)}, bf16[2,768,384]{2,1,0:T(8,128)(2,1)S(1)}, u32[]{:S(2)}, u32[]{:S(2)}) collective-permute-start(bf16[2,768,384]{2,1,0:T(8,128)(2,1)S(1)} %get-tuple-element.111), channel_id=1, source_target_pairs={{0,8},{8,0},{16,24},{24,16},{1,9},{9,1},{17,25},{25,17},{2,10},{10... | collective-permute-start | bytes 3538952 | tf_op jit(solution)/shard_map/ppermute | solution.py:322
  162.3 11.0 %collective-permute-start.30 = (bf16[2,768,384]{2,1,0:T(8,128)(2,1)}, bf16[2,768,384]{2,1,0:T(8,128)(2,1)S(1)}, u32[]{:S(2)}, u32[]{:S(2)}) collective-permute-start(bf16[2,768,384]{2,1,0:T(8,128)(2,1)} %get-tuple-element.119), channel_id=1, source_target_pairs={{0,8},{8,0},{16,24},{24,16},{1,9},{9,1},{17,25},{25,17},{2,10},{10... | collective-permute-start | bytes 3538952 | tf_op jit(solution)/shard_map/ppermute | solution.py:322
  167.5 39.5 %all-to-all-start.2 = ((bf16[8,96,512]{2,1,0:T(8,128)(2,1)}), bf16[8,96,512]{2,1,0:T(8,128)(2,1)}, u32[]{:S(2)}, u32[]{:S(2)}) async-start(bf16[8,96,512]{2,1,0:T(8,128)(2,1)} %bitcast.39), calls=%async_computation.2 | async-start | bytes 1572864 | tf_op jit(solution)/shard_map/all_to_all | solution.py:344
  174.2 22.9 %collective-permute-start.31 = (bf16[2,4,96,384]{3,2,1,0:T(8,128)(2,1)S(1)}, bf16[2,4,96,384]{3,2,1,0:T(8,128)(2,1)S(1)}, u32[]{:S(2)}, u32[]{:S(2)}) collective-permute-start(bf16[2,4,96,384]{3,2,1,0:T(8,128)(2,1)S(1)} %get-tuple-element.121), channel_id=1, source_target_pairs={{0,1},{1,0},{2,3},{3,2},{4,5},{5,4},{6,7},{7,6},{8,9},{9,8},{10,11... | collective-permute-start | bytes 1769480 | tf_op jit(solution)/shard_map/ppermute | solution.py:322
  176.2 21.5 %collective-permute-start.28 = (bf16[768,384]{1,0:T(8,128)(2,1)S(1)}, bf16[768,384]{1,0:T(8,128)(2,1)S(1)}, u32[]{:S(2)}, u32[]{:S(2)}) collective-permute-start(bf16[768,384]{1,0:T(8,128)(2,1)S(1)} %copy-done.17), channel_id=1, source_target_pairs={{0,16},{8,24},{16,0},{24,8},{1,17},{9,25},{17,1},{25,9},{2,18},{10... | collective-permute-start | bytes 1769480 | tf_op jit(solution)/shard_map/ppermute | solution.py:322
  197.2 8.0 %collective-permute-start.32 = (bf16[4,96,384]{2,1,0:T(8,128)(2,1)S(1)}, bf16[4,96,384]{2,1,0:T(8,128)(2,1)S(1)}, u32[]{:S(2)}, u32[]{:S(2)}) collective-permute-start(bf16[4,96,384]{2,1,0:T(8,128)(2,1)S(1)} %get-tuple-element.123), channel_id=1, source_target_pairs={{0,16},{8,24},{16,0},{24,8},{1,17},{9,25},{17,1},{25,9},{2,18},{10... | collective-permute-start | bytes 884744 | tf_op jit(solution)/shard_map/ppermute | solution.py:322
  198.4 7.7 %collective-permute-start.29 = (bf16[4,96,384]{2,1,0:T(8,128)(2,1)S(1)}, bf16[4,96,384]{2,1,0:T(8,128)(2,1)S(1)}, u32[]{:S(2)}, u32[]{:S(2)}) collective-permute-start(bf16[4,96,384]{2,1,0:T(8,128)(2,1)S(1)} %get-tuple-element.117), channel_id=1, source_target_pairs={{0,1},{1,0},{2,3},{3,2},{4,5},{5,4},{6,7},{7,6},{8,9},{9,8},{10,11... | collective-permute-start | bytes 884744 | tf_op jit(solution)/shard_map/ppermute | solution.py:322
  207.1 19.6 %all-to-all-start.3 = ((bf16[4,96,768]{2,1,0:T(8,128)(2,1)}), bf16[4,96,768]{2,1,0:T(8,128)(2,1)S(1)}, u32[]{:S(2)}, u32[]{:S(2)}) async-start(bf16[4,96,768]{2,1,0:T(8,128)(2,1)} %shard_map.145), calls=%async_computation.3 | async-start | bytes 1179648 | tf_op jit(solution)/shard_map/all_to_all | solution.py:399
  (22 other events, 28.3 us)

commit v8 on v7

--- a/solution.py
+++ b/solution.py
@@ -116,7 +116,7 @@
     )(jnp.stack(starts + later).astype(jnp.int32), rows, *weights)
 
 
-def absorb(total, column, blocks, weights, final):
+def absorb(total, column, blocks, weights, final, mib):
     count = len(weights)
     row_count = total.shape[0]
     columns = weights[0].shape[1]
@@ -132,7 +132,7 @@
             out_ref[part] = sums.astype(out_ref.dtype)
 
     return call(
-        body, (total, *blocks, *weights), [((row_count, columns), BF if final else F32)], 60
+        body, (total, *blocks, *weights), [((row_count, columns), BF if final else F32)], mib
     )[0]
 
 
@@ -346,21 +346,31 @@
     )
 
 
-def far_body(keep_ref, came_ref, away_ref, here_ref):
-    away_ref[...] = (keep_ref[1].astype(F32) + came_ref[1].astype(F32)).astype(BF)
-    here_ref[...] = keep_ref[0].astype(F32) + came_ref[0].astype(F32)
-
-
-def side_body(ids_ref, held_ref, came_ref, other_ref, own_ref):
+def side_rows(value, side):
+    groups = lax.axis_size("seq")
+    *blocks, rows, columns = value.shape
+    value = value.reshape(*blocks, groups // 2, 2, rows // groups, columns)
+    return lax.dynamic_index_in_dim(value, side, axis=len(blocks) + 1, keepdims=False).astype(F32)
+
+
+def left_body(ids_ref, keep_ref, came_ref, x_ref, other_ref, own_ref):
     side = ids_ref[1] & 1
-    lead = (slice(None),) * (len(held_ref.shape) - 3)
 
     def total(at):
-        place = (*lead, at)
-        return held_ref[place].astype(F32) + came_ref[place].astype(F32)
+        return keep_ref[0, :, at].astype(F32) + came_ref[0, :, at].astype(F32) + x_ref[:, at].astype(F32)
 
     other_ref[...] = total(1 - side).astype(BF)
     own_ref[...] = total(side)
+
+
+def right_body(ids_ref, keep_ref, came_ref, side_ref, away_ref, here_ref):
+    side = ids_ref[1] & 1
+
+    def total(at):
+        return keep_ref[at, :, side].astype(F32) + came_ref[at, :, side].astype(F32) + side_ref[at].astype(F32)
+
+    away_ref[...] = total(1).astype(BF)
+    here_ref[...] = total(0)
 
 
 def both_body(left_ref, left_came_ref, right_ref, right_came_ref, both_ref):
@@ -371,24 +381,29 @@
 
 def crossed_sums(place, left_keep, left_send, right_keep, right_send, first, first_came):
     groups = lax.axis_size("seq")
+    side = lax.axis_index("seq") % 2
     blocks, rows, columns = left_keep.shape
     pairs = (groups // 2, 2, rows // groups, columns)
     half = (groups // 2, rows // groups, columns)
     right_came = swap(right_send, "dp", 1)
     left_came = swap(left_send, "dp", 1)
-    other, own = call(
-        side_body, (place, right_keep.reshape(blocks, *pairs), right_came.reshape(blocks, *pairs)),
-        [((blocks, *half), BF), ((blocks, *half), F32)], 20, smem=1,
-    )
-    side_came = swap(other, "seq", 1)
-    away, here = call(far_body, (left_keep, left_came), [((rows, columns), BF), ((rows, columns), F32)], 20)
-    away, first_came = lax.optimization_barrier((away, first_came))
-    x_came = swap(away, "dp", 2)
+    left_away = (left_keep[1].astype(F32) + left_came[1].astype(F32)).astype(BF)
+    left_away, first_came = lax.optimization_barrier((left_away, first_came))
+    x_came = swap(left_away, "dp", 2)
+    other = side_rows(right_keep, 1 - side) + side_rows(right_came, 1 - side)
+    side_came = swap(other.astype(BF), "seq", 1)
+
+    def split(value):
+        return value.reshape(blocks, *pairs)
+
     other, left = call(
-        side_body, (place, here.reshape(pairs), x_came.reshape(pairs)), [(half, BF), (half, F32)], 20, smem=1
+        left_body, (place, split(left_keep), split(left_came), x_came.reshape(pairs)),
+        [(half, BF), (half, F32)], 20, smem=1,
     )
     left_came = swap(other, "seq", 1)
-    away, right = call(far_body, (own, side_came), [(half, BF), (half, F32)], 20)
+    away, right = call(
+        right_body, (place, split(right_keep), split(right_came), side_came), [(half, BF), (half, F32)], 20, smem=1
+    )
     right_came = swap(away, "dp", 2)
     both, = call(
         both_body, (left, left_came, right, right_came), [((groups // 2, rows // groups, 2 * columns), BF)], 20
@@ -444,10 +459,9 @@
             sums.reshape(groups, block, columns), "seq", split_axis=0, concat_axis=0, tiled=True
         ).reshape(row_count, columns)
 
-    left = send(absorb(total, 0, blocks, weights[0] + weights[1], True))
-    right = absorb(total, columns, blocks[:6], weights[2] + weights[3][:2], False)
-    left, last = lax.optimization_barrier((left, weights[3][2]))
-    right = send(absorb(right, 0, blocks[6:], [last, weights[3][3]], True))
+    left = send(absorb(total, 0, blocks, weights[0] + weights[1], True, 20))
+    right = absorb(total, columns, blocks[:6], weights[2] + weights[3][:2], False, 20)
+    right = send(absorb(right, 0, blocks[6:], weights[3][2:], True, 60))
 
     column = lax.dynamic_index_in_dim(layout[0], device, axis=1, keepdims=True)
     position = column * block + jnp.arange(block, dtype=jnp.int32)[None, :]

time: 228 us -> 234 us (1.026)
  Pallas kernels: 52 us -> 45.2 us
  local copies, waits for them, and re-layouts: 15.2 us -> 20 us
  starting transfers between devices: 60.2 us -> 63.6 us
    pallas_call x17 -> x15, Pallas kernels: 41.5 us -> 34.7 us  [call(): pl.pallas_call(body, out_shape=outs, in_specs=[SMEM] * smem + [ANY] * aft...]
    unnamed x66 -> x72, local copies, waits for them, and re-layouts: 12.4 us -> 18.3 us
    ppermute x25, waiting for transfers between devices: 53.5 us -> 56.1 us  [swap(): return lax.ppermute(value, axis, [(i, i ^ bit) for i in range(size)])]
  transfers between devices with their start and end apart: 37 -> 37, of which waited for: 15 -> 18; matrix products, arithmetic and copies ran while one was open for 3% -> 3% of each run, Pallas kernels for 17% -> 15%
where the time goes in v8:
time: 234 us; the launch traced here: 233 us
  waiting for transfers between devices  96.5 us (41%)
  starting transfers between devices  63.6 us (27%)
  Pallas kernels  45.2 us (19%)
  local copies, waits for them, and re-layouts  20 us (9%)
  other arithmetic  6.02 us (3%)
    ppermute x25, waiting for transfers between devices, swap(): return lax.ppermute(value, axis, [(i, i ^ bit) for i in range(size)])  56.1 us
    pallas_call x15, Pallas kernels, call(): pl.pallas_call(body, out_shape=outs, in_specs=[SMEM] * smem + [ANY] * aft...  34.7 us
    ppermute x25, starting transfers between devices, swap(): return lax.ppermute(value, axis, [(i, i ^ bit) for i in range(size)])  20 us
    unnamed x72, local copies, waits for them, and re-layouts  18.3 us
    ppermute x4, starting transfers between devices, halo(): lax.ppermute(high, 'seq', up)  15.1 us
    all_to_all x2, starting transfers between devices, send(): lax.all_to_all(sums.reshape(groups, block, columns), 'seq', split_axis=0,...  13.4 us
    all_to_all x1, waiting for transfers between devices, crossed_sums(): lax.all_to_all(both, 'seq', split_axis=0, concat_axis=0, axis_index_group...  12.6 us
    all_to_all x2, waiting for transfers between devices, send(): lax.all_to_all(sums.reshape(groups, block, columns), 'seq', split_axis=0,...  11 us
  transfers between devices with their start and end apart: 37, of which 18 were waited for; matrix products, arithmetic and copies ran while one was open for 3% of the time, Pallas kernels for 15%

profile of v8, /device:TPU:0, one launch (start us, length us, event | category | flops | bytes accessed | tf_op | source)
XLA Modules:
  0.0 233.0 jit_solution(12514726163602174451)
XLA Ops:
  1.1 1.5 fusion.4
  2.7 2.6 %collective-permute-start.9 = (bf16[512,384]{1,0:T(8,128)(2,1)S(1)}, bf16[512,384]{1,0:T(8,128)(2,1)S(1)}, u32[]{:S(2)}, u32[]{:S(2)}) collective-permute-start(bf16[512,384]{1,0:T(8,128)(2,1)S(1)} %get-tuple-element.119), channel_id=1, source_target_pairs={{0,16},{8,24},{16,0},{24,8},{1,17},{9,25},{17,1},{25,9},{2,18},{10... | collective-permute-start | bytes 1179656 | tf_op jit(solution)/shard_map/ppermute | solution.py:322
  5.4 1.9 collective-permute-start
  7.3 7.9 %collective-permute-done.9.refs_6_ = bf16[512,384]{1,0:T(8,128)(2,1)S(1)} collective-permute-done((bf16[512,384]{1,0:T(8,128)(2,1)S(1)}, bf16[512,384]{1,0:T(8,128)(2,1)S(1)}, u32[]{:S(2)}, u32[]{:S(2)}) %collective-permute-start.9) | collective-permute-done | bytes 393248 | tf_op jit(solution)/shard_map/ppermute | solution.py:322
  15.2 2.0 collective-permute-start.11
  17.2 6.4 %collective-permute-done.13.refs_10_ = bf16[512,384]{1,0:T(8,128)(2,1)S(1)} collective-permute-done((bf16[512,384]{1,0:T(8,128)(2,1)S(1)}, bf16[512,384]{1,0:T(8,128)(2,1)S(1)}, u32[]{:S(2)}, u32[]{:S(2)}) %collective-permute-start.13) | collective-permute-done | bytes 393248 | tf_op jit(solution)/shard_map/ppermute | solution.py:322
  23.7 2.0 collective-permute-start.15
  25.6 1.5 collective-permute-start.5
  27.1 5.0 %collective-permute-done.refs_8_ = bf16[512,384]{1,0:T(8,128)(2,1)S(1)} collective-permute-done((bf16[512,384]{1,0:T(8,128)(2,1)S(1)}, bf16[512,384]{1,0:T(8,128)(2,1)S(1)}, u32[]{:S(2)}, u32[]{:S(2)}) %collective-permute-start) | collective-permute-done | bytes 393248 | tf_op jit(solution)/shard_map/ppermute | solution.py:322
  32.6 1.8 collective-permute-done.15.refs_2_
  35.0 10.5 %shard_map.129 = (f32[512,768]{1,0:T(8,128)}, bf16[512,512]{1,0:T(8,128)(2,1)S(1)}, bf16[512,512]{1,0:T(8,128)(2,1)S(1)}, bf16[512,512]{1,0:T(8,128)(2,1)S(1)}, ...) custom-call(s32[10]{0:T(128)S(1)} %stack.60.starts_ref, ...), custom_call_target="tpu_custom_call" | custom-call | flops 1024 | bytes 1024 | tf_op jit(solution)/shard_map/pallas_call | solution.py:103
  45.6 1.6 collective-permute-start.7
  47.7 1.4 copy-done.2
  49.1 2.8 %shard_map.131.old_ref = f32[512,384]{1,0:T(8,128)S(1)} custom-call(f32[512,768]{1,0:T(8,128)S(1)} %copy-done.2, bf16[512,512]{1,0:T(8,128)(2,1)S(1)} %get-tuple-element.63.refs_0_, bf16[512,512]{1,0:T(8,128)(2,1)S(1)} %get-tuple-element.64.refs_1_, bf16[512,512]{1,0:T(8,128)(2,1)S(1)} %get-tuple-element.65.refs_2_, ...), custom_call_target="tpu_custom_call" | custom-call | flops 1024 | bytes 1024 | tf_op jit(solution)/shard_map/pallas_call | solution.py:52
  52.9 3.1 %shard_map.132 = bf16[512,384]{1,0:T(8,128)(2,1)} custom-call(f32[512,384]{1,0:T(8,128)} %copy-done.7, bf16[512,512]{1,0:T(8,128)(2,1)} %copy-done.8, bf16[512,512]{1,0:T(8,128)(2,1)} %copy-done.10, bf16[512,384]{1,0:T(8,128)(2,1)} %collective-permute-done.15.refs_2_, bf16[512,384]{1,0:T(8,128)(2,1)} %collective-permute-done.16.refs_3_), custom_call_target="tpu_custom_call" | custom-call | flops 1024 | bytes 1024 | tf_op jit(solution)/shard_map/pallas_call | solution.py:52
  56.0 6.0 %all-to-all-start.1 = ((bf16[8,64,384]{2,1,0:T(8,128)(2,1)}), bf16[8,64,384]{2,1,0:T(8,128)(2,1)}, u32[]{:S(2)}, u32[]{:S(2)}) async-start(bf16[8,64,384]{2,1,0:T(8,128)(2,1)} %bitcast.50), calls=%async_computation.1 | async-start | bytes 786432 | tf_op jit(solution)/shard_map/all_to_all | solution.py:458
  63.5 3.2 %collective-permute-done.3.refs_10_ = bf16[512,384]{1,0:T(8,128)(2,1)S(1)} collective-permute-done((bf16[512,384]{1,0:T(8,128)(2,1)S(1)}, bf16[512,384]{1,0:T(8,128)(2,1)S(1)}, u32[]{:S(2)}, u32[]{:S(2)}) %collective-permute-start.3) | collective-permute-done | bytes 393248 | tf_op jit(solution)/shard_map/ppermute | solution.py:322
  68.4 1.4 copy-done.3
  82.2 2.3 %shard_map.130 = bf16[512,384]{1,0:T(8,128)(2,1)S(1)} custom-call(f32[512,768]{1,0:T(8,128)S(1)} %copy-done.3, bf16[512,512]{1,0:T(8,128)(2,1)S(1)} %copy-done.13, bf16[512,512]{1,0:T(8,128)(2,1)S(1)} %copy-done.15, bf16[512,512]{1,0:T(8,128)(2,1)S(1)} %copy-done.17, bf16[512,512]{1,0:T(8,128)(2,1)S(1)} %copy-done.19, bf16[512,512]{1,0:T(8,128)(2,1)S(1)} %copy-done.21, ...), custom_call_target="tpu_custom_call" | custom-call | flops 1024 | bytes 1024 | tf_op jit(solution)/shard_map/pallas_call | solution.py:52
  85.3 7.4 %all-to-all-start = ((bf16[8,64,384]{2,1,0:T(8,128)(2,1)}), bf16[8,64,384]{2,1,0:T(8,128)(2,1)}, u32[]{:S(2)}, u32[]{:S(2)}) async-start(bf16[8,64,384]{2,1,0:T(8,128)(2,1)} %bitcast.45), calls=%async_computation | async-start | bytes 786432 | tf_op jit(solution)/shard_map/all_to_all | solution.py:458
  93.7 11.0 %all-to-all-done = bf16[8,64,384]{2,1,0:T(8,128)(2,1)} async-done(((bf16[8,64,384]{2,1,0:T(8,128)(2,1)}), bf16[8,64,384]{2,1,0:T(8,128)(2,1)}, u32[]{:S(2)}, u32[]{:S(2)}) %all-to-all-start) | async-done | bytes 393248 | tf_op jit(solution)/shard_map/all_to_all | solution.py:458
  104.8 2.3 shard_map.133
  107.0 3.4 %collective-permute-start.17 = (bf16[256,384]{1,0:T(8,128)(2,1)S(1)}, bf16[256,384]{1,0:T(8,128)(2,1)S(1)}, u32[]{:S(2)}, u32[]{:S(2)}) collective-permute-start(bf16[256,384]{1,0:T(8,128)(2,1)S(1)} %get-tuple-element.72), channel_id=1, source_target_pairs={{0,1},{1,2},{2,3},{3,4},{4,5},{5,6},{6,7},{8,9},{9,10},{10,11},{11... | collective-permute-start | bytes 589832 | tf_op jit(solution)/shard_map/ppermute | solution.py:329
  110.4 1.5 collective-permute-start.18
  112.9 5.1 %collective-permute-done.17.prev_ref = bf16[256,384]{1,0:T(8,128)(2,1)S(1)} collective-permute-done((bf16[256,384]{1,0:T(8,128)(2,1)S(1)}, bf16[256,384]{1,0:T(8,128)(2,1)S(1)}, u32[]{:S(2)}, u32[]{:S(2)}) %collective-permute-start.17) | collective-permute-done | bytes 196640 | tf_op jit(solution)/shard_map/ppermute | solution.py:329
  118.9 4.5 %collective-permute-start.19 = (bf16[128,384]{1,0:T(8,128)(2,1)S(1)}, bf16[128,384]{1,0:T(8,128)(2,1)S(1)}, u32[]{:S(2)}, u32[]{:S(2)}) collective-permute-start(bf16[128,384]{1,0:T(8,128)(2,1)S(1)} %get-tuple-element.77), channel_id=1, source_target_pairs={{0,1},{1,2},{2,3},{3,4},{4,5},{5,6},{6,7},{8,9},{9,10},{10,11},{11... | collective-permute-start | bytes 294920 | tf_op jit(solution)/shard_map/ppermute | solution.py:329
  123.4 1.3 collective-permute-start.20
  125.6 4.3 %collective-permute-done.20.refs_4_ = bf16[128,384]{1,0:T(8,128)(2,1)S(1)} collective-permute-done((bf16[128,384]{1,0:T(8,128)(2,1)S(1)}, bf16[128,384]{1,0:T(8,128)(2,1)S(1)}, u32[]{:S(2)}, u32[]{:S(2)}) %collective-permute-start.20) | collective-permute-done | bytes 98336 | tf_op jit(solution)/shard_map/ppermute | solution.py:330
  129.9 3.7 %shard_map.136 = (bf16[256,384]{1,0:T(8,128)(2,1)S(1)}, bf16[128,768]{1,0:T(8,128)(2,1)S(1)}, bf16[128,2048]{1,0:T(8,128)(2,1)S(1)}, bf16[128,768]{1,0:T(8,128)(...) custom-call(s32[2]{0:T(128)S(1)} %get-tuple-element.123.refs_0_, ...), custom_call_target="tpu_custom_call" | custom-call | flops 1024 | bytes 1024 | tf_op jit(solution)/shard_map/pallas_call | solution.py:52
  133.6 1.5 shard_map.137
  135.3 4.0 %collective-permute-start.22 = (bf16[128,384]{1,0:T(8,128)(2,1)S(1)}, bf16[128,384]{1,0:T(8,128)(2,1)S(1)}, u32[]{:S(2)}, u32[]{:S(2)}) collective-permute-start(bf16[128,384]{1,0:T(8,128)(2,1)S(1)} %get-tuple-element.86.refs_3_.refs_6_), channel_id=1, source_target_pairs={{0,1},{1,2},{2,3},{3,4},{4,5},{5,6},{6,7},{8,9},{9,10},{10,11},{11... | collective-permute-start | bytes 294920 | tf_op jit(solution)/shard_map/ppermute | solution.py:329
  139.2 1.3 collective-permute-start.23
  141.9 4.1 %collective-permute-done.23.refs_4_.refs_7_ = bf16[128,384]{1,0:T(8,128)(2,1)S(1)} collective-permute-done((bf16[128,384]{1,0:T(8,128)(2,1)S(1)}, bf16[128,384]{1,0:T(8,128)(2,1)S(1)}, u32[]{:S(2)}, u32[]{:S(2)}) %collective-permute-start.23) | collective-permute-done | bytes 98336 | tf_op jit(solution)/shard_map/ppermute | solution.py:330
  146.0 1.5 collective-permute-start.26
  147.6 2.5 %shard_map.138 = (f32[256,768]{1,0:T(8,128)}, bf16[256,768]{1,0:T(8,128)(2,1)S(1)}, bf16[256,384]{1,0:T(8,128)(2,1)S(1)}, bf16[256,384]{1,0:T(8,128)(2,1)S(1)}) custom-call(bf16[768,512]{1,0:T(8,128)(2,1)S(1)} %fusion.1.refs_0_, bf16[128,384]{1,0:T(8,128)(2,1)S(1)} %collective-permute-done.22.refs_1_.refs_4_, ...), custom_call_target="tpu_custom_call" | custom-call | flops 1024 | bytes 1024 | tf_op jit(solution)/shard_map/pallas_call | solution.py:52
  150.0 3.2 %collective-permute-start.24 = (bf16[256,384]{1,0:T(8,128)(2,1)S(1)}, bf16[256,384]{1,0:T(8,128)(2,1)S(1)}, u32[]{:S(2)}, u32[]{:S(2)}) collective-permute-start(bf16[256,384]{1,0:T(8,128)(2,1)S(1)} %get-tuple-element.94.refs_6_), channel_id=1, source_target_pairs={{0,1},{1,2},{2,3},{3,4},{4,5},{5,6},{6,7},{8,9},{9,10},{10,11},{11... | collective-permute-start | bytes 589832 | tf_op jit(solution)/shard_map/ppermute | solution.py:329
  153.3 1.3 collective-permute-start.25
  154.6 5.2 %shard_map.139 = (bf16[2,768,384]{2,1,0:T(8,128)(2,1)S(1)}, bf16[2,768,384]{2,1,0:T(8,128)(2,1)}) custom-call(s32[2]{0:T(128)S(1)} %get-tuple-element.122.ids_ref.refs_0_, bf16[256,384]{1,0:T(8,128)(2,1)S(1)} %get-tuple-element.93.refs_1_.refs_5_, bf16[128,768]{1,0:T(8,128)(2,1)S(1)} %get-tuple-element.78.refs_2_, ...), custom_call_target="tpu_custom_call" | custom-call | flops 1024 | bytes 1024 | tf_op jit(solution)/shard_map/pallas_call | solution.py:52
  161.0 5.3 %shard_map.140 = (bf16[2,768,384]{2,1,0:T(8,128)(2,1)S(1)}, bf16[2,768,384]{2,1,0:T(8,128)(2,1)S(1)}) custom-call(s32[2]{0:T(128)S(1)} %get-tuple-element.122.ids_ref.refs_0_, bf16[256,384]{1,0:T(8,128)(2,1)S(1)} %get-tuple-element.93.refs_1_.refs_5_, bf16[256,768]{1,0:T(8,128)(2,1)S(1)} %get-tuple-element.74.low_ref.refs_2_, ...), custom_call_target="tpu_custom_call" | custom-call | flops 1024 | bytes 1024 | tf_op jit(solution)/shard_map/pallas_call | solution.py:52
  166.8 3.2 %collective-permute-done.27 = bf16[2,768,384]{2,1,0:T(8,128)(2,1)S(1)} collective-permute-done((bf16[2,768,384]{2,1,0:T(8,128)(2,1)S(1)}, bf16[2,768,384]{2,1,0:T(8,128)(2,1)S(1)}, u32[]{:S(2)}, u32[]{:S(2)}) %collective-permute-start.27) | collective-permute-done | bytes 1179680 | tf_op jit(solution)/shard_map/ppermute | solution.py:322
  172.3 5.2 %all-to-all-start.2 = ((bf16[8,96,512]{2,1,0:T(8,128)(2,1)}), bf16[8,96,512]{2,1,0:T(8,128)(2,1)}, u32[]{:S(2)}, u32[]{:S(2)}) async-start(bf16[8,96,512]{2,1,0:T(8,128)(2,1)} %bitcast.49), calls=%async_computation.2 | async-start | bytes 1572864 | tf_op jit(solution)/shard_map/all_to_all | solution.py:344
  178.8 2.1 collective-permute-start.31
  181.4 19.9 %collective-permute-done.31.side_ref = bf16[2,4,96,384]{3,2,1,0:T(8,128)(2,1)S(1)} collective-permute-done((bf16[2,4,96,384]{3,2,1,0:T(8,128)(2,1)S(1)}, bf16[2,4,96,384]{3,2,1,0:T(8,128)(2,1)S(1)}, u32[]{:S(2)}, u32[]{:S(2)}) %collective-permute-start.31) | collective-permute-done | bytes 589856 | tf_op jit(solution)/shard_map/ppermute | solution.py:322
  201.2 1.5 shard_map.142
  204.5 6.5 %collective-permute-done.32.right_came_ref = bf16[4,96,384]{2,1,0:T(8,128)(2,1)S(1)} collective-permute-done((bf16[4,96,384]{2,1,0:T(8,128)(2,1)S(1)}, bf16[4,96,384]{2,1,0:T(8,128)(2,1)S(1)}, u32[]{:S(2)}, u32[]{:S(2)}) %collective-permute-start.32) | collective-permute-done | bytes 294944 | tf_op jit(solution)/shard_map/ppermute | solution.py:322
  213.0 4.5 %all-to-all-start.3 = ((bf16[4,96,768]{2,1,0:T(8,128)(2,1)}), bf16[4,96,768]{2,1,0:T(8,128)(2,1)S(1)}, u32[]{:S(2)}, u32[]{:S(2)}) async-start(bf16[4,96,768]{2,1,0:T(8,128)(2,1)} %shard_map.143), calls=%async_computation.3 | async-start | bytes 1179648 | tf_op jit(solution)/shard_map/all_to_all | solution.py:414
  217.5 1.9 convert_reduce_fusion
  219.4 12.6 %all-to-all-done.3.parts_ref = bf16[4,96,768]{2,1,0:T(8,128)(2,1)S(1)} async-done(((bf16[4,96,768]{2,1,0:T(8,128)(2,1)}), bf16[4,96,768]{2,1,0:T(8,128)(2,1)S(1)}, u32[]{:S(2)}, u32[]{:S(2)}) %all-to-all-start.3) | async-done | bytes 589856 | tf_op jit(solution)/shard_map/all_to_all | solution.py:414
  (126 shorter events, 34.4 us)
Async XLA Ops:
  0.6 33.8 %collective-permute-start.1 = (bf16[2048,768]{1,0:T(8,128)(2,1)}, bf16[2048,768]{1,0:T(8,128)(2,1)}, u32[]{:S(2)}, u32[]{:S(2)}) collective-permute-start(bf16[2048,768]{1,0:T(8,128)(2,1)} %refs_0_.1), channel_id=1, source_target_pairs={{0,8},{8,0},{16,24},{24,16},{1,9},{9,1},{17,25},{25,17},{2,10},{10... | collective-permute-start | bytes 9437192 | tf_op jit(solution)/shard_map/ppermute | solution.py:322
  2.7 12.6 %collective-permute-start.9 = (bf16[512,384]{1,0:T(8,128)(2,1)S(1)}, bf16[512,384]{1,0:T(8,128)(2,1)S(1)}, u32[]{:S(2)}, u32[]{:S(2)}) collective-permute-start(bf16[512,384]{1,0:T(8,128)(2,1)S(1)} %get-tuple-element.119), channel_id=1, source_target_pairs={{0,16},{8,24},{16,0},{24,8},{1,17},{9,25},{17,1},{25,9},{2,18},{10... | collective-permute-start | bytes 1179656 | tf_op jit(solution)/shard_map/ppermute | solution.py:322
  5.3 18.4 %collective-permute-start.13 = (bf16[512,384]{1,0:T(8,128)(2,1)S(1)}, bf16[512,384]{1,0:T(8,128)(2,1)S(1)}, u32[]{:S(2)}, u32[]{:S(2)}) collective-permute-start(bf16[512,384]{1,0:T(8,128)(2,1)S(1)} %get-tuple-element.118), channel_id=1, source_target_pairs={{0,16},{8,24},{16,0},{24,8},{1,17},{9,25},{17,1},{25,9},{2,18},{10... | collective-permute-start | bytes 1179656 | tf_op jit(solution)/shard_map/ppermute | solution.py:322
  5.4 26.7 %collective-permute-start = (bf16[512,384]{1,0:T(8,128)(2,1)S(1)}, bf16[512,384]{1,0:T(8,128)(2,1)S(1)}, u32[]{:S(2)}, u32[]{:S(2)}) collective-permute-start(bf16[512,384]{1,0:T(8,128)(2,1)S(1)} %get-tuple-element.121), channel_id=1, source_target_pairs={{0,16},{8,24},{16,0},{24,8},{1,17},{9,25},{17,1},{25,9},{2,18},{10... | collective-permute-start | bytes 1179656 | tf_op jit(solution)/shard_map/ppermute | solution.py:322
  15.2 16.9 %collective-permute-start.11 = (bf16[512,384]{1,0:T(8,128)(2,1)S(1)}, bf16[512,384]{1,0:T(8,128)(2,1)S(1)}, u32[]{:S(2)}, u32[]{:S(2)}) collective-permute-start(bf16[512,384]{1,0:T(8,128)(2,1)S(1)} %collective-permute-done.9.refs_6_), channel_id=1, source_target_pairs={{0,1},{1,0},{2,3},{3,2},{4,5},{5,4},{6,7},{7,6},{8,9},{9,8},{10,11... | collective-permute-start | bytes 1179656 | tf_op jit(solution)/shard_map/ppermute | solution.py:322
  23.7 10.8 %collective-permute-start.15 = (bf16[512,384]{1,0:T(8,128)(2,1)S(1)}, bf16[512,384]{1,0:T(8,128)(2,1)}, u32[]{:S(2)}, u32[]{:S(2)}) collective-permute-start(bf16[512,384]{1,0:T(8,128)(2,1)S(1)} %collective-permute-done.13.refs_10_), channel_id=1, source_target_pairs={{0,1},{1,0},{2,3},{3,2},{4,5},{5,4},{6,7},{7,6},{8,9},{9,8},{10,11... | collective-permute-start | bytes 1179656 | tf_op jit(solution)/shard_map/ppermute | solution.py:322
  25.6 20.0 %collective-permute-start.5 = (bf16[512,384]{1,0:T(8,128)(2,1)S(1)}, bf16[512,384]{1,0:T(8,128)(2,1)S(1)}, u32[]{:S(2)}, u32[]{:S(2)}) collective-permute-start(bf16[512,384]{1,0:T(8,128)(2,1)S(1)} %get-tuple-element.120), channel_id=1, source_target_pairs={{0,16},{8,24},{16,0},{24,8},{1,17},{9,25},{17,1},{25,9},{2,18},{10... | collective-permute-start | bytes 1179656 | tf_op jit(solution)/shard_map/ppermute | solution.py:322
  32.1 30.5 %copy-start.26 = (bf16[512,384]{1,0:T(8,128)(2,1)}, bf16[512,384]{1,0:T(8,128)(2,1)S(1)}, u32[]{:S(2)}) copy-start(bf16[512,384]{1,0:T(8,128)(2,1)S(1)} %collective-permute-done.refs_8_) | copy-start | bytes 1179652
  32.1 15.2 %collective-permute-start.10 = (bf16[512,384]{1,0:T(8,128)(2,1)S(1)}, bf16[512,384]{1,0:T(8,128)(2,1)S(1)}, u32[]{:S(2)}, u32[]{:S(2)}) collective-permute-start(bf16[512,384]{1,0:T(8,128)(2,1)S(1)} %collective-permute-done.9.refs_6_), channel_id=1, source_target_pairs={{0,8},{8,0},{16,24},{24,16},{1,9},{9,1},{17,25},{25,17},{2,10},{10... | collective-permute-start | bytes 1179656 | tf_op jit(solution)/shard_map/ppermute | solution.py:322
  32.1 15.6 %collective-permute-start.14 = (bf16[512,384]{1,0:T(8,128)(2,1)S(1)}, bf16[512,384]{1,0:T(8,128)(2,1)S(1)}, u32[]{:S(2)}, u32[]{:S(2)}) collective-permute-start(bf16[512,384]{1,0:T(8,128)(2,1)S(1)} %collective-permute-done.13.refs_10_), channel_id=1, source_target_pairs={{0,8},{8,0},{16,24},{24,16},{1,9},{9,1},{17,25},{25,17},{2,10},{10... | collective-permute-start | bytes 1179656 | tf_op jit(solution)/shard_map/ppermute | solution.py:322
  34.4 13.3 %collective-permute-start.12 = (bf16[512,384]{1,0:T(8,128)(2,1)S(1)}, bf16[512,384]{1,0:T(8,128)(2,1)}, u32[]{:S(2)}, u32[]{:S(2)}) collective-permute-start(bf16[512,384]{1,0:T(8,128)(2,1)S(1)} %collective-permute-done.11.refs_8_), channel_id=1, source_target_pairs={{0,8},{8,0},{16,24},{24,16},{1,9},{9,1},{17,25},{25,17},{2,10},{10... | collective-permute-start | bytes 1179656 | tf_op jit(solution)/shard_map/ppermute | solution.py:322
  34.4 18.4 %collective-permute-start.16 = (bf16[512,384]{1,0:T(8,128)(2,1)}, bf16[512,384]{1,0:T(8,128)(2,1)}, u32[]{:S(2)}, u32[]{:S(2)}) collective-permute-start(bf16[512,384]{1,0:T(8,128)(2,1)} %collective-permute-done.15.refs_2_), channel_id=1, source_target_pairs={{0,8},{8,0},{16,24},{24,16},{1,9},{9,1},{17,25},{25,17},{2,10},{10... | collective-permute-start | bytes 1179656 | tf_op jit(solution)/shard_map/ppermute | solution.py:322
  45.5 6.4 %copy-start.8 = (bf16[512,512]{1,0:T(8,128)(2,1)}, bf16[512,512]{1,0:T(8,128)(2,1)S(1)}, u32[]{:S(2)}) copy-start(bf16[512,512]{1,0:T(8,128)(2,1)S(1)} %get-tuple-element.69.refs_6_.refs_0_) | copy-start | bytes 1572868
  45.5 6.4 %copy-start.10 = (bf16[512,512]{1,0:T(8,128)(2,1)}, bf16[512,512]{1,0:T(8,128)(2,1)S(1)}, u32[]{:S(2)}) copy-start(bf16[512,512]{1,0:T(8,128)(2,1)S(1)} %get-tuple-element.70.refs_7_.refs_1_) | copy-start | bytes 1572868
  45.5 6.4 %copy-start.12 = (bf16[512,512]{1,0:T(8,128)(2,1)}, bf16[512,512]{1,0:T(8,128)(2,1)S(1)}, u32[]{:S(2)}) copy-start(bf16[512,512]{1,0:T(8,128)(2,1)S(1)} %get-tuple-element.63.refs_0_) | copy-start | bytes 1572868
  45.6 16.4 %copy-start.28 = (bf16[512,384]{1,0:T(8,128)(2,1)}, bf16[512,384]{1,0:T(8,128)(2,1)S(1)}, u32[]{:S(2)}) copy-start(bf16[512,384]{1,0:T(8,128)(2,1)S(1)} %collective-permute-done.5.refs_12_) | copy-start | bytes 1179652
  45.6 16.5 %collective-permute-start.7 = (bf16[512,384]{1,0:T(8,128)(2,1)S(1)}, bf16[512,384]{1,0:T(8,128)(2,1)S(1)}, u32[]{:S(2)}, u32[]{:S(2)}) collective-permute-start(bf16[512,384]{1,0:T(8,128)(2,1)S(1)} %collective-permute-done.5.refs_12_), channel_id=1, source_target_pairs={{0,1},{1,0},{2,3},{3,2},{4,5},{5,4},{6,7},{7,6},{8,9},{9,8},{10,11... | collective-permute-start | bytes 1179656 | tf_op jit(solution)/shard_map/ppermute | solution.py:322
  47.2 19.5 %collective-permute-start.3 = (bf16[512,384]{1,0:T(8,128)(2,1)S(1)}, bf16[512,384]{1,0:T(8,128)(2,1)S(1)}, u32[]{:S(2)}, u32[]{:S(2)}) collective-permute-start(bf16[512,384]{1,0:T(8,128)(2,1)S(1)} %collective-permute-done.refs_8_), channel_id=1, source_target_pairs={{0,1},{1,0},{2,3},{3,2},{4,5},{5,4},{6,7},{7,6},{8,9},{9,8},{10,11... | collective-permute-start | bytes 1179656 | tf_op jit(solution)/shard_map/ppermute | solution.py:322
  56.0 36.6 %copy-start.35 = (s32[1,8,8]{2,1,0:T(8,128)S(1)}, s32[1,8,8]{2,1,0:T(8,128)}, u32[]{:S(2)}) copy-start(s32[1,8,8]{2,1,0:T(8,128)} %param.11) | copy-start | bytes 772
  56.0 29.2 %all-to-all-start.1 = ((bf16[8,64,384]{2,1,0:T(8,128)(2,1)}), bf16[8,64,384]{2,1,0:T(8,128)(2,1)}, u32[]{:S(2)}, u32[]{:S(2)}) async-start(bf16[8,64,384]{2,1,0:T(8,128)(2,1)} %bitcast.50), calls=%async_computation.1 | async-start | bytes 786432 | tf_op jit(solution)/shard_map/all_to_all | solution.py:458
  62.0 5.4 %collective-permute-start.6 = (bf16[512,384]{1,0:T(8,128)(2,1)S(1)}, bf16[512,384]{1,0:T(8,128)(2,1)S(1)}, u32[]{:S(2)}, u32[]{:S(2)}) collective-permute-start(bf16[512,384]{1,0:T(8,128)(2,1)S(1)} %collective-permute-done.5.refs_12_), channel_id=1, source_target_pairs={{0,8},{8,0},{16,24},{24,16},{1,9},{9,1},{17,25},{25,17},{2,10},{10... | collective-permute-start | bytes 1179656 | tf_op jit(solution)/shard_map/ppermute | solution.py:322
  62.1 5.3 %collective-permute-start.8 = (bf16[512,384]{1,0:T(8,128)(2,1)S(1)}, bf16[512,384]{1,0:T(8,128)(2,1)S(1)}, u32[]{:S(2)}, u32[]{:S(2)}) collective-permute-start(bf16[512,384]{1,0:T(8,128)(2,1)S(1)} %collective-permute-done.7.refs_14_), channel_id=1, source_target_pairs={{0,8},{8,0},{16,24},{24,16},{1,9},{9,1},{17,25},{25,17},{2,10},{10... | collective-permute-start | bytes 1179656 | tf_op jit(solution)/shard_map/ppermute | solution.py:322
  63.4 4.1 %collective-permute-start.2 = (bf16[512,384]{1,0:T(8,128)(2,1)S(1)}, bf16[512,384]{1,0:T(8,128)(2,1)S(1)}, u32[]{:S(2)}, u32[]{:S(2)}) collective-permute-start(bf16[512,384]{1,0:T(8,128)(2,1)S(1)} %collective-permute-done.refs_8_), channel_id=1, source_target_pairs={{0,8},{8,0},{16,24},{24,16},{1,9},{9,1},{17,25},{25,17},{2,10},{10... | collective-permute-start | bytes 1179656 | tf_op jit(solution)/shard_map/ppermute | solution.py:322
  66.7 1.7 collective-permute-start.4
  82.2 22.6 %copy-start = (bf16[2,3,768,384]{3,2,1,0:T(8,128)(2,1)S(1)}, bf16[2,3,768,384]{3,2,1,0:T(8,128)(2,1)}, u32[]{:S(2)}) copy-start(bf16[2,3,768,384]{3,2,1,0:T(8,128)(2,1)} %refs_7_.3) | copy-start | bytes 10616836
  85.3 19.5 %all-to-all-start = ((bf16[8,64,384]{2,1,0:T(8,128)(2,1)}), bf16[8,64,384]{2,1,0:T(8,128)(2,1)}, u32[]{:S(2)}, u32[]{:S(2)}) async-start(bf16[8,64,384]{2,1,0:T(8,128)(2,1)} %bitcast.45), calls=%async_computation | async-start | bytes 786432 | tf_op jit(solution)/shard_map/all_to_all | solution.py:458
  107.0 11.0 %collective-permute-start.17 = (bf16[256,384]{1,0:T(8,128)(2,1)S(1)}, bf16[256,384]{1,0:T(8,128)(2,1)S(1)}, u32[]{:S(2)}, u32[]{:S(2)}) collective-permute-start(bf16[256,384]{1,0:T(8,128)(2,1)S(1)} %get-tuple-element.72), channel_id=1, source_target_pairs={{0,1},{1,2},{2,3},{3,4},{4,5},{5,6},{6,7},{8,9},{9,10},{10,11},{11... | collective-permute-start | bytes 589832 | tf_op jit(solution)/shard_map/ppermute | solution.py:329
  110.4 7.6 %collective-permute-start.18 = (bf16[256,384]{1,0:T(8,128)(2,1)S(1)}, bf16[256,384]{1,0:T(8,128)(2,1)S(1)}, u32[]{:S(2)}, u32[]{:S(2)}) collective-permute-start(bf16[256,384]{1,0:T(8,128)(2,1)S(1)} %get-tuple-element.73), channel_id=1, source_target_pairs={{1,0},{2,1},{3,2},{4,3},{5,4},{6,5},{7,6},{9,8},{10,9},{11,10},{12... | collective-permute-start | bytes 589832 | tf_op jit(solution)/shard_map/ppermute | solution.py:330
  118.0 11.9 %copy-start.6 = (bf16[768,2048]{1,0:T(8,128)(2,1)S(1)}, bf16[768,2048]{1,0:T(8,128)(2,1)}, u32[]{:S(2)}) copy-start(bf16[768,2048]{1,0:T(8,128)(2,1)} %refs_8_.2) | copy-start | bytes 9437188
  118.1 11.9 %copy-start.25 = (s32[1,128,2048]{2,1,0:T(8,128)S(1)}, s32[1,128,2048]{2,1,0:T(8,128)}, u32[]{:S(2)}) copy-start(s32[1,128,2048]{2,1,0:T(8,128)} %param.13) | copy-start | bytes 3145732
  118.9 6.7 %collective-permute-start.19 = (bf16[128,384]{1,0:T(8,128)(2,1)S(1)}, bf16[128,384]{1,0:T(8,128)(2,1)S(1)}, u32[]{:S(2)}, u32[]{:S(2)}) collective-permute-start(bf16[128,384]{1,0:T(8,128)(2,1)S(1)} %get-tuple-element.77), channel_id=1, source_target_pairs={{0,1},{1,2},{2,3},{3,4},{4,5},{5,6},{6,7},{8,9},{9,10},{10,11},{11... | collective-permute-start | bytes 294920 | tf_op jit(solution)/shard_map/ppermute | solution.py:329
  123.4 6.5 %collective-permute-start.20 = (bf16[128,384]{1,0:T(8,128)(2,1)S(1)}, bf16[128,384]{1,0:T(8,128)(2,1)S(1)}, u32[]{:S(2)}, u32[]{:S(2)}) collective-permute-start(bf16[128,384]{1,0:T(8,128)(2,1)S(1)} %get-tuple-element.80), channel_id=1, source_target_pairs={{1,0},{2,1},{3,2},{4,3},{5,4},{6,5},{7,6},{9,8},{10,9},{11,10},{12... | collective-permute-start | bytes 294920 | tf_op jit(solution)/shard_map/ppermute | solution.py:330
  135.2 5.4 %collective-permute-start.21 = (bf16[2,768,512]{2,1,0:T(8,128)(2,1)S(1)}, bf16[2,768,512]{2,1,0:T(8,128)(2,1)S(1)}, u32[]{:S(2)}, u32[]{:S(2)}) collective-permute-start(bf16[2,768,512]{2,1,0:T(8,128)(2,1)S(1)} %get-tuple-element.85), channel_id=1, source_target_pairs={{0,8},{8,0},{16,24},{24,16},{1,9},{9,1},{17,25},{25,17},{2,10},{10... | collective-permute-start | bytes 4718600 | tf_op jit(solution)/shard_map/ppermute | solution.py:322
  135.3 6.7 %collective-permute-start.22 = (bf16[128,384]{1,0:T(8,128)(2,1)S(1)}, bf16[128,384]{1,0:T(8,128)(2,1)S(1)}, u32[]{:S(2)}, u32[]{:S(2)}) collective-permute-start(bf16[128,384]{1,0:T(8,128)(2,1)S(1)} %get-tuple-element.86.refs_3_.refs_6_), channel_id=1, source_target_pairs={{0,1},{1,2},{2,3},{3,4},{4,5},{5,6},{6,7},{8,9},{9,10},{10,11},{11... | collective-permute-start | bytes 294920 | tf_op jit(solution)/shard_map/ppermute | solution.py:329
  139.2 6.8 %collective-permute-start.23 = (bf16[128,384]{1,0:T(8,128)(2,1)S(1)}, bf16[128,384]{1,0:T(8,128)(2,1)S(1)}, u32[]{:S(2)}, u32[]{:S(2)}) collective-permute-start(bf16[128,384]{1,0:T(8,128)(2,1)S(1)} %get-tuple-element.87.refs_2_.refs_5_), channel_id=1, source_target_pairs={{1,0},{2,1},{3,2},{4,3},{5,4},{6,5},{7,6},{9,8},{10,9},{11,10},{12... | collective-permute-start | bytes 294920 | tf_op jit(solution)/shard_map/ppermute | solution.py:330
  146.0 20.2 %collective-permute-start.26 = (bf16[768,512]{1,0:T(8,128)(2,1)S(1)}, bf16[768,512]{1,0:T(8,128)(2,1)S(1)}, u32[]{:S(2)}, u32[]{:S(2)}) collective-permute-start(bf16[768,512]{1,0:T(8,128)(2,1)S(1)} %fusion.1.refs_0_), channel_id=1, source_target_pairs={{0,16},{8,24},{16,0},{24,8},{1,17},{9,25},{17,1},{25,9},{2,18},{10... | collective-permute-start | bytes 2359304 | tf_op jit(solution)/shard_map/ppermute | solution.py:322
  147.5 7.0 %copy-start.4 = (bf16[2,384,768]{2,1,0:T(8,128)(2,1)S(1)}, bf16[2,384,768]{2,1,0:T(8,128)(2,1)}, u32[]{:S(2)}) copy-start(bf16[2,384,768]{2,1,0:T(8,128)(2,1)} %constant.100.clone.refs_10_) | copy-start | bytes 3538948
  147.6 7.0 %copy-start.5 = (bf16[2,768,384]{2,1,0:T(8,128)(2,1)S(1)}, bf16[2,768,384]{2,1,0:T(8,128)(2,1)}, u32[]{:S(2)}) copy-start(bf16[2,768,384]{2,1,0:T(8,128)(2,1)} %constant.101.clone.refs_11_) | copy-start | bytes 3538948
  150.0 9.8 %collective-permute-start.24 = (bf16[256,384]{1,0:T(8,128)(2,1)S(1)}, bf16[256,384]{1,0:T(8,128)(2,1)S(1)}, u32[]{:S(2)}, u32[]{:S(2)}) collective-permute-start(bf16[256,384]{1,0:T(8,128)(2,1)S(1)} %get-tuple-element.94.refs_6_), channel_id=1, source_target_pairs={{0,1},{1,2},{2,3},{3,4},{4,5},{5,6},{6,7},{8,9},{9,10},{10,11},{11... | collective-permute-start | bytes 589832 | tf_op jit(solution)/shard_map/ppermute | solution.py:329
  153.3 7.7 %collective-permute-start.25 = (bf16[256,384]{1,0:T(8,128)(2,1)S(1)}, bf16[256,384]{1,0:T(8,128)(2,1)S(1)}, u32[]{:S(2)}, u32[]{:S(2)}) collective-permute-start(bf16[256,384]{1,0:T(8,128)(2,1)S(1)} %get-tuple-element.93.refs_1_.refs_5_), channel_id=1, source_target_pairs={{1,0},{2,1},{3,2},{4,3},{5,4},{6,5},{7,6},{9,8},{10,9},{11,10},{12... | collective-permute-start | bytes 589832 | tf_op jit(solution)/shard_map/ppermute | solution.py:330
  166.3 3.8 %collective-permute-start.27 = (bf16[2,768,384]{2,1,0:T(8,128)(2,1)S(1)}, bf16[2,768,384]{2,1,0:T(8,128)(2,1)S(1)}, u32[]{:S(2)}, u32[]{:S(2)}) collective-permute-start(bf16[2,768,384]{2,1,0:T(8,128)(2,1)S(1)} %get-tuple-element.103), channel_id=1, source_target_pairs={{0,8},{8,0},{16,24},{24,16},{1,9},{9,1},{17,25},{25,17},{2,10},{10... | collective-permute-start | bytes 3538952 | tf_op jit(solution)/shard_map/ppermute | solution.py:322
  166.3 11.1 %collective-permute-start.30 = (bf16[2,768,384]{2,1,0:T(8,128)(2,1)}, bf16[2,768,384]{2,1,0:T(8,128)(2,1)}, u32[]{:S(2)}, u32[]{:S(2)}) collective-permute-start(bf16[2,768,384]{2,1,0:T(8,128)(2,1)} %get-tuple-element.109), channel_id=1, source_target_pairs={{0,8},{8,0},{16,24},{24,16},{1,9},{9,1},{17,25},{25,17},{2,10},{10... | collective-permute-start | bytes 3538952 | tf_op jit(solution)/shard_map/ppermute | solution.py:322
  172.3 40.7 %all-to-all-start.2 = ((bf16[8,96,512]{2,1,0:T(8,128)(2,1)}), bf16[8,96,512]{2,1,0:T(8,128)(2,1)}, u32[]{:S(2)}, u32[]{:S(2)}) async-start(bf16[8,96,512]{2,1,0:T(8,128)(2,1)} %bitcast.49), calls=%async_computation.2 | async-start | bytes 1572864 | tf_op jit(solution)/shard_map/all_to_all | solution.py:344
  178.8 22.5 %collective-permute-start.31 = (bf16[2,4,96,384]{3,2,1,0:T(8,128)(2,1)S(1)}, bf16[2,4,96,384]{3,2,1,0:T(8,128)(2,1)S(1)}, u32[]{:S(2)}, u32[]{:S(2)}) collective-permute-start(bf16[2,4,96,384]{3,2,1,0:T(8,128)(2,1)S(1)} %fusion.3), channel_id=1, source_target_pairs={{0,1},{1,0},{2,3},{3,2},{4,5},{5,4},{6,7},{7,6},{8,9},{9,8},{10,11... | collective-permute-start | bytes 1769480 | tf_op jit(solution)/shard_map/ppermute | solution.py:322
  180.9 22.5 %collective-permute-start.28 = (bf16[768,384]{1,0:T(8,128)(2,1)S(1)}, bf16[768,384]{1,0:T(8,128)(2,1)S(1)}, u32[]{:S(2)}, u32[]{:S(2)}) collective-permute-start(bf16[768,384]{1,0:T(8,128)(2,1)S(1)} %copy-done.34), channel_id=1, source_target_pairs={{0,16},{8,24},{16,0},{24,8},{1,17},{9,25},{17,1},{25,9},{2,18},{10... | collective-permute-start | bytes 1769480 | tf_op jit(solution)/shard_map/ppermute | solution.py:322
  202.7 8.2 %collective-permute-start.32 = (bf16[4,96,384]{2,1,0:T(8,128)(2,1)S(1)}, bf16[4,96,384]{2,1,0:T(8,128)(2,1)S(1)}, u32[]{:S(2)}, u32[]{:S(2)}) collective-permute-start(bf16[4,96,384]{2,1,0:T(8,128)(2,1)S(1)} %get-tuple-element.111), channel_id=1, source_target_pairs={{0,16},{8,24},{16,0},{24,8},{1,17},{9,25},{17,1},{25,9},{2,18},{10... | collective-permute-start | bytes 884744 | tf_op jit(solution)/shard_map/ppermute | solution.py:322
  204.1 7.9 %collective-permute-start.29 = (bf16[4,96,384]{2,1,0:T(8,128)(2,1)S(1)}, bf16[4,96,384]{2,1,0:T(8,128)(2,1)S(1)}, u32[]{:S(2)}, u32[]{:S(2)}) collective-permute-start(bf16[4,96,384]{2,1,0:T(8,128)(2,1)S(1)} %get-tuple-element.107), channel_id=1, source_target_pairs={{0,1},{1,0},{2,3},{3,2},{4,5},{5,4},{6,7},{7,6},{8,9},{9,8},{10,11... | collective-permute-start | bytes 884744 | tf_op jit(solution)/shard_map/ppermute | solution.py:322
  213.0 19.1 %all-to-all-start.3 = ((bf16[4,96,768]{2,1,0:T(8,128)(2,1)}), bf16[4,96,768]{2,1,0:T(8,128)(2,1)S(1)}, u32[]{:S(2)}, u32[]{:S(2)}) async-start(bf16[4,96,768]{2,1,0:T(8,128)(2,1)} %shard_map.143), calls=%async_computation.3 | async-start | bytes 1179648 | tf_op jit(solution)/shard_map/all_to_all | solution.py:414
  (25 other events, 59.9 us)

commit v9 on v6

--- a/solution.py
+++ b/solution.py
@@ -73,8 +73,12 @@
         for n, (k, at) in enumerate(blocks):
             start = pl.multiple_of(starts_ref[k] + at, block)
             copies.append((
-                pltpu.make_async_copy(rows_ref.at[:, pl.ds(start, block)], held_ref.at[n], sems.at[0, n]),
-                pltpu.make_async_copy(weight_refs[k].at[pl.ds(at, block)], piece_ref.at[n], sems.at[1, n]),
+                pltpu.make_async_copy(
+                    rows_ref.at[:, pl.ds(start, block)], held_ref.at[:, pl.ds(n * block, block)], sems.at[0, n]
+                ),
+                pltpu.make_async_copy(
+                    weight_refs[k].at[pl.ds(at, block)], piece_ref.at[pl.ds(n * block, block)], sems.at[1, n]
+                ),
             ))
             for copy in copies[-1]:
                 copy.start()
@@ -89,11 +93,14 @@
         for h in range(2):
             part = slice(h * half, (h + 1) * half)
             sums = 0.0
-            for n in range(len(blocks)):
+            for k in range(count):
                 if h == 0:
-                    for copy in copies[n]:
-                        copy.wait()
-                sums = sums + nn(held_ref[n, part], piece_ref[n])
+                    for n in range(len(blocks)):
+                        if blocks[n][0] == k:
+                            for copy in copies[n]:
+                                copy.wait()
+                span = slice(k * depth, (k + 1) * depth)
+                sums = sums + nn(held_ref[part, span], piece_ref[span])
             out_ref[part] = sums
         for copy in rest:
             copy.wait()
@@ -106,8 +113,8 @@
         in_specs=[SMEM] + [HBM] * (count + 1),
         out_specs=[VMEM] * (1 + spare),
         scratch_shapes=[
-            pltpu.VMEM((len(blocks), row_count, block), BF),
-            pltpu.VMEM((len(blocks), block, columns), BF),
+            pltpu.VMEM((row_count, count * depth), BF),
+            pltpu.VMEM((count * depth, columns), BF),
             pltpu.SemaphoreType.DMA((2, len(blocks))),
             pltpu.SemaphoreType.DMA((spare,)),
         ],
@@ -116,7 +123,7 @@
     )(jnp.stack(starts + later).astype(jnp.int32), rows, *weights)
 
 
-def absorb(total, column, blocks, weights, final):
+def absorb(total, column, blocks, weights, mib):
     count = len(weights)
     row_count = total.shape[0]
     columns = weights[0].shape[1]
@@ -129,10 +136,10 @@
             sums = old_ref[part, column : column + columns]
             for k in range(count):
                 sums = sums + nn(refs[k][part], refs[count + k][...])
-            out_ref[part] = sums.astype(out_ref.dtype)
+            out_ref[part] = sums.astype(BF)
 
     return call(
-        body, (total, *blocks, *weights), [((row_count, columns), BF if final else F32)], 20
+        body, (total, *blocks, *weights), [((row_count, columns), BF)], mib
     )[0]
 
 
@@ -426,10 +433,9 @@
             sums.reshape(groups, block, columns), "seq", split_axis=0, concat_axis=0, tiled=True
         ).reshape(row_count, columns)
 
-    left = send(absorb(total, 0, blocks, weights[0] + weights[1], True))
-    right = absorb(total, columns, blocks[:6], weights[2] + weights[3][:2], False)
+    left = send(absorb(total, 0, blocks, weights[0] + weights[1], 20))
     left, last = lax.optimization_barrier((left, weights[3][2]))
-    right = send(absorb(right, 0, blocks[6:], [last, weights[3][3]], True))
+    right = send(absorb(total, columns, blocks, weights[2] + weights[3][:2] + [last, weights[3][3]], 60))
 
     column = lax.dynamic_index_in_dim(layout[0], device, axis=1, keepdims=True)
     position = column * block + jnp.arange(block, dtype=jnp.int32)[None, :]

time: 220 us -> 213 us (0.968)
  local copies, waits for them, and re-layouts: 20.4 us -> 11.4 us
    unnamed x68 -> x66, local copies, waits for them, and re-layouts: 14.1 us -> 5.86 us
    pallas_call x12 -> x11, Pallas kernels: 31 us -> 33 us  [call(): pl.pallas_call(body, out_shape=outs, in_specs=[SMEM] * smem + [ANY] * aft...]
  transfers between devices with their start and end apart: 37 -> 37, of which waited for: 16 -> 17; matrix products, arithmetic and copies ran while one was open for 7% -> 7% of each run, Pallas kernels for 14% -> 13%
where the time goes in v9:
time: 213 us; the launch traced here: 212 us
  waiting for transfers between devices  84.1 us (39%)
  starting transfers between devices  62.3 us (29%)
  Pallas kernels  43.4 us (20%)
  local copies, waits for them, and re-layouts  11.4 us (5%)
  other arithmetic  9.31 us (4%)
    ppermute x25, waiting for transfers between devices, swap(): return lax.ppermute(value, axis, [(i, i ^ bit) for i in range(size)])  42.9 us
    pallas_call x11, Pallas kernels, call(): pl.pallas_call(body, out_shape=outs, in_specs=[SMEM] * smem + [ANY] * aft...  33 us
    ppermute x25, starting transfers between devices, swap(): return lax.ppermute(value, axis, [(i, i ^ bit) for i in range(size)])  20.7 us
    ppermute x4, starting transfers between devices, halo(): lax.ppermute(high, 'seq', up)  15 us
    all_to_all x2, waiting for transfers between devices, send(): lax.all_to_all(sums.reshape(groups, block, columns), 'seq', split_axis=0,...  11.9 us
    all_to_all x2, starting transfers between devices, send(): lax.all_to_all(sums.reshape(groups, block, columns), 'seq', split_axis=0,...  11.8 us
    all_to_all x1, waiting for transfers between devices, crossed_sums(): lax.all_to_all(both, 'seq', split_axis=0, concat_axis=0, axis_index_group...  11.7 us
    ppermute x4, waiting for transfers between devices, halo(): lax.ppermute(low, 'seq', [(j, i) for i, j in up])  10.6 us
  transfers between devices with their start and end apart: 37, of which 17 were waited for; matrix products, arithmetic and copies ran while one was open for 7% of the time, Pallas kernels for 13%

profile of v9, /device:TPU:0, one launch (start us, length us, event | category | flops | bytes accessed | tf_op | source)
XLA Modules:
  0.0 212.2 jit_solution(677116403670195223)
XLA Ops:
  1.1 1.5 fusion.9
  2.7 2.6 %collective-permute-start.5 = (bf16[512,384]{1,0:T(8,128)(2,1)S(1)}, bf16[512,384]{1,0:T(8,128)(2,1)S(1)}, u32[]{:S(2)}, u32[]{:S(2)}) collective-permute-start(bf16[512,384]{1,0:T(8,128)(2,1)S(1)} %get-tuple-element.116), channel_id=1, source_target_pairs={{0,16},{8,24},{16,0},{24,8},{1,17},{9,25},{17,1},{25,9},{2,18},{10... | collective-permute-start | bytes 1179656 | tf_op jit(solution)/shard_map/ppermute | solution.py:329
  5.4 1.9 collective-permute-start.9
  7.4 7.9 %collective-permute-done.5.refs_12_ = bf16[512,384]{1,0:T(8,128)(2,1)S(1)} collective-permute-done((bf16[512,384]{1,0:T(8,128)(2,1)S(1)}, bf16[512,384]{1,0:T(8,128)(2,1)S(1)}, u32[]{:S(2)}, u32[]{:S(2)}) %collective-permute-start.5) | collective-permute-done | bytes 393248 | tf_op jit(solution)/shard_map/ppermute | solution.py:329
  15.2 2.0 collective-permute-start.7
  17.2 10.3 %shard_map.129 = (f32[512,768]{1,0:T(8,128)}, bf16[512,512]{1,0:T(8,128)(2,1)S(1)}, bf16[512,512]{1,0:T(8,128)(2,1)S(1)}, bf16[512,512]{1,0:T(8,128)(2,1)S(1)}, ...) custom-call(s32[10]{0:T(128)S(1)} %stack.60.starts_ref, ...), custom_call_target="tpu_custom_call" | custom-call | flops 1024 | bytes 1024 | tf_op jit(solution)/shard_map/pallas_call | solution.py:110
  27.7 1.9 collective-permute-start.11
  30.2 1.9 collective-permute-done.9.refs_12_
  32.1 5.6 %collective-permute-done.3.refs_10_ = bf16[512,384]{1,0:T(8,128)(2,1)S(1)} collective-permute-done((bf16[512,384]{1,0:T(8,128)(2,1)S(1)}, bf16[512,384]{1,0:T(8,128)(2,1)S(1)}, u32[]{:S(2)}, u32[]{:S(2)}) %collective-permute-start.3) | collective-permute-done | bytes 393248 | tf_op jit(solution)/shard_map/ppermute | solution.py:329
  37.7 2.6 %collective-permute-done.11.refs_8_ = bf16[512,384]{1,0:T(8,128)(2,1)S(1)} collective-permute-done((bf16[512,384]{1,0:T(8,128)(2,1)S(1)}, bf16[512,384]{1,0:T(8,128)(2,1)S(1)}, u32[]{:S(2)}, u32[]{:S(2)}) %collective-permute-start.11) | collective-permute-done | bytes 393248 | tf_op jit(solution)/shard_map/ppermute | solution.py:329
  40.3 1.8 collective-permute-start.13
  42.3 1.4 copy-done.2
  43.7 3.1 %shard_map.130 = bf16[512,384]{1,0:T(8,128)(2,1)} custom-call(f32[512,768]{1,0:T(8,128)S(1)} %copy-done.2, bf16[512,512]{1,0:T(8,128)(2,1)S(1)} %get-tuple-element.61.refs_0_, bf16[512,512]{1,0:T(8,128)(2,1)S(1)} %get-tuple-element.62.refs_1_, bf16[512,512]{1,0:T(8,128)(2,1)S(1)} %get-tuple-element.63.refs_2_, ...), custom_call_target="tpu_custom_call" | custom-call | flops 1024 | bytes 1024 | tf_op jit(solution)/shard_map/pallas_call | solution.py:52
  46.9 6.1 %all-to-all-start = ((bf16[8,64,384]{2,1,0:T(8,128)(2,1)}), bf16[8,64,384]{2,1,0:T(8,128)(2,1)S(1)}, u32[]{:S(2)}, u32[]{:S(2)}) async-start(bf16[8,64,384]{2,1,0:T(8,128)(2,1)} %bitcast.14), calls=%async_computation | async-start | bytes 786432 | tf_op jit(solution)/shard_map/all_to_all | solution.py:432
  53.7 9.3 %collective-permute-done.10.refs_14_ = bf16[512,384]{1,0:T(8,128)(2,1)S(1)} collective-permute-done((bf16[512,384]{1,0:T(8,128)(2,1)S(1)}, bf16[512,384]{1,0:T(8,128)(2,1)S(1)}, u32[]{:S(2)}, u32[]{:S(2)}) %collective-permute-start.10) | collective-permute-done | bytes 393248 | tf_op jit(solution)/shard_map/ppermute | solution.py:329
  66.4 6.8 %shard_map.131 = bf16[512,384]{1,0:T(8,128)(2,1)} custom-call(f32[512,768]{1,0:T(8,128)} %get-tuple-element.60.old_ref, bf16[512,512]{1,0:T(8,128)(2,1)} %copy-done.6, bf16[512,512]{1,0:T(8,128)(2,1)} %copy-done.7, bf16[512,512]{1,0:T(8,128)(2,1)} %copy-done.8, bf16[512,512]{1,0:T(8,128)(2,1)} %copy-done.9, bf16[512,512]{1,0:T(8,128)(2,1)} %copy-done.10, ...), custom_call_target="tpu_custom_call" | custom-call | flops 1024 | bytes 1024 | tf_op jit(solution)/shard_map/pallas_call | solution.py:52
  73.2 5.7 %all-to-all-start.1 = ((bf16[8,64,384]{2,1,0:T(8,128)(2,1)}), bf16[8,64,384]{2,1,0:T(8,128)(2,1)}, u32[]{:S(2)}, u32[]{:S(2)}) async-start(bf16[8,64,384]{2,1,0:T(8,128)(2,1)} %bitcast.93), calls=%async_computation.1 | async-start | bytes 786432 | tf_op jit(solution)/shard_map/all_to_all | solution.py:432
  80.0 10.9 %all-to-all-done.1 = bf16[8,64,384]{2,1,0:T(8,128)(2,1)} async-done(((bf16[8,64,384]{2,1,0:T(8,128)(2,1)}), bf16[8,64,384]{2,1,0:T(8,128)(2,1)}, u32[]{:S(2)}, u32[]{:S(2)}) %all-to-all-start.1) | async-done | bytes 393248 | tf_op jit(solution)/shard_map/all_to_all | solution.py:432
  91.9 2.1 %shard_map.132 = (bf16[512,768]{1,0:T(8,128)(2,1)S(1)}, bf16[256,768]{1,0:T(8,128)(2,1)S(1)}, bf16[256,768]{1,0:T(8,128)(2,1)S(1)}, bf16[256,384]{1,0:T(8,128)(2,1)S(1)}, bf16[256,384]{1,0:T(8,128)(2,1)S(1)}) custom-call(s32[1,512]{1,0:T(1,128)S(1)} %compare_select_fusion.target_ref, bf16[512,384]{1,0:T(8,128)(2,1)S(1)} %bitcast.86, ...), custom_call_target="tpu_custom_call" | custom-call | flops 1024 | bytes 1024 | tf_op jit(solution)/shard_map/pallas_call | solution.py:52
  94.0 3.4 %collective-permute-start.17 = (bf16[256,384]{1,0:T(8,128)(2,1)S(1)}, bf16[256,384]{1,0:T(8,128)(2,1)S(1)}, u32[]{:S(2)}, u32[]{:S(2)}) collective-permute-start(bf16[256,384]{1,0:T(8,128)(2,1)S(1)} %get-tuple-element.72), channel_id=1, source_target_pairs={{0,1},{1,2},{2,3},{3,4},{4,5},{5,6},{6,7},{8,9},{9,10},{10,11},{11... | collective-permute-start | bytes 589832 | tf_op jit(solution)/shard_map/ppermute | solution.py:336
  97.4 1.5 collective-permute-start.18
  99.9 5.1 %collective-permute-done.17.prev_ref = bf16[256,384]{1,0:T(8,128)(2,1)S(1)} collective-permute-done((bf16[256,384]{1,0:T(8,128)(2,1)S(1)}, bf16[256,384]{1,0:T(8,128)(2,1)S(1)}, u32[]{:S(2)}, u32[]{:S(2)}) %collective-permute-start.17) | collective-permute-done | bytes 196640 | tf_op jit(solution)/shard_map/ppermute | solution.py:336
  105.9 4.5 %collective-permute-start.19 = (bf16[128,384]{1,0:T(8,128)(2,1)S(1)}, bf16[128,384]{1,0:T(8,128)(2,1)S(1)}, u32[]{:S(2)}, u32[]{:S(2)}) collective-permute-start(bf16[128,384]{1,0:T(8,128)(2,1)S(1)} %get-tuple-element.77), channel_id=1, source_target_pairs={{0,1},{1,2},{2,3},{3,4},{4,5},{5,6},{6,7},{8,9},{9,10},{10,11},{11... | collective-permute-start | bytes 294920 | tf_op jit(solution)/shard_map/ppermute | solution.py:336
  110.4 1.3 collective-permute-start.20
  112.6 4.3 %collective-permute-done.20.refs_4_ = bf16[128,384]{1,0:T(8,128)(2,1)S(1)} collective-permute-done((bf16[128,384]{1,0:T(8,128)(2,1)S(1)}, bf16[128,384]{1,0:T(8,128)(2,1)S(1)}, u32[]{:S(2)}, u32[]{:S(2)}) %collective-permute-start.20) | collective-permute-done | bytes 98336 | tf_op jit(solution)/shard_map/ppermute | solution.py:337
  116.9 3.7 %shard_map.135 = (bf16[256,384]{1,0:T(8,128)(2,1)S(1)}, bf16[128,768]{1,0:T(8,128)(2,1)S(1)}, bf16[128,2048]{1,0:T(8,128)(2,1)S(1)}, bf16[128,768]{1,0:T(8,128)(...) custom-call(s32[2]{0:T(128)S(1)} %get-tuple-element.123.refs_0_, ...), custom_call_target="tpu_custom_call" | custom-call | flops 1024 | bytes 1024 | tf_op jit(solution)/shard_map/pallas_call | solution.py:52
  120.7 1.5 shard_map.136
  122.3 4.0 %collective-permute-start.22 = (bf16[128,384]{1,0:T(8,128)(2,1)S(1)}, bf16[128,384]{1,0:T(8,128)(2,1)S(1)}, u32[]{:S(2)}, u32[]{:S(2)}) collective-permute-start(bf16[128,384]{1,0:T(8,128)(2,1)S(1)} %get-tuple-element.86.refs_3_.refs_6_), channel_id=1, source_target_pairs={{0,1},{1,2},{2,3},{3,4},{4,5},{5,6},{6,7},{8,9},{9,10},{10,11},{11... | collective-permute-start | bytes 294920 | tf_op jit(solution)/shard_map/ppermute | solution.py:336
  126.3 1.3 collective-permute-start.23
  128.9 4.1 %collective-permute-done.23.refs_4_.refs_7_ = bf16[128,384]{1,0:T(8,128)(2,1)S(1)} collective-permute-done((bf16[128,384]{1,0:T(8,128)(2,1)S(1)}, bf16[128,384]{1,0:T(8,128)(2,1)S(1)}, u32[]{:S(2)}, u32[]{:S(2)}) %collective-permute-start.23) | collective-permute-done | bytes 98336 | tf_op jit(solution)/shard_map/ppermute | solution.py:337
  133.1 1.5 collective-permute-start.26
  134.6 2.5 %shard_map.137 = (f32[256,768]{1,0:T(8,128)}, bf16[256,768]{1,0:T(8,128)(2,1)S(1)}, bf16[256,384]{1,0:T(8,128)(2,1)S(1)}, bf16[256,384]{1,0:T(8,128)(2,1)S(1)}) custom-call(bf16[768,512]{1,0:T(8,128)(2,1)S(1)} %fusion.1.refs_0_, bf16[128,384]{1,0:T(8,128)(2,1)S(1)} %collective-permute-done.22.refs_1_.refs_4_, ...), custom_call_target="tpu_custom_call" | custom-call | flops 1024 | bytes 1024 | tf_op jit(solution)/shard_map/pallas_call | solution.py:52
  137.0 3.1 %collective-permute-start.24 = (bf16[256,384]{1,0:T(8,128)(2,1)S(1)}, bf16[256,384]{1,0:T(8,128)(2,1)S(1)}, u32[]{:S(2)}, u32[]{:S(2)}) collective-permute-start(bf16[256,384]{1,0:T(8,128)(2,1)S(1)} %get-tuple-element.94.refs_6_), channel_id=1, source_target_pairs={{0,1},{1,2},{2,3},{3,4},{4,5},{5,6},{6,7},{8,9},{9,10},{10,11},{11... | collective-permute-start | bytes 589832 | tf_op jit(solution)/shard_map/ppermute | solution.py:336
  140.2 1.3 collective-permute-start.25
  141.5 4.2 %shard_map.138 = (bf16[2,768,384]{2,1,0:T(8,128)(2,1)S(1)}, bf16[2,768,384]{2,1,0:T(8,128)(2,1)S(1)}) custom-call(s32[2]{0:T(128)S(1)} %get-tuple-element.122.ids_ref.refs_0_, bf16[256,384]{1,0:T(8,128)(2,1)S(1)} %get-tuple-element.93.refs_1_.refs_5_, bf16[128,768]{1,0:T(8,128)(2,1)S(1)} %get-tuple-element.78.refs_2_, ...), custom_call_target="tpu_custom_call" | custom-call | flops 1024 | bytes 1024 | tf_op jit(solution)/shard_map/pallas_call | solution.py:52
  145.7 2.1 %collective-permute-done.25.refs_7_ = bf16[256,384]{1,0:T(8,128)(2,1)S(1)} collective-permute-done((bf16[256,384]{1,0:T(8,128)(2,1)S(1)}, bf16[256,384]{1,0:T(8,128)(2,1)S(1)}, u32[]{:S(2)}, u32[]{:S(2)}) %collective-permute-start.25) | collective-permute-done | bytes 196640 | tf_op jit(solution)/shard_map/ppermute | solution.py:337
  147.9 6.3 %shard_map.139 = (bf16[2,768,384]{2,1,0:T(8,128)(2,1)S(1)}, bf16[2,768,384]{2,1,0:T(8,128)(2,1)}) custom-call(s32[2]{0:T(128)S(1)} %get-tuple-element.122.ids_ref.refs_0_, bf16[256,384]{1,0:T(8,128)(2,1)S(1)} %get-tuple-element.93.refs_1_.refs_5_, bf16[256,768]{1,0:T(8,128)(2,1)S(1)} %get-tuple-element.74.low_ref.refs_2_, ...), custom_call_target="tpu_custom_call" | custom-call | flops 1024 | bytes 1024 | tf_op jit(solution)/shard_map/pallas_call | solution.py:52
  156.9 2.1 %fusion.3 = bf16[2,4,96,384]{3,2,1,0:T(8,128)(2,1)} fusion(bf16[2,4,2,96,384]{4,3,2,1,0:T(8,128)(2,1)} %bitcast.30, s32[]{:T(128)S(6)} %select_n.100, bf16[2,4,2,96,384]{4,3,2,1,0:T(8,128)(2,1)S(1)} %bitcast.85), kind=kLoop, calls=%fused_computation.8 | loop fusion | flops 1179648 | bytes 1769476 | tf_op jit(solution)/shard_map/convert_element_type | solution.py:372
  159.0 2.6 %collective-permute-start.31 = (bf16[2,4,96,384]{3,2,1,0:T(8,128)(2,1)}, bf16[2,4,96,384]{3,2,1,0:T(8,128)(2,1)S(1)}, u32[]{:S(2)}, u32[]{:S(2)}) collective-permute-start(bf16[2,4,96,384]{3,2,1,0:T(8,128)(2,1)} %fusion.3), channel_id=1, source_target_pairs={{0,1},{1,0},{2,3},{3,2},{4,5},{5,4},{6,7},{7,6},{8,9},{9,8},{10,11... | collective-permute-start | bytes 1769480 | tf_op jit(solution)/shard_map/ppermute | solution.py:329
  163.4 1.3 fusion
  164.7 4.1 %all-to-all-start.2 = ((bf16[8,96,512]{2,1,0:T(8,128)(2,1)}), bf16[8,96,512]{2,1,0:T(8,128)(2,1)S(1)}, u32[]{:S(2)}, u32[]{:S(2)}) async-start(bf16[8,96,512]{2,1,0:T(8,128)(2,1)} %bitcast.38), calls=%async_computation.2 | async-start | bytes 1572864 | tf_op jit(solution)/shard_map/all_to_all | solution.py:351
  168.8 1.4 fusion.11
  170.3 10.6 %collective-permute-done.31 = bf16[2,4,96,384]{3,2,1,0:T(8,128)(2,1)S(1)} collective-permute-done((bf16[2,4,96,384]{3,2,1,0:T(8,128)(2,1)}, bf16[2,4,96,384]{3,2,1,0:T(8,128)(2,1)S(1)}, u32[]{:S(2)}, u32[]{:S(2)}) %collective-permute-start.31) | collective-permute-done | bytes 589856 | tf_op jit(solution)/shard_map/ppermute | solution.py:329
  184.0 2.4 %collective-permute-start.29 = (bf16[4,96,384]{2,1,0:T(8,128)(2,1)S(1)}, bf16[4,96,384]{2,1,0:T(8,128)(2,1)S(1)}, u32[]{:S(2)}, u32[]{:S(2)}) collective-permute-start(bf16[4,96,384]{2,1,0:T(8,128)(2,1)S(1)} %fusion.8), channel_id=1, source_target_pairs={{0,1},{1,0},{2,3},{3,2},{4,5},{5,4},{6,7},{7,6},{8,9},{9,8},{10,11... | collective-permute-start | bytes 884744 | tf_op jit(solution)/shard_map/ppermute | solution.py:329
  186.4 1.5 collective-permute-done.32
  188.1 3.4 %collective-permute-done.29 = bf16[4,96,384]{2,1,0:T(8,128)(2,1)S(1)} collective-permute-done((bf16[4,96,384]{2,1,0:T(8,128)(2,1)S(1)}, bf16[4,96,384]{2,1,0:T(8,128)(2,1)S(1)}, u32[]{:S(2)}, u32[]{:S(2)}) %collective-permute-start.29) | collective-permute-done | bytes 294944 | tf_op jit(solution)/shard_map/ppermute | solution.py:329
  193.5 5.3 %all-to-all-start.3 = ((bf16[4,96,768]{2,1,0:T(8,128)(2,1)}), bf16[4,96,768]{2,1,0:T(8,128)(2,1)S(1)}, u32[]{:S(2)}, u32[]{:S(2)}) async-start(bf16[4,96,768]{2,1,0:T(8,128)(2,1)} %pad_maximum_fusion), calls=%async_computation.3 | async-start | bytes 1179648 | tf_op jit(solution)/shard_map/all_to_all | solution.py:388
  199.6 11.7 %all-to-all-done.3.parts_ref = bf16[4,96,768]{2,1,0:T(8,128)(2,1)S(1)} async-done(((bf16[4,96,768]{2,1,0:T(8,128)(2,1)}), bf16[4,96,768]{2,1,0:T(8,128)(2,1)S(1)}, u32[]{:S(2)}, u32[]{:S(2)}) %all-to-all-start.3) | async-done | bytes 589856 | tf_op jit(solution)/shard_map/all_to_all | solution.py:388
  (125 shorter events, 22.7 us)
Async XLA Ops:
  0.6 16.6 %collective-permute-start.1 = (bf16[2048,768]{1,0:T(8,128)(2,1)}, bf16[2048,768]{1,0:T(8,128)(2,1)}, u32[]{:S(2)}, u32[]{:S(2)}) collective-permute-start(bf16[2048,768]{1,0:T(8,128)(2,1)} %refs_0_.1), channel_id=1, source_target_pairs={{0,8},{8,0},{16,24},{24,16},{1,9},{9,1},{17,25},{25,17},{2,10},{10... | collective-permute-start | bytes 9437192 | tf_op jit(solution)/shard_map/ppermute | solution.py:329
  2.7 12.6 %collective-permute-start.5 = (bf16[512,384]{1,0:T(8,128)(2,1)S(1)}, bf16[512,384]{1,0:T(8,128)(2,1)S(1)}, u32[]{:S(2)}, u32[]{:S(2)}) collective-permute-start(bf16[512,384]{1,0:T(8,128)(2,1)S(1)} %get-tuple-element.116), channel_id=1, source_target_pairs={{0,16},{8,24},{16,0},{24,8},{1,17},{9,25},{17,1},{25,9},{2,18},{10... | collective-permute-start | bytes 1179656 | tf_op jit(solution)/shard_map/ppermute | solution.py:329
  5.3 22.4 %collective-permute-start = (bf16[512,384]{1,0:T(8,128)(2,1)S(1)}, bf16[512,384]{1,0:T(8,128)(2,1)S(1)}, u32[]{:S(2)}, u32[]{:S(2)}) collective-permute-start(bf16[512,384]{1,0:T(8,128)(2,1)S(1)} %get-tuple-element.117), channel_id=1, source_target_pairs={{0,16},{8,24},{16,0},{24,8},{1,17},{9,25},{17,1},{25,9},{2,18},{10... | collective-permute-start | bytes 1179656 | tf_op jit(solution)/shard_map/ppermute | solution.py:329
  5.4 26.7 %collective-permute-start.9 = (bf16[512,384]{1,0:T(8,128)(2,1)S(1)}, bf16[512,384]{1,0:T(8,128)(2,1)S(1)}, u32[]{:S(2)}, u32[]{:S(2)}) collective-permute-start(bf16[512,384]{1,0:T(8,128)(2,1)S(1)} %get-tuple-element.115), channel_id=1, source_target_pairs={{0,16},{8,24},{16,0},{24,8},{1,17},{9,25},{17,1},{25,9},{2,18},{10... | collective-permute-start | bytes 1179656 | tf_op jit(solution)/shard_map/ppermute | solution.py:329
  15.2 14.5 %collective-permute-start.7 = (bf16[512,384]{1,0:T(8,128)(2,1)S(1)}, bf16[512,384]{1,0:T(8,128)(2,1)S(1)}, u32[]{:S(2)}, u32[]{:S(2)}) collective-permute-start(bf16[512,384]{1,0:T(8,128)(2,1)S(1)} %collective-permute-done.5.refs_12_), channel_id=1, source_target_pairs={{0,1},{1,0},{2,3},{3,2},{4,5},{5,4},{6,7},{7,6},{8,9},{9,8},{10,11... | collective-permute-start | bytes 1179656 | tf_op jit(solution)/shard_map/ppermute | solution.py:329
  27.5 19.3 %copy-start.6 = (bf16[512,512]{1,0:T(8,128)(2,1)}, bf16[512,512]{1,0:T(8,128)(2,1)S(1)}, u32[]{:S(2)}) copy-start(bf16[512,512]{1,0:T(8,128)(2,1)S(1)} %get-tuple-element.61.refs_0_) | copy-start | bytes 1572868
  27.5 19.3 %copy-start.7 = (bf16[512,512]{1,0:T(8,128)(2,1)}, bf16[512,512]{1,0:T(8,128)(2,1)S(1)}, u32[]{:S(2)}) copy-start(bf16[512,512]{1,0:T(8,128)(2,1)S(1)} %get-tuple-element.62.refs_1_) | copy-start | bytes 1572868
  27.6 19.3 %copy-start.8 = (bf16[512,512]{1,0:T(8,128)(2,1)}, bf16[512,512]{1,0:T(8,128)(2,1)S(1)}, u32[]{:S(2)}) copy-start(bf16[512,512]{1,0:T(8,128)(2,1)S(1)} %get-tuple-element.63.refs_2_) | copy-start | bytes 1572868
  27.6 19.3 %copy-start.9 = (bf16[512,512]{1,0:T(8,128)(2,1)}, bf16[512,512]{1,0:T(8,128)(2,1)S(1)}, u32[]{:S(2)}) copy-start(bf16[512,512]{1,0:T(8,128)(2,1)S(1)} %get-tuple-element.64.refs_3_) | copy-start | bytes 1572868
  27.6 19.3 %copy-start.10 = (bf16[512,512]{1,0:T(8,128)(2,1)}, bf16[512,512]{1,0:T(8,128)(2,1)S(1)}, u32[]{:S(2)}) copy-start(bf16[512,512]{1,0:T(8,128)(2,1)S(1)} %get-tuple-element.65.refs_4_) | copy-start | bytes 1572868
  27.6 19.3 %copy-start.11 = (bf16[512,512]{1,0:T(8,128)(2,1)}, bf16[512,512]{1,0:T(8,128)(2,1)S(1)}, u32[]{:S(2)}) copy-start(bf16[512,512]{1,0:T(8,128)(2,1)S(1)} %get-tuple-element.66.refs_5_) | copy-start | bytes 1572868
  27.6 19.3 %copy-start.12 = (bf16[512,512]{1,0:T(8,128)(2,1)}, bf16[512,512]{1,0:T(8,128)(2,1)S(1)}, u32[]{:S(2)}) copy-start(bf16[512,512]{1,0:T(8,128)(2,1)S(1)} %get-tuple-element.67.refs_6_) | copy-start | bytes 1572868
  27.6 19.3 %copy-start.13 = (bf16[512,512]{1,0:T(8,128)(2,1)}, bf16[512,512]{1,0:T(8,128)(2,1)S(1)}, u32[]{:S(2)}) copy-start(bf16[512,512]{1,0:T(8,128)(2,1)S(1)} %get-tuple-element.68.refs_7_) | copy-start | bytes 1572868
  27.6 10.0 %collective-permute-start.3 = (bf16[512,384]{1,0:T(8,128)(2,1)S(1)}, bf16[512,384]{1,0:T(8,128)(2,1)S(1)}, u32[]{:S(2)}, u32[]{:S(2)}) collective-permute-start(bf16[512,384]{1,0:T(8,128)(2,1)S(1)} %collective-permute-done.refs_8_), channel_id=1, source_target_pairs={{0,1},{1,0},{2,3},{3,2},{4,5},{5,4},{6,7},{7,6},{8,9},{9,8},{10,11... | collective-permute-start | bytes 1179656 | tf_op jit(solution)/shard_map/ppermute | solution.py:329
  27.7 12.5 %collective-permute-start.11 = (bf16[512,384]{1,0:T(8,128)(2,1)S(1)}, bf16[512,384]{1,0:T(8,128)(2,1)S(1)}, u32[]{:S(2)}, u32[]{:S(2)}) collective-permute-start(bf16[512,384]{1,0:T(8,128)(2,1)S(1)} %get-tuple-element.114), channel_id=1, source_target_pairs={{0,16},{8,24},{16,0},{24,8},{1,17},{9,25},{17,1},{25,9},{2,18},{10... | collective-permute-start | bytes 1179656 | tf_op jit(solution)/shard_map/ppermute | solution.py:329
  29.7 12.4 %collective-permute-start.6 = (bf16[512,384]{1,0:T(8,128)(2,1)S(1)}, bf16[512,384]{1,0:T(8,128)(2,1)S(1)}, u32[]{:S(2)}, u32[]{:S(2)}) collective-permute-start(bf16[512,384]{1,0:T(8,128)(2,1)S(1)} %collective-permute-done.5.refs_12_), channel_id=1, source_target_pairs={{0,8},{8,0},{16,24},{24,16},{1,9},{9,1},{17,25},{25,17},{2,10},{10... | collective-permute-start | bytes 1179656 | tf_op jit(solution)/shard_map/ppermute | solution.py:329
  29.7 12.6 %collective-permute-start.8 = (bf16[512,384]{1,0:T(8,128)(2,1)S(1)}, bf16[512,384]{1,0:T(8,128)(2,1)S(1)}, u32[]{:S(2)}, u32[]{:S(2)}) collective-permute-start(bf16[512,384]{1,0:T(8,128)(2,1)S(1)} %collective-permute-done.7.refs_14_), channel_id=1, source_target_pairs={{0,8},{8,0},{16,24},{24,16},{1,9},{9,1},{17,25},{25,17},{2,10},{10... | collective-permute-start | bytes 1179656 | tf_op jit(solution)/shard_map/ppermute | solution.py:329
  32.1 21.0 %copy-start.25 = (bf16[512,384]{1,0:T(8,128)(2,1)}, bf16[512,384]{1,0:T(8,128)(2,1)S(1)}, u32[]{:S(2)}) copy-start(bf16[512,384]{1,0:T(8,128)(2,1)S(1)} %collective-permute-done.9.refs_12_) | copy-start | bytes 1179652
  32.1 10.2 %collective-permute-start.2 = (bf16[512,384]{1,0:T(8,128)(2,1)S(1)}, bf16[512,384]{1,0:T(8,128)(2,1)S(1)}, u32[]{:S(2)}, u32[]{:S(2)}) collective-permute-start(bf16[512,384]{1,0:T(8,128)(2,1)S(1)} %collective-permute-done.refs_8_), channel_id=1, source_target_pairs={{0,8},{8,0},{16,24},{24,16},{1,9},{9,1},{17,25},{25,17},{2,10},{10... | collective-permute-start | bytes 1179656 | tf_op jit(solution)/shard_map/ppermute | solution.py:329
  37.7 4.6 %collective-permute-start.4 = (bf16[512,384]{1,0:T(8,128)(2,1)S(1)}, bf16[512,384]{1,0:T(8,128)(2,1)S(1)}, u32[]{:S(2)}, u32[]{:S(2)}) collective-permute-start(bf16[512,384]{1,0:T(8,128)(2,1)S(1)} %collective-permute-done.3.refs_10_), channel_id=1, source_target_pairs={{0,8},{8,0},{16,24},{24,16},{1,9},{9,1},{17,25},{25,17},{2,10},{10... | collective-permute-start | bytes 1179656 | tf_op jit(solution)/shard_map/ppermute | solution.py:329
  40.3 13.3 %collective-permute-start.13 = (bf16[512,384]{1,0:T(8,128)(2,1)S(1)}, bf16[512,384]{1,0:T(8,128)(2,1)S(1)}, u32[]{:S(2)}, u32[]{:S(2)}) collective-permute-start(bf16[512,384]{1,0:T(8,128)(2,1)S(1)} %collective-permute-done.11.refs_8_), channel_id=1, source_target_pairs={{0,1},{1,0},{2,3},{3,2},{4,5},{5,4},{6,7},{7,6},{8,9},{9,8},{10,11... | collective-permute-start | bytes 1179656 | tf_op jit(solution)/shard_map/ppermute | solution.py:329
  42.1 20.9 %collective-permute-start.10 = (bf16[512,384]{1,0:T(8,128)(2,1)S(1)}, bf16[512,384]{1,0:T(8,128)(2,1)S(1)}, u32[]{:S(2)}, u32[]{:S(2)}) collective-permute-start(bf16[512,384]{1,0:T(8,128)(2,1)S(1)} %collective-permute-done.9.refs_12_), channel_id=1, source_target_pairs={{0,1},{1,0},{2,3},{3,2},{4,5},{5,4},{6,7},{7,6},{8,9},{9,8},{10,11... | collective-permute-start | bytes 1179656 | tf_op jit(solution)/shard_map/ppermute | solution.py:329
  46.9 17.1 %all-to-all-start = ((bf16[8,64,384]{2,1,0:T(8,128)(2,1)}), bf16[8,64,384]{2,1,0:T(8,128)(2,1)S(1)}, u32[]{:S(2)}, u32[]{:S(2)}) async-start(bf16[8,64,384]{2,1,0:T(8,128)(2,1)} %bitcast.14), calls=%async_computation | async-start | bytes 786432 | tf_op jit(solution)/shard_map/all_to_all | solution.py:432
  53.0 11.7 %collective-permute-start.12 = (bf16[512,384]{1,0:T(8,128)(2,1)S(1)}, bf16[512,384]{1,0:T(8,128)(2,1)S(1)}, u32[]{:S(2)}, u32[]{:S(2)}) collective-permute-start(bf16[512,384]{1,0:T(8,128)(2,1)S(1)} %collective-permute-done.11.refs_8_), channel_id=1, source_target_pairs={{0,8},{8,0},{16,24},{24,16},{1,9},{9,1},{17,25},{25,17},{2,10},{10... | collective-permute-start | bytes 1179656 | tf_op jit(solution)/shard_map/ppermute | solution.py:329
  53.1 11.7 %collective-permute-start.15 = (bf16[512,384]{1,0:T(8,128)(2,1)S(1)}, bf16[512,384]{1,0:T(8,128)(2,1)S(1)}, u32[]{:S(2)}, u32[]{:S(2)}) collective-permute-start(bf16[512,384]{1,0:T(8,128)(2,1)S(1)} %collective-permute-done.9.refs_12_), channel_id=1, source_target_pairs={{0,8},{8,0},{16,24},{24,16},{1,9},{9,1},{17,25},{25,17},{2,10},{10... | collective-permute-start | bytes 1179656 | tf_op jit(solution)/shard_map/ppermute | solution.py:329
  53.6 11.2 %collective-permute-start.14 = (bf16[512,384]{1,0:T(8,128)(2,1)S(1)}, bf16[512,384]{1,0:T(8,128)(2,1)S(1)}, u32[]{:S(2)}, u32[]{:S(2)}) collective-permute-start(bf16[512,384]{1,0:T(8,128)(2,1)S(1)} %collective-permute-done.13.refs_10_), channel_id=1, source_target_pairs={{0,8},{8,0},{16,24},{24,16},{1,9},{9,1},{17,25},{25,17},{2,10},{10... | collective-permute-start | bytes 1179656 | tf_op jit(solution)/shard_map/ppermute | solution.py:329
  63.0 3.4 %collective-permute-start.16 = (bf16[512,384]{1,0:T(8,128)(2,1)S(1)}, bf16[512,384]{1,0:T(8,128)(2,1)}, u32[]{:S(2)}, u32[]{:S(2)}) collective-permute-start(bf16[512,384]{1,0:T(8,128)(2,1)S(1)} %collective-permute-done.10.refs_14_), channel_id=1, source_target_pairs={{0,8},{8,0},{16,24},{24,16},{1,9},{9,1},{17,25},{25,17},{2,10},{10... | collective-permute-start | bytes 1179656 | tf_op jit(solution)/shard_map/ppermute | solution.py:329
  64.7 14.8 %copy-start.32 = (s32[1,8,8]{2,1,0:T(8,128)S(1)}, s32[1,8,8]{2,1,0:T(8,128)}, u32[]{:S(2)}) copy-start(s32[1,8,8]{2,1,0:T(8,128)} %param.11) | copy-start | bytes 772
  66.4 24.5 %copy-start = (bf16[2,3,768,384]{3,2,1,0:T(8,128)(2,1)S(1)}, bf16[2,3,768,384]{3,2,1,0:T(8,128)(2,1)}, u32[]{:S(2)}) copy-start(bf16[2,3,768,384]{3,2,1,0:T(8,128)(2,1)} %refs_7_.3) | copy-start | bytes 10616836
  73.2 17.7 %all-to-all-start.1 = ((bf16[8,64,384]{2,1,0:T(8,128)(2,1)}), bf16[8,64,384]{2,1,0:T(8,128)(2,1)}, u32[]{:S(2)}, u32[]{:S(2)}) async-start(bf16[8,64,384]{2,1,0:T(8,128)(2,1)} %bitcast.93), calls=%async_computation.1 | async-start | bytes 786432 | tf_op jit(solution)/shard_map/all_to_all | solution.py:432
  94.0 11.0 %collective-permute-start.17 = (bf16[256,384]{1,0:T(8,128)(2,1)S(1)}, bf16[256,384]{1,0:T(8,128)(2,1)S(1)}, u32[]{:S(2)}, u32[]{:S(2)}) collective-permute-start(bf16[256,384]{1,0:T(8,128)(2,1)S(1)} %get-tuple-element.72), channel_id=1, source_target_pairs={{0,1},{1,2},{2,3},{3,4},{4,5},{5,6},{6,7},{8,9},{9,10},{10,11},{11... | collective-permute-start | bytes 589832 | tf_op jit(solution)/shard_map/ppermute | solution.py:336
  97.4 7.6 %collective-permute-start.18 = (bf16[256,384]{1,0:T(8,128)(2,1)S(1)}, bf16[256,384]{1,0:T(8,128)(2,1)S(1)}, u32[]{:S(2)}, u32[]{:S(2)}) collective-permute-start(bf16[256,384]{1,0:T(8,128)(2,1)S(1)} %get-tuple-element.73), channel_id=1, source_target_pairs={{1,0},{2,1},{3,2},{4,3},{5,4},{6,5},{7,6},{9,8},{10,9},{11,10},{12... | collective-permute-start | bytes 589832 | tf_op jit(solution)/shard_map/ppermute | solution.py:337
  105.9 6.7 %collective-permute-start.19 = (bf16[128,384]{1,0:T(8,128)(2,1)S(1)}, bf16[128,384]{1,0:T(8,128)(2,1)S(1)}, u32[]{:S(2)}, u32[]{:S(2)}) collective-permute-start(bf16[128,384]{1,0:T(8,128)(2,1)S(1)} %get-tuple-element.77), channel_id=1, source_target_pairs={{0,1},{1,2},{2,3},{3,4},{4,5},{5,6},{6,7},{8,9},{9,10},{10,11},{11... | collective-permute-start | bytes 294920 | tf_op jit(solution)/shard_map/ppermute | solution.py:336
  110.4 6.5 %collective-permute-start.20 = (bf16[128,384]{1,0:T(8,128)(2,1)S(1)}, bf16[128,384]{1,0:T(8,128)(2,1)S(1)}, u32[]{:S(2)}, u32[]{:S(2)}) collective-permute-start(bf16[128,384]{1,0:T(8,128)(2,1)S(1)} %get-tuple-element.80), channel_id=1, source_target_pairs={{1,0},{2,1},{3,2},{4,3},{5,4},{6,5},{7,6},{9,8},{10,9},{11,10},{12... | collective-permute-start | bytes 294920 | tf_op jit(solution)/shard_map/ppermute | solution.py:337
  122.2 5.4 %collective-permute-start.21 = (bf16[2,768,512]{2,1,0:T(8,128)(2,1)S(1)}, bf16[2,768,512]{2,1,0:T(8,128)(2,1)S(1)}, u32[]{:S(2)}, u32[]{:S(2)}) collective-permute-start(bf16[2,768,512]{2,1,0:T(8,128)(2,1)S(1)} %get-tuple-element.85), channel_id=1, source_target_pairs={{0,8},{8,0},{16,24},{24,16},{1,9},{9,1},{17,25},{25,17},{2,10},{10... | collective-permute-start | bytes 4718600 | tf_op jit(solution)/shard_map/ppermute | solution.py:329
  122.3 6.7 %collective-permute-start.22 = (bf16[128,384]{1,0:T(8,128)(2,1)S(1)}, bf16[128,384]{1,0:T(8,128)(2,1)S(1)}, u32[]{:S(2)}, u32[]{:S(2)}) collective-permute-start(bf16[128,384]{1,0:T(8,128)(2,1)S(1)} %get-tuple-element.86.refs_3_.refs_6_), channel_id=1, source_target_pairs={{0,1},{1,2},{2,3},{3,4},{4,5},{5,6},{6,7},{8,9},{9,10},{10,11},{11... | collective-permute-start | bytes 294920 | tf_op jit(solution)/shard_map/ppermute | solution.py:336
  126.3 6.8 %collective-permute-start.23 = (bf16[128,384]{1,0:T(8,128)(2,1)S(1)}, bf16[128,384]{1,0:T(8,128)(2,1)S(1)}, u32[]{:S(2)}, u32[]{:S(2)}) collective-permute-start(bf16[128,384]{1,0:T(8,128)(2,1)S(1)} %get-tuple-element.87.refs_2_.refs_5_), channel_id=1, source_target_pairs={{1,0},{2,1},{3,2},{4,3},{5,4},{6,5},{7,6},{9,8},{10,9},{11,10},{12... | collective-permute-start | bytes 294920 | tf_op jit(solution)/shard_map/ppermute | solution.py:337
  133.1 21.1 %collective-permute-start.26 = (bf16[768,512]{1,0:T(8,128)(2,1)S(1)}, bf16[768,512]{1,0:T(8,128)(2,1)S(1)}, u32[]{:S(2)}, u32[]{:S(2)}) collective-permute-start(bf16[768,512]{1,0:T(8,128)(2,1)S(1)} %fusion.1.refs_0_), channel_id=1, source_target_pairs={{0,16},{8,24},{16,0},{24,8},{1,17},{9,25},{17,1},{25,9},{2,18},{10... | collective-permute-start | bytes 2359304 | tf_op jit(solution)/shard_map/ppermute | solution.py:329
  137.0 8.7 %collective-permute-start.24 = (bf16[256,384]{1,0:T(8,128)(2,1)S(1)}, bf16[256,384]{1,0:T(8,128)(2,1)S(1)}, u32[]{:S(2)}, u32[]{:S(2)}) collective-permute-start(bf16[256,384]{1,0:T(8,128)(2,1)S(1)} %get-tuple-element.94.refs_6_), channel_id=1, source_target_pairs={{0,1},{1,2},{2,3},{3,4},{4,5},{5,6},{6,7},{8,9},{9,10},{10,11},{11... | collective-permute-start | bytes 589832 | tf_op jit(solution)/shard_map/ppermute | solution.py:336
  140.2 7.7 %collective-permute-start.25 = (bf16[256,384]{1,0:T(8,128)(2,1)S(1)}, bf16[256,384]{1,0:T(8,128)(2,1)S(1)}, u32[]{:S(2)}, u32[]{:S(2)}) collective-permute-start(bf16[256,384]{1,0:T(8,128)(2,1)S(1)} %get-tuple-element.93.refs_1_.refs_5_), channel_id=1, source_target_pairs={{1,0},{2,1},{3,2},{4,3},{5,4},{6,5},{7,6},{9,8},{10,9},{11,10},{12... | collective-permute-start | bytes 589832 | tf_op jit(solution)/shard_map/ppermute | solution.py:337
  147.9 9.0 %collective-permute-start.30 = (bf16[2,768,384]{2,1,0:T(8,128)(2,1)S(1)}, bf16[2,768,384]{2,1,0:T(8,128)(2,1)}, u32[]{:S(2)}, u32[]{:S(2)}) collective-permute-start(bf16[2,768,384]{2,1,0:T(8,128)(2,1)S(1)} %get-tuple-element.107), channel_id=1, source_target_pairs={{0,8},{8,0},{16,24},{24,16},{1,9},{9,1},{17,25},{25,17},{2,10},{10... | collective-permute-start | bytes 3538952 | tf_op jit(solution)/shard_map/ppermute | solution.py:329
  155.1 6.4 %collective-permute-start.27 = (bf16[2,768,384]{2,1,0:T(8,128)(2,1)}, bf16[2,768,384]{2,1,0:T(8,128)(2,1)}, u32[]{:S(2)}, u32[]{:S(2)}) collective-permute-start(bf16[2,768,384]{2,1,0:T(8,128)(2,1)} %get-tuple-element.103), channel_id=1, source_target_pairs={{0,8},{8,0},{16,24},{24,16},{1,9},{9,1},{17,25},{25,17},{2,10},{10... | collective-permute-start | bytes 3538952 | tf_op jit(solution)/shard_map/ppermute | solution.py:329
  159.0 21.9 %collective-permute-start.31 = (bf16[2,4,96,384]{3,2,1,0:T(8,128)(2,1)}, bf16[2,4,96,384]{3,2,1,0:T(8,128)(2,1)S(1)}, u32[]{:S(2)}, u32[]{:S(2)}) collective-permute-start(bf16[2,4,96,384]{3,2,1,0:T(8,128)(2,1)} %fusion.3), channel_id=1, source_target_pairs={{0,1},{1,0},{2,3},{3,2},{4,5},{5,4},{6,7},{7,6},{8,9},{9,8},{10,11... | collective-permute-start | bytes 1769480 | tf_op jit(solution)/shard_map/ppermute | solution.py:329
  162.8 20.1 %collective-permute-start.28 = (bf16[768,384]{1,0:T(8,128)(2,1)S(1)}, bf16[768,384]{1,0:T(8,128)(2,1)}, u32[]{:S(2)}, u32[]{:S(2)}) collective-permute-start(bf16[768,384]{1,0:T(8,128)(2,1)S(1)} %fusion.2), channel_id=1, source_target_pairs={{0,16},{8,24},{16,0},{24,8},{1,17},{9,25},{17,1},{25,9},{2,18},{10... | collective-permute-start | bytes 1769480 | tf_op jit(solution)/shard_map/ppermute | solution.py:329
  164.7 28.9 %all-to-all-start.2 = ((bf16[8,96,512]{2,1,0:T(8,128)(2,1)}), bf16[8,96,512]{2,1,0:T(8,128)(2,1)S(1)}, u32[]{:S(2)}, u32[]{:S(2)}) async-start(bf16[8,96,512]{2,1,0:T(8,128)(2,1)} %bitcast.38), calls=%async_computation.2 | async-start | bytes 1572864 | tf_op jit(solution)/shard_map/all_to_all | solution.py:351
  181.0 7.0 %collective-permute-start.32 = (bf16[4,96,384]{2,1,0:T(8,128)(2,1)S(1)}, bf16[4,96,384]{2,1,0:T(8,128)(2,1)S(1)}, u32[]{:S(2)}, u32[]{:S(2)}) collective-permute-start(bf16[4,96,384]{2,1,0:T(8,128)(2,1)S(1)} %fusion.4), channel_id=1, source_target_pairs={{0,16},{8,24},{16,0},{24,8},{1,17},{9,25},{17,1},{25,9},{2,18},{10... | collective-permute-start | bytes 884744 | tf_op jit(solution)/shard_map/ppermute | solution.py:329
  184.0 7.6 %collective-permute-start.29 = (bf16[4,96,384]{2,1,0:T(8,128)(2,1)S(1)}, bf16[4,96,384]{2,1,0:T(8,128)(2,1)S(1)}, u32[]{:S(2)}, u32[]{:S(2)}) collective-permute-start(bf16[4,96,384]{2,1,0:T(8,128)(2,1)S(1)} %fusion.8), channel_id=1, source_target_pairs={{0,1},{1,0},{2,3},{3,2},{4,5},{5,4},{6,7},{7,6},{8,9},{9,8},{10,11... | collective-permute-start | bytes 884744 | tf_op jit(solution)/shard_map/ppermute | solution.py:329
  193.5 17.8 %all-to-all-start.3 = ((bf16[4,96,768]{2,1,0:T(8,128)(2,1)}), bf16[4,96,768]{2,1,0:T(8,128)(2,1)S(1)}, u32[]{:S(2)}, u32[]{:S(2)}) async-start(bf16[4,96,768]{2,1,0:T(8,128)(2,1)} %pad_maximum_fusion), calls=%async_computation.3 | async-start | bytes 1179648 | tf_op jit(solution)/shard_map/all_to_all | solution.py:388
  (22 other events, 125.7 us)

commit v10 on v9

--- a/solution.py
+++ b/solution.py
@@ -413,6 +413,8 @@
         [swap(mine[i * piece : (i + 1) * piece, n * columns : (n + 1) * columns], "dp", 2) for i in range(2)]
         for n in range(2)
     ]
+    extra = lax.dynamic_slice(projection, ((1 - side) * share + piece, columns), (piece, columns))
+    extra = swap(extra, "dp", 2)
     near, away = (me ^ 2) * depth, (me ^ 3) * depth
     later = []
     for i in range(2):
@@ -425,7 +427,7 @@
             held = far[n][i]
             if n == 0 and i == 0:
                 held, total = lax.optimization_barrier((held, total))
-            crossed = swap(held, "seq", 1)
+            crossed = extra if n == 1 and i == 1 else swap(held, "seq", 1)
             weights.append([held, swap(held, "dp", 1), crossed, swap(crossed, "dp", 1)])
 
     def send(sums):
@@ -433,9 +435,12 @@
             sums.reshape(groups, block, columns), "seq", split_axis=0, concat_axis=0, tiled=True
         ).reshape(row_count, columns)
 
-    left = send(absorb(total, 0, blocks, weights[0] + weights[1], 20))
-    left, last = lax.optimization_barrier((left, weights[3][2]))
-    right = send(absorb(total, columns, blocks, weights[2] + weights[3][:2] + [last, weights[3][3]], 60))
+    left = absorb(total, 0, blocks, weights[0] + weights[1], 20)
+    left, weights[3][3] = lax.optimization_barrier((left, weights[3][3]))
+    left = send(left)
+    right = absorb(total, columns, blocks, weights[2] + weights[3], 60)
+    left, right = lax.optimization_barrier((left, right))
+    right = send(right)
 
     column = lax.dynamic_index_in_dim(layout[0], device, axis=1, keepdims=True)
     position = column * block + jnp.arange(block, dtype=jnp.int32)[None, :]

time: 213 us -> 204 us (0.958)
  waiting for transfers between devices: 84.1 us -> 79.2 us
  starting transfers between devices: 62.3 us -> 60.1 us
    ppermute x25, waiting for transfers between devices: 42.9 us -> 37 us  [swap(): return lax.ppermute(value, axis, [(i, i ^ bit) for i in range(size)])]
    all_to_all x2, starting transfers between devices: 11.8 us -> 9.55 us  [send(): lax.all_to_all(sums.reshape(groups, block, columns), 'seq', split_axis=0,...]
    unnamed x66 -> x62, local copies, waits for them, and re-layouts: 5.86 us -> 4.04 us
  transfers between devices with their start and end apart: 37 -> 37, of which waited for: 17 -> 18; matrix products, arithmetic and copies ran while one was open for 7% -> 7% of each run, Pallas kernels for 13% -> 17%
where the time goes in v10:
time: 204 us
  waiting for transfers between devices  79.2 us (39%)
  starting transfers between devices  60.1 us (29%)
  Pallas kernels  43.4 us (21%)
  local copies, waits for them, and re-layouts  9.74 us (5%)
  other arithmetic  9.33 us (5%)
    ppermute x25, waiting for transfers between devices, swap(): return lax.ppermute(value, axis, [(i, i ^ bit) for i in range(size)])  37 us
    pallas_call x11, Pallas kernels, call(): pl.pallas_call(body, out_shape=outs, in_specs=[SMEM] * smem + [ANY] * aft...  33.1 us
    ppermute x25, starting transfers between devices, swap(): return lax.ppermute(value, axis, [(i, i ^ bit) for i in range(size)])  21.1 us
    ppermute x4, starting transfers between devices, halo(): lax.ppermute(high, 'seq', up)  15.1 us
    all_to_all x2, waiting for transfers between devices, send(): lax.all_to_all(sums.reshape(groups, block, columns), 'seq', split_axis=0,...  12.4 us
    all_to_all x1, waiting for transfers between devices, crossed_sums(): lax.all_to_all(both, 'seq', split_axis=0, concat_axis=0, axis_index_group...  12.1 us
    ppermute x4, waiting for transfers between devices, halo(): lax.ppermute(low, 'seq', [(j, i) for i, j in up])  10.6 us
    pallas_call x1, Pallas kernels, product(): pl.pallas_call(body, out_shape=out, in_specs=[SMEM] + [HBM] * (count + 1)...  10.3 us
  transfers between devices with their start and end apart: 37, of which 18 were waited for; matrix products, arithmetic and copies ran while one was open for 7% of the time, Pallas kernels for 17%

profile of v10, /device:TPU:0, one launch (start us, length us, event | category | flops | bytes accessed | tf_op | source)
XLA Modules:
  0.0 203.5 jit_solution(8835456126006778910)
XLA Ops:
  1.1 1.7 fusion.9
  2.8 2.6 %collective-permute-start.5 = (bf16[512,384]{1,0:T(8,128)(2,1)S(1)}, bf16[512,384]{1,0:T(8,128)(2,1)S(1)}, u32[]{:S(2)}, u32[]{:S(2)}) collective-permute-start(bf16[512,384]{1,0:T(8,128)(2,1)S(1)} %get-tuple-element.120), channel_id=1, source_target_pairs={{0,16},{8,24},{16,0},{24,8},{1,17},{9,25},{17,1},{25,9},{2,18},{10... | collective-permute-start | bytes 1179656 | tf_op jit(solution)/shard_map/ppermute | solution.py:329
  5.5 9.9 %collective-permute-done.5.refs_12_ = bf16[512,384]{1,0:T(8,128)(2,1)S(1)} collective-permute-done((bf16[512,384]{1,0:T(8,128)(2,1)S(1)}, bf16[512,384]{1,0:T(8,128)(2,1)S(1)}, u32[]{:S(2)}, u32[]{:S(2)}) %collective-permute-start.5) | collective-permute-done | bytes 393248 | tf_op jit(solution)/shard_map/ppermute | solution.py:329
  15.4 2.0 collective-permute-start.7
  17.4 1.5 collective-permute-start.9
  19.0 10.3 %shard_map.129 = (f32[512,768]{1,0:T(8,128)}, bf16[512,512]{1,0:T(8,128)(2,1)S(1)}, bf16[512,512]{1,0:T(8,128)(2,1)S(1)}, bf16[512,512]{1,0:T(8,128)(2,1)S(1)}, ...) custom-call(s32[10]{0:T(128)S(1)} %stack.60.starts_ref, ...), custom_call_target="tpu_custom_call" | custom-call | flops 1024 | bytes 1024 | tf_op jit(solution)/shard_map/pallas_call | solution.py:110
  30.6 1.7 collective-permute-done.9.refs_14_
  32.3 6.9 %collective-permute-done.3.refs_10_ = bf16[512,384]{1,0:T(8,128)(2,1)S(1)} collective-permute-done((bf16[512,384]{1,0:T(8,128)(2,1)S(1)}, bf16[512,384]{1,0:T(8,128)(2,1)S(1)}, u32[]{:S(2)}, u32[]{:S(2)}) %collective-permute-start.3) | collective-permute-done | bytes 393248 | tf_op jit(solution)/shard_map/ppermute | solution.py:329
  39.1 1.3 collective-permute-done.11.refs_8_
  40.4 1.8 collective-permute-start.15
  42.3 1.5 collective-permute-start.13
  43.8 1.4 copy-done.2
  45.2 3.1 %shard_map.130 = bf16[512,384]{1,0:T(8,128)(2,1)} custom-call(f32[512,768]{1,0:T(8,128)S(1)} %copy-done.2, bf16[512,512]{1,0:T(8,128)(2,1)S(1)} %get-tuple-element.63.refs_0_, bf16[512,512]{1,0:T(8,128)(2,1)S(1)} %get-tuple-element.64.refs_1_, bf16[512,512]{1,0:T(8,128)(2,1)S(1)} %get-tuple-element.65.refs_2_, ...), custom_call_target="tpu_custom_call" | custom-call | flops 1024 | bytes 1024 | tf_op jit(solution)/shard_map/pallas_call | solution.py:52
  49.1 4.9 %all-to-all-start = ((bf16[8,64,384]{2,1,0:T(8,128)(2,1)}), bf16[8,64,384]{2,1,0:T(8,128)(2,1)}, u32[]{:S(2)}, u32[]{:S(2)}) async-start(bf16[8,64,384]{2,1,0:T(8,128)(2,1)} %bitcast.14), calls=%async_computation | async-start | bytes 786432 | tf_op jit(solution)/shard_map/all_to_all | solution.py:434
  57.7 6.8 %shard_map.131 = bf16[512,384]{1,0:T(8,128)(2,1)} custom-call(f32[512,768]{1,0:T(8,128)} %get-tuple-element.62.old_ref, bf16[512,512]{1,0:T(8,128)(2,1)} %copy-done.6, bf16[512,512]{1,0:T(8,128)(2,1)} %copy-done.7, bf16[512,512]{1,0:T(8,128)(2,1)} %copy-done.8, bf16[512,512]{1,0:T(8,128)(2,1)} %copy-done.9, bf16[512,512]{1,0:T(8,128)(2,1)} %copy-done.10, ...), custom_call_target="tpu_custom_call" | custom-call | flops 1024 | bytes 1024 | tf_op jit(solution)/shard_map/pallas_call | solution.py:52
  64.5 1.3 all-to-all-done
  65.9 4.7 %all-to-all-start.1 = ((bf16[8,64,384]{2,1,0:T(8,128)(2,1)}), bf16[8,64,384]{2,1,0:T(8,128)(2,1)}, u32[]{:S(2)}, u32[]{:S(2)}) async-start(bf16[8,64,384]{2,1,0:T(8,128)(2,1)} %bitcast.92), calls=%async_computation.1 | async-start | bytes 786432 | tf_op jit(solution)/shard_map/all_to_all | solution.py:434
  71.6 11.0 %all-to-all-done.1 = bf16[8,64,384]{2,1,0:T(8,128)(2,1)} async-done(((bf16[8,64,384]{2,1,0:T(8,128)(2,1)}), bf16[8,64,384]{2,1,0:T(8,128)(2,1)}, u32[]{:S(2)}, u32[]{:S(2)}) %all-to-all-start.1) | async-done | bytes 393248 | tf_op jit(solution)/shard_map/all_to_all | solution.py:434
  82.6 2.3 %shard_map.132 = (bf16[512,768]{1,0:T(8,128)(2,1)S(1)}, bf16[256,768]{1,0:T(8,128)(2,1)S(1)}, bf16[256,768]{1,0:T(8,128)(2,1)S(1)}, bf16[256,384]{1,0:T(8,128)(2,1)S(1)}, bf16[256,384]{1,0:T(8,128)(2,1)S(1)}) custom-call(s32[1,512]{1,0:T(1,128)S(1)} %compare_select_fusion.target_ref, bf16[512,384]{1,0:T(8,128)(2,1)} %bitcast.15.left_ref, ...), custom_call_target="tpu_custom_call" | custom-call | flops 1024 | bytes 1024 | tf_op jit(solution)/shard_map/pallas_call | solution.py:52
  84.9 3.4 %collective-permute-start.17 = (bf16[256,384]{1,0:T(8,128)(2,1)S(1)}, bf16[256,384]{1,0:T(8,128)(2,1)S(1)}, u32[]{:S(2)}, u32[]{:S(2)}) collective-permute-start(bf16[256,384]{1,0:T(8,128)(2,1)S(1)} %get-tuple-element.76), channel_id=1, source_target_pairs={{0,1},{1,2},{2,3},{3,4},{4,5},{5,6},{6,7},{8,9},{9,10},{10,11},{11... | collective-permute-start | bytes 589832 | tf_op jit(solution)/shard_map/ppermute | solution.py:336
  88.3 1.5 collective-permute-start.18
  90.7 5.2 %collective-permute-done.17.prev_ref = bf16[256,384]{1,0:T(8,128)(2,1)S(1)} collective-permute-done((bf16[256,384]{1,0:T(8,128)(2,1)S(1)}, bf16[256,384]{1,0:T(8,128)(2,1)S(1)}, u32[]{:S(2)}, u32[]{:S(2)}) %collective-permute-start.17) | collective-permute-done | bytes 196640 | tf_op jit(solution)/shard_map/ppermute | solution.py:336
  96.8 4.5 %collective-permute-start.19 = (bf16[128,384]{1,0:T(8,128)(2,1)S(1)}, bf16[128,384]{1,0:T(8,128)(2,1)S(1)}, u32[]{:S(2)}, u32[]{:S(2)}) collective-permute-start(bf16[128,384]{1,0:T(8,128)(2,1)S(1)} %get-tuple-element.81), channel_id=1, source_target_pairs={{0,1},{1,2},{2,3},{3,4},{4,5},{5,6},{6,7},{8,9},{9,10},{10,11},{11... | collective-permute-start | bytes 294920 | tf_op jit(solution)/shard_map/ppermute | solution.py:336
  101.3 1.3 collective-permute-start.20
  103.5 4.3 %collective-permute-done.20.refs_4_ = bf16[128,384]{1,0:T(8,128)(2,1)S(1)} collective-permute-done((bf16[128,384]{1,0:T(8,128)(2,1)S(1)}, bf16[128,384]{1,0:T(8,128)(2,1)S(1)}, u32[]{:S(2)}, u32[]{:S(2)}) %collective-permute-start.20) | collective-permute-done | bytes 98336 | tf_op jit(solution)/shard_map/ppermute | solution.py:337
  107.8 3.7 %shard_map.135 = (bf16[256,384]{1,0:T(8,128)(2,1)S(1)}, bf16[128,768]{1,0:T(8,128)(2,1)S(1)}, bf16[128,2048]{1,0:T(8,128)(2,1)S(1)}, bf16[128,768]{1,0:T(8,128)(...) custom-call(s32[2]{0:T(128)S(1)} %get-tuple-element.128.refs_0_, ...), custom_call_target="tpu_custom_call" | custom-call | flops 1024 | bytes 1024 | tf_op jit(solution)/shard_map/pallas_call | solution.py:52
  111.5 1.5 shard_map.136
  113.2 4.0 %collective-permute-start.22 = (bf16[128,384]{1,0:T(8,128)(2,1)S(1)}, bf16[128,384]{1,0:T(8,128)(2,1)S(1)}, u32[]{:S(2)}, u32[]{:S(2)}) collective-permute-start(bf16[128,384]{1,0:T(8,128)(2,1)S(1)} %get-tuple-element.90.refs_3_.refs_6_), channel_id=1, source_target_pairs={{0,1},{1,2},{2,3},{3,4},{4,5},{5,6},{6,7},{8,9},{9,10},{10,11},{11... | collective-permute-start | bytes 294920 | tf_op jit(solution)/shard_map/ppermute | solution.py:336
  117.2 1.3 collective-permute-start.23
  119.8 4.1 %collective-permute-done.23.refs_4_.refs_7_ = bf16[128,384]{1,0:T(8,128)(2,1)S(1)} collective-permute-done((bf16[128,384]{1,0:T(8,128)(2,1)S(1)}, bf16[128,384]{1,0:T(8,128)(2,1)S(1)}, u32[]{:S(2)}, u32[]{:S(2)}) %collective-permute-start.23) | collective-permute-done | bytes 98336 | tf_op jit(solution)/shard_map/ppermute | solution.py:337
  124.5 2.5 %shard_map.137 = (f32[256,768]{1,0:T(8,128)}, bf16[256,768]{1,0:T(8,128)(2,1)S(1)}, bf16[256,384]{1,0:T(8,128)(2,1)S(1)}, bf16[256,384]{1,0:T(8,128)(2,1)S(1)}) custom-call(bf16[768,512]{1,0:T(8,128)(2,1)S(1)} %fusion.1.refs_0_, bf16[128,384]{1,0:T(8,128)(2,1)S(1)} %collective-permute-done.22.refs_1_.refs_4_, ...), custom_call_target="tpu_custom_call" | custom-call | flops 1024 | bytes 1024 | tf_op jit(solution)/shard_map/pallas_call | solution.py:52
  127.0 3.2 %collective-permute-start.24 = (bf16[256,384]{1,0:T(8,128)(2,1)S(1)}, bf16[256,384]{1,0:T(8,128)(2,1)S(1)}, u32[]{:S(2)}, u32[]{:S(2)}) collective-permute-start(bf16[256,384]{1,0:T(8,128)(2,1)S(1)} %get-tuple-element.98.refs_6_), channel_id=1, source_target_pairs={{0,1},{1,2},{2,3},{3,4},{4,5},{5,6},{6,7},{8,9},{9,10},{10,11},{11... | collective-permute-start | bytes 589832 | tf_op jit(solution)/shard_map/ppermute | solution.py:336
  130.2 1.3 collective-permute-start.25
  131.5 4.2 %shard_map.138 = (bf16[2,768,384]{2,1,0:T(8,128)(2,1)S(1)}, bf16[2,768,384]{2,1,0:T(8,128)(2,1)S(1)}) custom-call(s32[2]{0:T(128)S(1)} %get-tuple-element.127.ids_ref.refs_0_, bf16[256,384]{1,0:T(8,128)(2,1)S(1)} %get-tuple-element.97.refs_1_.refs_5_, bf16[128,768]{1,0:T(8,128)(2,1)S(1)} %get-tuple-element.82.refs_2_, ...), custom_call_target="tpu_custom_call" | custom-call | flops 1024 | bytes 1024 | tf_op jit(solution)/shard_map/pallas_call | solution.py:52
  135.8 2.2 %collective-permute-done.25.refs_7_ = bf16[256,384]{1,0:T(8,128)(2,1)S(1)} collective-permute-done((bf16[256,384]{1,0:T(8,128)(2,1)S(1)}, bf16[256,384]{1,0:T(8,128)(2,1)S(1)}, u32[]{:S(2)}, u32[]{:S(2)}) %collective-permute-start.25) | collective-permute-done | bytes 196640 | tf_op jit(solution)/shard_map/ppermute | solution.py:337
  137.9 6.3 %shard_map.139 = (bf16[2,768,384]{2,1,0:T(8,128)(2,1)S(1)}, bf16[2,768,384]{2,1,0:T(8,128)(2,1)}) custom-call(s32[2]{0:T(128)S(1)} %get-tuple-element.127.ids_ref.refs_0_, bf16[256,384]{1,0:T(8,128)(2,1)S(1)} %get-tuple-element.97.refs_1_.refs_5_, bf16[256,768]{1,0:T(8,128)(2,1)S(1)} %get-tuple-element.78.low_ref.refs_2_, ...), custom_call_target="tpu_custom_call" | custom-call | flops 1024 | bytes 1024 | tf_op jit(solution)/shard_map/pallas_call | solution.py:52
  146.9 2.1 %fusion.3 = bf16[2,4,96,384]{3,2,1,0:T(8,128)(2,1)} fusion(bf16[2,4,2,96,384]{4,3,2,1,0:T(8,128)(2,1)} %bitcast.30, s32[]{:T(128)S(6)} %select_n.104, bf16[2,4,2,96,384]{4,3,2,1,0:T(8,128)(2,1)S(1)} %bitcast.85), kind=kLoop, calls=%fused_computation.8 | loop fusion | flops 1179648 | bytes 1769476 | tf_op jit(solution)/shard_map/convert_element_type | solution.py:372
  149.1 2.6 %collective-permute-start.31 = (bf16[2,4,96,384]{3,2,1,0:T(8,128)(2,1)}, bf16[2,4,96,384]{3,2,1,0:T(8,128)(2,1)S(1)}, u32[]{:S(2)}, u32[]{:S(2)}) collective-permute-start(bf16[2,4,96,384]{3,2,1,0:T(8,128)(2,1)} %fusion.3), channel_id=1, source_target_pairs={{0,1},{1,0},{2,3},{3,2},{4,5},{5,4},{6,7},{7,6},{8,9},{9,8},{10,11... | collective-permute-start | bytes 1769480 | tf_op jit(solution)/shard_map/ppermute | solution.py:329
  152.9 1.5 collective-permute-start.28
  154.4 1.3 fusion
  155.7 4.1 %all-to-all-start.2 = ((bf16[8,96,512]{2,1,0:T(8,128)(2,1)}), bf16[8,96,512]{2,1,0:T(8,128)(2,1)S(1)}, u32[]{:S(2)}, u32[]{:S(2)}) async-start(bf16[8,96,512]{2,1,0:T(8,128)(2,1)} %bitcast.38), calls=%async_computation.2 | async-start | bytes 1572864 | tf_op jit(solution)/shard_map/all_to_all | solution.py:351
  159.8 1.4 fusion.11
  161.2 9.8 %collective-permute-done.31 = bf16[2,4,96,384]{3,2,1,0:T(8,128)(2,1)S(1)} collective-permute-done((bf16[2,4,96,384]{3,2,1,0:T(8,128)(2,1)}, bf16[2,4,96,384]{3,2,1,0:T(8,128)(2,1)S(1)}, u32[]{:S(2)}, u32[]{:S(2)}) %collective-permute-start.31) | collective-permute-done | bytes 589856 | tf_op jit(solution)/shard_map/ppermute | solution.py:329
  171.1 1.5 collective-permute-start.32
  175.0 2.4 %collective-permute-start.29 = (bf16[4,96,384]{2,1,0:T(8,128)(2,1)S(1)}, bf16[4,96,384]{2,1,0:T(8,128)(2,1)S(1)}, u32[]{:S(2)}, u32[]{:S(2)}) collective-permute-start(bf16[4,96,384]{2,1,0:T(8,128)(2,1)S(1)} %fusion.8), channel_id=1, source_target_pairs={{0,1},{1,0},{2,3},{3,2},{4,5},{5,4},{6,7},{7,6},{8,9},{9,8},{10,11... | collective-permute-start | bytes 884744 | tf_op jit(solution)/shard_map/ppermute | solution.py:329
  178.0 4.8 %collective-permute-done.29 = bf16[4,96,384]{2,1,0:T(8,128)(2,1)S(1)} collective-permute-done((bf16[4,96,384]{2,1,0:T(8,128)(2,1)S(1)}, bf16[4,96,384]{2,1,0:T(8,128)(2,1)S(1)}, u32[]{:S(2)}, u32[]{:S(2)}) %collective-permute-start.29) | collective-permute-done | bytes 294944 | tf_op jit(solution)/shard_map/ppermute | solution.py:329
  184.8 5.0 %all-to-all-start.3 = ((bf16[4,96,768]{2,1,0:T(8,128)(2,1)}), bf16[4,96,768]{2,1,0:T(8,128)(2,1)S(1)}, u32[]{:S(2)}, u32[]{:S(2)}) async-start(bf16[4,96,768]{2,1,0:T(8,128)(2,1)} %pad_maximum_fusion), calls=%async_computation.3 | async-start | bytes 1179648 | tf_op jit(solution)/shard_map/all_to_all | solution.py:388
  190.6 12.1 %all-to-all-done.3.parts_ref = bf16[4,96,768]{2,1,0:T(8,128)(2,1)S(1)} async-done(((bf16[4,96,768]{2,1,0:T(8,128)(2,1)}), bf16[4,96,768]{2,1,0:T(8,128)(2,1)S(1)}, u32[]{:S(2)}, u32[]{:S(2)}) %all-to-all-start.3) | async-done | bytes 589856 | tf_op jit(solution)/shard_map/all_to_all | solution.py:388
  (121 shorter events, 22.2 us)
Async XLA Ops:
  0.6 18.3 %collective-permute-start.1 = (bf16[2048,768]{1,0:T(8,128)(2,1)}, bf16[2048,768]{1,0:T(8,128)(2,1)}, u32[]{:S(2)}, u32[]{:S(2)}) collective-permute-start(bf16[2048,768]{1,0:T(8,128)(2,1)} %refs_0_.1), channel_id=1, source_target_pairs={{0,8},{8,0},{16,24},{24,16},{1,9},{9,1},{17,25},{25,17},{2,10},{10... | collective-permute-start | bytes 9437192 | tf_op jit(solution)/shard_map/ppermute | solution.py:329
  2.8 12.6 %collective-permute-start.5 = (bf16[512,384]{1,0:T(8,128)(2,1)S(1)}, bf16[512,384]{1,0:T(8,128)(2,1)S(1)}, u32[]{:S(2)}, u32[]{:S(2)}) collective-permute-start(bf16[512,384]{1,0:T(8,128)(2,1)S(1)} %get-tuple-element.120), channel_id=1, source_target_pairs={{0,16},{8,24},{16,0},{24,8},{1,17},{9,25},{17,1},{25,9},{2,18},{10... | collective-permute-start | bytes 1179656 | tf_op jit(solution)/shard_map/ppermute | solution.py:329
  5.4 23.9 %collective-permute-start = (bf16[512,384]{1,0:T(8,128)(2,1)S(1)}, bf16[512,384]{1,0:T(8,128)(2,1)S(1)}, u32[]{:S(2)}, u32[]{:S(2)}) collective-permute-start(bf16[512,384]{1,0:T(8,128)(2,1)S(1)} %get-tuple-element.121), channel_id=1, source_target_pairs={{0,16},{8,24},{16,0},{24,8},{1,17},{9,25},{17,1},{25,9},{2,18},{10... | collective-permute-start | bytes 1179656 | tf_op jit(solution)/shard_map/ppermute | solution.py:329
  15.4 14.7 %collective-permute-start.7 = (bf16[512,384]{1,0:T(8,128)(2,1)S(1)}, bf16[512,384]{1,0:T(8,128)(2,1)S(1)}, u32[]{:S(2)}, u32[]{:S(2)}) collective-permute-start(bf16[512,384]{1,0:T(8,128)(2,1)S(1)} %collective-permute-done.5.refs_12_), channel_id=1, source_target_pairs={{0,1},{1,0},{2,3},{3,2},{4,5},{5,4},{6,7},{7,6},{8,9},{9,8},{10,11... | collective-permute-start | bytes 1179656 | tf_op jit(solution)/shard_map/ppermute | solution.py:329
  17.4 14.9 %collective-permute-start.9 = (bf16[512,384]{1,0:T(8,128)(2,1)S(1)}, bf16[512,384]{1,0:T(8,128)(2,1)S(1)}, u32[]{:S(2)}, u32[]{:S(2)}) collective-permute-start(bf16[512,384]{1,0:T(8,128)(2,1)S(1)} %get-tuple-element.122), channel_id=1, source_target_pairs={{0,16},{8,24},{16,0},{24,8},{1,17},{9,25},{17,1},{25,9},{2,18},{10... | collective-permute-start | bytes 1179656 | tf_op jit(solution)/shard_map/ppermute | solution.py:329
  29.3 19.0 %copy-start.6 = (bf16[512,512]{1,0:T(8,128)(2,1)}, bf16[512,512]{1,0:T(8,128)(2,1)S(1)}, u32[]{:S(2)}) copy-start(bf16[512,512]{1,0:T(8,128)(2,1)S(1)} %get-tuple-element.63.refs_0_) | copy-start | bytes 1572868
  29.3 19.0 %copy-start.7 = (bf16[512,512]{1,0:T(8,128)(2,1)}, bf16[512,512]{1,0:T(8,128)(2,1)S(1)}, u32[]{:S(2)}) copy-start(bf16[512,512]{1,0:T(8,128)(2,1)S(1)} %get-tuple-element.64.refs_1_) | copy-start | bytes 1572868
  29.3 19.0 %copy-start.8 = (bf16[512,512]{1,0:T(8,128)(2,1)}, bf16[512,512]{1,0:T(8,128)(2,1)S(1)}, u32[]{:S(2)}) copy-start(bf16[512,512]{1,0:T(8,128)(2,1)S(1)} %get-tuple-element.65.refs_2_) | copy-start | bytes 1572868
  29.3 19.0 %copy-start.9 = (bf16[512,512]{1,0:T(8,128)(2,1)}, bf16[512,512]{1,0:T(8,128)(2,1)S(1)}, u32[]{:S(2)}) copy-start(bf16[512,512]{1,0:T(8,128)(2,1)S(1)} %get-tuple-element.66.refs_3_) | copy-start | bytes 1572868
  29.3 19.0 %copy-start.10 = (bf16[512,512]{1,0:T(8,128)(2,1)}, bf16[512,512]{1,0:T(8,128)(2,1)S(1)}, u32[]{:S(2)}) copy-start(bf16[512,512]{1,0:T(8,128)(2,1)S(1)} %get-tuple-element.67.refs_4_) | copy-start | bytes 1572868
  29.3 19.0 %copy-start.11 = (bf16[512,512]{1,0:T(8,128)(2,1)}, bf16[512,512]{1,0:T(8,128)(2,1)S(1)}, u32[]{:S(2)}) copy-start(bf16[512,512]{1,0:T(8,128)(2,1)S(1)} %get-tuple-element.68.refs_5_) | copy-start | bytes 1572868
  29.3 19.0 %copy-start.12 = (bf16[512,512]{1,0:T(8,128)(2,1)}, bf16[512,512]{1,0:T(8,128)(2,1)S(1)}, u32[]{:S(2)}) copy-start(bf16[512,512]{1,0:T(8,128)(2,1)S(1)} %get-tuple-element.69.refs_6_) | copy-start | bytes 1572868
  29.3 19.0 %copy-start.13 = (bf16[512,512]{1,0:T(8,128)(2,1)}, bf16[512,512]{1,0:T(8,128)(2,1)S(1)}, u32[]{:S(2)}) copy-start(bf16[512,512]{1,0:T(8,128)(2,1)S(1)} %get-tuple-element.70.refs_7_) | copy-start | bytes 1572868
  29.4 9.7 %collective-permute-start.3 = (bf16[512,384]{1,0:T(8,128)(2,1)S(1)}, bf16[512,384]{1,0:T(8,128)(2,1)S(1)}, u32[]{:S(2)}, u32[]{:S(2)}) collective-permute-start(bf16[512,384]{1,0:T(8,128)(2,1)S(1)} %collective-permute-done.refs_8_), channel_id=1, source_target_pairs={{0,1},{1,0},{2,3},{3,2},{4,5},{5,4},{6,7},{7,6},{8,9},{9,8},{10,11... | collective-permute-start | bytes 1179656 | tf_op jit(solution)/shard_map/ppermute | solution.py:329
  29.9 10.5 %collective-permute-start.11 = (bf16[512,384]{1,0:T(8,128)(2,1)S(1)}, bf16[512,384]{1,0:T(8,128)(2,1)S(1)}, u32[]{:S(2)}, u32[]{:S(2)}) collective-permute-start(bf16[512,384]{1,0:T(8,128)(2,1)S(1)} %get-tuple-element.119), channel_id=1, source_target_pairs={{0,16},{8,24},{16,0},{24,8},{1,17},{9,25},{17,1},{25,9},{2,18},{10... | collective-permute-start | bytes 1179656 | tf_op jit(solution)/shard_map/ppermute | solution.py:329
  30.0 10.4 %collective-permute-start.6 = (bf16[512,384]{1,0:T(8,128)(2,1)S(1)}, bf16[512,384]{1,0:T(8,128)(2,1)S(1)}, u32[]{:S(2)}, u32[]{:S(2)}) collective-permute-start(bf16[512,384]{1,0:T(8,128)(2,1)S(1)} %collective-permute-done.5.refs_12_), channel_id=1, source_target_pairs={{0,8},{8,0},{16,24},{24,16},{1,9},{9,1},{17,25},{25,17},{2,10},{10... | collective-permute-start | bytes 1179656 | tf_op jit(solution)/shard_map/ppermute | solution.py:329
  30.1 12.2 %collective-permute-start.8 = (bf16[512,384]{1,0:T(8,128)(2,1)S(1)}, bf16[512,384]{1,0:T(8,128)(2,1)S(1)}, u32[]{:S(2)}, u32[]{:S(2)}) collective-permute-start(bf16[512,384]{1,0:T(8,128)(2,1)S(1)} %collective-permute-done.7.refs_14_), channel_id=1, source_target_pairs={{0,8},{8,0},{16,24},{24,16},{1,9},{9,1},{17,25},{25,17},{2,10},{10... | collective-permute-start | bytes 1179656 | tf_op jit(solution)/shard_map/ppermute | solution.py:329
  32.2 16.1 %copy-start.23 = (bf16[512,384]{1,0:T(8,128)(2,1)}, bf16[512,384]{1,0:T(8,128)(2,1)S(1)}, u32[]{:S(2)}) copy-start(bf16[512,384]{1,0:T(8,128)(2,1)S(1)} %collective-permute-done.9.refs_14_) | copy-start | bytes 1179652
  32.2 11.5 %collective-permute-start.2 = (bf16[512,384]{1,0:T(8,128)(2,1)S(1)}, bf16[512,384]{1,0:T(8,128)(2,1)S(1)}, u32[]{:S(2)}, u32[]{:S(2)}) collective-permute-start(bf16[512,384]{1,0:T(8,128)(2,1)S(1)} %collective-permute-done.refs_8_), channel_id=1, source_target_pairs={{0,8},{8,0},{16,24},{24,16},{1,9},{9,1},{17,25},{25,17},{2,10},{10... | collective-permute-start | bytes 1179656 | tf_op jit(solution)/shard_map/ppermute | solution.py:329
  39.1 4.7 %collective-permute-start.4 = (bf16[512,384]{1,0:T(8,128)(2,1)S(1)}, bf16[512,384]{1,0:T(8,128)(2,1)S(1)}, u32[]{:S(2)}, u32[]{:S(2)}) collective-permute-start(bf16[512,384]{1,0:T(8,128)(2,1)S(1)} %collective-permute-done.3.refs_10_), channel_id=1, source_target_pairs={{0,8},{8,0},{16,24},{24,16},{1,9},{9,1},{17,25},{25,17},{2,10},{10... | collective-permute-start | bytes 1179656 | tf_op jit(solution)/shard_map/ppermute | solution.py:329
  40.4 7.9 %collective-permute-start.10 = (bf16[512,384]{1,0:T(8,128)(2,1)S(1)}, bf16[512,384]{1,0:T(8,128)(2,1)S(1)}, u32[]{:S(2)}, u32[]{:S(2)}) collective-permute-start(bf16[512,384]{1,0:T(8,128)(2,1)S(1)} %collective-permute-done.9.refs_14_), channel_id=1, source_target_pairs={{0,8},{8,0},{16,24},{24,16},{1,9},{9,1},{17,25},{25,17},{2,10},{10... | collective-permute-start | bytes 1179656 | tf_op jit(solution)/shard_map/ppermute | solution.py:329
  40.4 13.7 %collective-permute-start.15 = (bf16[512,384]{1,0:T(8,128)(2,1)S(1)}, bf16[512,384]{1,0:T(8,128)(2,1)S(1)}, u32[]{:S(2)}, u32[]{:S(2)}) collective-permute-start(bf16[512,384]{1,0:T(8,128)(2,1)S(1)} %get-tuple-element.118), channel_id=1, source_target_pairs={{0,16},{8,24},{16,0},{24,8},{1,17},{9,25},{17,1},{25,9},{2,18},{10... | collective-permute-start | bytes 1179656 | tf_op jit(solution)/shard_map/ppermute | solution.py:329
  42.3 12.4 %collective-permute-start.13 = (bf16[512,384]{1,0:T(8,128)(2,1)S(1)}, bf16[512,384]{1,0:T(8,128)(2,1)S(1)}, u32[]{:S(2)}, u32[]{:S(2)}) collective-permute-start(bf16[512,384]{1,0:T(8,128)(2,1)S(1)} %collective-permute-done.11.refs_8_), channel_id=1, source_target_pairs={{0,1},{1,0},{2,3},{3,2},{4,5},{5,4},{6,7},{7,6},{8,9},{9,8},{10,11... | collective-permute-start | bytes 1179656 | tf_op jit(solution)/shard_map/ppermute | solution.py:329
  49.1 16.7 %all-to-all-start = ((bf16[8,64,384]{2,1,0:T(8,128)(2,1)}), bf16[8,64,384]{2,1,0:T(8,128)(2,1)}, u32[]{:S(2)}, u32[]{:S(2)}) async-start(bf16[8,64,384]{2,1,0:T(8,128)(2,1)} %bitcast.14), calls=%async_computation | async-start | bytes 786432 | tf_op jit(solution)/shard_map/all_to_all | solution.py:434
  54.0 17.2 %copy-start.30 = (s32[1,8,8]{2,1,0:T(8,128)S(1)}, s32[1,8,8]{2,1,0:T(8,128)}, u32[]{:S(2)}) copy-start(s32[1,8,8]{2,1,0:T(8,128)} %param.11) | copy-start | bytes 772
  54.0 1.8 collective-permute-start.12
  54.1 2.8 %collective-permute-start.16 = (bf16[512,384]{1,0:T(8,128)(2,1)S(1)}, bf16[512,384]{1,0:T(8,128)(2,1)S(1)}, u32[]{:S(2)}, u32[]{:S(2)}) collective-permute-start(bf16[512,384]{1,0:T(8,128)(2,1)S(1)} %collective-permute-done.15.refs_12_), channel_id=1, source_target_pairs={{0,8},{8,0},{16,24},{24,16},{1,9},{9,1},{17,25},{25,17},{2,10},{10... | collective-permute-start | bytes 1179656 | tf_op jit(solution)/shard_map/ppermute | solution.py:329
  54.6 3.1 %collective-permute-start.14 = (bf16[512,384]{1,0:T(8,128)(2,1)S(1)}, bf16[512,384]{1,0:T(8,128)(2,1)}, u32[]{:S(2)}, u32[]{:S(2)}) collective-permute-start(bf16[512,384]{1,0:T(8,128)(2,1)S(1)} %collective-permute-done.13.refs_10_), channel_id=1, source_target_pairs={{0,8},{8,0},{16,24},{24,16},{1,9},{9,1},{17,25},{25,17},{2,10},{10... | collective-permute-start | bytes 1179656 | tf_op jit(solution)/shard_map/ppermute | solution.py:329
  57.7 24.9 %copy-start = (bf16[2,3,768,384]{3,2,1,0:T(8,128)(2,1)S(1)}, bf16[2,3,768,384]{3,2,1,0:T(8,128)(2,1)}, u32[]{:S(2)}) copy-start(bf16[2,3,768,384]{3,2,1,0:T(8,128)(2,1)} %refs_7_.3) | copy-start | bytes 10616836
  65.9 16.8 %all-to-all-start.1 = ((bf16[8,64,384]{2,1,0:T(8,128)(2,1)}), bf16[8,64,384]{2,1,0:T(8,128)(2,1)}, u32[]{:S(2)}, u32[]{:S(2)}) async-start(bf16[8,64,384]{2,1,0:T(8,128)(2,1)} %bitcast.92), calls=%async_computation.1 | async-start | bytes 786432 | tf_op jit(solution)/shard_map/all_to_all | solution.py:434
  84.9 11.0 %collective-permute-start.17 = (bf16[256,384]{1,0:T(8,128)(2,1)S(1)}, bf16[256,384]{1,0:T(8,128)(2,1)S(1)}, u32[]{:S(2)}, u32[]{:S(2)}) collective-permute-start(bf16[256,384]{1,0:T(8,128)(2,1)S(1)} %get-tuple-element.76), channel_id=1, source_target_pairs={{0,1},{1,2},{2,3},{3,4},{4,5},{5,6},{6,7},{8,9},{9,10},{10,11},{11... | collective-permute-start | bytes 589832 | tf_op jit(solution)/shard_map/ppermute | solution.py:336
  88.3 7.6 %collective-permute-start.18 = (bf16[256,384]{1,0:T(8,128)(2,1)S(1)}, bf16[256,384]{1,0:T(8,128)(2,1)S(1)}, u32[]{:S(2)}, u32[]{:S(2)}) collective-permute-start(bf16[256,384]{1,0:T(8,128)(2,1)S(1)} %get-tuple-element.77), channel_id=1, source_target_pairs={{1,0},{2,1},{3,2},{4,3},{5,4},{6,5},{7,6},{9,8},{10,9},{11,10},{12... | collective-permute-start | bytes 589832 | tf_op jit(solution)/shard_map/ppermute | solution.py:337
  96.8 6.7 %collective-permute-start.19 = (bf16[128,384]{1,0:T(8,128)(2,1)S(1)}, bf16[128,384]{1,0:T(8,128)(2,1)S(1)}, u32[]{:S(2)}, u32[]{:S(2)}) collective-permute-start(bf16[128,384]{1,0:T(8,128)(2,1)S(1)} %get-tuple-element.81), channel_id=1, source_target_pairs={{0,1},{1,2},{2,3},{3,4},{4,5},{5,6},{6,7},{8,9},{9,10},{10,11},{11... | collective-permute-start | bytes 294920 | tf_op jit(solution)/shard_map/ppermute | solution.py:336
  101.3 6.5 %collective-permute-start.20 = (bf16[128,384]{1,0:T(8,128)(2,1)S(1)}, bf16[128,384]{1,0:T(8,128)(2,1)S(1)}, u32[]{:S(2)}, u32[]{:S(2)}) collective-permute-start(bf16[128,384]{1,0:T(8,128)(2,1)S(1)} %get-tuple-element.84), channel_id=1, source_target_pairs={{1,0},{2,1},{3,2},{4,3},{5,4},{6,5},{7,6},{9,8},{10,9},{11,10},{12... | collective-permute-start | bytes 294920 | tf_op jit(solution)/shard_map/ppermute | solution.py:337
  113.1 5.4 %collective-permute-start.21 = (bf16[2,768,512]{2,1,0:T(8,128)(2,1)S(1)}, bf16[2,768,512]{2,1,0:T(8,128)(2,1)S(1)}, u32[]{:S(2)}, u32[]{:S(2)}) collective-permute-start(bf16[2,768,512]{2,1,0:T(8,128)(2,1)S(1)} %get-tuple-element.89), channel_id=1, source_target_pairs={{0,8},{8,0},{16,24},{24,16},{1,9},{9,1},{17,25},{25,17},{2,10},{10... | collective-permute-start | bytes 4718600 | tf_op jit(solution)/shard_map/ppermute | solution.py:329
  113.2 6.7 %collective-permute-start.22 = (bf16[128,384]{1,0:T(8,128)(2,1)S(1)}, bf16[128,384]{1,0:T(8,128)(2,1)S(1)}, u32[]{:S(2)}, u32[]{:S(2)}) collective-permute-start(bf16[128,384]{1,0:T(8,128)(2,1)S(1)} %get-tuple-element.90.refs_3_.refs_6_), channel_id=1, source_target_pairs={{0,1},{1,2},{2,3},{3,4},{4,5},{5,6},{6,7},{8,9},{9,10},{10,11},{11... | collective-permute-start | bytes 294920 | tf_op jit(solution)/shard_map/ppermute | solution.py:336
  117.2 6.8 %collective-permute-start.23 = (bf16[128,384]{1,0:T(8,128)(2,1)S(1)}, bf16[128,384]{1,0:T(8,128)(2,1)S(1)}, u32[]{:S(2)}, u32[]{:S(2)}) collective-permute-start(bf16[128,384]{1,0:T(8,128)(2,1)S(1)} %get-tuple-element.91.refs_2_.refs_5_), channel_id=1, source_target_pairs={{1,0},{2,1},{3,2},{4,3},{5,4},{6,5},{7,6},{9,8},{10,9},{11,10},{12... | collective-permute-start | bytes 294920 | tf_op jit(solution)/shard_map/ppermute | solution.py:337
  124.0 20.3 %collective-permute-start.26 = (bf16[768,512]{1,0:T(8,128)(2,1)S(1)}, bf16[768,512]{1,0:T(8,128)(2,1)S(1)}, u32[]{:S(2)}, u32[]{:S(2)}) collective-permute-start(bf16[768,512]{1,0:T(8,128)(2,1)S(1)} %fusion.1.refs_0_), channel_id=1, source_target_pairs={{0,16},{8,24},{16,0},{24,8},{1,17},{9,25},{17,1},{25,9},{2,18},{10... | collective-permute-start | bytes 2359304 | tf_op jit(solution)/shard_map/ppermute | solution.py:329
  127.0 8.8 %collective-permute-start.24 = (bf16[256,384]{1,0:T(8,128)(2,1)S(1)}, bf16[256,384]{1,0:T(8,128)(2,1)S(1)}, u32[]{:S(2)}, u32[]{:S(2)}) collective-permute-start(bf16[256,384]{1,0:T(8,128)(2,1)S(1)} %get-tuple-element.98.refs_6_), channel_id=1, source_target_pairs={{0,1},{1,2},{2,3},{3,4},{4,5},{5,6},{6,7},{8,9},{9,10},{10,11},{11... | collective-permute-start | bytes 589832 | tf_op jit(solution)/shard_map/ppermute | solution.py:336
  130.2 7.7 %collective-permute-start.25 = (bf16[256,384]{1,0:T(8,128)(2,1)S(1)}, bf16[256,384]{1,0:T(8,128)(2,1)S(1)}, u32[]{:S(2)}, u32[]{:S(2)}) collective-permute-start(bf16[256,384]{1,0:T(8,128)(2,1)S(1)} %get-tuple-element.97.refs_1_.refs_5_), channel_id=1, source_target_pairs={{1,0},{2,1},{3,2},{4,3},{5,4},{6,5},{7,6},{9,8},{10,9},{11,10},{12... | collective-permute-start | bytes 589832 | tf_op jit(solution)/shard_map/ppermute | solution.py:337
  137.9 9.0 %collective-permute-start.30 = (bf16[2,768,384]{2,1,0:T(8,128)(2,1)S(1)}, bf16[2,768,384]{2,1,0:T(8,128)(2,1)}, u32[]{:S(2)}, u32[]{:S(2)}) collective-permute-start(bf16[2,768,384]{2,1,0:T(8,128)(2,1)S(1)} %get-tuple-element.111), channel_id=1, source_target_pairs={{0,8},{8,0},{16,24},{24,16},{1,9},{9,1},{17,25},{25,17},{2,10},{10... | collective-permute-start | bytes 3538952 | tf_op jit(solution)/shard_map/ppermute | solution.py:329
  145.2 6.4 %collective-permute-start.27 = (bf16[2,768,384]{2,1,0:T(8,128)(2,1)}, bf16[2,768,384]{2,1,0:T(8,128)(2,1)}, u32[]{:S(2)}, u32[]{:S(2)}) collective-permute-start(bf16[2,768,384]{2,1,0:T(8,128)(2,1)} %get-tuple-element.107), channel_id=1, source_target_pairs={{0,8},{8,0},{16,24},{24,16},{1,9},{9,1},{17,25},{25,17},{2,10},{10... | collective-permute-start | bytes 3538952 | tf_op jit(solution)/shard_map/ppermute | solution.py:329
  149.1 21.9 %collective-permute-start.31 = (bf16[2,4,96,384]{3,2,1,0:T(8,128)(2,1)}, bf16[2,4,96,384]{3,2,1,0:T(8,128)(2,1)S(1)}, u32[]{:S(2)}, u32[]{:S(2)}) collective-permute-start(bf16[2,4,96,384]{3,2,1,0:T(8,128)(2,1)} %fusion.3), channel_id=1, source_target_pairs={{0,1},{1,0},{2,3},{3,2},{4,5},{5,4},{6,7},{7,6},{8,9},{9,8},{10,11... | collective-permute-start | bytes 1769480 | tf_op jit(solution)/shard_map/ppermute | solution.py:329
  152.9 21.0 %collective-permute-start.28 = (bf16[768,384]{1,0:T(8,128)(2,1)S(1)}, bf16[768,384]{1,0:T(8,128)(2,1)}, u32[]{:S(2)}, u32[]{:S(2)}) collective-permute-start(bf16[768,384]{1,0:T(8,128)(2,1)S(1)} %fusion.2), channel_id=1, source_target_pairs={{0,16},{8,24},{16,0},{24,8},{1,17},{9,25},{17,1},{25,9},{2,18},{10... | collective-permute-start | bytes 1769480 | tf_op jit(solution)/shard_map/ppermute | solution.py:329
  155.7 29.1 %all-to-all-start.2 = ((bf16[8,96,512]{2,1,0:T(8,128)(2,1)}), bf16[8,96,512]{2,1,0:T(8,128)(2,1)S(1)}, u32[]{:S(2)}, u32[]{:S(2)}) async-start(bf16[8,96,512]{2,1,0:T(8,128)(2,1)} %bitcast.38), calls=%async_computation.2 | async-start | bytes 1572864 | tf_op jit(solution)/shard_map/all_to_all | solution.py:351
  171.1 6.8 %collective-permute-start.32 = (bf16[4,96,384]{2,1,0:T(8,128)(2,1)S(1)}, bf16[4,96,384]{2,1,0:T(8,128)(2,1)S(1)}, u32[]{:S(2)}, u32[]{:S(2)}) collective-permute-start(bf16[4,96,384]{2,1,0:T(8,128)(2,1)S(1)} %fusion.4), channel_id=1, source_target_pairs={{0,16},{8,24},{16,0},{24,8},{1,17},{9,25},{17,1},{25,9},{2,18},{10... | collective-permute-start | bytes 884744 | tf_op jit(solution)/shard_map/ppermute | solution.py:329
  175.0 7.8 %collective-permute-start.29 = (bf16[4,96,384]{2,1,0:T(8,128)(2,1)S(1)}, bf16[4,96,384]{2,1,0:T(8,128)(2,1)S(1)}, u32[]{:S(2)}, u32[]{:S(2)}) collective-permute-start(bf16[4,96,384]{2,1,0:T(8,128)(2,1)S(1)} %fusion.8), channel_id=1, source_target_pairs={{0,1},{1,0},{2,3},{3,2},{4,5},{5,4},{6,7},{7,6},{8,9},{9,8},{10,11... | collective-permute-start | bytes 884744 | tf_op jit(solution)/shard_map/ppermute | solution.py:329
  184.8 17.8 %all-to-all-start.3 = ((bf16[4,96,768]{2,1,0:T(8,128)(2,1)}), bf16[4,96,768]{2,1,0:T(8,128)(2,1)S(1)}, u32[]{:S(2)}, u32[]{:S(2)}) async-start(bf16[4,96,768]{2,1,0:T(8,128)(2,1)} %pad_maximum_fusion), calls=%async_computation.3 | async-start | bytes 1179648 | tf_op jit(solution)/shard_map/all_to_all | solution.py:388
  (20 other events, 118.1 us)

commit v11 on v10

--- a/solution.py
+++ b/solution.py
@@ -241,15 +241,17 @@
         out[k >> 1] = tn(second, logit_ref[:, pl.ds(start, width)]).astype(BF)
 
 
-def store_blocks(ids_ref, pieces, keep_ref, send_ref):
+def store_blocks(ids_ref, pieces, keep_refs, send_ref):
     width = pieces[0].shape[1] // 4
     for d in range(4):
         block = jnp.concatenate([p[:, d * width : (d + 1) * width] for p in pieces], axis=1)
         far = (ids_ref[0] >> 1) ^ (d >> 1)
 
-        @pl.when((ids_ref[0] & 1) == (d & 1))
-        def _(block=block, far=far):
-            keep_ref[far] = block
+        for k in range(2):
+
+            @pl.when(((ids_ref[0] & 1) == (d & 1)) & (far == k))
+            def _(block=block, k=k):
+                keep_refs[k][...] = block
 
         @pl.when((ids_ref[0] & 1) != (d & 1))
         def _(block=block, far=far):
@@ -270,14 +272,17 @@
 
 def weight_body(
     slab, ids_ref, after_ref, low_ref, high_ref, gprev_ref, glow_ref, ghigh_ref, gnext_ref, gated_ref, up_ref,
-    spread_ref, split_ref, keep_ref, send_ref,
+    spread_ref, split_ref, *out_refs,
 ):
     grads = (gprev_ref, glow_ref, ghigh_ref, gnext_ref)
     pieces = []
     for t in range(3):
         pieces.append((tn(low_ref[...], grads[2 - t][...]) + tn(high_ref[...], grads[3 - t][...])).astype(BF))
     pieces.append(mixer_piece(slab, gated_ref[...], up_ref[...], spread_ref, split_ref))
-    store_blocks(ids_ref, pieces, keep_ref, send_ref)
+    *keep_refs, send_ref = out_refs
+    if len(keep_refs) == 1:
+        keep_refs = [keep_refs[0].at[k] for k in range(2)]
+    store_blocks(ids_ref, pieces, keep_refs, send_ref)
 
 
 def fine_back_body(
@@ -360,6 +365,12 @@
     return lax.dynamic_index_in_dim(value, side, axis=len(blocks) + 1, keepdims=False).astype(F32)
 
 
+def both_body(left_ref, left_came_ref, right_ref, right_came_ref, both_ref):
+    columns = left_ref.shape[2]
+    both_ref[:, :, :columns] = (left_ref[...] + left_came_ref[...].astype(F32)).astype(BF)
+    both_ref[:, :, columns:] = (right_ref[...] + right_came_ref[...].astype(F32)).astype(BF)
+
+
 def crossed_sums(left_keep, left_send, right_keep, right_send, first, first_came):
     groups = lax.axis_size("seq")
     side = lax.axis_index("seq") % 2
@@ -374,14 +385,12 @@
     def left_half(at):
         return side_rows(left_keep[0], at) + side_rows(left_came[0], at) + side_rows(x_came, at)
 
-    def right_half(at):
-        return side_rows(right_keep[at], side) + side_rows(right_came[at], side) + side_came[at].astype(F32)
-
+    own = side_rows(right_keep, side) + side_rows(right_came, side) + side_came.astype(F32)
     left = swap(left_half(1 - side).astype(BF), "seq", 1)
-    right = swap(right_half(1).astype(BF), "dp", 2)
-    left = left_half(side) + left.astype(F32)
-    right = right_half(0) + right.astype(F32)
-    both = jnp.concatenate([left, right], axis=2).astype(BF)
+    right = swap(own[1].astype(BF), "dp", 2)
+    both, = call(
+        both_body, (left_half(side), left, own[0], right), [((*left.shape[:2], 2 * left.shape[2]), BF)], 20
+    )
     first = seq_parts((first + first_came.astype(F32)).astype(BF))
     both, first = lax.optimization_barrier((both, first))
     lines = [list(range(start, groups, 2)) for start in range(2)]
@@ -495,6 +504,7 @@
             split[j, (b // piece_width) * 2 * piece_width + j * piece_width + b % piece_width, b] = 1
     fold, split = jnp.asarray(fold), jnp.asarray(split)
     pair = [((2, channels, width), BF)] * 2
+    parts = [((channels, width), BF)] * 2 + pair[:1]
 
     def fine_back(*refs):
         fine_back_body(math.sqrt(windows * groups * bins) * 0.5, *refs)
@@ -515,8 +525,8 @@
         32, smem=1, after=1,
     )
     iprev, inext, coarse_send = lax.optimization_barrier((iprev, inext, coarse_send))
-    fine_keep, fine_send = call(
-        weights, (place, ilow, low, high, iprev, ilow, ihigh, inext, gated, lower, fold, split), pair,
+    *fine_keep, fine_send = call(
+        weights, (place, ilow, low, high, iprev, ilow, ihigh, inext, gated, lower, fold, split), parts,
         32, smem=1, after=1,
     )
     fine_send, track_x = lax.optimization_barrier((fine_send, track_x))

time: 204 us -> 202 us (level)
  local copies, waits for them, and re-layouts: 9.74 us -> 7.05 us
    slice x3 -> x0, local copies, waits for them, and re-layouts: 2.69 us -> none  [the longest x1 1.42 us: right_half(): right_came[at]]
    pallas_call x11 -> x12, Pallas kernels: 33.1 us -> 34.1 us  [call(): pl.pallas_call(body, out_shape=outs, in_specs=[SMEM] * smem + [ANY] * aft...]
  transfers between devices with their start and end apart: 37 -> 37, of which waited for: 18 -> 19; matrix products, arithmetic and copies ran while one was open for 7% -> 6% of each run, Pallas kernels for 17% -> 17%
where the time goes in v11:
time: 202 us; the launch traced here: 201 us
  waiting for transfers between devices  77.8 us (39%)
  starting transfers between devices  60.5 us (30%)
  Pallas kernels  44.4 us (22%)
  other arithmetic  9.82 us (5%)
  local copies, waits for them, and re-layouts  7.05 us (3%)
    ppermute x25, waiting for transfers between devices, swap(): return lax.ppermute(value, axis, [(i, i ^ bit) for i in range(size)])  37.2 us
    pallas_call x12, Pallas kernels, call(): pl.pallas_call(body, out_shape=outs, in_specs=[SMEM] * smem + [ANY] * aft...  34.1 us
    ppermute x25, starting transfers between devices, swap(): return lax.ppermute(value, axis, [(i, i ^ bit) for i in range(size)])  20.9 us
    ppermute x4, starting transfers between devices, halo(): lax.ppermute(high, 'seq', up)  15.1 us
    all_to_all x2, waiting for transfers between devices, send(): lax.all_to_all(sums.reshape(groups, block, columns), 'seq', split_axis=0,...  12.4 us
    ppermute x4, waiting for transfers between devices, halo(): lax.ppermute(low, 'seq', [(j, i) for i, j in up])  10.6 us
    all_to_all x1, waiting for transfers between devices, crossed_sums(): lax.all_to_all(both, 'seq', split_axis=0, concat_axis=0, axis_index_group...  10.5 us
    pallas_call x1, Pallas kernels, product(): pl.pallas_call(body, out_shape=out, in_specs=[SMEM] + [HBM] * (count + 1)...  10.3 us
  transfers between devices with their start and end apart: 37, of which 19 were waited for; matrix products, arithmetic and copies ran while one was open for 6% of the time, Pallas kernels for 17%

profile of v11, /device:TPU:0, one launch (start us, length us, event | category | flops | bytes accessed | tf_op | source)
XLA Modules:
  0.0 201.3 jit_solution(10788080437587989151)
XLA Ops:
  1.1 1.7 fusion.6
  2.8 2.6 %collective-permute-start.5 = (bf16[512,384]{1,0:T(8,128)(2,1)S(1)}, bf16[512,384]{1,0:T(8,128)(2,1)S(1)}, u32[]{:S(2)}, u32[]{:S(2)}) collective-permute-start(bf16[512,384]{1,0:T(8,128)(2,1)S(1)} %get-tuple-element.122), channel_id=1, source_target_pairs={{0,16},{8,24},{16,0},{24,8},{1,17},{9,25},{17,1},{25,9},{2,18},{10... | collective-permute-start | bytes 1179656 | tf_op jit(solution)/shard_map/ppermute | solution.py:334
  5.5 9.9 %collective-permute-done.5.refs_12_ = bf16[512,384]{1,0:T(8,128)(2,1)S(1)} collective-permute-done((bf16[512,384]{1,0:T(8,128)(2,1)S(1)}, bf16[512,384]{1,0:T(8,128)(2,1)S(1)}, u32[]{:S(2)}, u32[]{:S(2)}) %collective-permute-start.5) | collective-permute-done | bytes 393248 | tf_op jit(solution)/shard_map/ppermute | solution.py:334
  15.4 2.0 collective-permute-start.7
  17.4 1.5 collective-permute-start.9
  19.0 10.3 %shard_map.129 = (f32[512,768]{1,0:T(8,128)}, bf16[512,512]{1,0:T(8,128)(2,1)S(1)}, bf16[512,512]{1,0:T(8,128)(2,1)S(1)}, bf16[512,512]{1,0:T(8,128)(2,1)S(1)}, ...) custom-call(s32[10]{0:T(128)S(1)} %stack.60.starts_ref, ...), custom_call_target="tpu_custom_call" | custom-call | flops 1024 | bytes 1024 | tf_op jit(solution)/shard_map/pallas_call | solution.py:110
  30.5 1.7 collective-permute-done.9.refs_14_
  32.3 6.8 %collective-permute-done.3.refs_10_ = bf16[512,384]{1,0:T(8,128)(2,1)S(1)} collective-permute-done((bf16[512,384]{1,0:T(8,128)(2,1)S(1)}, bf16[512,384]{1,0:T(8,128)(2,1)S(1)}, u32[]{:S(2)}, u32[]{:S(2)}) %collective-permute-start.3) | collective-permute-done | bytes 393248 | tf_op jit(solution)/shard_map/ppermute | solution.py:334
  39.1 1.3 collective-permute-done.11.refs_8_
  40.4 1.8 collective-permute-start.15
  42.3 1.5 collective-permute-start.13
  43.8 1.4 copy-done.2
  45.2 3.1 %shard_map.130 = bf16[512,384]{1,0:T(8,128)(2,1)} custom-call(f32[512,768]{1,0:T(8,128)S(1)} %copy-done.2, bf16[512,512]{1,0:T(8,128)(2,1)S(1)} %get-tuple-element.64.refs_0_, bf16[512,512]{1,0:T(8,128)(2,1)S(1)} %get-tuple-element.65.refs_1_, bf16[512,512]{1,0:T(8,128)(2,1)S(1)} %get-tuple-element.66.refs_2_, ...), custom_call_target="tpu_custom_call" | custom-call | flops 1024 | bytes 1024 | tf_op jit(solution)/shard_map/pallas_call | solution.py:52
  49.2 4.9 %all-to-all-start = ((bf16[8,64,384]{2,1,0:T(8,128)(2,1)}), bf16[8,64,384]{2,1,0:T(8,128)(2,1)}, u32[]{:S(2)}, u32[]{:S(2)}) async-start(bf16[8,64,384]{2,1,0:T(8,128)(2,1)} %bitcast.14), calls=%async_computation | async-start | bytes 786432 | tf_op jit(solution)/shard_map/all_to_all | solution.py:443
  57.8 6.8 %shard_map.131 = bf16[512,384]{1,0:T(8,128)(2,1)} custom-call(f32[512,768]{1,0:T(8,128)} %get-tuple-element.63.old_ref, bf16[512,512]{1,0:T(8,128)(2,1)} %copy-done.6, bf16[512,512]{1,0:T(8,128)(2,1)} %copy-done.7, bf16[512,512]{1,0:T(8,128)(2,1)} %copy-done.8, bf16[512,512]{1,0:T(8,128)(2,1)} %copy-done.9, bf16[512,512]{1,0:T(8,128)(2,1)} %copy-done.10, ...), custom_call_target="tpu_custom_call" | custom-call | flops 1024 | bytes 1024 | tf_op jit(solution)/shard_map/pallas_call | solution.py:52
  64.6 1.3 all-to-all-done
  65.9 4.7 %all-to-all-start.1 = ((bf16[8,64,384]{2,1,0:T(8,128)(2,1)}), bf16[8,64,384]{2,1,0:T(8,128)(2,1)}, u32[]{:S(2)}, u32[]{:S(2)}) async-start(bf16[8,64,384]{2,1,0:T(8,128)(2,1)} %bitcast.76), calls=%async_computation.1 | async-start | bytes 786432 | tf_op jit(solution)/shard_map/all_to_all | solution.py:443
  71.6 11.0 %all-to-all-done.1 = bf16[8,64,384]{2,1,0:T(8,128)(2,1)} async-done(((bf16[8,64,384]{2,1,0:T(8,128)(2,1)}), bf16[8,64,384]{2,1,0:T(8,128)(2,1)}, u32[]{:S(2)}, u32[]{:S(2)}) %all-to-all-start.1) | async-done | bytes 393248 | tf_op jit(solution)/shard_map/all_to_all | solution.py:443
  82.6 2.3 %shard_map.132 = (bf16[512,768]{1,0:T(8,128)(2,1)S(1)}, bf16[256,768]{1,0:T(8,128)(2,1)S(1)}, bf16[256,768]{1,0:T(8,128)(2,1)S(1)}, bf16[256,384]{1,0:T(8,128)(2,1)S(1)}, bf16[256,384]{1,0:T(8,128)(2,1)S(1)}) custom-call(s32[1,512]{1,0:T(1,128)S(1)} %compare_select_fusion.target_ref, bf16[512,384]{1,0:T(8,128)(2,1)} %bitcast.15.left_ref, ...), custom_call_target="tpu_custom_call" | custom-call | flops 1024 | bytes 1024 | tf_op jit(solution)/shard_map/pallas_call | solution.py:52
  84.9 3.4 %collective-permute-start.17 = (bf16[256,384]{1,0:T(8,128)(2,1)S(1)}, bf16[256,384]{1,0:T(8,128)(2,1)S(1)}, u32[]{:S(2)}, u32[]{:S(2)}) collective-permute-start(bf16[256,384]{1,0:T(8,128)(2,1)S(1)} %get-tuple-element.77), channel_id=1, source_target_pairs={{0,1},{1,2},{2,3},{3,4},{4,5},{5,6},{6,7},{8,9},{9,10},{10,11},{11... | collective-permute-start | bytes 589832 | tf_op jit(solution)/shard_map/ppermute | solution.py:341
  88.3 1.5 collective-permute-start.18
  90.8 5.2 %collective-permute-done.17.prev_ref = bf16[256,384]{1,0:T(8,128)(2,1)S(1)} collective-permute-done((bf16[256,384]{1,0:T(8,128)(2,1)S(1)}, bf16[256,384]{1,0:T(8,128)(2,1)S(1)}, u32[]{:S(2)}, u32[]{:S(2)}) %collective-permute-start.17) | collective-permute-done | bytes 196640 | tf_op jit(solution)/shard_map/ppermute | solution.py:341
  96.8 4.5 %collective-permute-start.19 = (bf16[128,384]{1,0:T(8,128)(2,1)S(1)}, bf16[128,384]{1,0:T(8,128)(2,1)S(1)}, u32[]{:S(2)}, u32[]{:S(2)}) collective-permute-start(bf16[128,384]{1,0:T(8,128)(2,1)S(1)} %get-tuple-element.82), channel_id=1, source_target_pairs={{0,1},{1,2},{2,3},{3,4},{4,5},{5,6},{6,7},{8,9},{9,10},{10,11},{11... | collective-permute-start | bytes 294920 | tf_op jit(solution)/shard_map/ppermute | solution.py:341
  101.3 1.3 collective-permute-start.20
  103.5 4.3 %collective-permute-done.20.refs_4_ = bf16[128,384]{1,0:T(8,128)(2,1)S(1)} collective-permute-done((bf16[128,384]{1,0:T(8,128)(2,1)S(1)}, bf16[128,384]{1,0:T(8,128)(2,1)S(1)}, u32[]{:S(2)}, u32[]{:S(2)}) %collective-permute-start.20) | collective-permute-done | bytes 98336 | tf_op jit(solution)/shard_map/ppermute | solution.py:342
  107.8 3.7 %shard_map.135 = (bf16[256,384]{1,0:T(8,128)(2,1)S(1)}, bf16[128,768]{1,0:T(8,128)(2,1)S(1)}, bf16[128,2048]{1,0:T(8,128)(2,1)S(1)}, bf16[128,768]{1,0:T(8,128)(...) custom-call(s32[2]{0:T(128)S(1)} %get-tuple-element.128.refs_0_, ...), custom_call_target="tpu_custom_call" | custom-call | flops 1024 | bytes 1024 | tf_op jit(solution)/shard_map/pallas_call | solution.py:52
  111.6 1.5 shard_map.136
  113.2 4.0 %collective-permute-start.22 = (bf16[128,384]{1,0:T(8,128)(2,1)S(1)}, bf16[128,384]{1,0:T(8,128)(2,1)S(1)}, u32[]{:S(2)}, u32[]{:S(2)}) collective-permute-start(bf16[128,384]{1,0:T(8,128)(2,1)S(1)} %get-tuple-element.91.refs_3_.refs_6_), channel_id=1, source_target_pairs={{0,1},{1,2},{2,3},{3,4},{4,5},{5,6},{6,7},{8,9},{9,10},{10,11},{11... | collective-permute-start | bytes 294920 | tf_op jit(solution)/shard_map/ppermute | solution.py:341
  117.2 1.3 collective-permute-start.23
  119.9 4.1 %collective-permute-done.23.refs_4_.refs_7_ = bf16[128,384]{1,0:T(8,128)(2,1)S(1)} collective-permute-done((bf16[128,384]{1,0:T(8,128)(2,1)S(1)}, bf16[128,384]{1,0:T(8,128)(2,1)S(1)}, u32[]{:S(2)}, u32[]{:S(2)}) %collective-permute-start.23) | collective-permute-done | bytes 98336 | tf_op jit(solution)/shard_map/ppermute | solution.py:342
  124.5 2.5 %shard_map.137 = (f32[256,768]{1,0:T(8,128)}, bf16[256,768]{1,0:T(8,128)(2,1)S(1)}, bf16[256,384]{1,0:T(8,128)(2,1)S(1)}, bf16[256,384]{1,0:T(8,128)(2,1)S(1)}) custom-call(bf16[768,512]{1,0:T(8,128)(2,1)S(1)} %fusion.2.refs_0_, bf16[128,384]{1,0:T(8,128)(2,1)S(1)} %collective-permute-done.22.refs_1_.refs_4_, ...), custom_call_target="tpu_custom_call" | custom-call | flops 1024 | bytes 1024 | tf_op jit(solution)/shard_map/pallas_call | solution.py:52
  127.0 3.2 %collective-permute-start.24 = (bf16[256,384]{1,0:T(8,128)(2,1)S(1)}, bf16[256,384]{1,0:T(8,128)(2,1)S(1)}, u32[]{:S(2)}, u32[]{:S(2)}) collective-permute-start(bf16[256,384]{1,0:T(8,128)(2,1)S(1)} %get-tuple-element.99.refs_6_), channel_id=1, source_target_pairs={{0,1},{1,2},{2,3},{3,4},{4,5},{5,6},{6,7},{8,9},{9,10},{10,11},{11... | collective-permute-start | bytes 589832 | tf_op jit(solution)/shard_map/ppermute | solution.py:341
  131.5 4.2 %shard_map.138 = (bf16[2,768,384]{2,1,0:T(8,128)(2,1)S(1)}, bf16[2,768,384]{2,1,0:T(8,128)(2,1)S(1)}) custom-call(s32[2]{0:T(128)S(1)} %get-tuple-element.127.ids_ref.refs_0_, bf16[256,384]{1,0:T(8,128)(2,1)S(1)} %get-tuple-element.98.refs_1_.refs_5_, bf16[128,768]{1,0:T(8,128)(2,1)S(1)} %get-tuple-element.83.refs_2_, ...), custom_call_target="tpu_custom_call" | custom-call | flops 1024 | bytes 1024 | tf_op jit(solution)/shard_map/pallas_call | solution.py:52
  135.8 2.1 %collective-permute-done.25.refs_7_ = bf16[256,384]{1,0:T(8,128)(2,1)S(1)} collective-permute-done((bf16[256,384]{1,0:T(8,128)(2,1)S(1)}, bf16[256,384]{1,0:T(8,128)(2,1)S(1)}, u32[]{:S(2)}, u32[]{:S(2)}) %collective-permute-start.25) | collective-permute-done | bytes 196640 | tf_op jit(solution)/shard_map/ppermute | solution.py:342
  137.9 6.3 %shard_map.139 = (bf16[768,384]{1,0:T(8,128)(2,1)S(1)}, bf16[768,384]{1,0:T(8,128)(2,1)S(1)}, bf16[2,768,384]{2,1,0:T(8,128)(2,1)}) custom-call(s32[2]{0:T(128)S(1)} %get-tuple-element.127.ids_ref.refs_0_, bf16[256,384]{1,0:T(8,128)(2,1)S(1)} %get-tuple-element.98.refs_1_.refs_5_, bf16[256,768]{1,0:T(8,128)(2,1)S(1)} %get-tuple-element.79.low_ref.refs_2_, ...), custom_call_target="tpu_custom_call" | custom-call | flops 1024 | bytes 1024 | tf_op jit(solution)/shard_map/pallas_call | solution.py:52
  145.7 2.2 %fusion.3 = bf16[2,4,96,384]{3,2,1,0:T(8,128)(2,1)} fusion(bf16[2,4,2,96,384]{4,3,2,1,0:T(8,128)(2,1)} %bitcast.27, s32[]{:T(128)S(6)} %select_n.102, bf16[2,4,2,96,384]{4,3,2,1,0:T(8,128)(2,1)S(1)} %bitcast.70), kind=kLoop, calls=%fused_computation.9 | loop fusion | flops 1179648 | bytes 1769476 | tf_op jit(solution)/shard_map/convert_element_type | solution.py:383
  147.9 2.6 %collective-permute-start.31 = (bf16[2,4,96,384]{3,2,1,0:T(8,128)(2,1)}, bf16[2,4,96,384]{3,2,1,0:T(8,128)(2,1)}, u32[]{:S(2)}, u32[]{:S(2)}) collective-permute-start(bf16[2,4,96,384]{3,2,1,0:T(8,128)(2,1)} %fusion.3), channel_id=1, source_target_pairs={{0,1},{1,0},{2,3},{3,2},{4,5},{5,4},{6,7},{7,6},{8,9},{9,8},{10,11... | collective-permute-start | bytes 1769480 | tf_op jit(solution)/shard_map/ppermute | solution.py:334
  151.7 2.4 %fusion = bf16[768,512]{1,0:T(8,128)(2,1)} fusion(bf16[768,512]{1,0:T(8,128)(2,1)} %copy-done.19, bf16[2,768,512]{2,1,0:T(8,128)(2,1)S(1)} %copy-done.18, bf16[2,768,512]{2,1,0:T(8,128)(2,1)S(1)} %copy-done.15), kind=kLoop, calls=%fused_computation.1 | loop fusion | flops 2359296 | bytes 3145728 | tf_op jit(solution)/shard_map/convert_element_type | solution.py:394
  154.1 4.1 %all-to-all-start.2 = ((bf16[8,96,512]{2,1,0:T(8,128)(2,1)}), bf16[8,96,512]{2,1,0:T(8,128)(2,1)S(1)}, u32[]{:S(2)}, u32[]{:S(2)}) async-start(bf16[8,96,512]{2,1,0:T(8,128)(2,1)} %bitcast.33), calls=%async_computation.2 | async-start | bytes 1572864 | tf_op jit(solution)/shard_map/all_to_all | solution.py:356
  158.2 1.5 collective-permute-start.28
  159.6 10.1 %collective-permute-done.31 = bf16[2,4,96,384]{3,2,1,0:T(8,128)(2,1)} collective-permute-done((bf16[2,4,96,384]{3,2,1,0:T(8,128)(2,1)}, bf16[2,4,96,384]{3,2,1,0:T(8,128)(2,1)}, u32[]{:S(2)}, u32[]{:S(2)}) %collective-permute-start.31) | collective-permute-done | bytes 589856 | tf_op jit(solution)/shard_map/ppermute | solution.py:334
  169.8 1.4 bitcast_add_fusion.1
  171.2 1.6 collective-permute-start.32
  175.5 2.3 %collective-permute-start.29 = (bf16[4,96,384]{2,1,0:T(8,128)(2,1)S(1)}, bf16[4,96,384]{2,1,0:T(8,128)(2,1)S(1)}, u32[]{:S(2)}, u32[]{:S(2)}) collective-permute-start(bf16[4,96,384]{2,1,0:T(8,128)(2,1)S(1)} %get-tuple-element.125), channel_id=1, source_target_pairs={{0,1},{1,0},{2,3},{3,2},{4,5},{5,4},{6,7},{7,6},{8,9},{9,8},{10,11... | collective-permute-start | bytes 884744 | tf_op jit(solution)/shard_map/ppermute | solution.py:334
  177.8 1.4 collective-permute-done.32.right_came_ref
  179.2 3.4 %collective-permute-done.29.left_came_ref = bf16[4,96,384]{2,1,0:T(8,128)(2,1)S(1)} collective-permute-done((bf16[4,96,384]{2,1,0:T(8,128)(2,1)S(1)}, bf16[4,96,384]{2,1,0:T(8,128)(2,1)S(1)}, u32[]{:S(2)}, u32[]{:S(2)}) %collective-permute-start.29) | collective-permute-done | bytes 294944 | tf_op jit(solution)/shard_map/ppermute | solution.py:334
  183.5 5.5 %all-to-all-start.3 = ((bf16[4,96,768]{2,1,0:T(8,128)(2,1)}), bf16[4,96,768]{2,1,0:T(8,128)(2,1)S(1)}, u32[]{:S(2)}, u32[]{:S(2)}) async-start(bf16[4,96,768]{2,1,0:T(8,128)(2,1)} %shard_map.140), calls=%async_computation.3 | async-start | bytes 1179648 | tf_op jit(solution)/shard_map/all_to_all | solution.py:397
  189.8 10.5 %all-to-all-done.3.parts_ref = bf16[4,96,768]{2,1,0:T(8,128)(2,1)S(1)} async-done(((bf16[4,96,768]{2,1,0:T(8,128)(2,1)}), bf16[4,96,768]{2,1,0:T(8,128)(2,1)S(1)}, u32[]{:S(2)}, u32[]{:S(2)}) %all-to-all-start.3) | async-done | bytes 589856 | tf_op jit(solution)/shard_map/all_to_all | solution.py:397
  (112 shorter events, 20.9 us)
Async XLA Ops:
  0.6 18.3 %collective-permute-start.1 = (bf16[2048,768]{1,0:T(8,128)(2,1)}, bf16[2048,768]{1,0:T(8,128)(2,1)}, u32[]{:S(2)}, u32[]{:S(2)}) collective-permute-start(bf16[2048,768]{1,0:T(8,128)(2,1)} %refs_0_.1), channel_id=1, source_target_pairs={{0,8},{8,0},{16,24},{24,16},{1,9},{9,1},{17,25},{25,17},{2,10},{10... | collective-permute-start | bytes 9437192 | tf_op jit(solution)/shard_map/ppermute | solution.py:334
  2.8 12.6 %collective-permute-start.5 = (bf16[512,384]{1,0:T(8,128)(2,1)S(1)}, bf16[512,384]{1,0:T(8,128)(2,1)S(1)}, u32[]{:S(2)}, u32[]{:S(2)}) collective-permute-start(bf16[512,384]{1,0:T(8,128)(2,1)S(1)} %get-tuple-element.122), channel_id=1, source_target_pairs={{0,16},{8,24},{16,0},{24,8},{1,17},{9,25},{17,1},{25,9},{2,18},{10... | collective-permute-start | bytes 1179656 | tf_op jit(solution)/shard_map/ppermute | solution.py:334
  5.4 23.9 %collective-permute-start = (bf16[512,384]{1,0:T(8,128)(2,1)S(1)}, bf16[512,384]{1,0:T(8,128)(2,1)S(1)}, u32[]{:S(2)}, u32[]{:S(2)}) collective-permute-start(bf16[512,384]{1,0:T(8,128)(2,1)S(1)} %get-tuple-element.123), channel_id=1, source_target_pairs={{0,16},{8,24},{16,0},{24,8},{1,17},{9,25},{17,1},{25,9},{2,18},{10... | collective-permute-start | bytes 1179656 | tf_op jit(solution)/shard_map/ppermute | solution.py:334
  15.4 14.6 %collective-permute-start.7 = (bf16[512,384]{1,0:T(8,128)(2,1)S(1)}, bf16[512,384]{1,0:T(8,128)(2,1)S(1)}, u32[]{:S(2)}, u32[]{:S(2)}) collective-permute-start(bf16[512,384]{1,0:T(8,128)(2,1)S(1)} %collective-permute-done.5.refs_12_), channel_id=1, source_target_pairs={{0,1},{1,0},{2,3},{3,2},{4,5},{5,4},{6,7},{7,6},{8,9},{9,8},{10,11... | collective-permute-start | bytes 1179656 | tf_op jit(solution)/shard_map/ppermute | solution.py:334
  17.4 14.9 %collective-permute-start.9 = (bf16[512,384]{1,0:T(8,128)(2,1)S(1)}, bf16[512,384]{1,0:T(8,128)(2,1)S(1)}, u32[]{:S(2)}, u32[]{:S(2)}) collective-permute-start(bf16[512,384]{1,0:T(8,128)(2,1)S(1)} %get-tuple-element.124), channel_id=1, source_target_pairs={{0,16},{8,24},{16,0},{24,8},{1,17},{9,25},{17,1},{25,9},{2,18},{10... | collective-permute-start | bytes 1179656 | tf_op jit(solution)/shard_map/ppermute | solution.py:334
  29.3 19.0 %copy-start.6 = (bf16[512,512]{1,0:T(8,128)(2,1)}, bf16[512,512]{1,0:T(8,128)(2,1)S(1)}, u32[]{:S(2)}) copy-start(bf16[512,512]{1,0:T(8,128)(2,1)S(1)} %get-tuple-element.64.refs_0_) | copy-start | bytes 1572868
  29.3 19.0 %copy-start.7 = (bf16[512,512]{1,0:T(8,128)(2,1)}, bf16[512,512]{1,0:T(8,128)(2,1)S(1)}, u32[]{:S(2)}) copy-start(bf16[512,512]{1,0:T(8,128)(2,1)S(1)} %get-tuple-element.65.refs_1_) | copy-start | bytes 1572868
  29.3 19.0 %copy-start.8 = (bf16[512,512]{1,0:T(8,128)(2,1)}, bf16[512,512]{1,0:T(8,128)(2,1)S(1)}, u32[]{:S(2)}) copy-start(bf16[512,512]{1,0:T(8,128)(2,1)S(1)} %get-tuple-element.66.refs_2_) | copy-start | bytes 1572868
  29.3 19.0 %copy-start.9 = (bf16[512,512]{1,0:T(8,128)(2,1)}, bf16[512,512]{1,0:T(8,128)(2,1)S(1)}, u32[]{:S(2)}) copy-start(bf16[512,512]{1,0:T(8,128)(2,1)S(1)} %get-tuple-element.67.refs_3_) | copy-start | bytes 1572868
  29.3 19.0 %copy-start.10 = (bf16[512,512]{1,0:T(8,128)(2,1)}, bf16[512,512]{1,0:T(8,128)(2,1)S(1)}, u32[]{:S(2)}) copy-start(bf16[512,512]{1,0:T(8,128)(2,1)S(1)} %get-tuple-element.68.refs_4_) | copy-start | bytes 1572868
  29.3 19.0 %copy-start.11 = (bf16[512,512]{1,0:T(8,128)(2,1)}, bf16[512,512]{1,0:T(8,128)(2,1)S(1)}, u32[]{:S(2)}) copy-start(bf16[512,512]{1,0:T(8,128)(2,1)S(1)} %get-tuple-element.69.refs_5_) | copy-start | bytes 1572868
  29.3 19.0 %copy-start.12 = (bf16[512,512]{1,0:T(8,128)(2,1)}, bf16[512,512]{1,0:T(8,128)(2,1)S(1)}, u32[]{:S(2)}) copy-start(bf16[512,512]{1,0:T(8,128)(2,1)S(1)} %get-tuple-element.70.refs_6_) | copy-start | bytes 1572868
  29.3 19.0 %copy-start.13 = (bf16[512,512]{1,0:T(8,128)(2,1)}, bf16[512,512]{1,0:T(8,128)(2,1)S(1)}, u32[]{:S(2)}) copy-start(bf16[512,512]{1,0:T(8,128)(2,1)S(1)} %get-tuple-element.71.refs_7_) | copy-start | bytes 1572868
  29.4 9.7 %collective-permute-start.3 = (bf16[512,384]{1,0:T(8,128)(2,1)S(1)}, bf16[512,384]{1,0:T(8,128)(2,1)S(1)}, u32[]{:S(2)}, u32[]{:S(2)}) collective-permute-start(bf16[512,384]{1,0:T(8,128)(2,1)S(1)} %collective-permute-done.refs_8_), channel_id=1, source_target_pairs={{0,1},{1,0},{2,3},{3,2},{4,5},{5,4},{6,7},{7,6},{8,9},{9,8},{10,11... | collective-permute-start | bytes 1179656 | tf_op jit(solution)/shard_map/ppermute | solution.py:334
  29.9 10.5 %collective-permute-start.11 = (bf16[512,384]{1,0:T(8,128)(2,1)S(1)}, bf16[512,384]{1,0:T(8,128)(2,1)S(1)}, u32[]{:S(2)}, u32[]{:S(2)}) collective-permute-start(bf16[512,384]{1,0:T(8,128)(2,1)S(1)} %get-tuple-element.121), channel_id=1, source_target_pairs={{0,16},{8,24},{16,0},{24,8},{1,17},{9,25},{17,1},{25,9},{2,18},{10... | collective-permute-start | bytes 1179656 | tf_op jit(solution)/shard_map/ppermute | solution.py:334
  30.0 10.4 %collective-permute-start.6 = (bf16[512,384]{1,0:T(8,128)(2,1)S(1)}, bf16[512,384]{1,0:T(8,128)(2,1)S(1)}, u32[]{:S(2)}, u32[]{:S(2)}) collective-permute-start(bf16[512,384]{1,0:T(8,128)(2,1)S(1)} %collective-permute-done.5.refs_12_), channel_id=1, source_target_pairs={{0,8},{8,0},{16,24},{24,16},{1,9},{9,1},{17,25},{25,17},{2,10},{10... | collective-permute-start | bytes 1179656 | tf_op jit(solution)/shard_map/ppermute | solution.py:334
  30.0 12.2 %collective-permute-start.8 = (bf16[512,384]{1,0:T(8,128)(2,1)S(1)}, bf16[512,384]{1,0:T(8,128)(2,1)S(1)}, u32[]{:S(2)}, u32[]{:S(2)}) collective-permute-start(bf16[512,384]{1,0:T(8,128)(2,1)S(1)} %collective-permute-done.7.refs_14_), channel_id=1, source_target_pairs={{0,8},{8,0},{16,24},{24,16},{1,9},{9,1},{17,25},{25,17},{2,10},{10... | collective-permute-start | bytes 1179656 | tf_op jit(solution)/shard_map/ppermute | solution.py:334
  32.2 16.1 %copy-start.20 = (bf16[512,384]{1,0:T(8,128)(2,1)}, bf16[512,384]{1,0:T(8,128)(2,1)S(1)}, u32[]{:S(2)}) copy-start(bf16[512,384]{1,0:T(8,128)(2,1)S(1)} %collective-permute-done.9.refs_14_) | copy-start | bytes 1179652
  32.2 11.5 %collective-permute-start.2 = (bf16[512,384]{1,0:T(8,128)(2,1)S(1)}, bf16[512,384]{1,0:T(8,128)(2,1)S(1)}, u32[]{:S(2)}, u32[]{:S(2)}) collective-permute-start(bf16[512,384]{1,0:T(8,128)(2,1)S(1)} %collective-permute-done.refs_8_), channel_id=1, source_target_pairs={{0,8},{8,0},{16,24},{24,16},{1,9},{9,1},{17,25},{25,17},{2,10},{10... | collective-permute-start | bytes 1179656 | tf_op jit(solution)/shard_map/ppermute | solution.py:334
  39.1 4.7 %collective-permute-start.4 = (bf16[512,384]{1,0:T(8,128)(2,1)S(1)}, bf16[512,384]{1,0:T(8,128)(2,1)S(1)}, u32[]{:S(2)}, u32[]{:S(2)}) collective-permute-start(bf16[512,384]{1,0:T(8,128)(2,1)S(1)} %collective-permute-done.3.refs_10_), channel_id=1, source_target_pairs={{0,8},{8,0},{16,24},{24,16},{1,9},{9,1},{17,25},{25,17},{2,10},{10... | collective-permute-start | bytes 1179656 | tf_op jit(solution)/shard_map/ppermute | solution.py:334
  40.4 7.9 %collective-permute-start.10 = (bf16[512,384]{1,0:T(8,128)(2,1)S(1)}, bf16[512,384]{1,0:T(8,128)(2,1)S(1)}, u32[]{:S(2)}, u32[]{:S(2)}) collective-permute-start(bf16[512,384]{1,0:T(8,128)(2,1)S(1)} %collective-permute-done.9.refs_14_), channel_id=1, source_target_pairs={{0,8},{8,0},{16,24},{24,16},{1,9},{9,1},{17,25},{25,17},{2,10},{10... | collective-permute-start | bytes 1179656 | tf_op jit(solution)/shard_map/ppermute | solution.py:334
  40.4 13.7 %collective-permute-start.15 = (bf16[512,384]{1,0:T(8,128)(2,1)S(1)}, bf16[512,384]{1,0:T(8,128)(2,1)S(1)}, u32[]{:S(2)}, u32[]{:S(2)}) collective-permute-start(bf16[512,384]{1,0:T(8,128)(2,1)S(1)} %get-tuple-element.120), channel_id=1, source_target_pairs={{0,16},{8,24},{16,0},{24,8},{1,17},{9,25},{17,1},{25,9},{2,18},{10... | collective-permute-start | bytes 1179656 | tf_op jit(solution)/shard_map/ppermute | solution.py:334
  42.3 12.4 %collective-permute-start.13 = (bf16[512,384]{1,0:T(8,128)(2,1)S(1)}, bf16[512,384]{1,0:T(8,128)(2,1)S(1)}, u32[]{:S(2)}, u32[]{:S(2)}) collective-permute-start(bf16[512,384]{1,0:T(8,128)(2,1)S(1)} %collective-permute-done.11.refs_8_), channel_id=1, source_target_pairs={{0,1},{1,0},{2,3},{3,2},{4,5},{5,4},{6,7},{7,6},{8,9},{9,8},{10,11... | collective-permute-start | bytes 1179656 | tf_op jit(solution)/shard_map/ppermute | solution.py:334
  49.2 16.7 %all-to-all-start = ((bf16[8,64,384]{2,1,0:T(8,128)(2,1)}), bf16[8,64,384]{2,1,0:T(8,128)(2,1)}, u32[]{:S(2)}, u32[]{:S(2)}) async-start(bf16[8,64,384]{2,1,0:T(8,128)(2,1)} %bitcast.14), calls=%async_computation | async-start | bytes 786432 | tf_op jit(solution)/shard_map/all_to_all | solution.py:443
  54.1 16.5 %copy-start.27 = (s32[1,8,8]{2,1,0:T(8,128)S(1)}, s32[1,8,8]{2,1,0:T(8,128)}, u32[]{:S(2)}) copy-start(s32[1,8,8]{2,1,0:T(8,128)} %param.11) | copy-start | bytes 772
  54.1 1.8 collective-permute-start.12
  54.2 2.8 %collective-permute-start.16 = (bf16[512,384]{1,0:T(8,128)(2,1)S(1)}, bf16[512,384]{1,0:T(8,128)(2,1)S(1)}, u32[]{:S(2)}, u32[]{:S(2)}) collective-permute-start(bf16[512,384]{1,0:T(8,128)(2,1)S(1)} %collective-permute-done.15.refs_12_), channel_id=1, source_target_pairs={{0,8},{8,0},{16,24},{24,16},{1,9},{9,1},{17,25},{25,17},{2,10},{10... | collective-permute-start | bytes 1179656 | tf_op jit(solution)/shard_map/ppermute | solution.py:334
  54.7 3.1 %collective-permute-start.14 = (bf16[512,384]{1,0:T(8,128)(2,1)S(1)}, bf16[512,384]{1,0:T(8,128)(2,1)}, u32[]{:S(2)}, u32[]{:S(2)}) collective-permute-start(bf16[512,384]{1,0:T(8,128)(2,1)S(1)} %collective-permute-done.13.refs_10_), channel_id=1, source_target_pairs={{0,8},{8,0},{16,24},{24,16},{1,9},{9,1},{17,25},{25,17},{2,10},{10... | collective-permute-start | bytes 1179656 | tf_op jit(solution)/shard_map/ppermute | solution.py:334
  57.8 24.9 %copy-start = (bf16[2,3,768,384]{3,2,1,0:T(8,128)(2,1)S(1)}, bf16[2,3,768,384]{3,2,1,0:T(8,128)(2,1)}, u32[]{:S(2)}) copy-start(bf16[2,3,768,384]{3,2,1,0:T(8,128)(2,1)} %refs_7_.3) | copy-start | bytes 10616836
  65.9 16.8 %all-to-all-start.1 = ((bf16[8,64,384]{2,1,0:T(8,128)(2,1)}), bf16[8,64,384]{2,1,0:T(8,128)(2,1)}, u32[]{:S(2)}, u32[]{:S(2)}) async-start(bf16[8,64,384]{2,1,0:T(8,128)(2,1)} %bitcast.76), calls=%async_computation.1 | async-start | bytes 786432 | tf_op jit(solution)/shard_map/all_to_all | solution.py:443
  84.9 11.0 %collective-permute-start.17 = (bf16[256,384]{1,0:T(8,128)(2,1)S(1)}, bf16[256,384]{1,0:T(8,128)(2,1)S(1)}, u32[]{:S(2)}, u32[]{:S(2)}) collective-permute-start(bf16[256,384]{1,0:T(8,128)(2,1)S(1)} %get-tuple-element.77), channel_id=1, source_target_pairs={{0,1},{1,2},{2,3},{3,4},{4,5},{5,6},{6,7},{8,9},{9,10},{10,11},{11... | collective-permute-start | bytes 589832 | tf_op jit(solution)/shard_map/ppermute | solution.py:341
  88.3 7.6 %collective-permute-start.18 = (bf16[256,384]{1,0:T(8,128)(2,1)S(1)}, bf16[256,384]{1,0:T(8,128)(2,1)S(1)}, u32[]{:S(2)}, u32[]{:S(2)}) collective-permute-start(bf16[256,384]{1,0:T(8,128)(2,1)S(1)} %get-tuple-element.78), channel_id=1, source_target_pairs={{1,0},{2,1},{3,2},{4,3},{5,4},{6,5},{7,6},{9,8},{10,9},{11,10},{12... | collective-permute-start | bytes 589832 | tf_op jit(solution)/shard_map/ppermute | solution.py:342
  96.8 6.7 %collective-permute-start.19 = (bf16[128,384]{1,0:T(8,128)(2,1)S(1)}, bf16[128,384]{1,0:T(8,128)(2,1)S(1)}, u32[]{:S(2)}, u32[]{:S(2)}) collective-permute-start(bf16[128,384]{1,0:T(8,128)(2,1)S(1)} %get-tuple-element.82), channel_id=1, source_target_pairs={{0,1},{1,2},{2,3},{3,4},{4,5},{5,6},{6,7},{8,9},{9,10},{10,11},{11... | collective-permute-start | bytes 294920 | tf_op jit(solution)/shard_map/ppermute | solution.py:341
  101.3 6.5 %collective-permute-start.20 = (bf16[128,384]{1,0:T(8,128)(2,1)S(1)}, bf16[128,384]{1,0:T(8,128)(2,1)S(1)}, u32[]{:S(2)}, u32[]{:S(2)}) collective-permute-start(bf16[128,384]{1,0:T(8,128)(2,1)S(1)} %get-tuple-element.85), channel_id=1, source_target_pairs={{1,0},{2,1},{3,2},{4,3},{5,4},{6,5},{7,6},{9,8},{10,9},{11,10},{12... | collective-permute-start | bytes 294920 | tf_op jit(solution)/shard_map/ppermute | solution.py:342
  113.1 5.4 %collective-permute-start.21 = (bf16[2,768,512]{2,1,0:T(8,128)(2,1)S(1)}, bf16[2,768,512]{2,1,0:T(8,128)(2,1)S(1)}, u32[]{:S(2)}, u32[]{:S(2)}) collective-permute-start(bf16[2,768,512]{2,1,0:T(8,128)(2,1)S(1)} %get-tuple-element.90), channel_id=1, source_target_pairs={{0,8},{8,0},{16,24},{24,16},{1,9},{9,1},{17,25},{25,17},{2,10},{10... | collective-permute-start | bytes 4718600 | tf_op jit(solution)/shard_map/ppermute | solution.py:334
  113.2 6.7 %collective-permute-start.22 = (bf16[128,384]{1,0:T(8,128)(2,1)S(1)}, bf16[128,384]{1,0:T(8,128)(2,1)S(1)}, u32[]{:S(2)}, u32[]{:S(2)}) collective-permute-start(bf16[128,384]{1,0:T(8,128)(2,1)S(1)} %get-tuple-element.91.refs_3_.refs_6_), channel_id=1, source_target_pairs={{0,1},{1,2},{2,3},{3,4},{4,5},{5,6},{6,7},{8,9},{9,10},{10,11},{11... | collective-permute-start | bytes 294920 | tf_op jit(solution)/shard_map/ppermute | solution.py:341
  117.2 6.8 %collective-permute-start.23 = (bf16[128,384]{1,0:T(8,128)(2,1)S(1)}, bf16[128,384]{1,0:T(8,128)(2,1)S(1)}, u32[]{:S(2)}, u32[]{:S(2)}) collective-permute-start(bf16[128,384]{1,0:T(8,128)(2,1)S(1)} %get-tuple-element.92.refs_2_.refs_5_), channel_id=1, source_target_pairs={{1,0},{2,1},{3,2},{4,3},{5,4},{6,5},{7,6},{9,8},{10,9},{11,10},{12... | collective-permute-start | bytes 294920 | tf_op jit(solution)/shard_map/ppermute | solution.py:342
  124.0 20.3 %collective-permute-start.26 = (bf16[768,512]{1,0:T(8,128)(2,1)S(1)}, bf16[768,512]{1,0:T(8,128)(2,1)S(1)}, u32[]{:S(2)}, u32[]{:S(2)}) collective-permute-start(bf16[768,512]{1,0:T(8,128)(2,1)S(1)} %fusion.2.refs_0_), channel_id=1, source_target_pairs={{0,16},{8,24},{16,0},{24,8},{1,17},{9,25},{17,1},{25,9},{2,18},{10... | collective-permute-start | bytes 2359304 | tf_op jit(solution)/shard_map/ppermute | solution.py:334
  127.0 8.8 %collective-permute-start.24 = (bf16[256,384]{1,0:T(8,128)(2,1)S(1)}, bf16[256,384]{1,0:T(8,128)(2,1)S(1)}, u32[]{:S(2)}, u32[]{:S(2)}) collective-permute-start(bf16[256,384]{1,0:T(8,128)(2,1)S(1)} %get-tuple-element.99.refs_6_), channel_id=1, source_target_pairs={{0,1},{1,2},{2,3},{3,4},{4,5},{5,6},{6,7},{8,9},{9,10},{10,11},{11... | collective-permute-start | bytes 589832 | tf_op jit(solution)/shard_map/ppermute | solution.py:341
  130.2 7.7 %collective-permute-start.25 = (bf16[256,384]{1,0:T(8,128)(2,1)S(1)}, bf16[256,384]{1,0:T(8,128)(2,1)S(1)}, u32[]{:S(2)}, u32[]{:S(2)}) collective-permute-start(bf16[256,384]{1,0:T(8,128)(2,1)S(1)} %get-tuple-element.98.refs_1_.refs_5_), channel_id=1, source_target_pairs={{1,0},{2,1},{3,2},{4,3},{5,4},{6,5},{7,6},{9,8},{10,9},{11,10},{12... | collective-permute-start | bytes 589832 | tf_op jit(solution)/shard_map/ppermute | solution.py:342
  137.9 7.8 %collective-permute-start.30 = (bf16[2,768,384]{2,1,0:T(8,128)(2,1)S(1)}, bf16[2,768,384]{2,1,0:T(8,128)(2,1)}, u32[]{:S(2)}, u32[]{:S(2)}) collective-permute-start(bf16[2,768,384]{2,1,0:T(8,128)(2,1)S(1)} %get-tuple-element.113), channel_id=1, source_target_pairs={{0,8},{8,0},{16,24},{24,16},{1,9},{9,1},{17,25},{25,17},{2,10},{10... | collective-permute-start | bytes 3538952 | tf_op jit(solution)/shard_map/ppermute | solution.py:334
  145.2 5.2 %collective-permute-start.27 = (bf16[2,768,384]{2,1,0:T(8,128)(2,1)}, bf16[2,768,384]{2,1,0:T(8,128)(2,1)}, u32[]{:S(2)}, u32[]{:S(2)}) collective-permute-start(bf16[2,768,384]{2,1,0:T(8,128)(2,1)} %get-tuple-element.108), channel_id=1, source_target_pairs={{0,8},{8,0},{16,24},{24,16},{1,9},{9,1},{17,25},{25,17},{2,10},{10... | collective-permute-start | bytes 3538952 | tf_op jit(solution)/shard_map/ppermute | solution.py:334
  147.9 21.9 %collective-permute-start.31 = (bf16[2,4,96,384]{3,2,1,0:T(8,128)(2,1)}, bf16[2,4,96,384]{3,2,1,0:T(8,128)(2,1)}, u32[]{:S(2)}, u32[]{:S(2)}) collective-permute-start(bf16[2,4,96,384]{3,2,1,0:T(8,128)(2,1)} %fusion.3), channel_id=1, source_target_pairs={{0,1},{1,0},{2,3},{3,2},{4,5},{5,4},{6,7},{7,6},{8,9},{9,8},{10,11... | collective-permute-start | bytes 1769480 | tf_op jit(solution)/shard_map/ppermute | solution.py:334
  154.1 29.4 %all-to-all-start.2 = ((bf16[8,96,512]{2,1,0:T(8,128)(2,1)}), bf16[8,96,512]{2,1,0:T(8,128)(2,1)S(1)}, u32[]{:S(2)}, u32[]{:S(2)}) async-start(bf16[8,96,512]{2,1,0:T(8,128)(2,1)} %bitcast.33), calls=%async_computation.2 | async-start | bytes 1572864 | tf_op jit(solution)/shard_map/all_to_all | solution.py:356
  158.2 16.0 %collective-permute-start.28 = (bf16[768,384]{1,0:T(8,128)(2,1)S(1)}, bf16[768,384]{1,0:T(8,128)(2,1)}, u32[]{:S(2)}, u32[]{:S(2)}) collective-permute-start(bf16[768,384]{1,0:T(8,128)(2,1)S(1)} %fusion.1), channel_id=1, source_target_pairs={{0,16},{8,24},{16,0},{24,8},{1,17},{9,25},{17,1},{25,9},{2,18},{10... | collective-permute-start | bytes 1769480 | tf_op jit(solution)/shard_map/ppermute | solution.py:334
  171.2 7.9 %collective-permute-start.32 = (bf16[4,96,384]{2,1,0:T(8,128)(2,1)S(1)}, bf16[4,96,384]{2,1,0:T(8,128)(2,1)S(1)}, u32[]{:S(2)}, u32[]{:S(2)}) collective-permute-start(bf16[4,96,384]{2,1,0:T(8,128)(2,1)S(1)} %fusion.5), channel_id=1, source_target_pairs={{0,16},{8,24},{16,0},{24,8},{1,17},{9,25},{17,1},{25,9},{2,18},{10... | collective-permute-start | bytes 884744 | tf_op jit(solution)/shard_map/ppermute | solution.py:334
  175.5 7.1 %collective-permute-start.29 = (bf16[4,96,384]{2,1,0:T(8,128)(2,1)S(1)}, bf16[4,96,384]{2,1,0:T(8,128)(2,1)S(1)}, u32[]{:S(2)}, u32[]{:S(2)}) collective-permute-start(bf16[4,96,384]{2,1,0:T(8,128)(2,1)S(1)} %get-tuple-element.125), channel_id=1, source_target_pairs={{0,1},{1,0},{2,3},{3,2},{4,5},{5,4},{6,7},{7,6},{8,9},{9,8},{10,11... | collective-permute-start | bytes 884744 | tf_op jit(solution)/shard_map/ppermute | solution.py:334
  183.5 16.9 %all-to-all-start.3 = ((bf16[4,96,768]{2,1,0:T(8,128)(2,1)}), bf16[4,96,768]{2,1,0:T(8,128)(2,1)S(1)}, u32[]{:S(2)}, u32[]{:S(2)}) async-start(bf16[4,96,768]{2,1,0:T(8,128)(2,1)} %shard_map.140), calls=%async_computation.3 | async-start | bytes 1179648 | tf_op jit(solution)/shard_map/all_to_all | solution.py:397
  (17 other events, 90.0 us)

commit v12 on v11

--- a/solution.py
+++ b/solution.py
@@ -67,8 +67,8 @@
     blocks = [(k, at) for k in range(count) for at in range(0, depth, block)]
 
     def body(starts_ref, rows_ref, *refs):
-        weight_refs, out_ref, later_refs = refs[:count], refs[count], refs[count + 1 : count + 1 + spare]
-        held_ref, piece_ref, sems, later_sems = refs[count + 1 + spare :]
+        weight_refs, out_refs, later_refs = refs[:count], refs[count : count + 2], refs[count + 2 : count + 2 + spare]
+        held_ref, piece_ref, sems, later_sems = refs[count + 2 + spare :]
         copies = []
         for n, (k, at) in enumerate(blocks):
             start = pl.multiple_of(starts_ref[k] + at, block)
@@ -101,17 +101,18 @@
                                 copy.wait()
                 span = slice(k * depth, (k + 1) * depth)
                 sums = sums + nn(held_ref[part, span], piece_ref[span])
-            out_ref[part] = sums
+            for n, out_ref in enumerate(out_refs):
+                out_ref[part] = sums[:, n * columns // 2 : (n + 1) * columns // 2]
         for copy in rest:
             copy.wait()
 
-    out = [jax.ShapeDtypeStruct((row_count, columns), F32)]
+    out = [jax.ShapeDtypeStruct((row_count, columns // 2), F32)] * 2
     out += [jax.ShapeDtypeStruct((row_count, block), BF)] * spare
     return pl.pallas_call(
         body,
         out_shape=out,
         in_specs=[SMEM] + [HBM] * (count + 1),
-        out_specs=[VMEM] * (1 + spare),
+        out_specs=[VMEM] * (2 + spare),
         scratch_shapes=[
             pltpu.VMEM((row_count, count * depth), BF),
             pltpu.VMEM((count * depth, columns), BF),
@@ -123,7 +124,7 @@
     )(jnp.stack(starts + later).astype(jnp.int32), rows, *weights)
 
 
-def absorb(total, column, blocks, weights, mib):
+def absorb(total, blocks, weights, mib):
     count = len(weights)
     row_count = total.shape[0]
     columns = weights[0].shape[1]
@@ -133,7 +134,7 @@
         half = row_count // 2
         for h in range(2):
             part = slice(h * half, (h + 1) * half)
-            sums = old_ref[part, column : column + columns]
+            sums = old_ref[part]
             for k in range(count):
                 sums = sums + nn(refs[k][part], refs[count + k][...])
             out_ref[part] = sums.astype(BF)
@@ -429,7 +430,7 @@
     for i in range(2):
         at, side_at = side * share + i * piece, (1 - side) * share + i * piece
         later += [near + at, away + at, near + side_at, away + side_at]
-    total, *blocks = product(rows, [projection, from_core], [me * depth, (me ^ 1) * depth], later, piece)
+    total, total_right, *blocks = product(rows, [projection, from_core], [me * depth, (me ^ 1) * depth], later, piece)
     weights = []
     for n in range(2):
         for i in range(2):
@@ -444,10 +445,10 @@
             sums.reshape(groups, block, columns), "seq", split_axis=0, concat_axis=0, tiled=True
         ).reshape(row_count, columns)
 
-    left = absorb(total, 0, blocks, weights[0] + weights[1], 20)
+    left = absorb(total, blocks, weights[0] + weights[1], 20)
     left, weights[3][3] = lax.optimization_barrier((left, weights[3][3]))
     left = send(left)
-    right = absorb(total, columns, blocks, weights[2] + weights[3], 60)
+    right = absorb(total_right, blocks, weights[2] + weights[3], 60)
     left, right = lax.optimization_barrier((left, right))
     right = send(right)
 

time: 202 us -> 201 us (level)
  transfers between devices with their start and end apart: 37 -> 37, of which waited for: 19 -> 21; matrix products, arithmetic and copies ran while one was open for 6% -> 6% of each run, Pallas kernels for 17% -> 17%
where the time goes in v12:
time: 201 us; the launch traced here: 200 us
  waiting for transfers between devices  78.2 us (39%)
  starting transfers between devices  60.3 us (30%)
  Pallas kernels  43.9 us (22%)
  other arithmetic  9.82 us (5%)
  local copies, waits for them, and re-layouts  5.76 us (3%)
    ppermute x25, waiting for transfers between devices, swap(): return lax.ppermute(value, axis, [(i, i ^ bit) for i in range(size)])  37.5 us
    pallas_call x12, Pallas kernels, call(): pl.pallas_call(body, out_shape=outs, in_specs=[SMEM] * smem + [ANY] * aft...  33.9 us
    ppermute x25, starting transfers between devices, swap(): return lax.ppermute(value, axis, [(i, i ^ bit) for i in range(size)])  20.8 us
    ppermute x4, starting transfers between devices, halo(): lax.ppermute(high, 'seq', up)  15.1 us
    all_to_all x2, waiting for transfers between devices, send(): lax.all_to_all(sums.reshape(groups, block, columns), 'seq', split_axis=0,...  12.4 us
    ppermute x4, waiting for transfers between devices, halo(): lax.ppermute(low, 'seq', [(j, i) for i, j in up])  10.6 us
    all_to_all x1, waiting for transfers between devices, crossed_sums(): lax.all_to_all(both, 'seq', split_axis=0, concat_axis=0, axis_index_group...  10.5 us
    pallas_call x1, Pallas kernels, product(): pl.pallas_call(body, out_shape=out, in_specs=[SMEM] + [HBM] * (count + 1)...  10 us
  transfers between devices with their start and end apart: 37, of which 21 were waited for; matrix products, arithmetic and copies ran while one was open for 6% of the time, Pallas kernels for 17%

profile of v12, /device:TPU:0, one launch (start us, length us, event | category | flops | bytes accessed | tf_op | source)
XLA Modules:
  0.0 199.7 jit_solution(7158897436154517313)
XLA Ops:
  1.1 1.7 fusion.6
  2.8 2.6 %collective-permute-start.5 = (bf16[512,384]{1,0:T(8,128)(2,1)S(1)}, bf16[512,384]{1,0:T(8,128)(2,1)S(1)}, u32[]{:S(2)}, u32[]{:S(2)}) collective-permute-start(bf16[512,384]{1,0:T(8,128)(2,1)S(1)} %get-tuple-element.124), channel_id=1, source_target_pairs={{0,16},{8,24},{16,0},{24,8},{1,17},{9,25},{17,1},{25,9},{2,18},{10... | collective-permute-start | bytes 1179656 | tf_op jit(solution)/shard_map/ppermute | solution.py:335
  5.5 9.9 %collective-permute-done.5.refs_12_ = bf16[512,384]{1,0:T(8,128)(2,1)S(1)} collective-permute-done((bf16[512,384]{1,0:T(8,128)(2,1)S(1)}, bf16[512,384]{1,0:T(8,128)(2,1)S(1)}, u32[]{:S(2)}, u32[]{:S(2)}) %collective-permute-start.5) | collective-permute-done | bytes 393248 | tf_op jit(solution)/shard_map/ppermute | solution.py:335
  15.4 2.0 collective-permute-start.7
  17.4 1.5 collective-permute-start.9
  19.0 10.0 %shard_map.129 = (f32[512,384]{1,0:T(8,128)S(1)}, f32[512,384]{1,0:T(8,128)}, bf16[512,512]{1,0:T(8,128)(2,1)S(1)}, bf16[512,512]{1,0:T(8,128)(2,1)S(1)}, bf16[5...) custom-call(s32[10]{0:T(128)S(1)} %stack.60.starts_ref, ...), custom_call_target="tpu_custom_call" | custom-call | flops 1024 | bytes 1024 | tf_op jit(solution)/shard_map/pallas_call | solution.py:111
  30.3 2.0 collective-permute-done.9.refs_14_
  32.3 6.6 %collective-permute-done.3.refs_10_ = bf16[512,384]{1,0:T(8,128)(2,1)S(1)} collective-permute-done((bf16[512,384]{1,0:T(8,128)(2,1)S(1)}, bf16[512,384]{1,0:T(8,128)(2,1)S(1)}, u32[]{:S(2)}, u32[]{:S(2)}) %collective-permute-start.3) | collective-permute-done | bytes 393248 | tf_op jit(solution)/shard_map/ppermute | solution.py:335
  38.8 1.6 collective-permute-done.11.refs_8_
  40.4 1.8 collective-permute-start.15
  42.3 1.5 collective-permute-start.13
  43.8 3.1 %shard_map.130 = bf16[512,384]{1,0:T(8,128)(2,1)} custom-call(f32[512,384]{1,0:T(8,128)S(1)} %get-tuple-element.64.old_ref, bf16[512,512]{1,0:T(8,128)(2,1)S(1)} %get-tuple-element.65.refs_0_, bf16[512,512]{1,0:T(8,128)(2,1)S(1)} %get-tuple-element.66.refs_1_, bf16[512,512]{1,0:T(8,128)(2,1)S(1)} %get-tuple-element.67.refs_2_, ...), custom_call_target="tpu_custom_call" | custom-call | flops 1024 | bytes 1024 | tf_op jit(solution)/shard_map/pallas_call | solution.py:52
  47.7 4.9 %all-to-all-start = ((bf16[8,64,384]{2,1,0:T(8,128)(2,1)}), bf16[8,64,384]{2,1,0:T(8,128)(2,1)}, u32[]{:S(2)}, u32[]{:S(2)}) async-start(bf16[8,64,384]{2,1,0:T(8,128)(2,1)} %bitcast.14), calls=%async_computation | async-start | bytes 786432 | tf_op jit(solution)/shard_map/all_to_all | solution.py:444
  56.4 6.6 %shard_map.131 = bf16[512,384]{1,0:T(8,128)(2,1)} custom-call(f32[512,384]{1,0:T(8,128)} %get-tuple-element.75.old_ref, bf16[512,512]{1,0:T(8,128)(2,1)} %copy-done.5, bf16[512,512]{1,0:T(8,128)(2,1)} %copy-done.6, bf16[512,512]{1,0:T(8,128)(2,1)} %copy-done.7, bf16[512,512]{1,0:T(8,128)(2,1)} %copy-done.8, bf16[512,512]{1,0:T(8,128)(2,1)} %copy-done.9, ...), custom_call_target="tpu_custom_call" | custom-call | flops 1024 | bytes 1024 | tf_op jit(solution)/shard_map/pallas_call | solution.py:52
  63.0 1.4 all-to-all-done
  64.4 4.5 %all-to-all-start.1 = ((bf16[8,64,384]{2,1,0:T(8,128)(2,1)}), bf16[8,64,384]{2,1,0:T(8,128)(2,1)}, u32[]{:S(2)}, u32[]{:S(2)}) async-start(bf16[8,64,384]{2,1,0:T(8,128)(2,1)} %bitcast.76), calls=%async_computation.1 | async-start | bytes 786432 | tf_op jit(solution)/shard_map/all_to_all | solution.py:444
  70.0 11.0 %all-to-all-done.1 = bf16[8,64,384]{2,1,0:T(8,128)(2,1)} async-done(((bf16[8,64,384]{2,1,0:T(8,128)(2,1)}), bf16[8,64,384]{2,1,0:T(8,128)(2,1)}, u32[]{:S(2)}, u32[]{:S(2)}) %all-to-all-start.1) | async-done | bytes 393248 | tf_op jit(solution)/shard_map/all_to_all | solution.py:444
  81.0 2.3 %shard_map.132 = (bf16[512,768]{1,0:T(8,128)(2,1)S(1)}, bf16[256,768]{1,0:T(8,128)(2,1)S(1)}, bf16[256,768]{1,0:T(8,128)(2,1)S(1)}, bf16[256,384]{1,0:T(8,128)(2,1)S(1)}, bf16[256,384]{1,0:T(8,128)(2,1)S(1)}) custom-call(s32[1,512]{1,0:T(1,128)S(1)} %compare_select_fusion.target_ref, bf16[512,384]{1,0:T(8,128)(2,1)} %bitcast.15.left_ref, ...), custom_call_target="tpu_custom_call" | custom-call | flops 1024 | bytes 1024 | tf_op jit(solution)/shard_map/pallas_call | solution.py:52
  83.3 3.4 %collective-permute-start.17 = (bf16[256,384]{1,0:T(8,128)(2,1)S(1)}, bf16[256,384]{1,0:T(8,128)(2,1)S(1)}, u32[]{:S(2)}, u32[]{:S(2)}) collective-permute-start(bf16[256,384]{1,0:T(8,128)(2,1)S(1)} %get-tuple-element.79), channel_id=1, source_target_pairs={{0,1},{1,2},{2,3},{3,4},{4,5},{5,6},{6,7},{8,9},{9,10},{10,11},{11... | collective-permute-start | bytes 589832 | tf_op jit(solution)/shard_map/ppermute | solution.py:342
  86.7 1.5 collective-permute-start.18
  89.1 5.2 %collective-permute-done.17.prev_ref = bf16[256,384]{1,0:T(8,128)(2,1)S(1)} collective-permute-done((bf16[256,384]{1,0:T(8,128)(2,1)S(1)}, bf16[256,384]{1,0:T(8,128)(2,1)S(1)}, u32[]{:S(2)}, u32[]{:S(2)}) %collective-permute-start.17) | collective-permute-done | bytes 196640 | tf_op jit(solution)/shard_map/ppermute | solution.py:342
  95.2 4.5 %collective-permute-start.19 = (bf16[128,384]{1,0:T(8,128)(2,1)S(1)}, bf16[128,384]{1,0:T(8,128)(2,1)S(1)}, u32[]{:S(2)}, u32[]{:S(2)}) collective-permute-start(bf16[128,384]{1,0:T(8,128)(2,1)S(1)} %get-tuple-element.84), channel_id=1, source_target_pairs={{0,1},{1,2},{2,3},{3,4},{4,5},{5,6},{6,7},{8,9},{9,10},{10,11},{11... | collective-permute-start | bytes 294920 | tf_op jit(solution)/shard_map/ppermute | solution.py:342
  99.7 1.3 collective-permute-start.20
  101.9 4.3 %collective-permute-done.20.refs_4_ = bf16[128,384]{1,0:T(8,128)(2,1)S(1)} collective-permute-done((bf16[128,384]{1,0:T(8,128)(2,1)S(1)}, bf16[128,384]{1,0:T(8,128)(2,1)S(1)}, u32[]{:S(2)}, u32[]{:S(2)}) %collective-permute-start.20) | collective-permute-done | bytes 98336 | tf_op jit(solution)/shard_map/ppermute | solution.py:343
  106.2 3.7 %shard_map.135 = (bf16[256,384]{1,0:T(8,128)(2,1)S(1)}, bf16[128,768]{1,0:T(8,128)(2,1)S(1)}, bf16[128,2048]{1,0:T(8,128)(2,1)S(1)}, bf16[128,768]{1,0:T(8,128)(...) custom-call(s32[2]{0:T(128)S(1)} %get-tuple-element.130.refs_0_, ...), custom_call_target="tpu_custom_call" | custom-call | flops 1024 | bytes 1024 | tf_op jit(solution)/shard_map/pallas_call | solution.py:52
  109.9 1.5 shard_map.136
  111.6 4.0 %collective-permute-start.22 = (bf16[128,384]{1,0:T(8,128)(2,1)S(1)}, bf16[128,384]{1,0:T(8,128)(2,1)S(1)}, u32[]{:S(2)}, u32[]{:S(2)}) collective-permute-start(bf16[128,384]{1,0:T(8,128)(2,1)S(1)} %get-tuple-element.93.refs_3_.refs_6_), channel_id=1, source_target_pairs={{0,1},{1,2},{2,3},{3,4},{4,5},{5,6},{6,7},{8,9},{9,10},{10,11},{11... | collective-permute-start | bytes 294920 | tf_op jit(solution)/shard_map/ppermute | solution.py:342
  115.6 1.3 collective-permute-start.23
  118.2 4.1 %collective-permute-done.23.refs_4_.refs_7_ = bf16[128,384]{1,0:T(8,128)(2,1)S(1)} collective-permute-done((bf16[128,384]{1,0:T(8,128)(2,1)S(1)}, bf16[128,384]{1,0:T(8,128)(2,1)S(1)}, u32[]{:S(2)}, u32[]{:S(2)}) %collective-permute-start.23) | collective-permute-done | bytes 98336 | tf_op jit(solution)/shard_map/ppermute | solution.py:343
  122.9 2.5 %shard_map.137 = (f32[256,768]{1,0:T(8,128)}, bf16[256,768]{1,0:T(8,128)(2,1)S(1)}, bf16[256,384]{1,0:T(8,128)(2,1)S(1)}, bf16[256,384]{1,0:T(8,128)(2,1)S(1)}) custom-call(bf16[768,512]{1,0:T(8,128)(2,1)S(1)} %fusion.2.refs_0_, bf16[128,384]{1,0:T(8,128)(2,1)S(1)} %collective-permute-done.22.refs_1_.refs_4_, ...), custom_call_target="tpu_custom_call" | custom-call | flops 1024 | bytes 1024 | tf_op jit(solution)/shard_map/pallas_call | solution.py:52
  125.4 3.2 %collective-permute-start.24 = (bf16[256,384]{1,0:T(8,128)(2,1)S(1)}, bf16[256,384]{1,0:T(8,128)(2,1)S(1)}, u32[]{:S(2)}, u32[]{:S(2)}) collective-permute-start(bf16[256,384]{1,0:T(8,128)(2,1)S(1)} %get-tuple-element.101.refs_6_), channel_id=1, source_target_pairs={{0,1},{1,2},{2,3},{3,4},{4,5},{5,6},{6,7},{8,9},{9,10},{10,11},{11... | collective-permute-start | bytes 589832 | tf_op jit(solution)/shard_map/ppermute | solution.py:342
  128.6 1.3 collective-permute-start.25
  129.9 4.2 %shard_map.138 = (bf16[2,768,384]{2,1,0:T(8,128)(2,1)S(1)}, bf16[2,768,384]{2,1,0:T(8,128)(2,1)S(1)}) custom-call(s32[2]{0:T(128)S(1)} %get-tuple-element.129.ids_ref.refs_0_, bf16[256,384]{1,0:T(8,128)(2,1)S(1)} %get-tuple-element.100.refs_1_.refs_5_, bf16[128,768]{1,0:T(8,128)(2,1)S(1)} %get-tuple-element.85.refs_2_, ...), custom_call_target="tpu_custom_call" | custom-call | flops 1024 | bytes 1024 | tf_op jit(solution)/shard_map/pallas_call | solution.py:52
  134.2 2.2 %collective-permute-done.25.refs_7_ = bf16[256,384]{1,0:T(8,128)(2,1)S(1)} collective-permute-done((bf16[256,384]{1,0:T(8,128)(2,1)S(1)}, bf16[256,384]{1,0:T(8,128)(2,1)S(1)}, u32[]{:S(2)}, u32[]{:S(2)}) %collective-permute-start.25) | collective-permute-done | bytes 196640 | tf_op jit(solution)/shard_map/ppermute | solution.py:343
  136.4 6.3 %shard_map.139 = (bf16[768,384]{1,0:T(8,128)(2,1)S(1)}, bf16[768,384]{1,0:T(8,128)(2,1)S(1)}, bf16[2,768,384]{2,1,0:T(8,128)(2,1)}) custom-call(s32[2]{0:T(128)S(1)} %get-tuple-element.129.ids_ref.refs_0_, bf16[256,384]{1,0:T(8,128)(2,1)S(1)} %get-tuple-element.100.refs_1_.refs_5_, bf16[256,768]{1,0:T(8,128)(2,1)S(1)} %get-tuple-element.81.low_ref.refs_2_, ...), custom_call_target="tpu_custom_call" | custom-call | flops 1024 | bytes 1024 | tf_op jit(solution)/shard_map/pallas_call | solution.py:52
  144.1 2.2 %fusion.3 = bf16[2,4,96,384]{3,2,1,0:T(8,128)(2,1)} fusion(bf16[2,4,2,96,384]{4,3,2,1,0:T(8,128)(2,1)} %bitcast.27, s32[]{:T(128)S(6)} %select_n.102, bf16[2,4,2,96,384]{4,3,2,1,0:T(8,128)(2,1)S(1)} %bitcast.70), kind=kLoop, calls=%fused_computation.9 | loop fusion | flops 1179648 | bytes 1769476 | tf_op jit(solution)/shard_map/convert_element_type | solution.py:384
  146.3 2.6 %collective-permute-start.31 = (bf16[2,4,96,384]{3,2,1,0:T(8,128)(2,1)}, bf16[2,4,96,384]{3,2,1,0:T(8,128)(2,1)}, u32[]{:S(2)}, u32[]{:S(2)}) collective-permute-start(bf16[2,4,96,384]{3,2,1,0:T(8,128)(2,1)} %fusion.3), channel_id=1, source_target_pairs={{0,1},{1,0},{2,3},{3,2},{4,5},{5,4},{6,7},{7,6},{8,9},{9,8},{10,11... | collective-permute-start | bytes 1769480 | tf_op jit(solution)/shard_map/ppermute | solution.py:335
  150.1 2.4 %fusion = bf16[768,512]{1,0:T(8,128)(2,1)} fusion(bf16[768,512]{1,0:T(8,128)(2,1)} %copy-done.18, bf16[2,768,512]{2,1,0:T(8,128)(2,1)S(1)} %copy-done.17, bf16[2,768,512]{2,1,0:T(8,128)(2,1)S(1)} %copy-done.14), kind=kLoop, calls=%fused_computation.1 | loop fusion | flops 2359296 | bytes 3145728 | tf_op jit(solution)/shard_map/convert_element_type | solution.py:395
  152.5 4.1 %all-to-all-start.2 = ((bf16[8,96,512]{2,1,0:T(8,128)(2,1)}), bf16[8,96,512]{2,1,0:T(8,128)(2,1)S(1)}, u32[]{:S(2)}, u32[]{:S(2)}) async-start(bf16[8,96,512]{2,1,0:T(8,128)(2,1)} %bitcast.33), calls=%async_computation.2 | async-start | bytes 1572864 | tf_op jit(solution)/shard_map/all_to_all | solution.py:357
  156.6 1.5 collective-permute-start.28
  158.0 10.1 %collective-permute-done.31 = bf16[2,4,96,384]{3,2,1,0:T(8,128)(2,1)} collective-permute-done((bf16[2,4,96,384]{3,2,1,0:T(8,128)(2,1)}, bf16[2,4,96,384]{3,2,1,0:T(8,128)(2,1)}, u32[]{:S(2)}, u32[]{:S(2)}) %collective-permute-start.31) | collective-permute-done | bytes 589856 | tf_op jit(solution)/shard_map/ppermute | solution.py:335
  168.2 1.4 bitcast_add_fusion.1
  169.6 1.5 collective-permute-start.32
  173.8 2.3 %collective-permute-start.29 = (bf16[4,96,384]{2,1,0:T(8,128)(2,1)S(1)}, bf16[4,96,384]{2,1,0:T(8,128)(2,1)S(1)}, u32[]{:S(2)}, u32[]{:S(2)}) collective-permute-start(bf16[4,96,384]{2,1,0:T(8,128)(2,1)S(1)} %get-tuple-element.127), channel_id=1, source_target_pairs={{0,1},{1,0},{2,3},{3,2},{4,5},{5,4},{6,7},{7,6},{8,9},{9,8},{10,11... | collective-permute-start | bytes 884744 | tf_op jit(solution)/shard_map/ppermute | solution.py:335
  176.2 1.4 collective-permute-done.32.right_came_ref
  177.6 3.4 %collective-permute-done.29.left_came_ref = bf16[4,96,384]{2,1,0:T(8,128)(2,1)S(1)} collective-permute-done((bf16[4,96,384]{2,1,0:T(8,128)(2,1)S(1)}, bf16[4,96,384]{2,1,0:T(8,128)(2,1)S(1)}, u32[]{:S(2)}, u32[]{:S(2)}) %collective-permute-start.29) | collective-permute-done | bytes 294944 | tf_op jit(solution)/shard_map/ppermute | solution.py:335
  181.9 5.6 %all-to-all-start.3 = ((bf16[4,96,768]{2,1,0:T(8,128)(2,1)}), bf16[4,96,768]{2,1,0:T(8,128)(2,1)S(1)}, u32[]{:S(2)}, u32[]{:S(2)}) async-start(bf16[4,96,768]{2,1,0:T(8,128)(2,1)} %shard_map.140), calls=%async_computation.3 | async-start | bytes 1179648 | tf_op jit(solution)/shard_map/all_to_all | solution.py:398
  188.2 10.5 %all-to-all-done.3.parts_ref = bf16[4,96,768]{2,1,0:T(8,128)(2,1)S(1)} async-done(((bf16[4,96,768]{2,1,0:T(8,128)(2,1)}), bf16[4,96,768]{2,1,0:T(8,128)(2,1)S(1)}, u32[]{:S(2)}, u32[]{:S(2)}) %all-to-all-start.3) | async-done | bytes 589856 | tf_op jit(solution)/shard_map/all_to_all | solution.py:398
  (112 shorter events, 19.7 us)
Async XLA Ops:
  0.6 18.3 %collective-permute-start.1 = (bf16[2048,768]{1,0:T(8,128)(2,1)}, bf16[2048,768]{1,0:T(8,128)(2,1)}, u32[]{:S(2)}, u32[]{:S(2)}) collective-permute-start(bf16[2048,768]{1,0:T(8,128)(2,1)} %refs_0_.1), channel_id=1, source_target_pairs={{0,8},{8,0},{16,24},{24,16},{1,9},{9,1},{17,25},{25,17},{2,10},{10... | collective-permute-start | bytes 9437192 | tf_op jit(solution)/shard_map/ppermute | solution.py:335
  2.8 12.6 %collective-permute-start.5 = (bf16[512,384]{1,0:T(8,128)(2,1)S(1)}, bf16[512,384]{1,0:T(8,128)(2,1)S(1)}, u32[]{:S(2)}, u32[]{:S(2)}) collective-permute-start(bf16[512,384]{1,0:T(8,128)(2,1)S(1)} %get-tuple-element.124), channel_id=1, source_target_pairs={{0,16},{8,24},{16,0},{24,8},{1,17},{9,25},{17,1},{25,9},{2,18},{10... | collective-permute-start | bytes 1179656 | tf_op jit(solution)/shard_map/ppermute | solution.py:335
  5.4 23.6 %collective-permute-start = (bf16[512,384]{1,0:T(8,128)(2,1)S(1)}, bf16[512,384]{1,0:T(8,128)(2,1)S(1)}, u32[]{:S(2)}, u32[]{:S(2)}) collective-permute-start(bf16[512,384]{1,0:T(8,128)(2,1)S(1)} %get-tuple-element.125), channel_id=1, source_target_pairs={{0,16},{8,24},{16,0},{24,8},{1,17},{9,25},{17,1},{25,9},{2,18},{10... | collective-permute-start | bytes 1179656 | tf_op jit(solution)/shard_map/ppermute | solution.py:335
  15.4 14.4 %collective-permute-start.7 = (bf16[512,384]{1,0:T(8,128)(2,1)S(1)}, bf16[512,384]{1,0:T(8,128)(2,1)S(1)}, u32[]{:S(2)}, u32[]{:S(2)}) collective-permute-start(bf16[512,384]{1,0:T(8,128)(2,1)S(1)} %collective-permute-done.5.refs_12_), channel_id=1, source_target_pairs={{0,1},{1,0},{2,3},{3,2},{4,5},{5,4},{6,7},{7,6},{8,9},{9,8},{10,11... | collective-permute-start | bytes 1179656 | tf_op jit(solution)/shard_map/ppermute | solution.py:335
  17.4 14.9 %collective-permute-start.9 = (bf16[512,384]{1,0:T(8,128)(2,1)S(1)}, bf16[512,384]{1,0:T(8,128)(2,1)S(1)}, u32[]{:S(2)}, u32[]{:S(2)}) collective-permute-start(bf16[512,384]{1,0:T(8,128)(2,1)S(1)} %get-tuple-element.126), channel_id=1, source_target_pairs={{0,16},{8,24},{16,0},{24,8},{1,17},{9,25},{17,1},{25,9},{2,18},{10... | collective-permute-start | bytes 1179656 | tf_op jit(solution)/shard_map/ppermute | solution.py:335
  29.0 17.9 %copy-start.5 = (bf16[512,512]{1,0:T(8,128)(2,1)}, bf16[512,512]{1,0:T(8,128)(2,1)S(1)}, u32[]{:S(2)}) copy-start(bf16[512,512]{1,0:T(8,128)(2,1)S(1)} %get-tuple-element.65.refs_0_) | copy-start | bytes 1572868
  29.0 17.9 %copy-start.6 = (bf16[512,512]{1,0:T(8,128)(2,1)}, bf16[512,512]{1,0:T(8,128)(2,1)S(1)}, u32[]{:S(2)}) copy-start(bf16[512,512]{1,0:T(8,128)(2,1)S(1)} %get-tuple-element.66.refs_1_) | copy-start | bytes 1572868
  29.0 17.9 %copy-start.7 = (bf16[512,512]{1,0:T(8,128)(2,1)}, bf16[512,512]{1,0:T(8,128)(2,1)S(1)}, u32[]{:S(2)}) copy-start(bf16[512,512]{1,0:T(8,128)(2,1)S(1)} %get-tuple-element.67.refs_2_) | copy-start | bytes 1572868
  29.0 17.9 %copy-start.8 = (bf16[512,512]{1,0:T(8,128)(2,1)}, bf16[512,512]{1,0:T(8,128)(2,1)S(1)}, u32[]{:S(2)}) copy-start(bf16[512,512]{1,0:T(8,128)(2,1)S(1)} %get-tuple-element.68.refs_3_) | copy-start | bytes 1572868
  29.0 17.9 %copy-start.9 = (bf16[512,512]{1,0:T(8,128)(2,1)}, bf16[512,512]{1,0:T(8,128)(2,1)S(1)}, u32[]{:S(2)}) copy-start(bf16[512,512]{1,0:T(8,128)(2,1)S(1)} %get-tuple-element.69.refs_4_) | copy-start | bytes 1572868
  29.0 17.9 %copy-start.10 = (bf16[512,512]{1,0:T(8,128)(2,1)}, bf16[512,512]{1,0:T(8,128)(2,1)S(1)}, u32[]{:S(2)}) copy-start(bf16[512,512]{1,0:T(8,128)(2,1)S(1)} %get-tuple-element.70.refs_5_) | copy-start | bytes 1572868
  29.0 17.9 %copy-start.11 = (bf16[512,512]{1,0:T(8,128)(2,1)}, bf16[512,512]{1,0:T(8,128)(2,1)S(1)}, u32[]{:S(2)}) copy-start(bf16[512,512]{1,0:T(8,128)(2,1)S(1)} %get-tuple-element.71.refs_6_) | copy-start | bytes 1572868
  29.0 17.9 %copy-start.12 = (bf16[512,512]{1,0:T(8,128)(2,1)}, bf16[512,512]{1,0:T(8,128)(2,1)S(1)}, u32[]{:S(2)}) copy-start(bf16[512,512]{1,0:T(8,128)(2,1)S(1)} %get-tuple-element.72.refs_7_) | copy-start | bytes 1572868
  29.1 9.7 %collective-permute-start.3 = (bf16[512,384]{1,0:T(8,128)(2,1)S(1)}, bf16[512,384]{1,0:T(8,128)(2,1)S(1)}, u32[]{:S(2)}, u32[]{:S(2)}) collective-permute-start(bf16[512,384]{1,0:T(8,128)(2,1)S(1)} %collective-permute-done.refs_8_), channel_id=1, source_target_pairs={{0,1},{1,0},{2,3},{3,2},{4,5},{5,4},{6,7},{7,6},{8,9},{9,8},{10,11... | collective-permute-start | bytes 1179656 | tf_op jit(solution)/shard_map/ppermute | solution.py:335
  29.6 10.8 %collective-permute-start.11 = (bf16[512,384]{1,0:T(8,128)(2,1)S(1)}, bf16[512,384]{1,0:T(8,128)(2,1)S(1)}, u32[]{:S(2)}, u32[]{:S(2)}) collective-permute-start(bf16[512,384]{1,0:T(8,128)(2,1)S(1)} %get-tuple-element.123), channel_id=1, source_target_pairs={{0,16},{8,24},{16,0},{24,8},{1,17},{9,25},{17,1},{25,9},{2,18},{10... | collective-permute-start | bytes 1179656 | tf_op jit(solution)/shard_map/ppermute | solution.py:335
  29.7 10.7 %collective-permute-start.6 = (bf16[512,384]{1,0:T(8,128)(2,1)S(1)}, bf16[512,384]{1,0:T(8,128)(2,1)S(1)}, u32[]{:S(2)}, u32[]{:S(2)}) collective-permute-start(bf16[512,384]{1,0:T(8,128)(2,1)S(1)} %collective-permute-done.5.refs_12_), channel_id=1, source_target_pairs={{0,8},{8,0},{16,24},{24,16},{1,9},{9,1},{17,25},{25,17},{2,10},{10... | collective-permute-start | bytes 1179656 | tf_op jit(solution)/shard_map/ppermute | solution.py:335
  29.7 12.5 %collective-permute-start.8 = (bf16[512,384]{1,0:T(8,128)(2,1)S(1)}, bf16[512,384]{1,0:T(8,128)(2,1)S(1)}, u32[]{:S(2)}, u32[]{:S(2)}) collective-permute-start(bf16[512,384]{1,0:T(8,128)(2,1)S(1)} %collective-permute-done.7.refs_14_), channel_id=1, source_target_pairs={{0,8},{8,0},{16,24},{24,16},{1,9},{9,1},{17,25},{25,17},{2,10},{10... | collective-permute-start | bytes 1179656 | tf_op jit(solution)/shard_map/ppermute | solution.py:335
  32.2 14.7 %copy-start.19 = (bf16[512,384]{1,0:T(8,128)(2,1)}, bf16[512,384]{1,0:T(8,128)(2,1)S(1)}, u32[]{:S(2)}) copy-start(bf16[512,384]{1,0:T(8,128)(2,1)S(1)} %collective-permute-done.9.refs_14_) | copy-start | bytes 1179652
  32.2 11.5 %collective-permute-start.2 = (bf16[512,384]{1,0:T(8,128)(2,1)S(1)}, bf16[512,384]{1,0:T(8,128)(2,1)S(1)}, u32[]{:S(2)}, u32[]{:S(2)}) collective-permute-start(bf16[512,384]{1,0:T(8,128)(2,1)S(1)} %collective-permute-done.refs_8_), channel_id=1, source_target_pairs={{0,8},{8,0},{16,24},{24,16},{1,9},{9,1},{17,25},{25,17},{2,10},{10... | collective-permute-start | bytes 1179656 | tf_op jit(solution)/shard_map/ppermute | solution.py:335
  38.8 5.0 %collective-permute-start.4 = (bf16[512,384]{1,0:T(8,128)(2,1)S(1)}, bf16[512,384]{1,0:T(8,128)(2,1)S(1)}, u32[]{:S(2)}, u32[]{:S(2)}) collective-permute-start(bf16[512,384]{1,0:T(8,128)(2,1)S(1)} %collective-permute-done.3.refs_10_), channel_id=1, source_target_pairs={{0,8},{8,0},{16,24},{24,16},{1,9},{9,1},{17,25},{25,17},{2,10},{10... | collective-permute-start | bytes 1179656 | tf_op jit(solution)/shard_map/ppermute | solution.py:335
  40.4 6.5 %collective-permute-start.10 = (bf16[512,384]{1,0:T(8,128)(2,1)S(1)}, bf16[512,384]{1,0:T(8,128)(2,1)S(1)}, u32[]{:S(2)}, u32[]{:S(2)}) collective-permute-start(bf16[512,384]{1,0:T(8,128)(2,1)S(1)} %collective-permute-done.9.refs_14_), channel_id=1, source_target_pairs={{0,8},{8,0},{16,24},{24,16},{1,9},{9,1},{17,25},{25,17},{2,10},{10... | collective-permute-start | bytes 1179656 | tf_op jit(solution)/shard_map/ppermute | solution.py:335
  40.4 12.2 %collective-permute-start.15 = (bf16[512,384]{1,0:T(8,128)(2,1)S(1)}, bf16[512,384]{1,0:T(8,128)(2,1)S(1)}, u32[]{:S(2)}, u32[]{:S(2)}) collective-permute-start(bf16[512,384]{1,0:T(8,128)(2,1)S(1)} %get-tuple-element.122), channel_id=1, source_target_pairs={{0,16},{8,24},{16,0},{24,8},{1,17},{9,25},{17,1},{25,9},{2,18},{10... | collective-permute-start | bytes 1179656 | tf_op jit(solution)/shard_map/ppermute | solution.py:335
  42.3 11.2 %collective-permute-start.13 = (bf16[512,384]{1,0:T(8,128)(2,1)S(1)}, bf16[512,384]{1,0:T(8,128)(2,1)S(1)}, u32[]{:S(2)}, u32[]{:S(2)}) collective-permute-start(bf16[512,384]{1,0:T(8,128)(2,1)S(1)} %collective-permute-done.11.refs_8_), channel_id=1, source_target_pairs={{0,1},{1,0},{2,3},{3,2},{4,5},{5,4},{6,7},{7,6},{8,9},{9,8},{10,11... | collective-permute-start | bytes 1179656 | tf_op jit(solution)/shard_map/ppermute | solution.py:335
  47.7 16.7 %all-to-all-start = ((bf16[8,64,384]{2,1,0:T(8,128)(2,1)}), bf16[8,64,384]{2,1,0:T(8,128)(2,1)}, u32[]{:S(2)}, u32[]{:S(2)}) async-start(bf16[8,64,384]{2,1,0:T(8,128)(2,1)} %bitcast.14), calls=%async_computation | async-start | bytes 786432 | tf_op jit(solution)/shard_map/all_to_all | solution.py:444
  52.6 1.8 collective-permute-start.12
  52.7 2.3 %collective-permute-start.16 = (bf16[512,384]{1,0:T(8,128)(2,1)S(1)}, bf16[512,384]{1,0:T(8,128)(2,1)S(1)}, u32[]{:S(2)}, u32[]{:S(2)}) collective-permute-start(bf16[512,384]{1,0:T(8,128)(2,1)S(1)} %collective-permute-done.15.refs_12_), channel_id=1, source_target_pairs={{0,8},{8,0},{16,24},{24,16},{1,9},{9,1},{17,25},{25,17},{2,10},{10... | collective-permute-start | bytes 1179656 | tf_op jit(solution)/shard_map/ppermute | solution.py:335
  53.4 2.0 %collective-permute-start.14 = (bf16[512,384]{1,0:T(8,128)(2,1)S(1)}, bf16[512,384]{1,0:T(8,128)(2,1)S(1)}, u32[]{:S(2)}, u32[]{:S(2)}) collective-permute-start(bf16[512,384]{1,0:T(8,128)(2,1)S(1)} %collective-permute-done.13.refs_10_), channel_id=1, source_target_pairs={{0,8},{8,0},{16,24},{24,16},{1,9},{9,1},{17,25},{25,17},{2,10},{10... | collective-permute-start | bytes 1179656 | tf_op jit(solution)/shard_map/ppermute | solution.py:335
  56.4 12.5 %copy-start.27 = (s32[1,8,8]{2,1,0:T(8,128)S(1)}, s32[1,8,8]{2,1,0:T(8,128)}, u32[]{:S(2)}) copy-start(s32[1,8,8]{2,1,0:T(8,128)} %param.11) | copy-start | bytes 772
  56.4 24.6 %copy-start = (bf16[2,3,768,384]{3,2,1,0:T(8,128)(2,1)S(1)}, bf16[2,3,768,384]{3,2,1,0:T(8,128)(2,1)}, u32[]{:S(2)}) copy-start(bf16[2,3,768,384]{3,2,1,0:T(8,128)(2,1)} %refs_7_.3) | copy-start | bytes 10616836
  64.4 16.6 %all-to-all-start.1 = ((bf16[8,64,384]{2,1,0:T(8,128)(2,1)}), bf16[8,64,384]{2,1,0:T(8,128)(2,1)}, u32[]{:S(2)}, u32[]{:S(2)}) async-start(bf16[8,64,384]{2,1,0:T(8,128)(2,1)} %bitcast.76), calls=%async_computation.1 | async-start | bytes 786432 | tf_op jit(solution)/shard_map/all_to_all | solution.py:444
  83.3 11.0 %collective-permute-start.17 = (bf16[256,384]{1,0:T(8,128)(2,1)S(1)}, bf16[256,384]{1,0:T(8,128)(2,1)S(1)}, u32[]{:S(2)}, u32[]{:S(2)}) collective-permute-start(bf16[256,384]{1,0:T(8,128)(2,1)S(1)} %get-tuple-element.79), channel_id=1, source_target_pairs={{0,1},{1,2},{2,3},{3,4},{4,5},{5,6},{6,7},{8,9},{9,10},{10,11},{11... | collective-permute-start | bytes 589832 | tf_op jit(solution)/shard_map/ppermute | solution.py:342
  86.7 7.6 %collective-permute-start.18 = (bf16[256,384]{1,0:T(8,128)(2,1)S(1)}, bf16[256,384]{1,0:T(8,128)(2,1)S(1)}, u32[]{:S(2)}, u32[]{:S(2)}) collective-permute-start(bf16[256,384]{1,0:T(8,128)(2,1)S(1)} %get-tuple-element.80), channel_id=1, source_target_pairs={{1,0},{2,1},{3,2},{4,3},{5,4},{6,5},{7,6},{9,8},{10,9},{11,10},{12... | collective-permute-start | bytes 589832 | tf_op jit(solution)/shard_map/ppermute | solution.py:343
  95.2 6.7 %collective-permute-start.19 = (bf16[128,384]{1,0:T(8,128)(2,1)S(1)}, bf16[128,384]{1,0:T(8,128)(2,1)S(1)}, u32[]{:S(2)}, u32[]{:S(2)}) collective-permute-start(bf16[128,384]{1,0:T(8,128)(2,1)S(1)} %get-tuple-element.84), channel_id=1, source_target_pairs={{0,1},{1,2},{2,3},{3,4},{4,5},{5,6},{6,7},{8,9},{9,10},{10,11},{11... | collective-permute-start | bytes 294920 | tf_op jit(solution)/shard_map/ppermute | solution.py:342
  99.7 6.5 %collective-permute-start.20 = (bf16[128,384]{1,0:T(8,128)(2,1)S(1)}, bf16[128,384]{1,0:T(8,128)(2,1)S(1)}, u32[]{:S(2)}, u32[]{:S(2)}) collective-permute-start(bf16[128,384]{1,0:T(8,128)(2,1)S(1)} %get-tuple-element.87), channel_id=1, source_target_pairs={{1,0},{2,1},{3,2},{4,3},{5,4},{6,5},{7,6},{9,8},{10,9},{11,10},{12... | collective-permute-start | bytes 294920 | tf_op jit(solution)/shard_map/ppermute | solution.py:343
  111.5 5.4 %collective-permute-start.21 = (bf16[2,768,512]{2,1,0:T(8,128)(2,1)S(1)}, bf16[2,768,512]{2,1,0:T(8,128)(2,1)S(1)}, u32[]{:S(2)}, u32[]{:S(2)}) collective-permute-start(bf16[2,768,512]{2,1,0:T(8,128)(2,1)S(1)} %get-tuple-element.92), channel_id=1, source_target_pairs={{0,8},{8,0},{16,24},{24,16},{1,9},{9,1},{17,25},{25,17},{2,10},{10... | collective-permute-start | bytes 4718600 | tf_op jit(solution)/shard_map/ppermute | solution.py:335
  111.6 6.7 %collective-permute-start.22 = (bf16[128,384]{1,0:T(8,128)(2,1)S(1)}, bf16[128,384]{1,0:T(8,128)(2,1)S(1)}, u32[]{:S(2)}, u32[]{:S(2)}) collective-permute-start(bf16[128,384]{1,0:T(8,128)(2,1)S(1)} %get-tuple-element.93.refs_3_.refs_6_), channel_id=1, source_target_pairs={{0,1},{1,2},{2,3},{3,4},{4,5},{5,6},{6,7},{8,9},{9,10},{10,11},{11... | collective-permute-start | bytes 294920 | tf_op jit(solution)/shard_map/ppermute | solution.py:342
  115.6 6.8 %collective-permute-start.23 = (bf16[128,384]{1,0:T(8,128)(2,1)S(1)}, bf16[128,384]{1,0:T(8,128)(2,1)S(1)}, u32[]{:S(2)}, u32[]{:S(2)}) collective-permute-start(bf16[128,384]{1,0:T(8,128)(2,1)S(1)} %get-tuple-element.94.refs_2_.refs_5_), channel_id=1, source_target_pairs={{1,0},{2,1},{3,2},{4,3},{5,4},{6,5},{7,6},{9,8},{10,9},{11,10},{12... | collective-permute-start | bytes 294920 | tf_op jit(solution)/shard_map/ppermute | solution.py:343
  122.4 20.3 %collective-permute-start.26 = (bf16[768,512]{1,0:T(8,128)(2,1)S(1)}, bf16[768,512]{1,0:T(8,128)(2,1)S(1)}, u32[]{:S(2)}, u32[]{:S(2)}) collective-permute-start(bf16[768,512]{1,0:T(8,128)(2,1)S(1)} %fusion.2.refs_0_), channel_id=1, source_target_pairs={{0,16},{8,24},{16,0},{24,8},{1,17},{9,25},{17,1},{25,9},{2,18},{10... | collective-permute-start | bytes 2359304 | tf_op jit(solution)/shard_map/ppermute | solution.py:335
  125.4 8.8 %collective-permute-start.24 = (bf16[256,384]{1,0:T(8,128)(2,1)S(1)}, bf16[256,384]{1,0:T(8,128)(2,1)S(1)}, u32[]{:S(2)}, u32[]{:S(2)}) collective-permute-start(bf16[256,384]{1,0:T(8,128)(2,1)S(1)} %get-tuple-element.101.refs_6_), channel_id=1, source_target_pairs={{0,1},{1,2},{2,3},{3,4},{4,5},{5,6},{6,7},{8,9},{9,10},{10,11},{11... | collective-permute-start | bytes 589832 | tf_op jit(solution)/shard_map/ppermute | solution.py:342
  128.6 7.7 %collective-permute-start.25 = (bf16[256,384]{1,0:T(8,128)(2,1)S(1)}, bf16[256,384]{1,0:T(8,128)(2,1)S(1)}, u32[]{:S(2)}, u32[]{:S(2)}) collective-permute-start(bf16[256,384]{1,0:T(8,128)(2,1)S(1)} %get-tuple-element.100.refs_1_.refs_5_), channel_id=1, source_target_pairs={{1,0},{2,1},{3,2},{4,3},{5,4},{6,5},{7,6},{9,8},{10,9},{11,10},{12... | collective-permute-start | bytes 589832 | tf_op jit(solution)/shard_map/ppermute | solution.py:343
  136.3 7.8 %collective-permute-start.30 = (bf16[2,768,384]{2,1,0:T(8,128)(2,1)S(1)}, bf16[2,768,384]{2,1,0:T(8,128)(2,1)}, u32[]{:S(2)}, u32[]{:S(2)}) collective-permute-start(bf16[2,768,384]{2,1,0:T(8,128)(2,1)S(1)} %get-tuple-element.115), channel_id=1, source_target_pairs={{0,8},{8,0},{16,24},{24,16},{1,9},{9,1},{17,25},{25,17},{2,10},{10... | collective-permute-start | bytes 3538952 | tf_op jit(solution)/shard_map/ppermute | solution.py:335
  143.6 5.2 %collective-permute-start.27 = (bf16[2,768,384]{2,1,0:T(8,128)(2,1)}, bf16[2,768,384]{2,1,0:T(8,128)(2,1)}, u32[]{:S(2)}, u32[]{:S(2)}) collective-permute-start(bf16[2,768,384]{2,1,0:T(8,128)(2,1)} %get-tuple-element.110), channel_id=1, source_target_pairs={{0,8},{8,0},{16,24},{24,16},{1,9},{9,1},{17,25},{25,17},{2,10},{10... | collective-permute-start | bytes 3538952 | tf_op jit(solution)/shard_map/ppermute | solution.py:335
  146.3 21.9 %collective-permute-start.31 = (bf16[2,4,96,384]{3,2,1,0:T(8,128)(2,1)}, bf16[2,4,96,384]{3,2,1,0:T(8,128)(2,1)}, u32[]{:S(2)}, u32[]{:S(2)}) collective-permute-start(bf16[2,4,96,384]{3,2,1,0:T(8,128)(2,1)} %fusion.3), channel_id=1, source_target_pairs={{0,1},{1,0},{2,3},{3,2},{4,5},{5,4},{6,7},{7,6},{8,9},{9,8},{10,11... | collective-permute-start | bytes 1769480 | tf_op jit(solution)/shard_map/ppermute | solution.py:335
  152.5 29.4 %all-to-all-start.2 = ((bf16[8,96,512]{2,1,0:T(8,128)(2,1)}), bf16[8,96,512]{2,1,0:T(8,128)(2,1)S(1)}, u32[]{:S(2)}, u32[]{:S(2)}) async-start(bf16[8,96,512]{2,1,0:T(8,128)(2,1)} %bitcast.33), calls=%async_computation.2 | async-start | bytes 1572864 | tf_op jit(solution)/shard_map/all_to_all | solution.py:357
  156.6 16.0 %collective-permute-start.28 = (bf16[768,384]{1,0:T(8,128)(2,1)S(1)}, bf16[768,384]{1,0:T(8,128)(2,1)}, u32[]{:S(2)}, u32[]{:S(2)}) collective-permute-start(bf16[768,384]{1,0:T(8,128)(2,1)S(1)} %fusion.1), channel_id=1, source_target_pairs={{0,16},{8,24},{16,0},{24,8},{1,17},{9,25},{17,1},{25,9},{2,18},{10... | collective-permute-start | bytes 1769480 | tf_op jit(solution)/shard_map/ppermute | solution.py:335
  169.6 7.9 %collective-permute-start.32 = (bf16[4,96,384]{2,1,0:T(8,128)(2,1)S(1)}, bf16[4,96,384]{2,1,0:T(8,128)(2,1)S(1)}, u32[]{:S(2)}, u32[]{:S(2)}) collective-permute-start(bf16[4,96,384]{2,1,0:T(8,128)(2,1)S(1)} %fusion.5), channel_id=1, source_target_pairs={{0,16},{8,24},{16,0},{24,8},{1,17},{9,25},{17,1},{25,9},{2,18},{10... | collective-permute-start | bytes 884744 | tf_op jit(solution)/shard_map/ppermute | solution.py:335
  173.8 7.2 %collective-permute-start.29 = (bf16[4,96,384]{2,1,0:T(8,128)(2,1)S(1)}, bf16[4,96,384]{2,1,0:T(8,128)(2,1)S(1)}, u32[]{:S(2)}, u32[]{:S(2)}) collective-permute-start(bf16[4,96,384]{2,1,0:T(8,128)(2,1)S(1)} %get-tuple-element.127), channel_id=1, source_target_pairs={{0,1},{1,0},{2,3},{3,2},{4,5},{5,4},{6,7},{7,6},{8,9},{9,8},{10,11... | collective-permute-start | bytes 884744 | tf_op jit(solution)/shard_map/ppermute | solution.py:335
  181.9 16.9 %all-to-all-start.3 = ((bf16[4,96,768]{2,1,0:T(8,128)(2,1)}), bf16[4,96,768]{2,1,0:T(8,128)(2,1)S(1)}, u32[]{:S(2)}, u32[]{:S(2)}) async-start(bf16[4,96,768]{2,1,0:T(8,128)(2,1)} %shard_map.140), calls=%async_computation.3 | async-start | bytes 1179648 | tf_op jit(solution)/shard_map/all_to_all | solution.py:398
  (17 other events, 87.7 us)
